TPU v7x, 32 devices: a whole 2x2x4 slice. The times are simulated.
32 devices in a mesh: grp: 2 (over y), gene: 4 (over z), cell: 4 (over x, core).
Axes of the slice: x: 2, y: 2, z: 4, core: 2. Of those that a mesh axis runs over, the one named last changes fastest.
Arguments:
- expression: bfloat16 [4096, 32768], P(('grp', 'cell'), 'gene'), parts along dimension 0, may hold values from -6 to 6
- gene_mask: int32 [4096, 32768], P(('grp', 'cell'), 'gene'), parts along dimension 0, may hold values 0 or 1
- mask_value: bfloat16 [32768], P('gene'), may hold values from -4 to 4
- w_qkv: bfloat16 [32768, 3072], P('gene'), may hold values from -0.03125 to 0.03125
- w_out: bfloat16 [1024, 32768], P(None, 'gene'), may hold values from -1.5 to 1.5
- w_first: bfloat16 [128, 256, 256], P('gene'), may hold values from -0.375 to 0.375
- w_second: bfloat16 [128, 256, 256], P('gene'), may hold values from -0.375 to 0.375
- cotangent: bfloat16 [4096, 32768], P(('grp', 'cell'), 'gene'), parts along dimension 0, may hold values from -6 to 6
Outputs:
- denoised: bfloat16 [4096, 32768], P(('grp', 'cell'), 'gene'), parts along dimension 0
- grad_first: float32 [256, 256, 256], P(('grp', 'gene'), 'cell'), parts along dimension 0
- grad_second: float32 [256, 256, 256], P(('grp', 'gene'), 'cell'), parts along dimension 0
There are 2 independent parts, one for each index of `grp`. A program takes and returns all parts, laid end to end along the dimension named above; an argument that names none is the same for every part. Nothing has to cross between parts.
All inputs are finite; a program needn't handle non-finite values. No bound on the sum of `gene_mask` on one device may be relied on, other than what follows from the above.
Results may differ from a plain program's by a relative error of at most 0.02.
Values may be sent and summed in bfloat16 or wider, within the bound.
No kernel may reach another device: no remote copies, remote signals or barrier semaphores. Data moves between devices by JAX's collectives and lax.ppermute only.
A program may use at most 256 MiB of HBM per device.

v0:
```python
import jax
import jax.numpy as jnp
from jax import lax
from jax.sharding import PartitionSpec as P

HEADS = 16
HEAD_DIM = 64


def normalize(part):
    count = part.shape[0]
    shaped = part.reshape(count, HEADS, HEAD_DIM)
    meansq = jnp.mean(shaped * shaped, axis=-1, keepdims=True)
    return (
        (shaped * lax.rsqrt(meansq + 1e-06)).astype(jnp.bfloat16).reshape(count, HEADS * HEAD_DIM)
    )


def split_heads(qkv_sums):
    columns = qkv_sums.shape[1] // 3
    queries = normalize(qkv_sums[:, :columns])
    keys_normed = normalize(qkv_sums[:, columns : 2 * columns])
    values_b = qkv_sums[:, 2 * columns :].astype(jnp.bfloat16)
    return (queries, keys_normed, values_b)


def attend(queries, pieces):
    key_piece, value_piece = pieces
    query_count = queries.shape[0]
    key_count = key_piece.shape[0]
    query_heads = queries.reshape(query_count, HEADS, HEAD_DIM)
    key_heads = key_piece.reshape(key_count, HEADS, HEAD_DIM)
    value_heads = value_piece.reshape(key_count, HEADS, HEAD_DIM)
    scores = jnp.einsum(
        "qhd,khd->hqk", query_heads, key_heads, preferred_element_type=jnp.float32
    ) * HEAD_DIM ** (-0.5)
    expw = jnp.exp(scores).astype(jnp.bfloat16)
    denom = jnp.sum(expw, axis=2, dtype=jnp.float32)
    numer = jnp.einsum("hqk,khd->qhd", expw, value_heads, preferred_element_type=jnp.float32)
    return (numer, denom)


def finish(totals):
    numer, denom = totals
    query_count = numer.shape[0]
    return (numer / denom.T[:, :, None]).astype(jnp.bfloat16).reshape(query_count, HEADS * HEAD_DIM)


def on_device(expression, gene_mask, mask_value, w_qkv, w_out, w_first, w_second, cotangent):
    groups = lax.axis_size("gene")
    local_blocks = w_first.shape[0]
    block_size = w_first.shape[1]
    block_total = local_blocks * groups
    cell_rows = expression.shape[0]
    masked_in = jnp.where(gene_mask == 1, mask_value[None, :], expression)
    qkv_part = jnp.dot(masked_in, w_qkv, preferred_element_type=jnp.float32)
    qkv_full = lax.psum(qkv_part.astype(jnp.bfloat16), "gene").astype(jnp.float32)
    queries, keys_normed, values_b = split_heads(qkv_full)
    totals = attend(
        queries,
        (
            lax.all_gather(keys_normed, "cell", axis=0, tiled=True),
            lax.all_gather(values_b, "cell", axis=0, tiled=True),
        ),
    )
    attended = finish(totals)
    added = jnp.dot(attended, w_out, preferred_element_type=jnp.float32)
    hidden = (masked_in.astype(jnp.float32) + added).astype(jnp.bfloat16)
    blocks = hidden.reshape(cell_rows, local_blocks, block_size)
    first = jnp.einsum("cbi,bio->cbo", blocks, w_first, preferred_element_type=jnp.float32).astype(
        jnp.bfloat16
    )
    cot_blocks = cotangent.reshape(cell_rows, local_blocks, block_size)
    back_perm = jnp.einsum(
        "cjo,jko->cjk", cot_blocks, w_second, preferred_element_type=jnp.float32
    ).astype(jnp.bfloat16)
    back_send = back_perm.reshape(cell_rows, block_size // groups, block_total)
    received = lax.all_to_all(first, "gene", split_axis=2, concat_axis=1, tiled=True)
    permuted = jnp.swapaxes(received, 1, 2).reshape(cell_rows, local_blocks, block_size)
    mixed = jnp.einsum("cjk,jko->cjo", permuted, w_second, preferred_element_type=jnp.float32)
    denoised = (
        (blocks.astype(jnp.float32) + mixed)
        .astype(jnp.bfloat16)
        .reshape(cell_rows, local_blocks * block_size)
    )
    grad_second = jnp.einsum(
        "cjk,cjo->jko", permuted, cot_blocks, preferred_element_type=jnp.float32
    )
    back_recv = lax.all_to_all(back_send, "gene", split_axis=2, concat_axis=1, tiled=True)
    back_first = jnp.swapaxes(back_recv, 1, 2)
    grad_first = jnp.einsum("cbi,cbo->bio", blocks, back_first, preferred_element_type=jnp.float32)
    first_share, second_share = (
        lax.psum_scatter(
            grad_first.astype(jnp.bfloat16), "cell", scatter_dimension=1, tiled=True
        ).astype(jnp.float32),
        lax.psum_scatter(
            grad_second.astype(jnp.bfloat16), "cell", scatter_dimension=1, tiled=True
        ).astype(jnp.float32),
    )
    return (denoised, first_share, second_share)


def solution(mesh):
    placed = (
        P(("grp", "cell"), "gene"),
        P(("grp", "cell"), "gene"),
        P("gene"),
        P("gene", None),
        P(None, "gene"),
        P("gene", None, None),
        P("gene", None, None),
        P(("grp", "cell"), "gene"),
    )
    return jax.shard_map(
        on_device,
        mesh=mesh,
        in_specs=placed,
        out_specs=(
            P(("grp", "cell"), "gene"),
            P(("grp", "gene"), "cell", None),
            P(("grp", "gene"), "cell", None),
        ),
        check_vma=False,
    )
```

profile of v0, /device:TPU:0, one launch (start us, length us, event | category | flops | bytes accessed | tf_op | source)
XLA Modules:
  0.0 680.9 jit_solution(10328082861231233537)
XLA Ops:
  7.2 0.0 all-reduce.2.cloned.1.call-start
  7.2 9.0 %compare_select_fusion = bf16[512,8192]{1,0:T(8,128)(2,1)S(1)} fusion(bf16[512,8192]{1,0:T(8,128)(2,1)} %param.8, s32[512,8192]{1,0:T(8,128)} %param.9, bf16[8192]{0:T(1024)(128)(2,1)} %param.10), kind=kLoop, calls=%fused_computation.5 | loop fusion | flops 8388608 | bytes 33570816 | tf_op jit(solution)/shard_map/jit(_where)/select_n | solution.py:55
  16.3 3.4 copy-done
  19.7 32.1 %convolution_convert_fusion = bf16[512,3072]{1,0:T(8,128)(2,1)} fusion(bf16[512,8192]{1,0:T(8,128)(2,1)S(1)} %compare_select_fusion, bf16[8192,3072]{1,0:T(8,128)(2,1)} %param.11), kind=kOutput, calls=%fused_computation.16 | convolution fusion | flops 25771376640 | bytes 61865984 | tf_op jit(solution)/shard_map/dot_general | solution.py:56
  51.8 0.0 all-gather.5.cloned.1.call-start
  51.9 123.9 %all-reduce.2.cloned.1.call-done = bf16[512,3072]{1,0:T(8,128)(2,1)} async-done(((bf16[512,3072]{1,0:T(8,128)(2,1)}), bf16[512,3072]{1,0:T(8,128)(2,1)}) %all-reduce.2.cloned.1.call-update) | async-done | bytes 3145744 | tf_op jit(solution)/shard_map/psum | solution.py:57
  175.8 2.7 convert_element_type.61
  178.4 2.6 copy-done.1
  181.1 0.2 slice_multiply_fusion
  181.3 1.8 copy.61
  183.1 2.0 bitcast_reduce_fusion
  185.1 1.6 mul.39
  186.7 2.9 copy.62
  189.6 3.5 multiply_convert_fusion
  193.1 0.6 all-gather.3.cloned.1.call-start
  193.7 1.0 slice.13
  194.8 10.7 %fusion.9 = bf16[32,256,512]{2,1,0:T(8,128)(2,1)} fusion(bf16[32,256,256]{2,1,0:T(8,128)(2,1)} %param.14, bf16[64,32,8,256]{3,2,1,0:T(8,128)(2,1)} %bitcast.75), kind=kOutput, calls=%fused_computation.15 | convolution fusion | flops 2151677952 | bytes 20971520 | tf_op jit(solution)/shard_map/cjo,jko->cjk/dot_general | solution.py:74
  205.5 11.4 %copy.73 = bf16[512,64,128]{0,1,2:T(8,128)(2,1)} copy(bf16[512,64,128]{0,2,1:T(8,128)(2,1)} %bitcast.72) | data formatting | bytes 16777216 | tf_op jit(solution)/shard_map/reshape | solution.py:77
  216.8 5.8 all-to-all-start.1
  222.7 1.6 slice.14
  224.2 1.9 copy.60
  226.2 0.3 multiply_reduce_fusion
  226.5 0.3 all-gather.5.cloned.1.call-done
  226.8 6.5 copy.63
  233.3 30.1 %all-gather.3.cloned.1.call-done = bf16[2048,1024]{1,0:T(8,128)(2,1)} async-done(((bf16[512,1024]{1,0:T(8,128)(2,1)}), bf16[2048,1024]{1,0:T(8,128)(2,1)}) %all-gather.3.cloned.1.call-update) | async-done | bytes 4194320 | tf_op jit(solution)/shard_map/all_gather | solution.py:63
  263.4 6.5 copy.59
  269.9 18.0 %convert_reduce_fusion = (f32[16,512]{1,0:T(8,128)S(1)}, bf16[16,512,2048]{2,1,0:T(8,128)(2,1)}) fusion(bf16[2048,16,64]{0,2,1:T(8,128)(2,1)} %bitcast.79, f32[512,16,64]{0,2,1:T(8,128)S(1)} %bitcast.77, f32[512,16]{0,1:T(8,128)S(1)} %add_rsqrt_fusion.1), kind=kOutput, calls=%fused_computation | convolution fusion | flops 2215632896 | bytes 39911424 | tf_op jit(solution)/shard_map/qhd,khd->hqk/dot_general | solution.py:34
  287.9 17.0 %fusion.18 = bf16[512,16,64]{0,2,1:T(8,128)(2,1)S(1)} fusion(bf16[2048,16,64]{0,2,1:T(8,128)(2,1)} %bitcast.73, bf16[16,512,2048]{2,1,0:T(8,128)(2,1)} %get-tuple-element.16, f32[512,16]{0,1:T(8,128)S(1)} %bitcast.80), kind=kOutput, calls=%fused_computation.20 | convolution fusion | flops 2148532224 | bytes 38830080 | tf_op jit(solution)/shard_map/hqk,khd->qhd/dot_general | solution.py:39
  304.9 18.4 %add_convert_fusion = bf16[512,8192]{1,0:T(8,128)(2,1)} fusion(bf16[512,8192]{1,0:T(8,128)(2,1)} %copy-done, bf16[512,1024]{0,1:T(8,128)(2,1)S(1)} %bitcast.74, bf16[1024,8192]{1,0:T(8,128)(2,1)} %param.12), kind=kOutput, calls=%fused_computation.4 | convolution fusion | flops 8602517504 | bytes 34603008 | tf_op jit(solution)/shard_map/dot_general | solution.py:67
  323.3 12.0 %copy.84 = bf16[512,8192]{0,1:T(8,128)(2,1)} copy(bf16[512,8192]{1,0:T(8,128)(2,1)} %add_convert_fusion) | data formatting | bytes 16777216 | tf_op jit(solution)/shard_map/reshape | solution.py:69
  335.3 8.4 %convert_bitcast_fusion = bf16[512,32,256]{2,0,1:T(8,128)(2,1)} fusion(bf16[512,32,256]{0,2,1:T(8,128)(2,1)} %bitcast.64, bf16[32,256,256]{2,1,0:T(8,128)(2,1)} %param.13), kind=kOutput, calls=%fused_computation.12 | convolution fusion | flops 2151677952 | bytes 20971520 | tf_op jit(solution)/shard_map/cbi,bio->cbo/dot_general | solution.py:70
  343.7 14.7 %copy.66 = bf16[512,32,256]{0,1,2:T(8,128)(2,1)} copy(bf16[512,32,256]{2,0,1:T(8,128)(2,1)} %convert_bitcast_fusion) | data formatting | bytes 16777216 | tf_op jit(solution)/shard_map/convert_element_type | solution.py:70
  358.4 47.4 %all-to-all-done.1 = bf16[512,64,128]{0,1,2:T(8,128)(2,1)} async-done(((bf16[512,64,128]{0,1,2:T(8,128)(2,1)}), bf16[512,64,128]{0,1,2:T(8,128)(2,1)}, u32[]{:S(2)}, u32[]{:S(2)}) %all-to-all-start.1) | async-done | bytes 8388640 | tf_op jit(solution)/shard_map/all_to_all | solution.py:89
  405.8 5.6 all-to-all-start
  411.5 0.0 reduce-scatter.3.cloned.1.call-start
  411.5 11.6 %copy.75 = bf16[512,4,64,32]{0,3,2,1:T(8,128)(2,1)} copy(bf16[512,4,64,32]{0,2,3,1:T(8,128)(2,1)} %bitcast.21) | data formatting | bytes 16777216 | tf_op jit(solution)/shard_map/all_to_all | solution.py:89
  423.1 13.7 %copy.76 = bf16[512,256,32]{1,0,2:T(8,128)(2,1)} copy(bf16[512,256,32]{0,2,1:T(8,128)(2,1)} %bitcast.70) | data formatting | bytes 16777216 | tf_op jit(solution)/shard_map/all_to_all | solution.py:89
  436.8 10.2 %fusion.12 = bf16[32,256,256]{2,1,0:T(8,128)(2,1)} fusion(bf16[512,32,256]{0,2,1:T(8,128)(2,1)} %bitcast.65, bf16[512,256,32]{1,0,2:T(8,128)(2,1)} %copy.76), kind=kOutput, calls=%fused_computation.17 | convolution fusion | flops 2149580800 | bytes 20971520 | tf_op jit(solution)/shard_map/cbi,cbo->bio/dot_general | solution.py:91
  447.0 0.3 reduce-scatter.5.cloned.1.call-start
  447.3 146.7 %all-to-all-done = bf16[512,32,256]{0,1,2:T(8,128)(2,1)} async-done(((bf16[512,32,256]{0,1,2:T(8,128)(2,1)}), bf16[512,32,256]{0,1,2:T(8,128)(2,1)}, u32[]{:S(2)}, u32[]{:S(2)}) %all-to-all-start) | async-done | bytes 8388640 | tf_op jit(solution)/shard_map/all_to_all | solution.py:78
  594.1 11.6 %copy.68 = bf16[512,4,32,64]{0,3,2,1:T(8,128)(2,1)} copy(bf16[512,4,32,64]{0,2,3,1:T(8,128)(2,1)} %bitcast.11) | data formatting | bytes 16777216 | tf_op jit(solution)/shard_map/all_to_all | solution.py:78
  605.7 11.3 %copy.69 = bf16[512,64,128]{0,2,1:T(8,128)(2,1)} copy(bf16[512,64,128]{0,1,2:T(8,128)(2,1)} %bitcast.71) | data formatting | bytes 16777216 | tf_op jit(solution)/shard_map/transpose | solution.py:79
  617.0 10.4 %fusion.15 = bf16[32,256,256]{2,1,0:T(8,128)(2,1)} fusion(bf16[512,32,256]{0,2,1:T(8,128)(2,1)} %bitcast.67, bf16[64,32,8,256]{3,2,1,0:T(8,128)(2,1)} %bitcast.76), kind=kOutput, calls=%fused_computation.18 | convolution fusion | flops 2149580800 | bytes 20971520 | tf_op jit(solution)/shard_map/cjk,cjo->jko/dot_general | solution.py:86
  627.4 2.8 convert_element_type.75
  630.2 12.9 %fusion = bf16[512,32,256]{0,2,1:T(8,128)(2,1)} fusion(bf16[512,32,256]{0,2,1:T(8,128)(2,1)} %bitcast.66, bf16[512,32,256]{0,2,1:T(8,128)(2,1)} %bitcast.68, bf16[32,256,256]{2,1,0:T(8,128)(2,1)} %param.14), kind=kOutput, calls=%fused_computation.3 | convolution fusion | flops 2160066560 | bytes 29360128 | tf_op jit(solution)/shard_map/cjk,jko->cjo/dot_general | solution.py:80
  643.1 12.0 %copy.79 = bf16[512,8192]{1,0:T(8,128)(2,1)} copy(bf16[512,8192]{0,1:T(8,128)(2,1)} %bitcast.69) | data formatting | bytes 16777216
  655.1 15.9 %reduce-scatter.5.cloned.1.call-done = bf16[32,64,256]{2,1,0:T(8,128)(2,1)} async-done(((bf16[32,256,256]{2,1,0:T(8,128)(2,1)}), bf16[32,64,256]{2,1,0:T(8,128)(2,1)}) %reduce-scatter.5.cloned.1.call-update) | async-done | bytes 1048592 | tf_op jit(solution)/shard_map/reduce_scatter | solution.py:96
  671.0 2.8 convert_element_type.77
  (12 shorter events, 0.1 us)
Async XLA Ops:
  7.2 168.6 %all-reduce.2.cloned.1.call-start = ((), (), s32[]{:S(2)}) async-start(), calls=%async_computation.4 | async-start | bytes 6291456 | tf_op jit(solution)/shard_map/psum | solution.py:57
  16.3 3.4 copy-start
  51.8 175.0 %all-gather.5.cloned.1.call-start = ((), (), s32[]{:S(2)}) async-start(), calls=%async_computation.6 | async-start | bytes 5242880 | tf_op jit(solution)/shard_map/all_gather | solution.py:62
  178.4 2.7 copy-start.1
  183.1 10.6 %copy-start.2 = (bf16[512,3072]{1,0:T(8,128)(2,1)S(1)}, bf16[512,3072]{1,0:T(8,128)(2,1)}, u32[]{:S(2)}) copy-start(bf16[512,3072]{1,0:T(8,128)(2,1)} %all-reduce.2.cloned.1.call-done) | copy-start | bytes 9437188
  193.1 70.3 %all-gather.3.cloned.1.call-start = ((), (), s32[]{:S(2)}) async-start(), calls=%async_computation.5 | async-start | bytes 5242880 | tf_op jit(solution)/shard_map/all_gather | solution.py:63
  216.8 189.0 %all-to-all-start.1 = ((bf16[512,64,128]{0,1,2:T(8,128)(2,1)}), bf16[512,64,128]{0,1,2:T(8,128)(2,1)}, u32[]{:S(2)}, u32[]{:S(2)}) async-start(bf16[512,64,128]{0,1,2:T(8,128)(2,1)} %copy.73), calls=%async_computation.1 | async-start | bytes 16777216 | tf_op jit(solution)/shard_map/all_to_all | solution.py:89
  405.8 188.3 %all-to-all-start = ((bf16[512,32,256]{0,1,2:T(8,128)(2,1)}), bf16[512,32,256]{0,1,2:T(8,128)(2,1)}, u32[]{:S(2)}, u32[]{:S(2)}) async-start(bf16[512,32,256]{0,1,2:T(8,128)(2,1)} %copy.66), calls=%async_computation | async-start | bytes 16777216 | tf_op jit(solution)/shard_map/all_to_all | solution.py:78
  411.5 216.0 %reduce-scatter.3.cloned.1.call-start = ((), (), s32[]{:S(2)}) async-start(), calls=%async_computation.7 | async-start | bytes 5242880 | tf_op jit(solution)/shard_map/reduce_scatter | solution.py:93
  447.0 224.0 %reduce-scatter.5.cloned.1.call-start = ((), (), s32[]{:S(2)}) async-start(), calls=%async_computation.8 | async-start | bytes 5242880 | tf_op jit(solution)/shard_map/reduce_scatter | solution.py:96
Sparse Core Ops, SparseCore 0:
  51.9 123.7 all-reduce.1
  193.3 33.4 all-gather.4
  228.9 34.4 all-gather.2
  447.2 45.6 reduce-scatter.2
  627.5 43.4 reduce-scatter.4
where the time goes:
time: 688 us; the launch traced here: 681 us
  waiting for transfers between devices  364 us (53%)
  matrix products  138 us (20%)
  local copies, waits for them, and re-layouts  128 us (19%)
  other arithmetic  23.4 us (3%)
  between operations  14.4 us (2%)
  starting transfers between devices  12.4 us (2%)
    all_to_all x1, waiting for transfers between devices, on_device(): lax.all_to_all(first, 'gene', split_axis=2, concat_axis=1, tiled=True)  147 us
    psum x1, waiting for transfers between devices, on_device(): lax.psum(qkv_part.astype(jnp.bfloat16), 'gene').astype(jnp.float32)  124 us
    all_to_all x1, waiting for transfers between devices, on_device(): lax.all_to_all(back_send, 'gene', split_axis=2, concat_axis=1, tiled=True)  47.4 us
    dot_general x1, matrix products, on_device(): qkv_part = jnp.dot(masked_in, w_qkv, preferred_element_type=jnp.float32)  32.1 us
    all_gather x1, waiting for transfers between devices, on_device(): lax.all_gather(values_b, 'cell', axis=0, tiled=True)  30.1 us
    all_to_all x2, local copies, waits for them, and re-layouts, on_device(): lax.all_to_all(back_send, 'gene', split_axis=2, concat_axis=1, tiled=True)  25.3 us
    dot_general x1, matrix products, on_device(): added = jnp.dot(attended, w_out, preferred_element_type=jnp.float32)  18.4 us
    unnamed x7, local copies, waits for them, and re-layouts  18 us
  transfers between devices with their start and end apart: 7, of which 6 were waited for; matrix products, arithmetic and copies ran while one was open for 33% of the time, Pallas kernels for 0%

commit v1 on v0

v1 whole, which is shorter than its diff:
```python
import jax
import jax.numpy as jnp
from jax import lax
from jax.experimental import pallas as pl
from jax.experimental.pallas import tpu as pltpu
from jax.sharding import PartitionSpec as P

HEADS = 16
HEAD_DIM = 64
TILE = 16
BF16 = jnp.bfloat16
F32 = jnp.float32


def normalize(part):
    count, columns = part.shape
    shaped = part.reshape(count, columns // HEAD_DIM, HEAD_DIM)
    meansq = jnp.mean(shaped * shaped, axis=-1, keepdims=True)
    return (shaped * lax.rsqrt(meansq + 1e-06)).astype(BF16).reshape(count, columns)


def attend(queries, key_piece, value_piece):
    query_count, columns = queries.shape
    key_count = key_piece.shape[0]
    heads = columns // HEAD_DIM
    query_heads = queries.reshape(query_count, heads, HEAD_DIM)
    key_heads = key_piece.reshape(key_count, heads, HEAD_DIM)
    value_heads = value_piece.reshape(key_count, heads, HEAD_DIM)
    scores = jnp.einsum(
        "qhd,khd->hqk", query_heads, key_heads, preferred_element_type=F32
    ) * HEAD_DIM ** (-0.5)
    expw = jnp.exp(scores).astype(BF16)
    denom = jnp.sum(expw, axis=2, dtype=F32)
    numer = jnp.einsum("hqk,khd->qhd", expw, value_heads, preferred_element_type=F32)
    return (numer / denom.T[:, :, None]).astype(BF16).reshape(query_count, columns)


def on_device_general(
    expression, gene_mask, mask_value, w_qkv, w_out, w_first, w_second, cotangent
):
    groups = lax.axis_size("gene")
    local_blocks = w_first.shape[0]
    block_size = w_first.shape[1]
    block_total = local_blocks * groups
    cell_rows = expression.shape[0]
    masked_in = jnp.where(gene_mask == 1, mask_value[None, :], expression)
    qkv_part = jnp.dot(masked_in, w_qkv, preferred_element_type=F32)
    qkv_full = lax.psum(qkv_part.astype(BF16), "gene").astype(F32)
    columns = qkv_full.shape[1] // 3
    queries = normalize(qkv_full[:, :columns])
    keys_normed = normalize(qkv_full[:, columns : 2 * columns])
    values_b = qkv_full[:, 2 * columns :].astype(BF16)
    attended = attend(
        queries,
        lax.all_gather(keys_normed, "cell", axis=0, tiled=True),
        lax.all_gather(values_b, "cell", axis=0, tiled=True),
    )
    added = jnp.dot(attended, w_out, preferred_element_type=F32)
    hidden = (masked_in.astype(F32) + added).astype(BF16)
    blocks = hidden.reshape(cell_rows, local_blocks, block_size)
    first = jnp.einsum("cbi,bio->cbo", blocks, w_first, preferred_element_type=F32).astype(BF16)
    cot_blocks = cotangent.reshape(cell_rows, local_blocks, block_size)
    back_perm = jnp.einsum(
        "cjo,jko->cjk", cot_blocks, w_second, preferred_element_type=F32
    ).astype(BF16)
    back_send = back_perm.reshape(cell_rows, block_size // groups, block_total)
    received = lax.all_to_all(first, "gene", split_axis=2, concat_axis=1, tiled=True)
    permuted = jnp.swapaxes(received, 1, 2).reshape(cell_rows, local_blocks, block_size)
    mixed = jnp.einsum("cjk,jko->cjo", permuted, w_second, preferred_element_type=F32)
    denoised = (
        (blocks.astype(F32) + mixed).astype(BF16).reshape(cell_rows, local_blocks * block_size)
    )
    grad_second = jnp.einsum("cjk,cjo->jko", permuted, cot_blocks, preferred_element_type=F32)
    back_recv = lax.all_to_all(back_send, "gene", split_axis=2, concat_axis=1, tiled=True)
    back_first = jnp.swapaxes(back_recv, 1, 2)
    grad_first = jnp.einsum("cbi,cbo->bio", blocks, back_first, preferred_element_type=F32)
    first_share, second_share = (
        lax.psum_scatter(
            grad_first.astype(BF16), "cell", scatter_dimension=1, tiled=True
        ).astype(F32),
        lax.psum_scatter(
            grad_second.astype(BF16), "cell", scatter_dimension=1, tiled=True
        ).astype(F32),
    )
    return (denoised, first_share, second_share)


def after(value, *earlier):
    return lax.optimization_barrier((value, *earlier))[0]


def flip(value, axis, bit):
    pairs = [(i, i ^ bit) for i in range(lax.axis_size(axis))]
    return lax.ppermute(value, axis, pairs)


def call(body, me, args, in_specs, outs, out_specs, grid=(1,), scratch=(), aliases=None):
    return pl.pallas_call(
        body,
        out_shape=outs,
        grid_spec=pltpu.PrefetchScalarGridSpec(
            num_scalar_prefetch=1,
            grid=grid,
            in_specs=in_specs,
            out_specs=out_specs,
            scratch_shapes=list(scratch),
        ),
        input_output_aliases=aliases or {},
        compiler_params=pltpu.CompilerParams(vmem_limit_bytes=52 * 2**20),
        cost_estimate=pl.CostEstimate(flops=1, bytes_accessed=1, transcendentals=0),
    )(me, *args)


def spec(shape, place):
    return pl.BlockSpec(shape, place)


def whole(shape):
    return pl.BlockSpec(shape, lambda *_: (0,) * len(shape))


def array(shape, dtype):
    return jax.ShapeDtypeStruct(shape, dtype)


def grid_turn():
    rows = lax.broadcasted_iota(jnp.int32, (TILE * TILE, TILE * TILE), 0)
    columns = lax.broadcasted_iota(jnp.int32, (TILE * TILE, TILE * TILE), 1)
    return ((rows % TILE) * TILE + rows // TILE == columns).astype(BF16)


def turn(matrix, tile):
    rows = tile.shape[-1]
    flat = tile.reshape(TILE * TILE, rows)
    return jnp.dot(matrix, flat, preferred_element_type=F32).astype(BF16).reshape(TILE, TILE, rows)


def back_kernel(me_ref, turn_ref, second_ref, cot_ref, *refs):
    outs, held = refs[:4], refs[4]
    blocks, rows = held.shape[2], held.shape[3]
    pair = held.shape[0] // (TILE // 2)
    at = pl.program_id(0) % (TILE // pair)
    back = lax.dot_general(
        second_ref[0], cot_ref[...], (((1,), (1,)), ((), ())), preferred_element_type=F32
    ).astype(BF16)
    held[pl.ds(at * pair, pair)] = back.reshape(pair, 4, blocks, rows)

    @pl.when(at == TILE // pair - 1)
    def _():
        for bits in range(4):
            there = me_ref[0] ^ bits
            for low in range(0, blocks, TILE):
                outs[bits][low : low + TILE] = turn(
                    turn_ref[...], held[:, there, low : low + TILE, :]
                )


def back_call(me, matrix, w_second, cotangent, part, parts):
    blocks, size, _ = w_second.shape
    rows = cotangent.shape[0]
    pair = size // (4 * blocks)
    count = blocks // parts
    per = TILE // pair
    first = part * count
    piece = array((blocks, count * pair, rows), BF16)
    return call(
        back_kernel,
        me,
        (matrix, w_second, cotangent),
        [
            whole(matrix.shape),
            spec((1, size, size), lambda j, _: (first + j, 0, 0)),
            spec((rows, size), lambda j, _: (0, first + j)),
        ],
        [piece] * 4,
        [spec((blocks, TILE, rows), lambda j, _: (0, j // per, 0))] * 4,
        grid=(count,),
        scratch=[pltpu.VMEM((TILE, 4, blocks, rows), BF16)],
    )


def project_kernel(me_ref, value_ref, mask_ref, fill_ref, *refs):
    weights, (masked_ref, send_ref, keep_ref), sums = refs[:3], refs[3:6], refs[6:]
    step = pl.program_id(0)
    masked = jnp.where(
        mask_ref[...] == 1, fill_ref[...].astype(F32), value_ref[...].astype(F32)
    ).astype(BF16)
    masked_ref[...] = masked

    @pl.when(step == 0)
    def _():
        for total in sums:
            total[...] = jnp.zeros_like(total)

    for weight, total in zip(weights, sums):
        total[...] += jnp.dot(masked, weight[...], preferred_element_type=F32)

    @pl.when(step == pl.num_programs(0) - 1)
    def _():
        share = sums[0].shape[1] // 4
        for out, flips in ((send_ref, (1, 3)), (keep_ref, (0, 2))):
            for slot, bits in enumerate(flips):
                columns = pl.ds(pl.multiple_of((me_ref[0] ^ bits) * share, share), share)
                for kind, total in enumerate(sums):
                    out[slot, :, kind * share : (kind + 1) * share] = total[:, columns].astype(
                        out.dtype
                    )


def project_call(me, expression, gene_mask, mask_value, w_qkv):
    rows, genes = expression.shape
    width = w_qkv.shape[1] // 3
    depth = min(genes, 512)
    wide = spec((rows, depth), lambda i, _: (0, i))
    shape = (2, rows, 3 * width // 4)
    return call(
        project_kernel,
        me,
        (expression, gene_mask, mask_value.reshape(1, genes), w_qkv, w_qkv, w_qkv),
        [
            wide,
            wide,
            spec((1, depth), lambda i, _: (0, i)),
            spec((depth, width), lambda i, _: (i, 0)),
            spec((depth, width), lambda i, _: (i, 1)),
            spec((depth, width), lambda i, _: (i, 2)),
        ],
        [array((rows, genes), BF16), array(shape, BF16), array(shape, F32)],
        [wide, whole(shape), whole(shape)],
        grid=(genes // depth,),
        scratch=[pltpu.VMEM((rows, width), F32)] * 3,
    )


def add_kernel(_, keep_ref, came_ref, mine_ref, other_ref):
    mine_ref[...] = keep_ref[0] + came_ref[0].astype(F32)
    other_ref[...] = (keep_ref[1] + came_ref[1].astype(F32)).astype(BF16)


def add_call(me, keep, came):
    shape = keep.shape
    return call(
        add_kernel,
        me,
        (keep, came),
        [whole(shape), whole(shape)],
        [array(shape[1:], F32), array(shape[1:], BF16)],
        [whole(shape[1:])] * 2,
    )


def normalize_heads(part):
    columns = part.shape[1]
    heads = [lax.broadcasted_iota(jnp.int32, (columns, columns), d) // HEAD_DIM for d in (0, 1)]
    same = (heads[0] == heads[1]).astype(F32)
    sums = jnp.dot(
        part * part, same, precision=lax.Precision.HIGHEST, preferred_element_type=F32
    )
    return (part * lax.rsqrt(sums * (1.0 / HEAD_DIM) + 1e-06)).astype(BF16)


def split_kernel(_, mine_ref, came_ref, query_ref, out_ref):
    total = mine_ref[...] + came_ref[...].astype(F32)
    share = total.shape[1] // 3
    query_ref[...] = normalize_heads(total[:, :share])
    out_ref[:, :share] = normalize_heads(total[:, share : 2 * share])
    out_ref[:, share:] = total[:, 2 * share :].astype(BF16)


def split_call(me, mine, came):
    rows, columns = mine.shape
    shapes = ((rows, columns // 3), (rows, 2 * columns // 3))
    return call(
        split_kernel,
        me,
        (mine, came),
        [whole(mine.shape)] * 2,
        [array(shape, BF16) for shape in shapes],
        [whole(shape) for shape in shapes],
    )


def attend_kernel(_, query_ref, *refs):
    pieces, out_ref = refs[:-1], refs[-1]
    queries = query_ref[...]
    rows, share = queries.shape
    head_of = lax.broadcasted_iota(jnp.int32, (rows, share), 1) // HEAD_DIM
    out = jnp.zeros((rows, share), F32)
    for head in range(share // HEAD_DIM):
        query = jnp.where(head_of == head, queries.astype(F32) * HEAD_DIM**-0.5, 0.0).astype(BF16)
        numer = jnp.zeros((rows, share), F32)
        denom = jnp.zeros((rows, 1), F32)
        for piece in pieces:
            scores = lax.dot_general(
                query, piece[:, :share], (((1,), (1,)), ((), ())), preferred_element_type=F32
            )
            expw = jnp.exp(scores).astype(BF16)
            denom += jnp.sum(expw.astype(F32), axis=1, keepdims=True)
            numer += jnp.dot(expw, piece[:, share:], preferred_element_type=F32)
        out = jnp.where(head_of == head, numer / denom, out)
    out_ref[...] = out.astype(BF16)


def attend_call(me, queries, pieces):
    rows, share = queries.shape
    some = rows // 2
    part = spec((some, share), lambda i, _: (i, 0))
    return call(
        attend_kernel,
        me,
        (queries, *pieces),
        [part] + [whole(piece.shape) for piece in pieces],
        array((rows, share), BF16),
        part,
        grid=(2,),
    )


def first_kernel(me_ref, turn_ref, own, near, far, rest, w_out_ref, masked_ref, wf_ref, *refs):
    hidden_ref, outs, gathered, held = refs[0], refs[1:-2], refs[-2], refs[-1]
    block = pl.program_id(0)
    share = own.shape[1]

    @pl.when(block == 0)
    def _():
        for bits, piece in enumerate((own, near, far, rest)):
            place = pl.multiple_of((me_ref[0] ^ bits) * share, share)
            gathered[:, pl.ds(place, share)] = piece[...]

    added = jnp.dot(gathered[...], w_out_ref[...], preferred_element_type=F32)
    hidden = (masked_ref[...].astype(F32) + added).astype(BF16)
    hidden_ref[...] = hidden
    held[block % TILE] = lax.dot_general(
        wf_ref[0], hidden, (((1,), (1,)), ((), ())), preferred_element_type=F32
    ).astype(BF16)

    @pl.when(block % TILE == TILE - 1)
    def _():
        deeps = [out.shape[0] for out in outs[: len(outs) // 4]]
        deep = sum(deeps)
        for bits in range(4):
            there = me_ref[0] ^ bits
            for low in range(0, deep, TILE):
                start = pl.multiple_of(there * deep + low, TILE)
                tile = turn(turn_ref[...], held[:, pl.ds(start, TILE), :])
                for chunk, count in enumerate(deeps):
                    begin = sum(deeps[:chunk])
                    least, most = max(begin, low), min(begin + count, low + TILE)
                    if least < most:
                        outs[bits * len(deeps) + chunk][least - begin : most - begin] = tile[
                            least - low : most - low
                        ]


def first_call(me, matrix, attended, w_out, masked, w_first_t, deeps):
    blocks, size, _ = w_first_t.shape
    rows, genes = masked.shape
    width = w_out.shape[0]
    wide = spec((rows, size), lambda b, _: (0, b))
    chunks = len(deeps)
    got = call(
        first_kernel,
        me,
        (matrix, *attended, w_out, masked, w_first_t),
        [whole(matrix.shape)]
        + [whole(part.shape) for part in attended]
        + [
            spec((width, size), lambda b, _: (0, b)),
            wide,
            spec((1, size, size), lambda b, _: (b, 0, 0)),
        ],
        [array((rows, genes), BF16)] + [array((deep, blocks, rows), BF16) for deep in deeps] * 4,
        [wide] + [spec((deep, TILE, rows), lambda b, _: (0, b // TILE, 0)) for deep in deeps] * 4,
        grid=(blocks,),
        scratch=[pltpu.VMEM((rows, width), BF16), pltpu.VMEM((TILE, size, rows), BF16)],
    )
    return got[0], [[got[1 + s * chunks + t] for s in range(4)] for t in range(chunks)]


def second_kernel(me_ref, *refs):
    pieces = refs[:4]
    w_ref, cot_ref, hidden_ref = refs[4:7]
    out_ref, grad_ref, held = refs[-3:]
    for bits, piece in enumerate(pieces):
        held[:, me_ref[0] ^ bits] = piece[...]
    size = w_ref.shape[1]
    permuted = held[...].reshape(size, held.shape[3])
    grad_ref[0] = jnp.dot(permuted, cot_ref[...], preferred_element_type=F32).astype(BF16)
    mixed = lax.dot_general(
        permuted, w_ref[0], (((0,), (0,)), ((), ())), preferred_element_type=F32
    )
    out_ref[...] = (hidden_ref[...].astype(F32) + mixed).astype(BF16)


def second_call(me, pieces, w_second, cotangent, hidden, denoised, start):
    blocks, size, _ = w_second.shape
    deep, _, rows = pieces[0].shape
    pair = size // (4 * blocks)
    count = deep // pair
    wide = spec((rows, size), lambda j, _: (0, start + j))
    square = spec((1, size, size), lambda j, _: (start + j, 0, 0))
    args = [*pieces, w_second, cotangent, hidden]
    in_specs = [spec((pair, blocks, rows), lambda j, _: (j, 0, 0))] * 4 + [square, wide, wide]
    aliases = {}
    if denoised is not None:
        args.append(denoised)
        in_specs.append(pl.BlockSpec(memory_space=pl.ANY))
        aliases = {len(args): 0}
    return call(
        second_kernel,
        me,
        args,
        in_specs,
        [array(hidden.shape, BF16), array((count, size, size), BF16)],
        [wide, spec((1, size, size), lambda j, _: (j, 0, 0))],
        grid=(count,),
        scratch=[pltpu.VMEM((pair, 4, blocks, rows), BF16)],
        aliases=aliases,
    )


def grad_first_kernel(me_ref, *refs):
    pieces, hidden_ref, out_ref, held = refs[:-3], refs[-3], refs[-2], refs[-1]
    for half in range(len(pieces) // 4):
        for bits in range(4):
            held[me_ref[0] ^ bits, half] = pieces[half * 4 + bits][0]
    back = held[...].reshape(-1, held.shape[3])
    grad = jnp.dot(back, hidden_ref[...], preferred_element_type=F32)
    out_ref[0] = grad.T.astype(BF16)


def grad_first_call(me, pieces, hidden, size):
    blocks, deep, rows = pieces[0].shape
    return call(
        grad_first_kernel,
        me,
        (*pieces, hidden),
        [spec((1, deep, rows), lambda b, _: (b, 0, 0))] * len(pieces)
        + [spec((rows, size), lambda b, _: (0, b))],
        array((blocks, size, size), BF16),
        spec((1, size, size), lambda b, _: (b, 0, 0)),
        grid=(blocks,),
        scratch=[pltpu.VMEM((4, len(pieces) // 4, deep, rows), BF16)],
    )


def scatter_cells(grad):
    return lax.psum_scatter(grad, "cell", scatter_dimension=1, tiled=True)


def scatter_cells_halving(grad):
    me = lax.axis_index("cell")
    count, size, columns = grad.shape
    rows = grad.reshape(count, 4, size // 4, columns)

    def part(bits):
        return lax.dynamic_index_in_dim(rows, me ^ bits, 1, keepdims=False)

    came = flip(jnp.stack([part(1), part(3)]), "cell", 1).astype(F32)
    other = (part(2).astype(F32) + came[1]).astype(BF16)
    return part(0).astype(F32) + came[0] + flip(other, "cell", 2).astype(F32)


def on_device_four(expression, gene_mask, mask_value, w_qkv, w_out, w_first, w_second, cotangent):
    me = lax.axis_index("gene").astype(jnp.int32).reshape(1)
    blocks, size, _ = w_first.shape
    parts = 4
    deep = size // 4
    deeps = [deep // 4] * 3 + [deep // 8] * 2
    matrix = grid_turn()
    sends, back = [None] * parts, [[None] * 4 for _ in range(parts)]

    def prepare(part, *earlier):
        sends[part] = back_call(me, matrix, w_second, after(cotangent, *earlier), part, parts)
        back[part][0] = sends[part][0]

    def begin(part, bits, *earlier):
        back[part][bits] = flip(after(sends[part][bits], *earlier), "gene", bits)
        return back[part][bits]

    prepare(0)
    first_part = [begin(0, bits) for bits in (3, 2, 1)]
    masked, send, keep = project_call(
        me, after(expression, sends[0][0]), gene_mask, mask_value, w_qkv
    )
    came = flip(after(send, *first_part), "gene", 1)
    prepare(1, send)
    beside_sum = [begin(1, 2), begin(1, 3)]
    mine, other = add_call(me, keep, after(came, *beside_sum))
    last = flip(other, "gene", 2)
    prepare(2, other)
    prepare(3, sends[2][0])
    w_first_t = jnp.swapaxes(after(w_first, other), 1, 2)
    beside_sum = [begin(1, 1, other)]
    queries, key_value = split_call(
        me, mine, after(last, *beside_sum, sends[3][0], w_first_t)
    )
    across = flip(key_value, "cell", 2)
    beside = flip(key_value, "cell", 1)
    corner = flip(across, "cell", 1)
    beside_keys = [begin(2, 2, key_value)]
    queries = after(queries, *beside_keys, beside, across, corner)
    attended = attend_call(me, queries, (key_value, beside, across, corner))
    attended = after(attended, begin(2, 3, queries))
    far = flip(attended, "gene", 2)
    near = flip(attended, "gene", 1)
    rest = flip(far, "gene", 1)
    beside_heads = [begin(2, 1, attended), begin(3, 1, attended)]
    hidden, first = first_call(
        me,
        matrix,
        (attended, near, far, after(rest, *beside_heads)),
        w_out,
        masked,
        w_first_t,
        deeps,
    )
    for bits in (2, 3):
        begin(3, bits, rest)

    got = []
    for t in range(len(deeps)):
        earlier = got[-1] if t else back[3]
        got.append(first[t][:1])
        for bits in (1, 2, 3):
            ready = (earlier[bits],) if t else earlier
            got[t].append(flip(after(first[t][bits], *ready), "gene", bits))
    grad_first = grad_first_call(me, sum(back, []), hidden, size)
    first_share = scatter_cells(grad_first)

    denoised, shares = None, []
    for t in range(len(deeps)):
        pieces = [after(got[t][0], grad_first), *got[t][1:]]
        start = sum(deeps[:t]) * blocks // deep
        denoised, grad = second_call(me, pieces, w_second, cotangent, hidden, denoised, start)
        if deeps[t] * 4 < deep:
            shares.append(scatter_cells_halving(grad))
        else:
            shares.append(scatter_cells(grad).astype(F32))
    return (denoised, first_share.astype(F32), jnp.concatenate(shares, axis=0))


def solution(mesh):
    placed = (
        P(("grp", "cell"), "gene"),
        P(("grp", "cell"), "gene"),
        P("gene"),
        P("gene", None),
        P(None, "gene"),
        P("gene", None, None),
        P("gene", None, None),
        P(("grp", "cell"), "gene"),
    )
    four = mesh.shape["gene"] == 4 and mesh.shape["cell"] == 4
    return jax.shard_map(
        on_device_four if four else on_device_general,
        mesh=mesh,
        in_specs=placed,
        out_specs=(
            P(("grp", "cell"), "gene"),
            P(("grp", "gene"), "cell", None),
            P(("grp", "gene"), "cell", None),
        ),
        check_vma=False,
    )
```

time: 688 us -> 576 us (0.84)
  Pallas kernels: 0 us -> 179 us
  matrix products: 138 us -> 0 us
  local copies, waits for them, and re-layouts: 128 us -> 19.3 us
  waiting for transfers between devices: 364 us -> 297 us
  starting transfers between devices: 12.4 us -> 53.7 us
  other arithmetic: 23.4 us -> 10.1 us
    ppermute x0 -> x39, waiting for transfers between devices: none -> 285 us  [flip(): return lax.ppermute(value, axis, pairs)]
    all_to_all x2 -> x0, waiting for transfers between devices: 194 us -> none  [the longest x1 147 us: on_device(): lax.all_to_all(first, 'gene', split_axis=2, concat_axis=1, tiled=True)]
    pallas_call x0 -> x15, Pallas kernels: none -> 179 us  [call(): pl.pallas_call(body, out_shape=outs, grid_spec=pltpu.PrefetchScalarGridSp...]
    dot_general x9 -> x0, matrix products: 138 us -> none  [the longest x1 32.1 us: on_device(): qkv_part = jnp.dot(masked_in, w_qkv, preferred_element_type=jnp.float32)]
    psum x1 -> x0, waiting for transfers between devices: 124 us -> none  [on_device(): lax.psum(qkv_part.astype(jnp.bfloat16), 'gene').astype(jnp.float32)]
    ppermute x0 -> x39, starting transfers between devices: none -> 53.6 us  [flip(): return lax.ppermute(value, axis, pairs)]
    all_to_all x3 -> x0, local copies, waits for them, and re-layouts: 37 us -> none  [the longest x2 25.3 us: on_device(): lax.all_to_all(back_send, 'gene', split_axis=2, concat_axis=1, tiled=True)]
    all_gather x2 -> x0, waiting for transfers between devices: 30.4 us -> none  [the longest x1 30.1 us: on_device(): lax.all_gather(values_b, 'cell', axis=0, tiled=True)]
  transfers between devices with their start and end apart: 7 -> 43, of which waited for: 6 -> 24; matrix products, arithmetic and copies ran while one was open for 33% -> 2% of each run, Pallas kernels for 0% -> 28%
where the time goes in v1:
time: 576 us; the launch traced here: 574 us
  waiting for transfers between devices  297 us (52%)
  Pallas kernels  179 us (31%)
  starting transfers between devices  53.7 us (9%)
  local copies, waits for them, and re-layouts  19.3 us (3%)
  between operations  14.3 us (2%)
  other arithmetic  10.1 us (2%)
    ppermute x39, waiting for transfers between devices, flip(): return lax.ppermute(value, axis, pairs)  285 us
    pallas_call x15, Pallas kernels, call(): pl.pallas_call(body, out_shape=outs, grid_spec=pltpu.PrefetchScalarGridSp...  179 us
    ppermute x39, starting transfers between devices, flip(): return lax.ppermute(value, axis, pairs)  53.6 us
    unnamed x108, local copies, waits for them, and re-layouts  12.9 us
    reduce_scatter x4, waiting for transfers between devices, scatter_cells(): return lax.psum_scatter(grad, 'cell', scatter_dimension=1, tiled=True)  11.7 us
  transfers between devices with their start and end apart: 43, of which 24 were waited for; matrix products, arithmetic and copies ran while one was open for 2% of the time, Pallas kernels for 28%

profile of v1, /device:TPU:0, one launch (start us, length us, event | category | flops | bytes accessed | tf_op | source)
XLA Modules:
  0.0 573.6 jit_solution(3112942049160444780)
XLA Ops:
  7.5 7.1 %shard_map.103 = (bf16[32,16,512]{2,1,0:T(8,128)(2,1)S(1)}, bf16[32,16,512]{2,1,0:T(8,128)(2,1)S(1)}, bf16[32,16,512]{2,1,0:T(8,128)(2,1)S(1)}, bf16[32,16,512]{2,1,0:T(8,128)(2,1)}) custom-call(s32[1]{0:T(128)} %bitcast.me_ref._, bf16[256,256]{1,0:T(8,128)(2,1)S(1)} %fusion.10.turn_ref, bf16[32,256,256]{2,1,0:T(8,128)(2,1)} %refs_4_.9, ...), custom_call_target="tpu_custom_call" | custom-call | flops 1 | bytes 1 | tf_op jit(solution)/shard_map/pallas_call | solution.py:98
  14.7 5.0 collective-permute-start
  20.3 41.1 %shard_map.104 = (bf16[512,8192]{1,0:T(8,128)(2,1)}, bf16[2,512,768]{2,1,0:T(8,128)(2,1)S(1)}, f32[2,512,768]{2,1,0:T(8,128)}) custom-call(s32[1]{0:T(128)} %bitcast.me_ref._, bf16[512,8192]{1,0:T(8,128)(2,1)} %value_ref, s32[512,8192]{1,0:T(8,128)} %mask_ref.1, bf16[1,8192]{1,0:T(2,128)(2,1)S(1)} %reshape.31.fill_ref, bf16[8192,3072]{1,0:T(8,128)(2,1)} %refs_2_.1, ...), custom_call_target="tpu_custom_call" | custom-call | flops 1 | bytes 1 | tf_op jit(solution)/shard_map/pallas_call | solution.py:98
  61.4 3.3 collective-permute-done.1.refs_2_
  64.7 7.3 %shard_map.105 = (bf16[32,16,512]{2,1,0:T(8,128)(2,1)S(1)}, bf16[32,16,512]{2,1,0:T(8,128)(2,1)}, bf16[32,16,512]{2,1,0:T(8,128)(2,1)S(1)}, bf16[32,16,512]{2,1,0:T(8,128)(2,1)}) custom-call(s32[1]{0:T(128)} %bitcast.me_ref._, bf16[256,256]{1,0:T(8,128)(2,1)S(1)} %fusion.10.turn_ref, bf16[32,256,256]{2,1,0:T(8,128)(2,1)} %refs_4_.9, bf16[512,8192]{1,0:T(8,128)(2,1)} %refs_5_.9), custom_call_target="tpu_custom_call" | custom-call | flops 1 | bytes 1 | tf_op jit(solution)/shard_map/pallas_call | solution.py:98
  72.8 3.0 collective-permute-start.4
  77.2 33.6 %collective-permute-done.4.refs_6_ = bf16[32,16,512]{2,1,0:T(8,128)(2,1)S(1)} collective-permute-done((bf16[32,16,512]{2,1,0:T(8,128)(2,1)S(1)}, bf16[32,16,512]{2,1,0:T(8,128)(2,1)S(1)}, u32[]{:S(2)}, u32[]{:S(2)}) %collective-permute-start.4) | collective-permute-done | bytes 524320 | tf_op jit(solution)/shard_map/ppermute | solution.py:94
  110.8 12.4 %collective-permute-done.5.refs_7_ = bf16[32,16,512]{2,1,0:T(8,128)(2,1)S(1)} collective-permute-done((bf16[32,16,512]{2,1,0:T(8,128)(2,1)}, bf16[32,16,512]{2,1,0:T(8,128)(2,1)S(1)}, u32[]{:S(2)}, u32[]{:S(2)}) %collective-permute-start.5) | collective-permute-done | bytes 524320 | tf_op jit(solution)/shard_map/ppermute | solution.py:94
  124.4 3.6 shard_map.106
  128.0 2.3 collective-permute-start.7
  130.3 7.1 %shard_map.107 = (bf16[32,16,512]{2,1,0:T(8,128)(2,1)S(1)}, bf16[32,16,512]{2,1,0:T(8,128)(2,1)S(1)}, bf16[32,16,512]{2,1,0:T(8,128)(2,1)S(1)}, bf16[32,16,512]{2,1,0:T(8,128)(2,1)}) custom-call(s32[1]{0:T(128)} %bitcast.me_ref._, bf16[256,256]{1,0:T(8,128)(2,1)S(1)} %fusion.10.turn_ref, bf16[32,256,256]{2,1,0:T(8,128)(2,1)} %refs_4_.9, ...), custom_call_target="tpu_custom_call" | custom-call | flops 1 | bytes 1 | tf_op jit(solution)/shard_map/pallas_call | solution.py:98
  139.9 7.1 %shard_map.108 = (bf16[32,16,512]{2,1,0:T(8,128)(2,1)S(1)}, bf16[32,16,512]{2,1,0:T(8,128)(2,1)S(1)}, bf16[32,16,512]{2,1,0:T(8,128)(2,1)S(1)}, bf16[32,16,512]{2,1,0:T(8,128)(2,1)}) custom-call(s32[1]{0:T(128)} %bitcast.me_ref._, bf16[256,256]{1,0:T(8,128)(2,1)S(1)} %fusion.10.turn_ref, bf16[32,256,256]{2,1,0:T(8,128)(2,1)} %refs_4_.9, ...), custom_call_target="tpu_custom_call" | custom-call | flops 1 | bytes 1 | tf_op jit(solution)/shard_map/pallas_call | solution.py:98
  149.4 6.4 %copy.15 = bf16[32,256,256]{1,2,0:T(8,128)(2,1)} copy(bf16[32,256,256]{2,1,0:T(8,128)(2,1)} %param.13) | data formatting | bytes 8388608 | tf_op jit(solution)/shard_map/optimization_barrier | solution.py:89
  155.8 6.8 %collective-permute-done.6.came_ref = bf16[512,768]{1,0:T(8,128)(2,1)S(1)} collective-permute-done((bf16[512,768]{1,0:T(8,128)(2,1)S(1)}, bf16[512,768]{1,0:T(8,128)(2,1)S(1)}, u32[]{:S(2)}, u32[]{:S(2)}) %collective-permute-start.6) | collective-permute-done | bytes 786464 | tf_op jit(solution)/shard_map/ppermute | solution.py:94
  162.6 2.8 shard_map.109
  166.9 12.4 %collective-permute-done.10.refs_2_ = bf16[512,512]{1,0:T(8,128)(2,1)S(1)} collective-permute-done((bf16[512,512]{1,0:T(8,128)(2,1)S(1)}, bf16[512,512]{1,0:T(8,128)(2,1)S(1)}, u32[]{:S(2)}, u32[]{:S(2)}) %collective-permute-start.10) | collective-permute-done | bytes 524320 | tf_op jit(solution)/shard_map/ppermute | solution.py:94
  179.3 13.6 %collective-permute-done.8.refs_10_ = bf16[32,16,512]{2,1,0:T(8,128)(2,1)S(1)} collective-permute-done((bf16[32,16,512]{2,1,0:T(8,128)(2,1)S(1)}, bf16[32,16,512]{2,1,0:T(8,128)(2,1)S(1)}, u32[]{:S(2)}, u32[]{:S(2)}) %collective-permute-start.8) | collective-permute-done | bytes 524320 | tf_op jit(solution)/shard_map/ppermute | solution.py:94
  194.7 6.5 %shard_map.110.own = bf16[512,256]{1,0:T(8,128)(2,1)S(1)} custom-call(s32[1]{0:T(128)} %bitcast.me_ref._, bf16[512,256]{1,0:T(8,128)(2,1)S(1)} %get-tuple-element.121.query_ref, bf16[512,512]{1,0:T(8,128)(2,1)S(1)} %get-tuple-element.119.refs_0_, bf16[512,512]{1,0:T(8,128)(2,1)S(1)} %collective-permute-done.9.refs_1_, bf16[512,512]{1,0:T(8,128)(2,1)} %copy-done.41, ...), custom_call_target="tpu_custom_call" | custom-call | flops 1 | bytes 1 | tf_op jit(solution)/shard_map/pallas_call | solution.py:98
  201.2 7.6 %collective-permute-done.12.refs_11_ = bf16[32,16,512]{2,1,0:T(8,128)(2,1)S(1)} collective-permute-done((bf16[32,16,512]{2,1,0:T(8,128)(2,1)S(1)}, bf16[32,16,512]{2,1,0:T(8,128)(2,1)S(1)}, u32[]{:S(2)}, u32[]{:S(2)}) %collective-permute-start.12) | collective-permute-done | bytes 524320 | tf_op jit(solution)/shard_map/ppermute | solution.py:94
  208.8 8.9 %collective-permute-start.14 = (bf16[512,256]{1,0:T(8,128)(2,1)S(1)}, bf16[512,256]{1,0:T(8,128)(2,1)S(1)}, u32[]{:S(2)}, u32[]{:S(2)}) collective-permute-start(bf16[512,256]{1,0:T(8,128)(2,1)S(1)} %shard_map.110.own), channel_id=1, source_target_pairs={{0,8},{4,12},{8,0},{12,4},{1,9},{5,13},{9,1},{13,5},{2,10},{6,14},... | collective-permute-start | bytes 786440 | tf_op jit(solution)/shard_map/ppermute | solution.py:94
  217.7 11.3 %collective-permute-done.14.far = bf16[512,256]{1,0:T(8,128)(2,1)S(1)} collective-permute-done((bf16[512,256]{1,0:T(8,128)(2,1)S(1)}, bf16[512,256]{1,0:T(8,128)(2,1)S(1)}, u32[]{:S(2)}, u32[]{:S(2)}) %collective-permute-start.14) | collective-permute-done | bytes 262176 | tf_op jit(solution)/shard_map/ppermute | solution.py:94
  231.1 7.1 %collective-permute-done.15.rest = bf16[512,256]{1,0:T(8,128)(2,1)S(1)} collective-permute-done((bf16[512,256]{1,0:T(8,128)(2,1)S(1)}, bf16[512,256]{1,0:T(8,128)(2,1)S(1)}, u32[]{:S(2)}, u32[]{:S(2)}) %collective-permute-start.15) | collective-permute-done | bytes 262176 | tf_op jit(solution)/shard_map/ppermute | solution.py:94
  239.9 2.7 collective-permute-start.13
  242.6 29.0 %collective-permute-done.17.refs_13_ = bf16[32,16,512]{2,1,0:T(8,128)(2,1)S(1)} collective-permute-done((bf16[32,16,512]{2,1,0:T(8,128)(2,1)S(1)}, bf16[32,16,512]{2,1,0:T(8,128)(2,1)S(1)}, u32[]{:S(2)}, u32[]{:S(2)}) %collective-permute-start.17) | collective-permute-done | bytes 524320 | tf_op jit(solution)/shard_map/ppermute | solution.py:94
  271.6 11.5 %collective-permute-done.16.refs_9_ = bf16[32,16,512]{2,1,0:T(8,128)(2,1)S(1)} collective-permute-done((bf16[32,16,512]{2,1,0:T(8,128)(2,1)S(1)}, bf16[32,16,512]{2,1,0:T(8,128)(2,1)S(1)}, u32[]{:S(2)}, u32[]{:S(2)}) %collective-permute-start.16) | collective-permute-done | bytes 524320 | tf_op jit(solution)/shard_map/ppermute | solution.py:94
  283.1 3.2 collective-permute-done.13.near
  287.0 39.1 %shard_map.111 = (bf16[512,8192]{1,0:T(8,128)(2,1)}, bf16[16,32,512]{2,1,0:T(8,128)(2,1)}, bf16[16,32,512]{2,1,0:T(8,128)(2,1)}, bf16[16,32,512]{2,1,0:T(8,128)(...) custom-call(s32[1]{0:T(128)} %bitcast.me_ref._, ...), custom_call_target="tpu_custom_call" | custom-call | flops 1 | bytes 1 | tf_op jit(solution)/shard_map/pallas_call | solution.py:98
  333.0 2.6 collective-permute-start.20
  335.6 25.3 %shard_map.112 = bf16[32,256,256]{2,1,0:T(8,128)(2,1)} custom-call(s32[1]{0:T(128)} %bitcast.me_ref._, bf16[32,16,512]{2,1,0:T(8,128)(2,1)S(1)} %get-tuple-element.95.refs_0_, bf16[32,16,512]{2,1,0:T(8,128)(2,1)S(1)} %collective-permute-done.2.refs_1_, bf16[32,16,512]{2,1,0:T(8,128)(2,1)S(1)} %collective-permute-done.1.refs_2_, ...), custom_call_target="tpu_custom_call" | custom-call | flops 1 | bytes 1 | tf_op jit(solution)/shard_map/pallas_call | solution.py:98
  361.0 15.6 %collective-permute-done.25.refs_2_ = bf16[16,32,512]{2,1,0:T(8,128)(2,1)S(1)} collective-permute-done((bf16[16,32,512]{2,1,0:T(8,128)(2,1)}, bf16[16,32,512]{2,1,0:T(8,128)(2,1)S(1)}, u32[]{:S(2)}, u32[]{:S(2)}) %collective-permute-start.25) | collective-permute-done | bytes 524320 | tf_op jit(solution)/shard_map/ppermute | solution.py:94
  376.6 7.6 %shard_map.113 = (bf16[512,8192]{1,0:T(8,128)(2,1)}, bf16[8,256,256]{2,1,0:T(8,128)(2,1)}) custom-call(s32[1]{0:T(128)} %bitcast.me_ref._, bf16[16,32,512]{2,1,0:T(8,128)(2,1)S(1)} %copy-done.6, bf16[16,32,512]{2,1,0:T(8,128)(2,1)S(1)} %collective-permute-done.20.refs_1_, bf16[16,32,512]{2,1,0:T(8,128)(2,1)S(1)} %collective-permute-done.25.refs_2_, ...), custom_call_target="tpu_custom_call" | custom-call | flops 1 | bytes 1 | tf_op jit(solution)/shard_map/pallas_call | solution.py:98
  386.1 2.7 collective-permute-start.21
  388.8 12.5 %collective-permute-done.31.refs_3_ = bf16[16,32,512]{2,1,0:T(8,128)(2,1)S(1)} collective-permute-done((bf16[16,32,512]{2,1,0:T(8,128)(2,1)}, bf16[16,32,512]{2,1,0:T(8,128)(2,1)S(1)}, u32[]{:S(2)}, u32[]{:S(2)}) %collective-permute-start.31) | collective-permute-done | bytes 524320 | tf_op jit(solution)/shard_map/ppermute | solution.py:94
  401.4 27.4 %collective-permute-done.26.refs_2_ = bf16[16,32,512]{2,1,0:T(8,128)(2,1)S(1)} collective-permute-done((bf16[16,32,512]{2,1,0:T(8,128)(2,1)}, bf16[16,32,512]{2,1,0:T(8,128)(2,1)S(1)}, u32[]{:S(2)}, u32[]{:S(2)}) %collective-permute-start.26) | collective-permute-done | bytes 524320 | tf_op jit(solution)/shard_map/ppermute | solution.py:94
  428.8 7.8 %shard_map.114 = (bf16[512,8192]{1,0:T(8,128)(2,1)}, bf16[8,256,256]{2,1,0:T(8,128)(2,1)}) custom-call(s32[1]{0:T(128)} %bitcast.me_ref._, bf16[16,32,512]{2,1,0:T(8,128)(2,1)S(1)} %copy-done.2, bf16[16,32,512]{2,1,0:T(8,128)(2,1)S(1)} %collective-permute-done.21.refs_1_, ...), custom_call_target="tpu_custom_call", output_to_operand_aliasing={{0}: (8, {})} | custom-call | flops 1 | bytes 1 | tf_op jit(solution)/shard_map/pallas_call | solution.py:98
  438.9 2.3 collective-permute-start.22
  441.1 12.3 %collective-permute-done.32.refs_3_ = bf16[16,32,512]{2,1,0:T(8,128)(2,1)S(1)} collective-permute-done((bf16[16,32,512]{2,1,0:T(8,128)(2,1)S(1)}, bf16[16,32,512]{2,1,0:T(8,128)(2,1)S(1)}, u32[]{:S(2)}, u32[]{:S(2)}) %collective-permute-start.32) | collective-permute-done | bytes 524320 | tf_op jit(solution)/shard_map/ppermute | solution.py:94
  453.5 26.9 %collective-permute-done.27.refs_2_ = bf16[16,32,512]{2,1,0:T(8,128)(2,1)S(1)} collective-permute-done((bf16[16,32,512]{2,1,0:T(8,128)(2,1)S(1)}, bf16[16,32,512]{2,1,0:T(8,128)(2,1)S(1)}, u32[]{:S(2)}, u32[]{:S(2)}) %collective-permute-start.27) | collective-permute-done | bytes 524320 | tf_op jit(solution)/shard_map/ppermute | solution.py:94
  480.4 7.6 %shard_map.115 = (bf16[512,8192]{1,0:T(8,128)(2,1)}, bf16[8,256,256]{2,1,0:T(8,128)(2,1)}) custom-call(s32[1]{0:T(128)} %bitcast.me_ref._, bf16[16,32,512]{2,1,0:T(8,128)(2,1)S(1)} %copy-done.1, bf16[16,32,512]{2,1,0:T(8,128)(2,1)S(1)} %collective-permute-done.22.refs_1_, ...), custom_call_target="tpu_custom_call", output_to_operand_aliasing={{0}: (8, {})} | custom-call | flops 1 | bytes 1 | tf_op jit(solution)/shard_map/pallas_call | solution.py:98
  490.7 2.6 collective-permute-start.23
  493.4 6.7 %collective-permute-done.33.refs_3_ = bf16[8,32,512]{2,1,0:T(8,128)(2,1)S(1)} collective-permute-done((bf16[8,32,512]{2,1,0:T(8,128)(2,1)S(1)}, bf16[8,32,512]{2,1,0:T(8,128)(2,1)S(1)}, u32[]{:S(2)}, u32[]{:S(2)}) %collective-permute-start.33) | collective-permute-done | bytes 262176 | tf_op jit(solution)/shard_map/ppermute | solution.py:94
  501.8 19.5 %collective-permute-done.28.refs_2_ = bf16[8,32,512]{2,1,0:T(8,128)(2,1)S(1)} collective-permute-done((bf16[8,32,512]{2,1,0:T(8,128)(2,1)S(1)}, bf16[8,32,512]{2,1,0:T(8,128)(2,1)S(1)}, u32[]{:S(2)}, u32[]{:S(2)}) %collective-permute-start.28) | collective-permute-done | bytes 262176 | tf_op jit(solution)/shard_map/ppermute | solution.py:94
  523.2 4.4 shard_map.116
  527.8 4.7 collective-permute-done.29.refs_2_
  532.5 4.5 shard_map.117
  547.1 4.7 collective-permute-done.38
  552.6 11.7 %reduce-scatter.5.cloned.1.call-done = bf16[32,64,256]{2,1,0:T(8,128)(2,1)} async-done(((bf16[32,256,256]{2,1,0:T(8,128)(2,1)}), bf16[32,64,256]{2,1,0:T(8,128)(2,1)}) %reduce-scatter.5.cloned.1.call-update) | async-done | bytes 1048592 | tf_op jit(solution)/shard_map/reduce_scatter | solution.py:448
  564.3 2.8 convert_element_type.66
  (185 shorter events, 45.1 us)
Async XLA Ops:
  7.2 532.3 %reduce-scatter.7.cloned.1.call-start = ((), (), s32[]{:S(2)}) async-start(), calls=%async_computation.5 | async-start | bytes 1310720 | tf_op jit(solution)/shard_map/reduce_scatter | solution.py:448
  14.7 46.7 %collective-permute-start = (bf16[32,16,512]{2,1,0:T(8,128)(2,1)}, bf16[32,16,512]{2,1,0:T(8,128)(2,1)S(1)}, u32[]{:S(2)}, u32[]{:S(2)}) collective-permute-start(bf16[32,16,512]{2,1,0:T(8,128)(2,1)} %get-tuple-element.99), channel_id=1, source_target_pairs={{0,12},{4,8},{8,4},{12,0},{1,13},{5,9},{9,5},{13,1},{2,14},{6,10},... | collective-permute-start | bytes 1572872 | tf_op jit(solution)/shard_map/ppermute | solution.py:94
  19.7 45.0 %collective-permute-start.1 = (bf16[32,16,512]{2,1,0:T(8,128)(2,1)S(1)}, bf16[32,16,512]{2,1,0:T(8,128)(2,1)S(1)}, u32[]{:S(2)}, u32[]{:S(2)}) collective-permute-start(bf16[32,16,512]{2,1,0:T(8,128)(2,1)S(1)} %get-tuple-element.100), channel_id=1, source_target_pairs={{0,8},{4,12},{8,0},{12,4},{1,9},{5,13},{9,1},{13,5},{2,10},{6,14},... | collective-permute-start | bytes 1572872 | tf_op jit(solution)/shard_map/ppermute | solution.py:94
  19.7 45.0 %collective-permute-start.2 = (bf16[32,16,512]{2,1,0:T(8,128)(2,1)S(1)}, bf16[32,16,512]{2,1,0:T(8,128)(2,1)S(1)}, u32[]{:S(2)}, u32[]{:S(2)}) collective-permute-start(bf16[32,16,512]{2,1,0:T(8,128)(2,1)S(1)} %get-tuple-element.101), channel_id=1, source_target_pairs={{0,4},{4,0},{8,12},{12,8},{1,5},{5,1},{9,13},{13,9},{2,6},{6,2},{1... | collective-permute-start | bytes 1572872 | tf_op jit(solution)/shard_map/ppermute | solution.py:94
  64.7 58.5 %collective-permute-start.3 = (bf16[2,512,768]{2,1,0:T(8,128)(2,1)S(1)}, bf16[2,512,768]{2,1,0:T(8,128)(2,1)S(1)}, u32[]{:S(2)}, u32[]{:S(2)}) collective-permute-start(bf16[2,512,768]{2,1,0:T(8,128)(2,1)S(1)} %get-tuple-element.102), channel_id=1, source_target_pairs={{0,4},{4,0},{8,12},{12,8},{1,5},{5,1},{9,13},{13,9},{2,6},{6,2},{1... | collective-permute-start | bytes 4718600 | tf_op jit(solution)/shard_map/ppermute | solution.py:94
  72.8 38.0 %collective-permute-start.4 = (bf16[32,16,512]{2,1,0:T(8,128)(2,1)S(1)}, bf16[32,16,512]{2,1,0:T(8,128)(2,1)S(1)}, u32[]{:S(2)}, u32[]{:S(2)}) collective-permute-start(bf16[32,16,512]{2,1,0:T(8,128)(2,1)S(1)} %get-tuple-element.104), channel_id=1, source_target_pairs={{0,8},{4,12},{8,0},{12,4},{1,9},{5,13},{9,1},{13,5},{2,10},{6,14},... | collective-permute-start | bytes 1572872 | tf_op jit(solution)/shard_map/ppermute | solution.py:94
  75.8 47.4 %collective-permute-start.5 = (bf16[32,16,512]{2,1,0:T(8,128)(2,1)}, bf16[32,16,512]{2,1,0:T(8,128)(2,1)S(1)}, u32[]{:S(2)}, u32[]{:S(2)}) collective-permute-start(bf16[32,16,512]{2,1,0:T(8,128)(2,1)} %get-tuple-element.105), channel_id=1, source_target_pairs={{0,12},{4,8},{8,4},{12,0},{1,13},{5,9},{9,5},{13,1},{2,14},{6,10},... | collective-permute-start | bytes 1572872 | tf_op jit(solution)/shard_map/ppermute | solution.py:94
  128.0 34.6 %collective-permute-start.6 = (bf16[512,768]{1,0:T(8,128)(2,1)S(1)}, bf16[512,768]{1,0:T(8,128)(2,1)S(1)}, u32[]{:S(2)}, u32[]{:S(2)}) collective-permute-start(bf16[512,768]{1,0:T(8,128)(2,1)S(1)} %get-tuple-element.108), channel_id=1, source_target_pairs={{0,8},{4,12},{8,0},{12,4},{1,9},{5,13},{9,1},{13,5},{2,10},{6,14},... | collective-permute-start | bytes 2359304 | tf_op jit(solution)/shard_map/ppermute | solution.py:94
  128.0 27.8 %collective-permute-start.7 = (bf16[32,16,512]{2,1,0:T(8,128)(2,1)}, bf16[32,16,512]{2,1,0:T(8,128)(2,1)}, u32[]{:S(2)}, u32[]{:S(2)}) collective-permute-start(bf16[32,16,512]{2,1,0:T(8,128)(2,1)} %get-tuple-element.110), channel_id=1, source_target_pairs={{0,4},{4,0},{8,12},{12,8},{1,5},{5,1},{9,13},{13,9},{2,6},{6,2},{1... | collective-permute-start | bytes 1572872 | tf_op jit(solution)/shard_map/ppermute | solution.py:94
  162.6 75.6 %copy-start.50 = (bf16[32,16,512]{2,1,0:T(8,128)(2,1)S(1)}, bf16[32,16,512]{2,1,0:T(8,128)(2,1)}, u32[]{:S(2)}) copy-start(bf16[32,16,512]{2,1,0:T(8,128)(2,1)} %get-tuple-element.136) | copy-start | bytes 1572868
  162.6 77.3 %copy-start.12 = (bf16[32,16,512]{2,1,0:T(8,128)(2,1)S(1)}, bf16[32,16,512]{2,1,0:T(8,128)(2,1)}, u32[]{:S(2)}) copy-start(bf16[32,16,512]{2,1,0:T(8,128)(2,1)} %copy-done.11) | copy-start | bytes 1572868
  165.4 13.9 %collective-permute-start.10 = (bf16[512,512]{1,0:T(8,128)(2,1)S(1)}, bf16[512,512]{1,0:T(8,128)(2,1)S(1)}, u32[]{:S(2)}, u32[]{:S(2)}) collective-permute-start(bf16[512,512]{1,0:T(8,128)(2,1)S(1)} %get-tuple-element.119.refs_0_), channel_id=1, source_target_pairs={{0,2},{1,3},{2,0},{3,1},{4,6},{5,7},{6,4},{7,5},{8,10},{9,11},{10,... | collective-permute-start | bytes 1572872 | tf_op jit(solution)/shard_map/ppermute | solution.py:94
  166.9 26.0 %collective-permute-start.9 = (bf16[512,512]{1,0:T(8,128)(2,1)S(1)}, bf16[512,512]{1,0:T(8,128)(2,1)S(1)}, u32[]{:S(2)}, u32[]{:S(2)}) collective-permute-start(bf16[512,512]{1,0:T(8,128)(2,1)S(1)} %get-tuple-element.119.refs_0_), channel_id=1, source_target_pairs={{0,1},{1,0},{2,3},{3,2},{4,5},{5,4},{6,7},{7,6},{8,9},{9,8},{10,11... | collective-permute-start | bytes 1572872 | tf_op jit(solution)/shard_map/ppermute | solution.py:94
  166.9 26.0 %collective-permute-start.8 = (bf16[32,16,512]{2,1,0:T(8,128)(2,1)S(1)}, bf16[32,16,512]{2,1,0:T(8,128)(2,1)S(1)}, u32[]{:S(2)}, u32[]{:S(2)}) collective-permute-start(bf16[32,16,512]{2,1,0:T(8,128)(2,1)S(1)} %copy-done.18), channel_id=1, source_target_pairs={{0,8},{4,12},{8,0},{12,4},{1,9},{5,13},{9,1},{13,5},{2,10},{6,14},... | collective-permute-start | bytes 1572872 | tf_op jit(solution)/shard_map/ppermute | solution.py:94
  179.3 13.6 %collective-permute-start.11 = (bf16[512,512]{1,0:T(8,128)(2,1)S(1)}, bf16[512,512]{1,0:T(8,128)(2,1)S(1)}, u32[]{:S(2)}, u32[]{:S(2)}) collective-permute-start(bf16[512,512]{1,0:T(8,128)(2,1)S(1)} %collective-permute-done.10.refs_2_), channel_id=1, source_target_pairs={{0,1},{1,0},{2,3},{3,2},{4,5},{5,4},{6,7},{7,6},{8,9},{9,8},{10,11... | collective-permute-start | bytes 1572872 | tf_op jit(solution)/shard_map/ppermute | solution.py:94
  192.9 133.3 %copy-start.35 = (bf16[32,16,512]{2,1,0:T(8,128)(2,1)}, bf16[32,16,512]{2,1,0:T(8,128)(2,1)S(1)}, u32[]{:S(2)}) copy-start(bf16[32,16,512]{2,1,0:T(8,128)(2,1)S(1)} %collective-permute-done.8.refs_10_) | copy-start | bytes 1572868
  192.9 15.9 %collective-permute-start.12 = (bf16[32,16,512]{2,1,0:T(8,128)(2,1)S(1)}, bf16[32,16,512]{2,1,0:T(8,128)(2,1)S(1)}, u32[]{:S(2)}, u32[]{:S(2)}) collective-permute-start(bf16[32,16,512]{2,1,0:T(8,128)(2,1)S(1)} %copy-done.52), channel_id=1, source_target_pairs={{0,12},{4,8},{8,4},{12,0},{1,13},{5,9},{9,5},{13,1},{2,14},{6,10},... | collective-permute-start | bytes 1572872 | tf_op jit(solution)/shard_map/ppermute | solution.py:94
  201.2 85.1 %copy-start = (bf16[512,256]{1,0:T(8,128)(2,1)}, bf16[512,256]{1,0:T(8,128)(2,1)S(1)}, u32[]{:S(2)}) copy-start(bf16[512,256]{1,0:T(8,128)(2,1)S(1)} %shard_map.110.own) | copy-start | bytes 786436
  208.8 117.4 %copy-start.36 = (bf16[32,16,512]{2,1,0:T(8,128)(2,1)}, bf16[32,16,512]{2,1,0:T(8,128)(2,1)S(1)}, u32[]{:S(2)}) copy-start(bf16[32,16,512]{2,1,0:T(8,128)(2,1)S(1)} %collective-permute-done.12.refs_11_) | copy-start | bytes 1572868
  208.8 20.2 %collective-permute-start.14 = (bf16[512,256]{1,0:T(8,128)(2,1)S(1)}, bf16[512,256]{1,0:T(8,128)(2,1)S(1)}, u32[]{:S(2)}, u32[]{:S(2)}) collective-permute-start(bf16[512,256]{1,0:T(8,128)(2,1)S(1)} %shard_map.110.own), channel_id=1, source_target_pairs={{0,8},{4,12},{8,0},{12,4},{1,9},{5,13},{9,1},{13,5},{2,10},{6,14},... | collective-permute-start | bytes 786440 | tf_op jit(solution)/shard_map/ppermute | solution.py:94
  229.0 9.2 %collective-permute-start.15 = (bf16[512,256]{1,0:T(8,128)(2,1)S(1)}, bf16[512,256]{1,0:T(8,128)(2,1)S(1)}, u32[]{:S(2)}, u32[]{:S(2)}) collective-permute-start(bf16[512,256]{1,0:T(8,128)(2,1)S(1)} %collective-permute-done.14.far), channel_id=1, source_target_pairs={{0,4},{4,0},{8,12},{12,8},{1,5},{5,1},{9,13},{13,9},{2,6},{6,2},{1... | collective-permute-start | bytes 786440 | tf_op jit(solution)/shard_map/ppermute | solution.py:94
  229.0 42.6 %collective-permute-start.17 = (bf16[32,16,512]{2,1,0:T(8,128)(2,1)S(1)}, bf16[32,16,512]{2,1,0:T(8,128)(2,1)S(1)}, u32[]{:S(2)}, u32[]{:S(2)}) collective-permute-start(bf16[32,16,512]{2,1,0:T(8,128)(2,1)S(1)} %copy-done.16), channel_id=1, source_target_pairs={{0,4},{4,0},{8,12},{12,8},{1,5},{5,1},{9,13},{13,9},{2,6},{6,2},{1... | collective-permute-start | bytes 1572872 | tf_op jit(solution)/shard_map/ppermute | solution.py:94
  231.0 52.2 %collective-permute-start.16 = (bf16[32,16,512]{2,1,0:T(8,128)(2,1)S(1)}, bf16[32,16,512]{2,1,0:T(8,128)(2,1)S(1)}, u32[]{:S(2)}, u32[]{:S(2)}) collective-permute-start(bf16[32,16,512]{2,1,0:T(8,128)(2,1)S(1)} %copy-done.14), channel_id=1, source_target_pairs={{0,4},{4,0},{8,12},{12,8},{1,5},{5,1},{9,13},{13,9},{2,6},{6,2},{1... | collective-permute-start | bytes 1572872 | tf_op jit(solution)/shard_map/ppermute | solution.py:94
  238.2 93.0 %collective-permute-start.19 = (bf16[32,16,512]{2,1,0:T(8,128)(2,1)S(1)}, bf16[32,16,512]{2,1,0:T(8,128)(2,1)S(1)}, u32[]{:S(2)}, u32[]{:S(2)}) collective-permute-start(bf16[32,16,512]{2,1,0:T(8,128)(2,1)S(1)} %copy-done.50), channel_id=1, source_target_pairs={{0,12},{4,8},{8,4},{12,0},{1,13},{5,9},{9,5},{13,1},{2,14},{6,10},... | collective-permute-start | bytes 1572872 | tf_op jit(solution)/shard_map/ppermute | solution.py:94
  239.9 91.3 %collective-permute-start.18 = (bf16[32,16,512]{2,1,0:T(8,128)(2,1)S(1)}, bf16[32,16,512]{2,1,0:T(8,128)(2,1)S(1)}, u32[]{:S(2)}, u32[]{:S(2)}) collective-permute-start(bf16[32,16,512]{2,1,0:T(8,128)(2,1)S(1)} %copy-done.12), channel_id=1, source_target_pairs={{0,8},{4,12},{8,0},{12,4},{1,9},{5,13},{9,1},{13,5},{2,10},{6,14},... | collective-permute-start | bytes 1572872 | tf_op jit(solution)/shard_map/ppermute | solution.py:94
  239.9 46.4 %collective-permute-start.13 = (bf16[512,256]{1,0:T(8,128)(2,1)S(1)}, bf16[512,256]{1,0:T(8,128)(2,1)S(1)}, u32[]{:S(2)}, u32[]{:S(2)}) collective-permute-start(bf16[512,256]{1,0:T(8,128)(2,1)S(1)} %shard_map.110.own), channel_id=1, source_target_pairs={{0,4},{4,0},{8,12},{12,8},{1,5},{5,1},{9,13},{13,9},{2,6},{6,2},{1... | collective-permute-start | bytes 786440 | tf_op jit(solution)/shard_map/ppermute | solution.py:94
  331.2 29.8 %collective-permute-start.30 = (bf16[16,32,512]{2,1,0:T(8,128)(2,1)}, bf16[16,32,512]{2,1,0:T(8,128)(2,1)}, u32[]{:S(2)}, u32[]{:S(2)}) collective-permute-start(bf16[16,32,512]{2,1,0:T(8,128)(2,1)} %get-tuple-element.164), channel_id=1, source_target_pairs={{0,12},{4,8},{8,4},{12,0},{1,13},{5,9},{9,5},{13,1},{2,14},{6,10},... | collective-permute-start | bytes 1572872 | tf_op jit(solution)/shard_map/ppermute | solution.py:94
  332.9 43.7 %collective-permute-start.25 = (bf16[16,32,512]{2,1,0:T(8,128)(2,1)}, bf16[16,32,512]{2,1,0:T(8,128)(2,1)S(1)}, u32[]{:S(2)}, u32[]{:S(2)}) collective-permute-start(bf16[16,32,512]{2,1,0:T(8,128)(2,1)} %get-tuple-element.154), channel_id=1, source_target_pairs={{0,8},{4,12},{8,0},{12,4},{1,9},{5,13},{9,1},{13,5},{2,10},{6,14},... | collective-permute-start | bytes 1572872 | tf_op jit(solution)/shard_map/ppermute | solution.py:94
  333.0 43.6 %collective-permute-start.20 = (bf16[16,32,512]{2,1,0:T(8,128)(2,1)}, bf16[16,32,512]{2,1,0:T(8,128)(2,1)S(1)}, u32[]{:S(2)}, u32[]{:S(2)}) collective-permute-start(bf16[16,32,512]{2,1,0:T(8,128)(2,1)} %get-tuple-element.144), channel_id=1, source_target_pairs={{0,4},{4,0},{8,12},{12,8},{1,5},{5,1},{9,13},{13,9},{2,6},{6,2},{1... | collective-permute-start | bytes 1572872 | tf_op jit(solution)/shard_map/ppermute | solution.py:94
  384.3 156.9 %reduce-scatter.9.cloned.1.call-start = ((), (), s32[]{:S(2)}) async-start(), calls=%async_computation.6 | async-start | bytes 1310720 | tf_op jit(solution)/shard_map/reduce_scatter | solution.py:448
  384.4 17.0 %collective-permute-start.31 = (bf16[16,32,512]{2,1,0:T(8,128)(2,1)}, bf16[16,32,512]{2,1,0:T(8,128)(2,1)S(1)}, u32[]{:S(2)}, u32[]{:S(2)}) collective-permute-start(bf16[16,32,512]{2,1,0:T(8,128)(2,1)} %get-tuple-element.165), channel_id=1, source_target_pairs={{0,12},{4,8},{8,4},{12,0},{1,13},{5,9},{9,5},{13,1},{2,14},{6,10},... | collective-permute-start | bytes 1572872 | tf_op jit(solution)/shard_map/ppermute | solution.py:94
  386.1 42.7 %collective-permute-start.26 = (bf16[16,32,512]{2,1,0:T(8,128)(2,1)}, bf16[16,32,512]{2,1,0:T(8,128)(2,1)S(1)}, u32[]{:S(2)}, u32[]{:S(2)}) collective-permute-start(bf16[16,32,512]{2,1,0:T(8,128)(2,1)} %get-tuple-element.155), channel_id=1, source_target_pairs={{0,8},{4,12},{8,0},{12,4},{1,9},{5,13},{9,1},{13,5},{2,10},{6,14},... | collective-permute-start | bytes 1572872 | tf_op jit(solution)/shard_map/ppermute | solution.py:94
  386.1 42.7 %collective-permute-start.21 = (bf16[16,32,512]{2,1,0:T(8,128)(2,1)S(1)}, bf16[16,32,512]{2,1,0:T(8,128)(2,1)S(1)}, u32[]{:S(2)}, u32[]{:S(2)}) collective-permute-start(bf16[16,32,512]{2,1,0:T(8,128)(2,1)S(1)} %copy-done.51), channel_id=1, source_target_pairs={{0,4},{4,0},{8,12},{12,8},{1,5},{5,1},{9,13},{13,9},{2,6},{6,2},{1... | collective-permute-start | bytes 1572872 | tf_op jit(solution)/shard_map/ppermute | solution.py:94
  436.6 106.4 %reduce-scatter.11.cloned.1.call-start = ((), (), s32[]{:S(2)}) async-start(), calls=%async_computation.7 | async-start | bytes 1310720 | tf_op jit(solution)/shard_map/reduce_scatter | solution.py:448
  436.7 16.8 %collective-permute-start.32 = (bf16[16,32,512]{2,1,0:T(8,128)(2,1)S(1)}, bf16[16,32,512]{2,1,0:T(8,128)(2,1)S(1)}, u32[]{:S(2)}, u32[]{:S(2)}) collective-permute-start(bf16[16,32,512]{2,1,0:T(8,128)(2,1)S(1)} %copy-done.49), channel_id=1, source_target_pairs={{0,12},{4,8},{8,4},{12,0},{1,13},{5,9},{9,5},{13,1},{2,14},{6,10},... | collective-permute-start | bytes 1572872 | tf_op jit(solution)/shard_map/ppermute | solution.py:94
  438.9 41.5 %collective-permute-start.27 = (bf16[16,32,512]{2,1,0:T(8,128)(2,1)S(1)}, bf16[16,32,512]{2,1,0:T(8,128)(2,1)S(1)}, u32[]{:S(2)}, u32[]{:S(2)}) collective-permute-start(bf16[16,32,512]{2,1,0:T(8,128)(2,1)S(1)} %copy-done.48), channel_id=1, source_target_pairs={{0,8},{4,12},{8,0},{12,4},{1,9},{5,13},{9,1},{13,5},{2,10},{6,14},... | collective-permute-start | bytes 1572872 | tf_op jit(solution)/shard_map/ppermute | solution.py:94
  438.9 41.5 %collective-permute-start.22 = (bf16[16,32,512]{2,1,0:T(8,128)(2,1)S(1)}, bf16[16,32,512]{2,1,0:T(8,128)(2,1)S(1)}, u32[]{:S(2)}, u32[]{:S(2)}) collective-permute-start(bf16[16,32,512]{2,1,0:T(8,128)(2,1)S(1)} %copy-done.47), channel_id=1, source_target_pairs={{0,4},{4,0},{8,12},{12,8},{1,5},{5,1},{9,13},{13,9},{2,6},{6,2},{1... | collective-permute-start | bytes 1572872 | tf_op jit(solution)/shard_map/ppermute | solution.py:94
  488.1 76.2 %reduce-scatter.5.cloned.1.call-start = ((), (), s32[]{:S(2)}) async-start(), calls=%async_computation.4 | async-start | bytes 5242880 | tf_op jit(solution)/shard_map/reduce_scatter | solution.py:448
  489.0 11.0 %collective-permute-start.33 = (bf16[8,32,512]{2,1,0:T(8,128)(2,1)S(1)}, bf16[8,32,512]{2,1,0:T(8,128)(2,1)S(1)}, u32[]{:S(2)}, u32[]{:S(2)}) collective-permute-start(bf16[8,32,512]{2,1,0:T(8,128)(2,1)S(1)} %copy-done.28), channel_id=1, source_target_pairs={{0,12},{4,8},{8,4},{12,0},{1,13},{5,9},{9,5},{13,1},{2,14},{6,10},... | collective-permute-start | bytes 786440 | tf_op jit(solution)/shard_map/ppermute | solution.py:94
  490.7 30.5 %collective-permute-start.28 = (bf16[8,32,512]{2,1,0:T(8,128)(2,1)S(1)}, bf16[8,32,512]{2,1,0:T(8,128)(2,1)S(1)}, u32[]{:S(2)}, u32[]{:S(2)}) collective-permute-start(bf16[8,32,512]{2,1,0:T(8,128)(2,1)S(1)} %copy-done.26), channel_id=1, source_target_pairs={{0,8},{4,12},{8,0},{12,4},{1,9},{5,13},{9,1},{13,5},{2,10},{6,14},... | collective-permute-start | bytes 786440 | tf_op jit(solution)/shard_map/ppermute | solution.py:94
  490.7 30.5 %collective-permute-start.23 = (bf16[8,32,512]{2,1,0:T(8,128)(2,1)S(1)}, bf16[8,32,512]{2,1,0:T(8,128)(2,1)S(1)}, u32[]{:S(2)}, u32[]{:S(2)}) collective-permute-start(bf16[8,32,512]{2,1,0:T(8,128)(2,1)S(1)} %copy-done.24), channel_id=1, source_target_pairs={{0,4},{4,0},{8,12},{12,8},{1,5},{5,1},{9,13},{13,9},{2,6},{6,2},{1... | collective-permute-start | bytes 786440 | tf_op jit(solution)/shard_map/ppermute | solution.py:94
  500.0 27.7 %collective-permute-start.34 = (bf16[8,32,512]{2,1,0:T(8,128)(2,1)S(1)}, bf16[8,32,512]{2,1,0:T(8,128)(2,1)S(1)}, u32[]{:S(2)}, u32[]{:S(2)}) collective-permute-start(bf16[8,32,512]{2,1,0:T(8,128)(2,1)S(1)} %copy-done.53), channel_id=1, source_target_pairs={{0,12},{4,8},{8,4},{12,0},{1,13},{5,9},{9,5},{13,1},{2,14},{6,10},... | collective-permute-start | bytes 786440 | tf_op jit(solution)/shard_map/ppermute | solution.py:94
  521.2 11.2 %collective-permute-start.29 = (bf16[8,32,512]{2,1,0:T(8,128)(2,1)S(1)}, bf16[8,32,512]{2,1,0:T(8,128)(2,1)S(1)}, u32[]{:S(2)}, u32[]{:S(2)}) collective-permute-start(bf16[8,32,512]{2,1,0:T(8,128)(2,1)S(1)} %copy-done.22), channel_id=1, source_target_pairs={{0,8},{4,12},{8,0},{12,4},{1,9},{5,13},{9,1},{13,5},{2,10},{6,14},... | collective-permute-start | bytes 786440 | tf_op jit(solution)/shard_map/ppermute | solution.py:94
  521.3 11.2 %collective-permute-start.24 = (bf16[8,32,512]{2,1,0:T(8,128)(2,1)S(1)}, bf16[8,32,512]{2,1,0:T(8,128)(2,1)S(1)}, u32[]{:S(2)}, u32[]{:S(2)}) collective-permute-start(bf16[8,32,512]{2,1,0:T(8,128)(2,1)S(1)} %copy-done.20), channel_id=1, source_target_pairs={{0,4},{4,0},{8,12},{12,8},{1,5},{5,1},{9,13},{13,9},{2,6},{6,2},{1... | collective-permute-start | bytes 786440 | tf_op jit(solution)/shard_map/ppermute | solution.py:94
  527.7 9.4 %collective-permute-start.35 = (bf16[2,4,64,256]{3,2,1,0:T(8,128)(2,1)S(1)}, bf16[2,4,64,256]{3,2,1,0:T(8,128)(2,1)S(1)}, u32[]{:S(2)}, u32[]{:S(2)}) collective-permute-start(bf16[2,4,64,256]{3,2,1,0:T(8,128)(2,1)S(1)} %pad_maximum_fusion), channel_id=1, source_target_pairs={{0,1},{1,0},{2,3},{3,2},{4,5},{5,4},{6,7},{7,6},{8,9},{9,8},{10,11... | collective-permute-start | bytes 786440 | tf_op jit(solution)/shard_map/ppermute | solution.py:94
  537.0 1.6 collective-permute-start.37
  537.2 9.2 %collective-permute-start.36 = (bf16[4,64,256]{2,1,0:T(8,128)(2,1)S(1)}, bf16[4,64,256]{2,1,0:T(8,128)(2,1)S(1)}, u32[]{:S(2)}, u32[]{:S(2)}) collective-permute-start(bf16[4,64,256]{2,1,0:T(8,128)(2,1)S(1)} %fusion.6), channel_id=1, source_target_pairs={{0,2},{1,3},{2,0},{3,1},{4,6},{5,7},{6,4},{7,5},{8,10},{9,11},{10,... | collective-permute-start | bytes 393224 | tf_op jit(solution)/shard_map/ppermute | solution.py:94
  538.7 13.2 %collective-permute-start.38 = (bf16[4,64,256]{2,1,0:T(8,128)(2,1)S(1)}, bf16[4,64,256]{2,1,0:T(8,128)(2,1)S(1)}, u32[]{:S(2)}, u32[]{:S(2)}) collective-permute-start(bf16[4,64,256]{2,1,0:T(8,128)(2,1)S(1)} %fusion.1), channel_id=1, source_target_pairs={{0,2},{1,3},{2,0},{3,1},{4,6},{5,7},{6,4},{7,5},{8,10},{9,11},{10,... | collective-permute-start | bytes 393224 | tf_op jit(solution)/shard_map/ppermute | solution.py:94
  (49 other events, 878.5 us)
Sparse Core Ops, SparseCore 0:
  384.4 23.3 reduce-scatter.6
  436.7 23.6 reduce-scatter.8
  488.1 23.3 reduce-scatter.10
  514.1 50.1 reduce-scatter.4

commit v2 on v1

--- a/solution.py
+++ b/solution.py
@@ -1,3 +1,5 @@
+import math
+
 import jax
 import jax.numpy as jnp
 from jax import lax
@@ -232,6 +234,20 @@
     )
 
 
+def store_quarters(me, held, send_ref, keep_ref):
+    quarter = held.shape[0] // 4
+    for out, flips in ((send_ref, (1, 3)), (keep_ref, (0, 2))):
+        for slot, bits in enumerate(flips):
+            start = pl.multiple_of((me ^ bits) * quarter, quarter)
+            out[slot, 0] = held[pl.ds(start, quarter), :].astype(out.dtype)
+
+
+def quarter_outs(count, size):
+    shape = (2, count, size // 4, size)
+    place = spec((2, 1, size // 4, size), lambda j, _: (0, j, 0, 0))
+    return [array(shape, BF16), array(shape, F32)], [place, place]
+
+
 def add_kernel(_, keep_ref, came_ref, mine_ref, other_ref):
     mine_ref[...] = keep_ref[0] + came_ref[0].astype(F32)
     other_ref[...] = (keep_ref[1] + came_ref[1].astype(F32)).astype(BF16)
@@ -257,6 +273,32 @@
         part * part, same, precision=lax.Precision.HIGHEST, preferred_element_type=F32
     )
     return (part * lax.rsqrt(sums * (1.0 / HEAD_DIM) + 1e-06)).astype(BF16)
+
+
+def finish_kernel(_, mine_ref, came_ref, *refs):
+    refs[-1][...] = mine_ref[...] + came_ref[...].astype(F32)
+
+
+def finish_call(me, mine, came, total, start, blocks):
+    count, quarter, size = mine.shape
+    step = math.gcd(count, start) if start else count
+    args = [mine, came]
+    in_specs = [spec((step, quarter, size), lambda i, _: (i, 0, 0))] * 2
+    aliases = {}
+    if total is not None:
+        args.append(total)
+        in_specs.append(pl.BlockSpec(memory_space=pl.ANY))
+        aliases = {len(args): 0}
+    return call(
+        finish_kernel,
+        me,
+        args,
+        in_specs,
+        array((blocks, quarter, size), F32),
+        spec((step, quarter, size), lambda i, _: (start // step + i, 0, 0)),
+        grid=(count // step,),
+        aliases=aliases,
+    )
 
 
 def split_kernel(_, mine_ref, came_ref, query_ref, out_ref):
@@ -380,12 +422,13 @@
 def second_kernel(me_ref, *refs):
     pieces = refs[:4]
     w_ref, cot_ref, hidden_ref = refs[4:7]
-    out_ref, grad_ref, held = refs[-3:]
+    out_ref, send_ref, keep_ref, held, square = refs[-5:]
     for bits, piece in enumerate(pieces):
         held[:, me_ref[0] ^ bits] = piece[...]
     size = w_ref.shape[1]
     permuted = held[...].reshape(size, held.shape[3])
-    grad_ref[0] = jnp.dot(permuted, cot_ref[...], preferred_element_type=F32).astype(BF16)
+    square[...] = jnp.dot(permuted, cot_ref[...], preferred_element_type=F32)
+    store_quarters(me_ref[1], square, send_ref, keep_ref)
     mixed = lax.dot_general(
         permuted, w_ref[0], (((0,), (0,)), ((), ())), preferred_element_type=F32
     )
@@ -401,6 +444,7 @@
     square = spec((1, size, size), lambda j, _: (start + j, 0, 0))
     args = [*pieces, w_second, cotangent, hidden]
     in_specs = [spec((pair, blocks, rows), lambda j, _: (j, 0, 0))] * 4 + [square, wide, wide]
+    quarters = quarter_outs(count, size)
     aliases = {}
     if denoised is not None:
         args.append(denoised)
@@ -411,22 +455,22 @@
         me,
         args,
         in_specs,
-        [array(hidden.shape, BF16), array((count, size, size), BF16)],
-        [wide, spec((1, size, size), lambda j, _: (j, 0, 0))],
+        [array(hidden.shape, BF16), *quarters[0]],
+        [wide, *quarters[1]],
         grid=(count,),
-        scratch=[pltpu.VMEM((pair, 4, blocks, rows), BF16)],
+        scratch=[pltpu.VMEM((pair, 4, blocks, rows), BF16), pltpu.VMEM((size, size), F32)],
         aliases=aliases,
     )
 
 
 def grad_first_kernel(me_ref, *refs):
-    pieces, hidden_ref, out_ref, held = refs[:-3], refs[-3], refs[-2], refs[-1]
+    pieces, (hidden_ref, send_ref, keep_ref, held, square) = refs[:-5], refs[-5:]
     for half in range(len(pieces) // 4):
         for bits in range(4):
             held[me_ref[0] ^ bits, half] = pieces[half * 4 + bits][0]
     back = held[...].reshape(-1, held.shape[3])
-    grad = jnp.dot(back, hidden_ref[...], preferred_element_type=F32)
-    out_ref[0] = grad.T.astype(BF16)
+    square[...] = jnp.dot(back, hidden_ref[...], preferred_element_type=F32).T
+    store_quarters(me_ref[1], square, send_ref, keep_ref)
 
 
 def grad_first_call(me, pieces, hidden, size):
@@ -437,36 +481,21 @@
         (*pieces, hidden),
         [spec((1, deep, rows), lambda b, _: (b, 0, 0))] * len(pieces)
         + [spec((rows, size), lambda b, _: (0, b))],
-        array((blocks, size, size), BF16),
-        spec((1, size, size), lambda b, _: (b, 0, 0)),
+        *quarter_outs(blocks, size),
         grid=(blocks,),
-        scratch=[pltpu.VMEM((4, len(pieces) // 4, deep, rows), BF16)],
-    )
-
-
-def scatter_cells(grad):
-    return lax.psum_scatter(grad, "cell", scatter_dimension=1, tiled=True)
-
-
-def scatter_cells_halving(grad):
-    me = lax.axis_index("cell")
-    count, size, columns = grad.shape
-    rows = grad.reshape(count, 4, size // 4, columns)
-
-    def part(bits):
-        return lax.dynamic_index_in_dim(rows, me ^ bits, 1, keepdims=False)
-
-    came = flip(jnp.stack([part(1), part(3)]), "cell", 1).astype(F32)
-    other = (part(2).astype(F32) + came[1]).astype(BF16)
-    return part(0).astype(F32) + came[0] + flip(other, "cell", 2).astype(F32)
+        scratch=[
+            pltpu.VMEM((4, len(pieces) // 4, deep, rows), BF16),
+            pltpu.VMEM((size, size), F32),
+        ],
+    )
 
 
 def on_device_four(expression, gene_mask, mask_value, w_qkv, w_out, w_first, w_second, cotangent):
-    me = lax.axis_index("gene").astype(jnp.int32).reshape(1)
+    me = jnp.stack([lax.axis_index("gene"), lax.axis_index("cell")]).astype(jnp.int32)
     blocks, size, _ = w_first.shape
     parts = 4
     deep = size // 4
-    deeps = [deep // 4] * 3 + [deep // 8] * 2
+    deeps = [deep // 4] * 3 + [3 * deep // 16, deep // 16]
     matrix = grid_turn()
     sends, back = [None] * parts, [[None] * 4 for _ in range(parts)]
 
@@ -502,42 +531,41 @@
     queries = after(queries, *beside_keys, beside, across, corner)
     attended = attend_call(me, queries, (key_value, beside, across, corner))
     attended = after(attended, begin(2, 3, queries))
+    near = flip(attended, "gene", 1)
     far = flip(attended, "gene", 2)
-    near = flip(attended, "gene", 1)
-    rest = flip(far, "gene", 1)
-    beside_heads = [begin(2, 1, attended), begin(3, 1, attended)]
+    rest = flip(after(far, near), "gene", 1)
     hidden, first = first_call(
-        me,
-        matrix,
-        (attended, near, far, after(rest, *beside_heads)),
-        w_out,
-        masked,
-        w_first_t,
-        deeps,
-    )
-    for bits in (2, 3):
-        begin(3, bits, rest)
+        me, matrix, (attended, near, far, rest), w_out, masked, w_first_t, deeps
+    )
+    for part, bits in ((3, 2), (3, 3), (2, 1), (3, 1)):
+        begin(part, bits, rest)
 
     got = []
     for t in range(len(deeps)):
-        earlier = got[-1] if t else back[3]
+        earlier = got[-1] if t else [back[2][1], *back[3][1:]]
         got.append(first[t][:1])
         for bits in (1, 2, 3):
             ready = (earlier[bits],) if t else earlier
             got[t].append(flip(after(first[t][bits], *ready), "gene", bits))
-    grad_first = grad_first_call(me, sum(back, []), hidden, size)
-    first_share = scatter_cells(grad_first)
-
-    denoised, shares = None, []
+
+    send, keep = grad_first_call(me, sum(back, []), hidden, size)
+    mine, other = add_call(me, keep, flip(send, "cell", 1))
+    first_share = finish_call(me, mine, flip(other, "cell", 2), None, 0, blocks)
+
+    denoised, share, pins = None, None, (send,)
     for t in range(len(deeps)):
-        pieces = [after(got[t][0], grad_first), *got[t][1:]]
+        if t < len(deeps) - 2:
+            pins += tuple(got[t + 1])
+        pieces = [after(got[t][0], *pins), *got[t][1:]]
         start = sum(deeps[:t]) * blocks // deep
-        denoised, grad = second_call(me, pieces, w_second, cotangent, hidden, denoised, start)
-        if deeps[t] * 4 < deep:
-            shares.append(scatter_cells_halving(grad))
-        else:
-            shares.append(scatter_cells(grad).astype(F32))
-    return (denoised, first_share.astype(F32), jnp.concatenate(shares, axis=0))
+        denoised, send, keep = second_call(
+            me, pieces, w_second, cotangent, hidden, denoised, start
+        )
+        pins = (first_share,) if share is None else (share,)
+        mine, other = add_call(me, keep, flip(send, "cell", 1))
+        pins += (other,)
+        share = finish_call(me, mine, flip(other, "cell", 2), share, start, blocks)
+    return (denoised, first_share, share)
 
 
 def solution(mesh):

time: 576 us -> 549 us (0.953)
  waiting for transfers between devices: 297 us -> 254 us
  Pallas kernels: 179 us -> 210 us
  between operations: 14.3 us -> 1.14 us
  starting transfers between devices: 53.7 us -> 64 us
  other arithmetic: 10.1 us -> 0.36 us
    pallas_call x15 -> x27, Pallas kernels: 179 us -> 210 us  [call(): pl.pallas_call(body, out_shape=outs, grid_spec=pltpu.PrefetchScalarGridSp...]
    ppermute x39 -> x47, waiting for transfers between devices: 285 us -> 254 us  [flip(): return lax.ppermute(value, axis, pairs)]
    reduce_scatter x4 -> x0, waiting for transfers between devices: 11.7 us -> none  [scatter_cells(): return lax.psum_scatter(grad, 'cell', scatter_dimension=1, tiled=True)]
    ppermute x39 -> x47, starting transfers between devices: 53.6 us -> 64 us  [flip(): return lax.ppermute(value, axis, pairs)]
    unnamed x4 -> x0, other arithmetic: 6.1 us -> none
    unnamed x108 -> x96, local copies, waits for them, and re-layouts: 12.9 us -> 9.76 us
  transfers between devices with their start and end apart: 43 -> 47, of which waited for: 24 -> 21; matrix products, arithmetic and copies ran while one was open for 2% -> 1% of each run, Pallas kernels for 28% -> 25%
where the time goes in v2:
time: 549 us; the launch traced here: 546 us
  waiting for transfers between devices  254 us (46%)
  Pallas kernels  210 us (38%)
  starting transfers between devices  64 us (12%)
  local copies, waits for them, and re-layouts  16.2 us (3%)
    ppermute x47, waiting for transfers between devices, flip(): return lax.ppermute(value, axis, pairs)  254 us
    pallas_call x27, Pallas kernels, call(): pl.pallas_call(body, out_shape=outs, grid_spec=pltpu.PrefetchScalarGridSp...  210 us
    ppermute x47, starting transfers between devices, flip(): return lax.ppermute(value, axis, pairs)  64 us
  transfers between devices with their start and end apart: 47, of which 21 were waited for; matrix products, arithmetic and copies ran while one was open for 1% of the time, Pallas kernels for 25%

profile of v2, /device:TPU:0, one launch (start us, length us, event | category | flops | bytes accessed | tf_op | source)
XLA Modules:
  0.0 546.0 jit_solution(9495412657204355468)
XLA Ops:
  1.0 7.7 %shard_map.103 = (bf16[32,16,512]{2,1,0:T(8,128)(2,1)S(1)}, bf16[32,16,512]{2,1,0:T(8,128)(2,1)S(1)}, bf16[32,16,512]{2,1,0:T(8,128)(2,1)S(1)}, bf16[32,16,512]{2,1,0:T(8,128)(2,1)}) custom-call(s32[2]{0:T(128)S(1)} %pad_add_fusion.me_ref._, bf16[256,256]{1,0:T(8,128)(2,1)S(1)} %fusion.turn_ref, bf16[32,256,256]{2,1,0:T(8,128)(2,1)} %refs_4_.9, ...), custom_call_target="tpu_custom_call" | custom-call | flops 1 | bytes 1 | tf_op jit(solution)/shard_map/pallas_call | solution.py:100
  8.7 4.0 collective-permute-start.1
  14.4 41.6 %shard_map.104 = (bf16[512,8192]{1,0:T(8,128)(2,1)}, bf16[2,512,768]{2,1,0:T(8,128)(2,1)S(1)}, f32[2,512,768]{2,1,0:T(8,128)}) custom-call(s32[2]{0:T(128)S(1)} %pad_add_fusion.me_ref._, bf16[512,8192]{1,0:T(8,128)(2,1)} %value_ref, s32[512,8192]{1,0:T(8,128)} %mask_ref.1, bf16[1,8192]{1,0:T(2,128)(2,1)S(1)} %reshape.9.fill_ref, bf16[8192,3072]{1,0:T(8,128)(2,1)} %refs_2_.1, ...), custom_call_target="tpu_custom_call" | custom-call | flops 1 | bytes 1 | tf_op jit(solution)/shard_map/pallas_call | solution.py:100
  56.8 3.2 collective-permute-start.3
  60.0 7.8 %shard_map.105 = (bf16[32,16,512]{2,1,0:T(8,128)(2,1)S(1)}, bf16[32,16,512]{2,1,0:T(8,128)(2,1)}, bf16[32,16,512]{2,1,0:T(8,128)(2,1)S(1)}, bf16[32,16,512]{2,1,0:T(8,128)(2,1)}) custom-call(s32[2]{0:T(128)S(1)} %pad_add_fusion.me_ref._, bf16[256,256]{1,0:T(8,128)(2,1)S(1)} %fusion.turn_ref, bf16[32,256,256]{2,1,0:T(8,128)(2,1)} %refs_4_.9, ...), custom_call_target="tpu_custom_call" | custom-call | flops 1 | bytes 1 | tf_op jit(solution)/shard_map/pallas_call | solution.py:100
  68.7 3.3 collective-permute-start.5
  72.0 37.9 %collective-permute-done.5.refs_7_ = bf16[32,16,512]{2,1,0:T(8,128)(2,1)S(1)} collective-permute-done((bf16[32,16,512]{2,1,0:T(8,128)(2,1)}, bf16[32,16,512]{2,1,0:T(8,128)(2,1)S(1)}, u32[]{:S(2)}, u32[]{:S(2)}) %collective-permute-start.5) | collective-permute-done | bytes 524320 | tf_op jit(solution)/shard_map/ppermute | solution.py:96
  109.8 6.5 %collective-permute-done.4.refs_6_ = bf16[32,16,512]{2,1,0:T(8,128)(2,1)S(1)} collective-permute-done((bf16[32,16,512]{2,1,0:T(8,128)(2,1)S(1)}, bf16[32,16,512]{2,1,0:T(8,128)(2,1)S(1)}, u32[]{:S(2)}, u32[]{:S(2)}) %collective-permute-start.4) | collective-permute-done | bytes 524320 | tf_op jit(solution)/shard_map/ppermute | solution.py:96
  118.2 4.2 shard_map.106
  122.4 2.7 collective-permute-start.6
  126.2 7.7 %shard_map.107 = (bf16[32,16,512]{2,1,0:T(8,128)(2,1)S(1)}, bf16[32,16,512]{2,1,0:T(8,128)(2,1)S(1)}, bf16[32,16,512]{2,1,0:T(8,128)(2,1)S(1)}, bf16[32,16,512]{2,1,0:T(8,128)(2,1)}) custom-call(s32[2]{0:T(128)S(1)} %pad_add_fusion.me_ref._, bf16[256,256]{1,0:T(8,128)(2,1)S(1)} %fusion.turn_ref, bf16[32,256,256]{2,1,0:T(8,128)(2,1)} %refs_4_.9, ...), custom_call_target="tpu_custom_call" | custom-call | flops 1 | bytes 1 | tf_op jit(solution)/shard_map/pallas_call | solution.py:100
  136.3 7.7 %shard_map.108 = (bf16[32,16,512]{2,1,0:T(8,128)(2,1)S(1)}, bf16[32,16,512]{2,1,0:T(8,128)(2,1)S(1)}, bf16[32,16,512]{2,1,0:T(8,128)(2,1)S(1)}, bf16[32,16,512]{2,1,0:T(8,128)(2,1)}) custom-call(s32[2]{0:T(128)S(1)} %pad_add_fusion.me_ref._, bf16[256,256]{1,0:T(8,128)(2,1)S(1)} %fusion.turn_ref, bf16[32,256,256]{2,1,0:T(8,128)(2,1)} %refs_4_.9, ...), custom_call_target="tpu_custom_call" | custom-call | flops 1 | bytes 1 | tf_op jit(solution)/shard_map/pallas_call | solution.py:100
  146.4 6.5 %copy.19 = bf16[32,256,256]{1,2,0:T(8,128)(2,1)} copy(bf16[32,256,256]{2,1,0:T(8,128)(2,1)} %param.13) | data formatting | bytes 8388608 | tf_op jit(solution)/shard_map/optimization_barrier | solution.py:91
  152.9 6.2 %collective-permute-done.6.came_ref = bf16[512,768]{1,0:T(8,128)(2,1)S(1)} collective-permute-done((bf16[512,768]{1,0:T(8,128)(2,1)S(1)}, bf16[512,768]{1,0:T(8,128)(2,1)S(1)}, u32[]{:S(2)}, u32[]{:S(2)}) %collective-permute-start.6) | collective-permute-done | bytes 786464 | tf_op jit(solution)/shard_map/ppermute | solution.py:96
  159.1 3.2 shard_map.109
  163.8 10.9 %collective-permute-done.10.refs_2_ = bf16[512,512]{1,0:T(8,128)(2,1)S(1)} collective-permute-done((bf16[512,512]{1,0:T(8,128)(2,1)S(1)}, bf16[512,512]{1,0:T(8,128)(2,1)S(1)}, u32[]{:S(2)}, u32[]{:S(2)}) %collective-permute-start.10) | collective-permute-done | bytes 524320 | tf_op jit(solution)/shard_map/ppermute | solution.py:96
  174.7 15.8 %collective-permute-done.8.refs_10_ = bf16[32,16,512]{2,1,0:T(8,128)(2,1)S(1)} collective-permute-done((bf16[32,16,512]{2,1,0:T(8,128)(2,1)}, bf16[32,16,512]{2,1,0:T(8,128)(2,1)S(1)}, u32[]{:S(2)}, u32[]{:S(2)}) %collective-permute-start.8) | collective-permute-done | bytes 524320 | tf_op jit(solution)/shard_map/ppermute | solution.py:96
  191.8 7.1 %shard_map.110.own = bf16[512,256]{1,0:T(8,128)(2,1)S(1)} custom-call(s32[2]{0:T(128)S(1)} %pad_add_fusion.me_ref._, bf16[512,256]{1,0:T(8,128)(2,1)S(1)} %get-tuple-element.140.query_ref, bf16[512,512]{1,0:T(8,128)(2,1)S(1)} %get-tuple-element.138.refs_0_, bf16[512,512]{1,0:T(8,128)(2,1)S(1)} %collective-permute-done.9.refs_1_, ...), custom_call_target="tpu_custom_call" | custom-call | flops 1 | bytes 1 | tf_op jit(solution)/shard_map/pallas_call | solution.py:100
  198.9 7.3 %collective-permute-done.12.refs_11_ = bf16[32,16,512]{2,1,0:T(8,128)(2,1)S(1)} collective-permute-done((bf16[32,16,512]{2,1,0:T(8,128)(2,1)}, bf16[32,16,512]{2,1,0:T(8,128)(2,1)S(1)}, u32[]{:S(2)}, u32[]{:S(2)}) %collective-permute-start.12) | collective-permute-done | bytes 524320 | tf_op jit(solution)/shard_map/ppermute | solution.py:96
  206.3 9.0 %collective-permute-start.14 = (bf16[512,256]{1,0:T(8,128)(2,1)S(1)}, bf16[512,256]{1,0:T(8,128)(2,1)S(1)}, u32[]{:S(2)}, u32[]{:S(2)}) collective-permute-start(bf16[512,256]{1,0:T(8,128)(2,1)S(1)} %shard_map.110.own), channel_id=1, source_target_pairs={{0,8},{4,12},{8,0},{12,4},{1,9},{5,13},{9,1},{13,5},{2,10},{6,14},... | collective-permute-start | bytes 786440 | tf_op jit(solution)/shard_map/ppermute | solution.py:96
  215.3 10.9 %collective-permute-done.14.far = bf16[512,256]{1,0:T(8,128)(2,1)S(1)} collective-permute-done((bf16[512,256]{1,0:T(8,128)(2,1)S(1)}, bf16[512,256]{1,0:T(8,128)(2,1)S(1)}, u32[]{:S(2)}, u32[]{:S(2)}) %collective-permute-start.14) | collective-permute-done | bytes 262176 | tf_op jit(solution)/shard_map/ppermute | solution.py:96
  228.0 4.7 collective-permute-done.15.rest
  232.7 2.2 collective-permute-start.16
  237.0 2.2 collective-permute-start.19
  239.3 39.5 %shard_map.111 = (bf16[512,8192]{1,0:T(8,128)(2,1)}, bf16[16,32,512]{2,1,0:T(8,128)(2,1)}, bf16[16,32,512]{2,1,0:T(8,128)(2,1)}, bf16[16,32,512]{2,1,0:T(8,128)(...) custom-call(s32[2]{0:T(128)S(1)} %pad_add_fusion.me_ref._, ...), custom_call_target="tpu_custom_call" | custom-call | flops 1 | bytes 1 | tf_op jit(solution)/shard_map/pallas_call | solution.py:100
  280.3 26.8 %shard_map.112 = (bf16[2,32,64,256]{3,2,1,0:T(8,128)(2,1)}, f32[2,32,64,256]{3,2,1,0:T(8,128)}) custom-call(s32[2]{0:T(128)S(1)} %pad_add_fusion.me_ref._, bf16[32,16,512]{2,1,0:T(8,128)(2,1)S(1)} %get-tuple-element.114.refs_0_, bf16[32,16,512]{2,1,0:T(8,128)(2,1)S(1)} %collective-permute-done.2.refs_1_, ...), custom_call_target="tpu_custom_call" | custom-call | flops 1 | bytes 1 | tf_op jit(solution)/shard_map/pallas_call | solution.py:100
  311.6 12.3 %collective-permute-done.24.refs_3_ = bf16[16,32,512]{2,1,0:T(8,128)(2,1)S(1)} collective-permute-done((bf16[16,32,512]{2,1,0:T(8,128)(2,1)S(1)}, bf16[16,32,512]{2,1,0:T(8,128)(2,1)S(1)}, u32[]{:S(2)}, u32[]{:S(2)}) %collective-permute-start.24) | collective-permute-done | bytes 524320 | tf_op jit(solution)/shard_map/ppermute | solution.py:96
  325.6 41.9 %collective-permute-done.22.refs_2_ = bf16[16,32,512]{2,1,0:T(8,128)(2,1)S(1)} collective-permute-done((bf16[16,32,512]{2,1,0:T(8,128)(2,1)S(1)}, bf16[16,32,512]{2,1,0:T(8,128)(2,1)S(1)}, u32[]{:S(2)}, u32[]{:S(2)}) %collective-permute-start.22) | collective-permute-done | bytes 524320 | tf_op jit(solution)/shard_map/ppermute | solution.py:96
  367.5 3.0 collective-permute-start.21
  371.9 4.9 shard_map.116
  378.7 33.7 %collective-permute-done.23.refs_2_ = bf16[16,32,512]{2,1,0:T(8,128)(2,1)S(1)} collective-permute-done((bf16[16,32,512]{2,1,0:T(8,128)(2,1)S(1)}, bf16[16,32,512]{2,1,0:T(8,128)(2,1)S(1)}, u32[]{:S(2)}, u32[]{:S(2)}) %collective-permute-start.23) | collective-permute-done | bytes 524320 | tf_op jit(solution)/shard_map/ppermute | solution.py:96
  412.5 8.5 %shard_map.113 = (bf16[512,8192]{1,0:T(8,128)(2,1)}, bf16[2,8,64,256]{3,2,1,0:T(8,128)(2,1)S(1)}, f32[2,8,64,256]{3,2,1,0:T(8,128)}) custom-call(s32[2]{0:T(128)S(1)} %pad_add_fusion.me_ref._, bf16[16,32,512]{2,1,0:T(8,128)(2,1)S(1)} %copy-done.6, bf16[16,32,512]{2,1,0:T(8,128)(2,1)S(1)} %collective-permute-done.20.refs_1_, bf16[16,32,512]{2,1,0:T(8,128)(2,1)} %copy-done.31, ...), custom_call_target="tpu_custom_call" | custom-call | flops 1 | bytes 1 | tf_op jit(solution)/shard_map/pallas_call | solution.py:100
  421.2 3.0 collective-permute-start.30
  426.1 3.6 shard_map.117
  429.7 17.8 %collective-permute-done.31.refs_2_ = bf16[16,32,512]{2,1,0:T(8,128)(2,1)S(1)} collective-permute-done((bf16[16,32,512]{2,1,0:T(8,128)(2,1)S(1)}, bf16[16,32,512]{2,1,0:T(8,128)(2,1)S(1)}, u32[]{:S(2)}, u32[]{:S(2)}) %collective-permute-start.31) | collective-permute-done | bytes 524320 | tf_op jit(solution)/shard_map/ppermute | solution.py:96
  447.7 8.4 %shard_map.118 = (bf16[512,8192]{1,0:T(8,128)(2,1)}, bf16[2,8,64,256]{3,2,1,0:T(8,128)(2,1)S(1)}, f32[2,8,64,256]{3,2,1,0:T(8,128)}) custom-call(s32[2]{0:T(128)S(1)} %pad_add_fusion.me_ref._, bf16[16,32,512]{2,1,0:T(8,128)(2,1)S(1)} %copy-done.2, bf16[16,32,512]{2,1,0:T(8,128)(2,1)S(1)} %collective-permute-done.21.refs_1_, ...), custom_call_target="tpu_custom_call", output_to_operand_aliasing={{0}: (8, {})} | custom-call | flops 1 | bytes 1 | tf_op jit(solution)/shard_map/pallas_call | solution.py:100
  457.8 2.8 collective-permute-start.34
  461.2 7.3 %collective-permute-done.27.came_ref = bf16[8,64,256]{2,1,0:T(8,128)(2,1)S(1)} collective-permute-done((bf16[8,64,256]{2,1,0:T(8,128)(2,1)S(1)}, bf16[8,64,256]{2,1,0:T(8,128)(2,1)S(1)}, u32[]{:S(2)}, u32[]{:S(2)}) %collective-permute-start.27) | collective-permute-done | bytes 262176 | tf_op jit(solution)/shard_map/ppermute | solution.py:96
  471.7 20.3 %collective-permute-done.35.refs_2_ = bf16[12,32,512]{2,1,0:T(8,128)(2,1)S(1)} collective-permute-done((bf16[12,32,512]{2,1,0:T(8,128)(2,1)S(1)}, bf16[12,32,512]{2,1,0:T(8,128)(2,1)S(1)}, u32[]{:S(2)}, u32[]{:S(2)}) %collective-permute-start.35) | collective-permute-done | bytes 393248 | tf_op jit(solution)/shard_map/ppermute | solution.py:96
  492.0 8.4 %shard_map.120 = (bf16[512,8192]{1,0:T(8,128)(2,1)}, bf16[2,8,64,256]{3,2,1,0:T(8,128)(2,1)S(1)}, f32[2,8,64,256]{3,2,1,0:T(8,128)}) custom-call(s32[2]{0:T(128)S(1)} %pad_add_fusion.me_ref._, bf16[16,32,512]{2,1,0:T(8,128)(2,1)S(1)} %copy-done.1, bf16[16,32,512]{2,1,0:T(8,128)(2,1)S(1)} %collective-permute-done.30.refs_1_, ...), custom_call_target="tpu_custom_call", output_to_operand_aliasing={{0}: (8, {})} | custom-call | flops 1 | bytes 1 | tf_op jit(solution)/shard_map/pallas_call | solution.py:100
  501.1 8.1 %collective-permute-done.39.came_ref = bf16[8,64,256]{2,1,0:T(8,128)(2,1)S(1)} collective-permute-done((bf16[8,64,256]{2,1,0:T(8,128)(2,1)S(1)}, bf16[8,64,256]{2,1,0:T(8,128)(2,1)S(1)}, u32[]{:S(2)}, u32[]{:S(2)}) %collective-permute-start.39) | collective-permute-done | bytes 262176 | tf_op jit(solution)/shard_map/ppermute | solution.py:96
  512.5 6.5 %shard_map.124 = (bf16[512,8192]{1,0:T(8,128)(2,1)}, bf16[2,6,64,256]{3,2,1,0:T(8,128)(2,1)S(1)}, f32[2,6,64,256]{3,2,1,0:T(8,128)}) custom-call(s32[2]{0:T(128)S(1)} %pad_add_fusion.me_ref._, bf16[12,32,512]{2,1,0:T(8,128)(2,1)S(1)} %copy-done.7, bf16[12,32,512]{2,1,0:T(8,128)(2,1)S(1)} %collective-permute-done.34.refs_1_, ...), custom_call_target="tpu_custom_call", output_to_operand_aliasing={{0}: (8, {})} | custom-call | flops 1 | bytes 1 | tf_op jit(solution)/shard_map/pallas_call | solution.py:100
  519.6 2.2 collective-permute-start.43
  521.8 2.2 collective-permute-start.41
  524.0 3.7 collective-permute-done.38.came_ref
  529.8 2.9 collective-permute-done.42.refs_2_
  532.7 3.1 shard_map.126
  539.2 4.2 collective-permute-done.46.came_ref
  (176 shorter events, 49.4 us)
Async XLA Ops:
  8.7 47.3 %collective-permute-start.1 = (bf16[32,16,512]{2,1,0:T(8,128)(2,1)S(1)}, bf16[32,16,512]{2,1,0:T(8,128)(2,1)S(1)}, u32[]{:S(2)}, u32[]{:S(2)}) collective-permute-start(bf16[32,16,512]{2,1,0:T(8,128)(2,1)S(1)} %get-tuple-element.119), channel_id=1, source_target_pairs={{0,8},{4,12},{8,0},{12,4},{1,9},{5,13},{9,1},{13,5},{2,10},{6,14},... | collective-permute-start | bytes 1572872 | tf_op jit(solution)/shard_map/ppermute | solution.py:96
  12.7 43.3 %collective-permute-start = (bf16[32,16,512]{2,1,0:T(8,128)(2,1)}, bf16[32,16,512]{2,1,0:T(8,128)(2,1)S(1)}, u32[]{:S(2)}, u32[]{:S(2)}) collective-permute-start(bf16[32,16,512]{2,1,0:T(8,128)(2,1)} %get-tuple-element.118), channel_id=1, source_target_pairs={{0,12},{4,8},{8,4},{12,0},{1,13},{5,9},{9,5},{13,1},{2,14},{6,10},... | collective-permute-start | bytes 1572872 | tf_op jit(solution)/shard_map/ppermute | solution.py:96
  14.1 41.9 %collective-permute-start.2 = (bf16[32,16,512]{2,1,0:T(8,128)(2,1)S(1)}, bf16[32,16,512]{2,1,0:T(8,128)(2,1)S(1)}, u32[]{:S(2)}, u32[]{:S(2)}) collective-permute-start(bf16[32,16,512]{2,1,0:T(8,128)(2,1)S(1)} %get-tuple-element.120), channel_id=1, source_target_pairs={{0,4},{4,0},{8,12},{12,8},{1,5},{5,1},{9,13},{13,9},{2,6},{6,2},{1... | collective-permute-start | bytes 1572872 | tf_op jit(solution)/shard_map/ppermute | solution.py:96
  56.8 60.3 %collective-permute-start.3 = (bf16[2,512,768]{2,1,0:T(8,128)(2,1)S(1)}, bf16[2,512,768]{2,1,0:T(8,128)(2,1)S(1)}, u32[]{:S(2)}, u32[]{:S(2)}) collective-permute-start(bf16[2,512,768]{2,1,0:T(8,128)(2,1)S(1)} %get-tuple-element.121), channel_id=1, source_target_pairs={{0,4},{4,0},{8,12},{12,8},{1,5},{5,1},{9,13},{13,9},{2,6},{6,2},{1... | collective-permute-start | bytes 4718600 | tf_op jit(solution)/shard_map/ppermute | solution.py:96
  68.7 41.1 %collective-permute-start.5 = (bf16[32,16,512]{2,1,0:T(8,128)(2,1)}, bf16[32,16,512]{2,1,0:T(8,128)(2,1)S(1)}, u32[]{:S(2)}, u32[]{:S(2)}) collective-permute-start(bf16[32,16,512]{2,1,0:T(8,128)(2,1)} %get-tuple-element.124), channel_id=1, source_target_pairs={{0,12},{4,8},{8,4},{12,0},{1,13},{5,9},{9,5},{13,1},{2,14},{6,10},... | collective-permute-start | bytes 1572872 | tf_op jit(solution)/shard_map/ppermute | solution.py:96
  72.0 44.4 %collective-permute-start.4 = (bf16[32,16,512]{2,1,0:T(8,128)(2,1)S(1)}, bf16[32,16,512]{2,1,0:T(8,128)(2,1)S(1)}, u32[]{:S(2)}, u32[]{:S(2)}) collective-permute-start(bf16[32,16,512]{2,1,0:T(8,128)(2,1)S(1)} %get-tuple-element.123), channel_id=1, source_target_pairs={{0,8},{4,12},{8,0},{12,4},{1,9},{5,13},{9,1},{13,5},{2,10},{6,14},... | collective-permute-start | bytes 1572872 | tf_op jit(solution)/shard_map/ppermute | solution.py:96
  122.4 36.7 %collective-permute-start.6 = (bf16[512,768]{1,0:T(8,128)(2,1)S(1)}, bf16[512,768]{1,0:T(8,128)(2,1)S(1)}, u32[]{:S(2)}, u32[]{:S(2)}) collective-permute-start(bf16[512,768]{1,0:T(8,128)(2,1)S(1)} %get-tuple-element.127), channel_id=1, source_target_pairs={{0,8},{4,12},{8,0},{12,4},{1,9},{5,13},{9,1},{13,5},{2,10},{6,14},... | collective-permute-start | bytes 2359304 | tf_op jit(solution)/shard_map/ppermute | solution.py:96
  125.1 27.8 %collective-permute-start.7 = (bf16[32,16,512]{2,1,0:T(8,128)(2,1)}, bf16[32,16,512]{2,1,0:T(8,128)(2,1)}, u32[]{:S(2)}, u32[]{:S(2)}) collective-permute-start(bf16[32,16,512]{2,1,0:T(8,128)(2,1)} %get-tuple-element.129), channel_id=1, source_target_pairs={{0,4},{4,0},{8,12},{12,8},{1,5},{5,1},{9,13},{13,9},{2,6},{6,2},{1... | collective-permute-start | bytes 1572872 | tf_op jit(solution)/shard_map/ppermute | solution.py:96
  162.3 12.5 %collective-permute-start.10 = (bf16[512,512]{1,0:T(8,128)(2,1)S(1)}, bf16[512,512]{1,0:T(8,128)(2,1)S(1)}, u32[]{:S(2)}, u32[]{:S(2)}) collective-permute-start(bf16[512,512]{1,0:T(8,128)(2,1)S(1)} %get-tuple-element.138.refs_0_), channel_id=1, source_target_pairs={{0,2},{1,3},{2,0},{3,1},{4,6},{5,7},{6,4},{7,5},{8,10},{9,11},{10,... | collective-permute-start | bytes 1572872 | tf_op jit(solution)/shard_map/ppermute | solution.py:96
  163.8 26.7 %collective-permute-start.9 = (bf16[512,512]{1,0:T(8,128)(2,1)S(1)}, bf16[512,512]{1,0:T(8,128)(2,1)S(1)}, u32[]{:S(2)}, u32[]{:S(2)}) collective-permute-start(bf16[512,512]{1,0:T(8,128)(2,1)S(1)} %get-tuple-element.138.refs_0_), channel_id=1, source_target_pairs={{0,1},{1,0},{2,3},{3,2},{4,5},{5,4},{6,7},{7,6},{8,9},{9,8},{10,11... | collective-permute-start | bytes 1572872 | tf_op jit(solution)/shard_map/ppermute | solution.py:96
  163.8 26.7 %collective-permute-start.8 = (bf16[32,16,512]{2,1,0:T(8,128)(2,1)}, bf16[32,16,512]{2,1,0:T(8,128)(2,1)S(1)}, u32[]{:S(2)}, u32[]{:S(2)}) collective-permute-start(bf16[32,16,512]{2,1,0:T(8,128)(2,1)} %copy-done.14), channel_id=1, source_target_pairs={{0,8},{4,12},{8,0},{12,4},{1,9},{5,13},{9,1},{13,5},{2,10},{6,14},... | collective-permute-start | bytes 1572872 | tf_op jit(solution)/shard_map/ppermute | solution.py:96
  174.7 15.8 %collective-permute-start.11 = (bf16[512,512]{1,0:T(8,128)(2,1)S(1)}, bf16[512,512]{1,0:T(8,128)(2,1)S(1)}, u32[]{:S(2)}, u32[]{:S(2)}) collective-permute-start(bf16[512,512]{1,0:T(8,128)(2,1)S(1)} %collective-permute-done.10.refs_2_), channel_id=1, source_target_pairs={{0,1},{1,0},{2,3},{3,2},{4,5},{5,4},{6,7},{7,6},{8,9},{9,8},{10,11... | collective-permute-start | bytes 1572872 | tf_op jit(solution)/shard_map/ppermute | solution.py:96
  190.5 15.7 %collective-permute-start.12 = (bf16[32,16,512]{2,1,0:T(8,128)(2,1)}, bf16[32,16,512]{2,1,0:T(8,128)(2,1)S(1)}, u32[]{:S(2)}, u32[]{:S(2)}) collective-permute-start(bf16[32,16,512]{2,1,0:T(8,128)(2,1)} %get-tuple-element.142), channel_id=1, source_target_pairs={{0,12},{4,8},{8,4},{12,0},{1,13},{5,9},{9,5},{13,1},{2,14},{6,10},... | collective-permute-start | bytes 1572872 | tf_op jit(solution)/shard_map/ppermute | solution.py:96
  206.3 19.9 %collective-permute-start.14 = (bf16[512,256]{1,0:T(8,128)(2,1)S(1)}, bf16[512,256]{1,0:T(8,128)(2,1)S(1)}, u32[]{:S(2)}, u32[]{:S(2)}) collective-permute-start(bf16[512,256]{1,0:T(8,128)(2,1)S(1)} %shard_map.110.own), channel_id=1, source_target_pairs={{0,8},{4,12},{8,0},{12,4},{1,9},{5,13},{9,1},{13,5},{2,10},{6,14},... | collective-permute-start | bytes 786440 | tf_op jit(solution)/shard_map/ppermute | solution.py:96
  215.2 10.9 %collective-permute-start.13 = (bf16[512,256]{1,0:T(8,128)(2,1)S(1)}, bf16[512,256]{1,0:T(8,128)(2,1)S(1)}, u32[]{:S(2)}, u32[]{:S(2)}) collective-permute-start(bf16[512,256]{1,0:T(8,128)(2,1)S(1)} %shard_map.110.own), channel_id=1, source_target_pairs={{0,4},{4,0},{8,12},{12,8},{1,5},{5,1},{9,13},{13,9},{2,6},{6,2},{1... | collective-permute-start | bytes 786440 | tf_op jit(solution)/shard_map/ppermute | solution.py:96
  226.2 6.5 %collective-permute-start.15 = (bf16[512,256]{1,0:T(8,128)(2,1)S(1)}, bf16[512,256]{1,0:T(8,128)(2,1)S(1)}, u32[]{:S(2)}, u32[]{:S(2)}) collective-permute-start(bf16[512,256]{1,0:T(8,128)(2,1)S(1)} %collective-permute-done.14.far), channel_id=1, source_target_pairs={{0,4},{4,0},{8,12},{12,8},{1,5},{5,1},{9,13},{13,9},{2,6},{6,2},{1... | collective-permute-start | bytes 786440 | tf_op jit(solution)/shard_map/ppermute | solution.py:96
  232.7 46.1 %collective-permute-start.16 = (bf16[32,16,512]{2,1,0:T(8,128)(2,1)S(1)}, bf16[32,16,512]{2,1,0:T(8,128)(2,1)S(1)}, u32[]{:S(2)}, u32[]{:S(2)}) collective-permute-start(bf16[32,16,512]{2,1,0:T(8,128)(2,1)S(1)} %copy-done.13), channel_id=1, source_target_pairs={{0,4},{4,0},{8,12},{12,8},{1,5},{5,1},{9,13},{13,9},{2,6},{6,2},{1... | collective-permute-start | bytes 1572872 | tf_op jit(solution)/shard_map/ppermute | solution.py:96
  234.9 44.0 %collective-permute-start.17 = (bf16[32,16,512]{2,1,0:T(8,128)(2,1)S(1)}, bf16[32,16,512]{2,1,0:T(8,128)(2,1)S(1)}, u32[]{:S(2)}, u32[]{:S(2)}) collective-permute-start(bf16[32,16,512]{2,1,0:T(8,128)(2,1)S(1)} %copy-done.11), channel_id=1, source_target_pairs={{0,4},{4,0},{8,12},{12,8},{1,5},{5,1},{9,13},{13,9},{2,6},{6,2},{1... | collective-permute-start | bytes 1572872 | tf_op jit(solution)/shard_map/ppermute | solution.py:96
  234.9 43.9 %collective-permute-start.18 = (bf16[32,16,512]{2,1,0:T(8,128)(2,1)S(1)}, bf16[32,16,512]{2,1,0:T(8,128)(2,1)S(1)}, u32[]{:S(2)}, u32[]{:S(2)}) collective-permute-start(bf16[32,16,512]{2,1,0:T(8,128)(2,1)S(1)} %copy-done.9), channel_id=1, source_target_pairs={{0,8},{4,12},{8,0},{12,4},{1,9},{5,13},{9,1},{13,5},{2,10},{6,14},... | collective-permute-start | bytes 1572872 | tf_op jit(solution)/shard_map/ppermute | solution.py:96
  237.0 42.5 %collective-permute-start.19 = (bf16[32,16,512]{2,1,0:T(8,128)(2,1)S(1)}, bf16[32,16,512]{2,1,0:T(8,128)(2,1)S(1)}, u32[]{:S(2)}, u32[]{:S(2)}) collective-permute-start(bf16[32,16,512]{2,1,0:T(8,128)(2,1)S(1)} %copy-done.38), channel_id=1, source_target_pairs={{0,12},{4,8},{8,4},{12,0},{1,13},{5,9},{9,5},{13,1},{2,14},{6,10},... | collective-permute-start | bytes 1572872 | tf_op jit(solution)/shard_map/ppermute | solution.py:96
  307.1 105.3 %copy-start.6 = (bf16[16,32,512]{2,1,0:T(8,128)(2,1)S(1)}, bf16[16,32,512]{2,1,0:T(8,128)(2,1)}, u32[]{:S(2)}) copy-start(bf16[16,32,512]{2,1,0:T(8,128)(2,1)} %get-tuple-element.173.refs_0_) | copy-start | bytes 1572868
  307.1 63.4 %collective-permute-start.28 = (bf16[2,32,64,256]{3,2,1,0:T(8,128)(2,1)}, bf16[2,32,64,256]{3,2,1,0:T(8,128)(2,1)S(1)}, u32[]{:S(2)}, u32[]{:S(2)}) collective-permute-start(bf16[2,32,64,256]{3,2,1,0:T(8,128)(2,1)} %get-tuple-element.159), channel_id=1, source_target_pairs={{0,1},{1,0},{2,3},{3,2},{4,5},{5,4},{6,7},{7,6},{8,9},{9,8},{10,11... | collective-permute-start | bytes 6291464 | tf_op jit(solution)/shard_map/ppermute | solution.py:96
  307.2 16.7 %collective-permute-start.24 = (bf16[16,32,512]{2,1,0:T(8,128)(2,1)S(1)}, bf16[16,32,512]{2,1,0:T(8,128)(2,1)S(1)}, u32[]{:S(2)}, u32[]{:S(2)}) collective-permute-start(bf16[16,32,512]{2,1,0:T(8,128)(2,1)S(1)} %copy-done.44), channel_id=1, source_target_pairs={{0,12},{4,8},{8,4},{12,0},{1,13},{5,9},{9,5},{13,1},{2,14},{6,10},... | collective-permute-start | bytes 1572872 | tf_op jit(solution)/shard_map/ppermute | solution.py:96
  308.9 58.5 %collective-permute-start.22 = (bf16[16,32,512]{2,1,0:T(8,128)(2,1)S(1)}, bf16[16,32,512]{2,1,0:T(8,128)(2,1)S(1)}, u32[]{:S(2)}, u32[]{:S(2)}) collective-permute-start(bf16[16,32,512]{2,1,0:T(8,128)(2,1)S(1)} %copy-done.43), channel_id=1, source_target_pairs={{0,8},{4,12},{8,0},{12,4},{1,9},{5,13},{9,1},{13,5},{2,10},{6,14},... | collective-permute-start | bytes 1572872 | tf_op jit(solution)/shard_map/ppermute | solution.py:96
  309.8 57.7 %collective-permute-start.20 = (bf16[16,32,512]{2,1,0:T(8,128)(2,1)S(1)}, bf16[16,32,512]{2,1,0:T(8,128)(2,1)S(1)}, u32[]{:S(2)}, u32[]{:S(2)}) collective-permute-start(bf16[16,32,512]{2,1,0:T(8,128)(2,1)S(1)} %copy-done.42), channel_id=1, source_target_pairs={{0,4},{4,0},{8,12},{12,8},{1,5},{5,1},{9,13},{13,9},{2,6},{6,2},{1... | collective-permute-start | bytes 1572872 | tf_op jit(solution)/shard_map/ppermute | solution.py:96
  323.9 53.3 %collective-permute-start.25 = (bf16[16,32,512]{2,1,0:T(8,128)(2,1)S(1)}, bf16[16,32,512]{2,1,0:T(8,128)(2,1)S(1)}, u32[]{:S(2)}, u32[]{:S(2)}) collective-permute-start(bf16[16,32,512]{2,1,0:T(8,128)(2,1)S(1)} %copy-done.41), channel_id=1, source_target_pairs={{0,12},{4,8},{8,4},{12,0},{1,13},{5,9},{9,5},{13,1},{2,14},{6,10},... | collective-permute-start | bytes 1572872 | tf_op jit(solution)/shard_map/ppermute | solution.py:96
  367.5 44.9 %collective-permute-start.23 = (bf16[16,32,512]{2,1,0:T(8,128)(2,1)S(1)}, bf16[16,32,512]{2,1,0:T(8,128)(2,1)S(1)}, u32[]{:S(2)}, u32[]{:S(2)}) collective-permute-start(bf16[16,32,512]{2,1,0:T(8,128)(2,1)S(1)} %copy-done.40), channel_id=1, source_target_pairs={{0,8},{4,12},{8,0},{12,4},{1,9},{5,13},{9,1},{13,5},{2,10},{6,14},... | collective-permute-start | bytes 1572872 | tf_op jit(solution)/shard_map/ppermute | solution.py:96
  367.5 44.9 %collective-permute-start.21 = (bf16[16,32,512]{2,1,0:T(8,128)(2,1)S(1)}, bf16[16,32,512]{2,1,0:T(8,128)(2,1)S(1)}, u32[]{:S(2)}, u32[]{:S(2)}) collective-permute-start(bf16[16,32,512]{2,1,0:T(8,128)(2,1)S(1)} %copy-done.39), channel_id=1, source_target_pairs={{0,4},{4,0},{8,12},{12,8},{1,5},{5,1},{9,13},{13,9},{2,6},{6,2},{1... | collective-permute-start | bytes 1572872 | tf_op jit(solution)/shard_map/ppermute | solution.py:96
  376.7 49.4 %collective-permute-start.29 = (bf16[32,64,256]{2,1,0:T(8,128)(2,1)S(1)}, bf16[32,64,256]{2,1,0:T(8,128)(2,1)S(1)}, u32[]{:S(2)}, u32[]{:S(2)}) collective-permute-start(bf16[32,64,256]{2,1,0:T(8,128)(2,1)S(1)} %get-tuple-element.180), channel_id=1, source_target_pairs={{0,2},{1,3},{2,0},{3,1},{4,6},{5,7},{6,4},{7,5},{8,10},{9,11},{10,... | collective-permute-start | bytes 3145736 | tf_op jit(solution)/shard_map/ppermute | solution.py:96
  377.3 52.4 %collective-permute-start.32 = (bf16[16,32,512]{2,1,0:T(8,128)(2,1)S(1)}, bf16[16,32,512]{2,1,0:T(8,128)(2,1)S(1)}, u32[]{:S(2)}, u32[]{:S(2)}) collective-permute-start(bf16[16,32,512]{2,1,0:T(8,128)(2,1)S(1)} %copy-done.37), channel_id=1, source_target_pairs={{0,12},{4,8},{8,4},{12,0},{1,13},{5,9},{9,5},{13,1},{2,14},{6,10},... | collective-permute-start | bytes 1572872 | tf_op jit(solution)/shard_map/ppermute | solution.py:96
  421.0 3.2 collective-permute-start.26
  421.1 26.4 %collective-permute-start.31 = (bf16[16,32,512]{2,1,0:T(8,128)(2,1)S(1)}, bf16[16,32,512]{2,1,0:T(8,128)(2,1)S(1)}, u32[]{:S(2)}, u32[]{:S(2)}) collective-permute-start(bf16[16,32,512]{2,1,0:T(8,128)(2,1)S(1)} %copy-done.36), channel_id=1, source_target_pairs={{0,8},{4,12},{8,0},{12,4},{1,9},{5,13},{9,1},{13,5},{2,10},{6,14},... | collective-permute-start | bytes 1572872 | tf_op jit(solution)/shard_map/ppermute | solution.py:96
  421.2 26.5 %collective-permute-start.30 = (bf16[16,32,512]{2,1,0:T(8,128)(2,1)S(1)}, bf16[16,32,512]{2,1,0:T(8,128)(2,1)S(1)}, u32[]{:S(2)}, u32[]{:S(2)}) collective-permute-start(bf16[16,32,512]{2,1,0:T(8,128)(2,1)S(1)} %copy-done.35), channel_id=1, source_target_pairs={{0,4},{4,0},{8,12},{12,8},{1,5},{5,1},{9,13},{13,9},{2,6},{6,2},{1... | collective-permute-start | bytes 1572872 | tf_op jit(solution)/shard_map/ppermute | solution.py:96
  456.1 13.7 %collective-permute-start.33 = (bf16[2,8,64,256]{3,2,1,0:T(8,128)(2,1)S(1)}, bf16[2,8,64,256]{3,2,1,0:T(8,128)(2,1)S(1)}, u32[]{:S(2)}, u32[]{:S(2)}) collective-permute-start(bf16[2,8,64,256]{3,2,1,0:T(8,128)(2,1)S(1)} %get-tuple-element.190), channel_id=1, source_target_pairs={{0,1},{1,0},{2,3},{3,2},{4,5},{5,4},{6,7},{7,6},{8,9},{9,8},{10,11... | collective-permute-start | bytes 1572872 | tf_op jit(solution)/shard_map/ppermute | solution.py:96
  456.2 15.5 %collective-permute-start.36 = (bf16[12,32,512]{2,1,0:T(8,128)(2,1)S(1)}, bf16[12,32,512]{2,1,0:T(8,128)(2,1)S(1)}, u32[]{:S(2)}, u32[]{:S(2)}) collective-permute-start(bf16[12,32,512]{2,1,0:T(8,128)(2,1)S(1)} %copy-done.47), channel_id=1, source_target_pairs={{0,12},{4,8},{8,4},{12,0},{1,13},{5,9},{9,5},{13,1},{2,14},{6,10},... | collective-permute-start | bytes 1179656 | tf_op jit(solution)/shard_map/ppermute | solution.py:96
  457.8 34.2 %collective-permute-start.35 = (bf16[12,32,512]{2,1,0:T(8,128)(2,1)S(1)}, bf16[12,32,512]{2,1,0:T(8,128)(2,1)S(1)}, u32[]{:S(2)}, u32[]{:S(2)}) collective-permute-start(bf16[12,32,512]{2,1,0:T(8,128)(2,1)S(1)} %copy-done.46), channel_id=1, source_target_pairs={{0,8},{4,12},{8,0},{12,4},{1,9},{5,13},{9,1},{13,5},{2,10},{6,14},... | collective-permute-start | bytes 1179656 | tf_op jit(solution)/shard_map/ppermute | solution.py:96
  457.8 34.2 %collective-permute-start.34 = (bf16[12,32,512]{2,1,0:T(8,128)(2,1)S(1)}, bf16[12,32,512]{2,1,0:T(8,128)(2,1)S(1)}, u32[]{:S(2)}, u32[]{:S(2)}) collective-permute-start(bf16[12,32,512]{2,1,0:T(8,128)(2,1)S(1)} %copy-done.45), channel_id=1, source_target_pairs={{0,4},{4,0},{8,12},{12,8},{1,5},{5,1},{9,13},{13,9},{2,6},{6,2},{1... | collective-permute-start | bytes 1179656 | tf_op jit(solution)/shard_map/ppermute | solution.py:96
  460.7 7.8 %collective-permute-start.27 = (bf16[8,64,256]{2,1,0:T(8,128)(2,1)S(1)}, bf16[8,64,256]{2,1,0:T(8,128)(2,1)S(1)}, u32[]{:S(2)}, u32[]{:S(2)}) collective-permute-start(bf16[8,64,256]{2,1,0:T(8,128)(2,1)S(1)} %get-tuple-element.177), channel_id=1, source_target_pairs={{0,2},{1,3},{2,0},{3,1},{4,6},{5,7},{6,4},{7,5},{8,10},{9,11},{10,... | collective-permute-start | bytes 786440 | tf_op jit(solution)/shard_map/ppermute | solution.py:96
  500.4 10.2 %collective-permute-start.37 = (bf16[2,8,64,256]{3,2,1,0:T(8,128)(2,1)S(1)}, bf16[2,8,64,256]{3,2,1,0:T(8,128)(2,1)S(1)}, u32[]{:S(2)}, u32[]{:S(2)}) collective-permute-start(bf16[2,8,64,256]{3,2,1,0:T(8,128)(2,1)S(1)} %get-tuple-element.202), channel_id=1, source_target_pairs={{0,1},{1,0},{2,3},{3,2},{4,5},{5,4},{6,7},{7,6},{8,9},{9,8},{10,11... | collective-permute-start | bytes 1572872 | tf_op jit(solution)/shard_map/ppermute | solution.py:96
  500.5 8.7 %collective-permute-start.39 = (bf16[8,64,256]{2,1,0:T(8,128)(2,1)S(1)}, bf16[8,64,256]{2,1,0:T(8,128)(2,1)S(1)}, u32[]{:S(2)}, u32[]{:S(2)}) collective-permute-start(bf16[8,64,256]{2,1,0:T(8,128)(2,1)S(1)} %get-tuple-element.191), channel_id=1, source_target_pairs={{0,2},{1,3},{2,0},{3,1},{4,6},{5,7},{6,4},{7,5},{8,10},{9,11},{10,... | collective-permute-start | bytes 786440 | tf_op jit(solution)/shard_map/ppermute | solution.py:96
  519.0 10.1 %collective-permute-start.40 = (bf16[2,6,64,256]{3,2,1,0:T(8,128)(2,1)S(1)}, bf16[2,6,64,256]{3,2,1,0:T(8,128)(2,1)S(1)}, u32[]{:S(2)}, u32[]{:S(2)}) collective-permute-start(bf16[2,6,64,256]{3,2,1,0:T(8,128)(2,1)S(1)} %get-tuple-element.209), channel_id=1, source_target_pairs={{0,1},{1,0},{2,3},{3,2},{4,5},{5,4},{6,7},{7,6},{8,9},{9,8},{10,11... | collective-permute-start | bytes 1179656 | tf_op jit(solution)/shard_map/ppermute | solution.py:96
  519.1 8.7 %collective-permute-start.38 = (bf16[8,64,256]{2,1,0:T(8,128)(2,1)S(1)}, bf16[8,64,256]{2,1,0:T(8,128)(2,1)S(1)}, u32[]{:S(2)}, u32[]{:S(2)}) collective-permute-start(bf16[8,64,256]{2,1,0:T(8,128)(2,1)S(1)} %get-tuple-element.204), channel_id=1, source_target_pairs={{0,2},{1,3},{2,0},{3,1},{4,6},{5,7},{6,4},{7,5},{8,10},{9,11},{10,... | collective-permute-start | bytes 786440 | tf_op jit(solution)/shard_map/ppermute | solution.py:96
  519.6 10.1 %collective-permute-start.43 = (bf16[4,32,512]{2,1,0:T(8,128)(2,1)S(1)}, bf16[4,32,512]{2,1,0:T(8,128)(2,1)S(1)}, u32[]{:S(2)}, u32[]{:S(2)}) collective-permute-start(bf16[4,32,512]{2,1,0:T(8,128)(2,1)S(1)} %get-tuple-element.217), channel_id=1, source_target_pairs={{0,12},{4,8},{8,4},{12,0},{1,13},{5,9},{9,5},{13,1},{2,14},{6,10},... | collective-permute-start | bytes 393224 | tf_op jit(solution)/shard_map/ppermute | solution.py:96
  521.8 10.8 %collective-permute-start.42 = (bf16[4,32,512]{2,1,0:T(8,128)(2,1)S(1)}, bf16[4,32,512]{2,1,0:T(8,128)(2,1)S(1)}, u32[]{:S(2)}, u32[]{:S(2)}) collective-permute-start(bf16[4,32,512]{2,1,0:T(8,128)(2,1)S(1)} %get-tuple-element.215), channel_id=1, source_target_pairs={{0,8},{4,12},{8,0},{12,4},{1,9},{5,13},{9,1},{13,5},{2,10},{6,14},... | collective-permute-start | bytes 393224 | tf_op jit(solution)/shard_map/ppermute | solution.py:96
  521.8 10.8 %collective-permute-start.41 = (bf16[4,32,512]{2,1,0:T(8,128)(2,1)S(1)}, bf16[4,32,512]{2,1,0:T(8,128)(2,1)S(1)}, u32[]{:S(2)}, u32[]{:S(2)}) collective-permute-start(bf16[4,32,512]{2,1,0:T(8,128)(2,1)S(1)} %get-tuple-element.213), channel_id=1, source_target_pairs={{0,4},{4,0},{8,12},{12,8},{1,5},{5,1},{9,13},{13,9},{2,6},{6,2},{1... | collective-permute-start | bytes 393224 | tf_op jit(solution)/shard_map/ppermute | solution.py:96
  535.7 1.5 collective-permute-start.44
  535.8 7.7 %collective-permute-start.46 = (bf16[6,64,256]{2,1,0:T(8,128)(2,1)S(1)}, bf16[6,64,256]{2,1,0:T(8,128)(2,1)S(1)}, u32[]{:S(2)}, u32[]{:S(2)}) collective-permute-start(bf16[6,64,256]{2,1,0:T(8,128)(2,1)S(1)} %get-tuple-element.210), channel_id=1, source_target_pairs={{0,2},{1,3},{2,0},{3,1},{4,6},{5,7},{6,4},{7,5},{8,10},{9,11},{10,... | collective-permute-start | bytes 589832 | tf_op jit(solution)/shard_map/ppermute | solution.py:96
  537.8 6.9 %collective-permute-start.45 = (bf16[2,64,256]{2,1,0:T(8,128)(2,1)S(1)}, bf16[2,64,256]{2,1,0:T(8,128)(2,1)S(1)}, u32[]{:S(2)}, u32[]{:S(2)}) collective-permute-start(bf16[2,64,256]{2,1,0:T(8,128)(2,1)S(1)} %get-tuple-element.223), channel_id=1, source_target_pairs={{0,2},{1,3},{2,0},{3,1},{4,6},{5,7},{6,4},{7,5},{8,10},{9,11},{10,... | collective-permute-start | bytes 196616 | tf_op jit(solution)/shard_map/ppermute | solution.py:96
  (47 other events, 1302.0 us)

commit v3 on v2

--- a/solution.py
+++ b/solution.py
@@ -236,16 +236,20 @@
 
 def store_quarters(me, held, send_ref, keep_ref):
     quarter = held.shape[0] // 4
-    for out, flips in ((send_ref, (1, 3)), (keep_ref, (0, 2))):
-        for slot, bits in enumerate(flips):
-            start = pl.multiple_of((me ^ bits) * quarter, quarter)
-            out[slot, 0] = held[pl.ds(start, quarter), :].astype(out.dtype)
+    for bits in range(4):
+        start = pl.multiple_of((me ^ bits) * quarter, quarter)
+        part = held[pl.ds(start, quarter), :]
+        if bits % 2:
+            send_ref[bits // 2][0] = part.astype(BF16)
+        else:
+            keep_ref[bits // 2, 0] = part
 
 
 def quarter_outs(count, size):
-    shape = (2, count, size // 4, size)
-    place = spec((2, 1, size // 4, size), lambda j, _: (0, j, 0, 0))
-    return [array(shape, BF16), array(shape, F32)], [place, place]
+    shape = (count, size // 4, size)
+    one = spec((1, *shape[1:]), lambda j, _: (j, 0, 0))
+    two = spec((2, 1, *shape[1:]), lambda j, _: (0, j, 0, 0))
+    return [array(shape, BF16)] * 2 + [array((2, *shape), F32)], [one, one, two]
 
 
 def add_kernel(_, keep_ref, came_ref, mine_ref, other_ref):
@@ -273,6 +277,23 @@
         part * part, same, precision=lax.Precision.HIGHEST, preferred_element_type=F32
     )
     return (part * lax.rsqrt(sums * (1.0 / HEAD_DIM) + 1e-06)).astype(BF16)
+
+
+def pair_kernel(_, keep_ref, came_ref, next_ref, mine_ref, other_ref):
+    mine_ref[...] = keep_ref[0] + came_ref[...].astype(F32)
+    other_ref[...] = (keep_ref[1] + next_ref[...].astype(F32)).astype(BF16)
+
+
+def pair_call(me, keep, came):
+    shape = keep.shape[1:]
+    return call(
+        pair_kernel,
+        me,
+        (keep, *came),
+        [whole(keep.shape), whole(shape), whole(shape)],
+        [array(shape, F32), array(shape, BF16)],
+        [whole(shape)] * 2,
+    )
 
 
 def finish_kernel(_, mine_ref, came_ref, *refs):
@@ -378,18 +399,17 @@
 
     @pl.when(block % TILE == TILE - 1)
     def _():
-        deeps = [out.shape[0] for out in outs[: len(outs) // 4]]
+        deeps = [out.shape[1] for out in outs]
         deep = sum(deeps)
-        for bits in range(4):
-            there = me_ref[0] ^ bits
+        for there in range(4):
             for low in range(0, deep, TILE):
-                start = pl.multiple_of(there * deep + low, TILE)
-                tile = turn(turn_ref[...], held[:, pl.ds(start, TILE), :])
+                start = there * deep + low
+                tile = turn(turn_ref[...], held[:, start : start + TILE, :])
                 for chunk, count in enumerate(deeps):
                     begin = sum(deeps[:chunk])
                     least, most = max(begin, low), min(begin + count, low + TILE)
                     if least < most:
-                        outs[bits * len(deeps) + chunk][least - begin : most - begin] = tile[
+                        outs[chunk][there, least - begin : most - begin] = tile[
                             least - low : most - low
                         ]
 
@@ -399,8 +419,7 @@
     rows, genes = masked.shape
     width = w_out.shape[0]
     wide = spec((rows, size), lambda b, _: (0, b))
-    chunks = len(deeps)
-    got = call(
+    hidden, *first = call(
         first_kernel,
         me,
         (matrix, *attended, w_out, masked, w_first_t),
@@ -411,20 +430,19 @@
             wide,
             spec((1, size, size), lambda b, _: (b, 0, 0)),
         ],
-        [array((rows, genes), BF16)] + [array((deep, blocks, rows), BF16) for deep in deeps] * 4,
-        [wide] + [spec((deep, TILE, rows), lambda b, _: (0, b // TILE, 0)) for deep in deeps] * 4,
+        [array((rows, genes), BF16)] + [array((4, deep, blocks, rows), BF16) for deep in deeps],
+        [wide] + [spec((4, deep, TILE, rows), lambda b, _: (0, 0, b // TILE, 0)) for deep in deeps],
         grid=(blocks,),
         scratch=[pltpu.VMEM((rows, width), BF16), pltpu.VMEM((TILE, size, rows), BF16)],
     )
-    return got[0], [[got[1 + s * chunks + t] for s in range(4)] for t in range(chunks)]
+    return hidden, first
 
 
 def second_kernel(me_ref, *refs):
-    pieces = refs[:4]
-    w_ref, cot_ref, hidden_ref = refs[4:7]
-    out_ref, send_ref, keep_ref, held, square = refs[-5:]
-    for bits, piece in enumerate(pieces):
-        held[:, me_ref[0] ^ bits] = piece[...]
+    piece, w_ref, cot_ref, hidden_ref = refs[:4]
+    out_ref, *send_ref, keep_ref, held, square = refs[-6:]
+    for source in range(4):
+        held[:, source] = piece[source]
     size = w_ref.shape[1]
     permuted = held[...].reshape(size, held.shape[3])
     square[...] = jnp.dot(permuted, cot_ref[...], preferred_element_type=F32)
@@ -435,15 +453,15 @@
     out_ref[...] = (hidden_ref[...].astype(F32) + mixed).astype(BF16)
 
 
-def second_call(me, pieces, w_second, cotangent, hidden, denoised, start):
+def second_call(me, piece, w_second, cotangent, hidden, denoised, start):
     blocks, size, _ = w_second.shape
-    deep, _, rows = pieces[0].shape
+    _, deep, _, rows = piece.shape
     pair = size // (4 * blocks)
     count = deep // pair
     wide = spec((rows, size), lambda j, _: (0, start + j))
     square = spec((1, size, size), lambda j, _: (start + j, 0, 0))
-    args = [*pieces, w_second, cotangent, hidden]
-    in_specs = [spec((pair, blocks, rows), lambda j, _: (j, 0, 0))] * 4 + [square, wide, wide]
+    args = [piece, w_second, cotangent, hidden]
+    in_specs = [spec((4, pair, blocks, rows), lambda j, _: (0, j, 0, 0)), square, wide, wide]
     quarters = quarter_outs(count, size)
     aliases = {}
     if denoised is not None:
@@ -464,7 +482,7 @@
 
 
 def grad_first_kernel(me_ref, *refs):
-    pieces, (hidden_ref, send_ref, keep_ref, held, square) = refs[:-5], refs[-5:]
+    pieces, (hidden_ref, *send_ref, keep_ref, held, square) = refs[:-6], refs[-6:]
     for half in range(len(pieces) // 4):
         for bits in range(4):
             held[me_ref[0] ^ bits, half] = pieces[half * 4 + bits][0]
@@ -473,16 +491,16 @@
     store_quarters(me_ref[1], square, send_ref, keep_ref)
 
 
-def grad_first_call(me, pieces, hidden, size):
-    blocks, deep, rows = pieces[0].shape
+def grad_first_call(me, pieces, hidden, size, start, count):
+    _, deep, rows = pieces[0].shape
     return call(
         grad_first_kernel,
         me,
         (*pieces, hidden),
-        [spec((1, deep, rows), lambda b, _: (b, 0, 0))] * len(pieces)
-        + [spec((rows, size), lambda b, _: (0, b))],
-        *quarter_outs(blocks, size),
-        grid=(blocks,),
+        [spec((1, deep, rows), lambda b, _: (start + b, 0, 0))] * len(pieces)
+        + [spec((rows, size), lambda b, _: (0, start + b))],
+        *quarter_outs(count, size),
+        grid=(count,),
         scratch=[
             pltpu.VMEM((4, len(pieces) // 4, deep, rows), BF16),
             pltpu.VMEM((size, size), F32),
@@ -541,31 +559,52 @@
         begin(part, bits, rest)
 
     got = []
+
+    def launch(t, *earlier):
+        piece = after(first[t], *earlier)
+        got.append(lax.all_to_all(piece, "gene", split_axis=0, concat_axis=0, tiled=True))
+
+    launch(0, back[2][1], *back[3][1:])
+    denoised, shares, made, added = None, [None, None], [], []
+    some = blocks // 2
+    back = sum(back, [])
+
+    def make_first(part, *earlier):
+        *send, keep = grad_first_call(
+            me, after(back, *earlier), hidden, size, part * some, some
+        )
+        made.append((0, part * some, [flip(piece, "cell", 1) for piece in send], keep))
+
+    def settle(*earlier):
+        pins = []
+        for which, start, mine, last in added:
+            shares[which] = finish_call(
+                me, mine, after(last, *earlier), shares[which], start, blocks
+            )
+        pins += [shares[which] for which in {entry[0]: 0 for entry in added}]
+        added.clear()
+        for which, start, came, keep in made:
+            mine, other = pair_call(me, keep, after(came, *earlier))
+            added.append((which, start, mine, flip(other, "cell", 2)))
+            pins.append(mine)
+        made.clear()
+        return pins
+
+    make_first(0)
+    make_first(1)
+    pins = []
     for t in range(len(deeps)):
-        earlier = got[-1] if t else [back[2][1], *back[3][1:]]
-        got.append(first[t][:1])
-        for bits in (1, 2, 3):
-            ready = (earlier[bits],) if t else earlier
-            got[t].append(flip(after(first[t][bits], *ready), "gene", bits))
-
-    send, keep = grad_first_call(me, sum(back, []), hidden, size)
-    mine, other = add_call(me, keep, flip(send, "cell", 1))
-    first_share = finish_call(me, mine, flip(other, "cell", 2), None, 0, blocks)
-
-    denoised, share, pins = None, None, (send,)
-    for t in range(len(deeps)):
-        if t < len(deeps) - 2:
-            pins += tuple(got[t + 1])
-        pieces = [after(got[t][0], *pins), *got[t][1:]]
+        if t + 1 < len(deeps):
+            launch(t + 1, got[t], *pins)
+        pins = settle(got[t])
         start = sum(deeps[:t]) * blocks // deep
-        denoised, send, keep = second_call(
-            me, pieces, w_second, cotangent, hidden, denoised, start
+        denoised, *send, keep = second_call(
+            me, got[t], w_second, cotangent, hidden, denoised, start
         )
-        pins = (first_share,) if share is None else (share,)
-        mine, other = add_call(me, keep, flip(send, "cell", 1))
-        pins += (other,)
-        share = finish_call(me, mine, flip(other, "cell", 2), share, start, blocks)
-    return (denoised, first_share, share)
+        made.append((1, start, [flip(piece, "cell", 1) for piece in send], keep))
+    settle()
+    settle()
+    return (denoised, *shares)
 
 
 def solution(mesh):

time: 549 us -> 518 us (0.944)
  waiting for transfers between devices: 254 us -> 173 us
  blocking collectives: 0 us -> 49.5 us
    ppermute x47 -> x41, waiting for transfers between devices: 254 us -> 119 us  [flip(): return lax.ppermute(value, axis, pairs)]
    all_to_all x0 -> x4, waiting for transfers between devices: none -> 53.9 us  [launch(): lax.all_to_all(piece, 'gene', split_axis=0, concat_axis=0, tiled=True)]
    all_to_all x0 -> x1, blocking collectives: none -> 49.5 us  [launch(): lax.all_to_all(piece, 'gene', split_axis=0, concat_axis=0, tiled=True)]
    ppermute x47 -> x41, starting transfers between devices: 64 us -> 45.8 us  [flip(): return lax.ppermute(value, axis, pairs)]
    all_to_all x0 -> x4, starting transfers between devices: none -> 16.8 us  [launch(): lax.all_to_all(piece, 'gene', split_axis=0, concat_axis=0, tiled=True)]
    pallas_call x27 -> x30, Pallas kernels: 210 us -> 213 us  [call(): pl.pallas_call(body, out_shape=outs, grid_spec=pltpu.PrefetchScalarGridSp...]
  transfers between devices with their start and end apart: 47 -> 45, of which waited for: 21 -> 20; matrix products, arithmetic and copies ran while one was open for 1% -> 1% of each run, Pallas kernels for 25% -> 38%
where the time goes in v3:
time: 518 us; the launch traced here: 514 us
  Pallas kernels  213 us (41%)
  waiting for transfers between devices  173 us (33%)
  starting transfers between devices  62.6 us (12%)
  blocking collectives  49.5 us (10%)
  local copies, waits for them, and re-layouts  15.4 us (3%)
    pallas_call x30, Pallas kernels, call(): pl.pallas_call(body, out_shape=outs, grid_spec=pltpu.PrefetchScalarGridSp...  213 us
    ppermute x41, waiting for transfers between devices, flip(): return lax.ppermute(value, axis, pairs)  119 us
    all_to_all x4, waiting for transfers between devices, launch(): lax.all_to_all(piece, 'gene', split_axis=0, concat_axis=0, tiled=True)  53.9 us
    all_to_all x1, blocking collectives, launch(): lax.all_to_all(piece, 'gene', split_axis=0, concat_axis=0, tiled=True)  49.5 us
    ppermute x41, starting transfers between devices, flip(): return lax.ppermute(value, axis, pairs)  45.8 us
    all_to_all x4, starting transfers between devices, launch(): lax.all_to_all(piece, 'gene', split_axis=0, concat_axis=0, tiled=True)  16.8 us
  transfers between devices with their start and end apart: 45, of which 20 were waited for; matrix products, arithmetic and copies ran while one was open for 1% of the time, Pallas kernels for 38%

profile of v3, /device:TPU:0, one launch (start us, length us, event | category | flops | bytes accessed | tf_op | source)
XLA Modules:
  0.0 514.5 jit_solution(12412715416749166432)
XLA Ops:
  1.0 7.7 %shard_map.103 = (bf16[32,16,512]{2,1,0:T(8,128)(2,1)S(1)}, bf16[32,16,512]{2,1,0:T(8,128)(2,1)S(1)}, bf16[32,16,512]{2,1,0:T(8,128)(2,1)S(1)}, bf16[32,16,512]{2,1,0:T(8,128)(2,1)}) custom-call(s32[2]{0:T(128)S(1)} %pad_add_fusion.me_ref._, bf16[256,256]{1,0:T(8,128)(2,1)S(1)} %fusion.turn_ref, bf16[32,256,256]{2,1,0:T(8,128)(2,1)} %refs_1_.11, ...), custom_call_target="tpu_custom_call" | custom-call | flops 1 | bytes 1 | tf_op jit(solution)/shard_map/pallas_call | solution.py:100
  8.7 4.0 collective-permute-start.1
  14.4 41.6 %shard_map.104 = (bf16[512,8192]{1,0:T(8,128)(2,1)}, bf16[2,512,768]{2,1,0:T(8,128)(2,1)S(1)}, f32[2,512,768]{2,1,0:T(8,128)}) custom-call(s32[2]{0:T(128)S(1)} %pad_add_fusion.me_ref._, bf16[512,8192]{1,0:T(8,128)(2,1)} %value_ref, s32[512,8192]{1,0:T(8,128)} %mask_ref.1, bf16[1,8192]{1,0:T(2,128)(2,1)S(1)} %reshape.9.fill_ref, bf16[8192,3072]{1,0:T(8,128)(2,1)} %refs_2_.6, ...), custom_call_target="tpu_custom_call" | custom-call | flops 1 | bytes 1 | tf_op jit(solution)/shard_map/pallas_call | solution.py:100
  56.8 2.5 collective-permute-start.3
  59.3 7.8 %shard_map.105 = (bf16[32,16,512]{2,1,0:T(8,128)(2,1)S(1)}, bf16[32,16,512]{2,1,0:T(8,128)(2,1)}, bf16[32,16,512]{2,1,0:T(8,128)(2,1)S(1)}, bf16[32,16,512]{2,1,0:T(8,128)(2,1)}) custom-call(s32[2]{0:T(128)S(1)} %pad_add_fusion.me_ref._, bf16[256,256]{1,0:T(8,128)(2,1)S(1)} %fusion.turn_ref, bf16[32,256,256]{2,1,0:T(8,128)(2,1)} %refs_1_.11, ...), custom_call_target="tpu_custom_call" | custom-call | flops 1 | bytes 1 | tf_op jit(solution)/shard_map/pallas_call | solution.py:100
  68.0 3.3 collective-permute-start.5
  71.2 37.9 %collective-permute-done.5.refs_7_ = bf16[32,16,512]{2,1,0:T(8,128)(2,1)S(1)} collective-permute-done((bf16[32,16,512]{2,1,0:T(8,128)(2,1)}, bf16[32,16,512]{2,1,0:T(8,128)(2,1)S(1)}, u32[]{:S(2)}, u32[]{:S(2)}) %collective-permute-start.5) | collective-permute-done | bytes 524320 | tf_op jit(solution)/shard_map/ppermute | solution.py:96
  109.1 6.5 %collective-permute-done.4.refs_6_ = bf16[32,16,512]{2,1,0:T(8,128)(2,1)S(1)} collective-permute-done((bf16[32,16,512]{2,1,0:T(8,128)(2,1)S(1)}, bf16[32,16,512]{2,1,0:T(8,128)(2,1)S(1)}, u32[]{:S(2)}, u32[]{:S(2)}) %collective-permute-start.4) | collective-permute-done | bytes 524320 | tf_op jit(solution)/shard_map/ppermute | solution.py:96
  117.5 4.2 shard_map.106
  121.7 2.7 collective-permute-start.6
  125.5 7.7 %shard_map.107 = (bf16[32,16,512]{2,1,0:T(8,128)(2,1)S(1)}, bf16[32,16,512]{2,1,0:T(8,128)(2,1)S(1)}, bf16[32,16,512]{2,1,0:T(8,128)(2,1)S(1)}, bf16[32,16,512]{2,1,0:T(8,128)(2,1)}) custom-call(s32[2]{0:T(128)S(1)} %pad_add_fusion.me_ref._, bf16[256,256]{1,0:T(8,128)(2,1)S(1)} %fusion.turn_ref, bf16[32,256,256]{2,1,0:T(8,128)(2,1)} %refs_1_.11, ...), custom_call_target="tpu_custom_call" | custom-call | flops 1 | bytes 1 | tf_op jit(solution)/shard_map/pallas_call | solution.py:100
  135.6 7.7 %shard_map.108 = (bf16[32,16,512]{2,1,0:T(8,128)(2,1)S(1)}, bf16[32,16,512]{2,1,0:T(8,128)(2,1)S(1)}, bf16[32,16,512]{2,1,0:T(8,128)(2,1)S(1)}, bf16[32,16,512]{2,1,0:T(8,128)(2,1)}) custom-call(s32[2]{0:T(128)S(1)} %pad_add_fusion.me_ref._, bf16[256,256]{1,0:T(8,128)(2,1)S(1)} %fusion.turn_ref, bf16[32,256,256]{2,1,0:T(8,128)(2,1)} %refs_1_.11, ...), custom_call_target="tpu_custom_call" | custom-call | flops 1 | bytes 1 | tf_op jit(solution)/shard_map/pallas_call | solution.py:100
  144.1 6.5 %copy.20 = bf16[32,256,256]{1,2,0:T(8,128)(2,1)} copy(bf16[32,256,256]{2,1,0:T(8,128)(2,1)} %param.13) | data formatting | bytes 8388608 | tf_op jit(solution)/shard_map/optimization_barrier | solution.py:91
  151.9 6.5 %collective-permute-done.6.came_ref = bf16[512,768]{1,0:T(8,128)(2,1)S(1)} collective-permute-done((bf16[512,768]{1,0:T(8,128)(2,1)S(1)}, bf16[512,768]{1,0:T(8,128)(2,1)S(1)}, u32[]{:S(2)}, u32[]{:S(2)}) %collective-permute-start.6) | collective-permute-done | bytes 786464 | tf_op jit(solution)/shard_map/ppermute | solution.py:96
  158.4 3.2 shard_map.109
  163.1 10.9 %collective-permute-done.10.refs_2_ = bf16[512,512]{1,0:T(8,128)(2,1)S(1)} collective-permute-done((bf16[512,512]{1,0:T(8,128)(2,1)S(1)}, bf16[512,512]{1,0:T(8,128)(2,1)S(1)}, u32[]{:S(2)}, u32[]{:S(2)}) %collective-permute-start.10) | collective-permute-done | bytes 524320 | tf_op jit(solution)/shard_map/ppermute | solution.py:96
  174.0 15.6 %collective-permute-done.8.refs_10_ = bf16[32,16,512]{2,1,0:T(8,128)(2,1)S(1)} collective-permute-done((bf16[32,16,512]{2,1,0:T(8,128)(2,1)S(1)}, bf16[32,16,512]{2,1,0:T(8,128)(2,1)S(1)}, u32[]{:S(2)}, u32[]{:S(2)}) %collective-permute-start.8) | collective-permute-done | bytes 524320 | tf_op jit(solution)/shard_map/ppermute | solution.py:96
  190.9 7.1 %shard_map.110.own = bf16[512,256]{1,0:T(8,128)(2,1)S(1)} custom-call(s32[2]{0:T(128)S(1)} %pad_add_fusion.me_ref._, bf16[512,256]{1,0:T(8,128)(2,1)S(1)} %get-tuple-element.156.query_ref, bf16[512,512]{1,0:T(8,128)(2,1)S(1)} %get-tuple-element.154.refs_0_, bf16[512,512]{1,0:T(8,128)(2,1)S(1)} %collective-permute-done.9.refs_1_, ...), custom_call_target="tpu_custom_call" | custom-call | flops 1 | bytes 1 | tf_op jit(solution)/shard_map/pallas_call | solution.py:100
  198.0 7.1 %collective-permute-done.12.refs_11_ = bf16[32,16,512]{2,1,0:T(8,128)(2,1)S(1)} collective-permute-done((bf16[32,16,512]{2,1,0:T(8,128)(2,1)S(1)}, bf16[32,16,512]{2,1,0:T(8,128)(2,1)S(1)}, u32[]{:S(2)}, u32[]{:S(2)}) %collective-permute-start.12) | collective-permute-done | bytes 524320 | tf_op jit(solution)/shard_map/ppermute | solution.py:96
  205.2 8.9 %collective-permute-start.14 = (bf16[512,256]{1,0:T(8,128)(2,1)S(1)}, bf16[512,256]{1,0:T(8,128)(2,1)S(1)}, u32[]{:S(2)}, u32[]{:S(2)}) collective-permute-start(bf16[512,256]{1,0:T(8,128)(2,1)S(1)} %shard_map.110.own), channel_id=1, source_target_pairs={{0,8},{4,12},{8,0},{12,4},{1,9},{5,13},{9,1},{13,5},{2,10},{6,14},... | collective-permute-start | bytes 786440 | tf_op jit(solution)/shard_map/ppermute | solution.py:96
  214.0 10.9 %collective-permute-done.14.far = bf16[512,256]{1,0:T(8,128)(2,1)S(1)} collective-permute-done((bf16[512,256]{1,0:T(8,128)(2,1)S(1)}, bf16[512,256]{1,0:T(8,128)(2,1)S(1)}, u32[]{:S(2)}, u32[]{:S(2)}) %collective-permute-start.14) | collective-permute-done | bytes 262176 | tf_op jit(solution)/shard_map/ppermute | solution.py:96
  226.7 4.8 collective-permute-done.15.rest
  231.5 2.1 collective-permute-start.16
  233.7 2.1 collective-permute-start.18
  235.7 2.3 collective-permute-start.19
  238.0 39.2 %shard_map.111 = (bf16[512,8192]{1,0:T(8,128)(2,1)}, bf16[4,16,32,512]{3,2,1,0:T(8,128)(2,1)}, bf16[4,16,32,512]{3,2,1,0:T(8,128)(2,1)}, bf16[4,16,32,512]{3,2,1...) custom-call(s32[2]{0:T(128)S(1)} %pad_add_fusion.me_ref._, ...), custom_call_target="tpu_custom_call" | custom-call | flops 1 | bytes 1 | tf_op jit(solution)/shard_map/pallas_call | solution.py:100
  278.2 49.5 %all_to_all.25.refs_0_ = bf16[4,16,32,512]{3,2,1,0:T(8,128)(2,1)} all-to-all(bf16[4,16,32,512]{3,2,1,0:T(8,128)(2,1)} %get-tuple-element.175), channel_id=1, replica_groups=mesh['grp'=2,'gene'=4,'cell'=4] {'gene'}, dimensions={0} | all-to-all | bytes 4194304 | tf_op jit(solution)/shard_map/all_to_all | solution.py:565
  327.7 4.4 all-to-all-start.1
  332.2 14.0 %shard_map.114 = (bf16[16,64,256]{2,1,0:T(8,128)(2,1)S(1)}, bf16[16,64,256]{2,1,0:T(8,128)(2,1)S(1)}, f32[2,16,64,256]{3,2,1,0:T(8,128)}) custom-call(s32[2]{0:T(128)S(1)} %pad_add_fusion.me_ref._, bf16[32,16,512]{2,1,0:T(8,128)(2,1)S(1)} %get-tuple-element.178.refs_0_, bf16[32,16,512]{2,1,0:T(8,128)(2,1)} %copy-done.14, bf16[32,16,512]{2,1,0:T(8,128)(2,1)} %copy-done.12, ...), custom_call_target="tpu_custom_call" | custom-call | flops 1 | bytes 1 | tf_op jit(solution)/shard_map/pallas_call | solution.py:100
  346.8 14.0 %shard_map.112 = (bf16[16,64,256]{2,1,0:T(8,128)(2,1)S(1)}, bf16[16,64,256]{2,1,0:T(8,128)(2,1)S(1)}, f32[2,16,64,256]{3,2,1,0:T(8,128)}) custom-call(s32[2]{0:T(128)S(1)} %pad_add_fusion.me_ref._, bf16[32,16,512]{2,1,0:T(8,128)(2,1)S(1)} %get-tuple-element.178.refs_0_, bf16[32,16,512]{2,1,0:T(8,128)(2,1)} %copy-done.14, bf16[32,16,512]{2,1,0:T(8,128)(2,1)} %copy-done.12, ...), custom_call_target="tpu_custom_call" | custom-call | flops 1 | bytes 1 | tf_op jit(solution)/shard_map/pallas_call | solution.py:100
  361.3 3.2 shard_map.115
  364.6 3.2 shard_map.113
  367.8 11.0 %all-to-all-done.1.refs_0_ = bf16[4,16,32,512]{3,2,1,0:T(8,128)(2,1)} async-done(((bf16[4,16,32,512]{3,2,1,0:T(8,128)(2,1)}), bf16[4,16,32,512]{3,2,1,0:T(8,128)(2,1)}, u32[]{:S(2)}, u32[]{:S(2)}) %all-to-all-start.1) | async-done | bytes 2097184 | tf_op jit(solution)/shard_map/all_to_all | solution.py:565
  378.8 4.5 all-to-all-start.2
  385.4 8.3 %shard_map.118 = (bf16[512,8192]{1,0:T(8,128)(2,1)}, bf16[8,64,256]{2,1,0:T(8,128)(2,1)S(1)}, bf16[8,64,256]{2,1,0:T(8,128)(2,1)S(1)}, f32[2,8,64,256]{3,2,1,0:T(8,128)S(1)}) custom-call(s32[2]{0:T(128)S(1)} %pad_add_fusion.me_ref._, bf16[4,16,32,512]{3,2,1,0:T(8,128)(2,1)} %all_to_all.25.refs_0_, bf16[32,256,256]{2,1,0:T(8,128)(2,1)} %refs_1_.11, ...), custom_call_target="tpu_custom_call" | custom-call | flops 1 | bytes 1 | tf_op jit(solution)/shard_map/pallas_call | solution.py:100
  395.3 3.0 collective-permute-done.25.came_ref
  399.8 7.7 %collective-permute-done.24.came_ref = bf16[16,64,256]{2,1,0:T(8,128)(2,1)S(1)} collective-permute-done((bf16[16,64,256]{2,1,0:T(8,128)(2,1)S(1)}, bf16[16,64,256]{2,1,0:T(8,128)(2,1)S(1)}, u32[]{:S(2)}, u32[]{:S(2)}) %collective-permute-start.24) | collective-permute-done | bytes 524320 | tf_op jit(solution)/shard_map/ppermute | solution.py:96
  409.1 1.9 shard_map.119
  411.0 20.1 %all-to-all-done.2.refs_0_ = bf16[4,16,32,512]{3,2,1,0:T(8,128)(2,1)} async-done(((bf16[4,16,32,512]{3,2,1,0:T(8,128)(2,1)}), bf16[4,16,32,512]{3,2,1,0:T(8,128)(2,1)}, u32[]{:S(2)}, u32[]{:S(2)}) %all-to-all-start.2) | async-done | bytes 2097184 | tf_op jit(solution)/shard_map/all_to_all | solution.py:565
  431.1 4.4 all-to-all-start.3
  436.0 8.3 %shard_map.121 = (bf16[512,8192]{1,0:T(8,128)(2,1)}, bf16[8,64,256]{2,1,0:T(8,128)(2,1)S(1)}, bf16[8,64,256]{2,1,0:T(8,128)(2,1)S(1)}, f32[2,8,64,256]{3,2,1,0:T(8,128)S(1)}) custom-call(s32[2]{0:T(128)S(1)} %pad_add_fusion.me_ref._, bf16[4,16,32,512]{3,2,1,0:T(8,128)(2,1)} %all-to-all-done.1.refs_0_, ...), custom_call_target="tpu_custom_call", output_to_operand_aliasing={{0}: (5, {})} | custom-call | flops 1 | bytes 1 | tf_op jit(solution)/shard_map/pallas_call | solution.py:100
  449.1 22.8 %all-to-all-done.3.refs_0_ = bf16[4,12,32,512]{3,2,1,0:T(8,128)(2,1)} async-done(((bf16[4,12,32,512]{3,2,1,0:T(8,128)(2,1)}), bf16[4,12,32,512]{3,2,1,0:T(8,128)(2,1)}, u32[]{:S(2)}, u32[]{:S(2)}) %all-to-all-start.3) | async-done | bytes 1572896 | tf_op jit(solution)/shard_map/all_to_all | solution.py:565
  471.9 3.5 all-to-all-start.4
  475.4 8.4 %shard_map.123 = (bf16[512,8192]{1,0:T(8,128)(2,1)}, bf16[8,64,256]{2,1,0:T(8,128)(2,1)S(1)}, bf16[8,64,256]{2,1,0:T(8,128)(2,1)S(1)}, f32[2,8,64,256]{3,2,1,0:T(8,128)S(1)}) custom-call(s32[2]{0:T(128)S(1)} %pad_add_fusion.me_ref._, bf16[4,16,32,512]{3,2,1,0:T(8,128)(2,1)} %all-to-all-done.2.refs_0_, ...), custom_call_target="tpu_custom_call", output_to_operand_aliasing={{0}: (5, {})} | custom-call | flops 1 | bytes 1 | tf_op jit(solution)/shard_map/pallas_call | solution.py:100
  485.3 6.7 %shard_map.124 = (bf16[512,8192]{1,0:T(8,128)(2,1)}, bf16[6,64,256]{2,1,0:T(8,128)(2,1)S(1)}, bf16[6,64,256]{2,1,0:T(8,128)(2,1)S(1)}, f32[2,6,64,256]{3,2,1,0:T(8,128)S(1)}) custom-call(s32[2]{0:T(128)S(1)} %pad_add_fusion.me_ref._, bf16[4,12,32,512]{3,2,1,0:T(8,128)(2,1)} %all-to-all-done.3.refs_0_, ...), custom_call_target="tpu_custom_call", output_to_operand_aliasing={{0}: (5, {})} | custom-call | flops 1 | bytes 1 | tf_op jit(solution)/shard_map/pallas_call | solution.py:100
  493.0 2.6 shard_map.128
  498.3 3.1 shard_map.125
  508.6 3.3 collective-permute-done.33.came_ref
  (138 shorter events, 45.1 us)
Async XLA Ops:
  8.7 47.3 %collective-permute-start.1 = (bf16[32,16,512]{2,1,0:T(8,128)(2,1)S(1)}, bf16[32,16,512]{2,1,0:T(8,128)(2,1)S(1)}, u32[]{:S(2)}, u32[]{:S(2)}) collective-permute-start(bf16[32,16,512]{2,1,0:T(8,128)(2,1)S(1)} %get-tuple-element.135), channel_id=1, source_target_pairs={{0,8},{4,12},{8,0},{12,4},{1,9},{5,13},{9,1},{13,5},{2,10},{6,14},... | collective-permute-start | bytes 1572872 | tf_op jit(solution)/shard_map/ppermute | solution.py:96
  12.7 43.3 %collective-permute-start = (bf16[32,16,512]{2,1,0:T(8,128)(2,1)}, bf16[32,16,512]{2,1,0:T(8,128)(2,1)S(1)}, u32[]{:S(2)}, u32[]{:S(2)}) collective-permute-start(bf16[32,16,512]{2,1,0:T(8,128)(2,1)} %get-tuple-element.134), channel_id=1, source_target_pairs={{0,12},{4,8},{8,4},{12,0},{1,13},{5,9},{9,5},{13,1},{2,14},{6,10},... | collective-permute-start | bytes 1572872 | tf_op jit(solution)/shard_map/ppermute | solution.py:96
  14.1 41.9 %collective-permute-start.2 = (bf16[32,16,512]{2,1,0:T(8,128)(2,1)S(1)}, bf16[32,16,512]{2,1,0:T(8,128)(2,1)S(1)}, u32[]{:S(2)}, u32[]{:S(2)}) collective-permute-start(bf16[32,16,512]{2,1,0:T(8,128)(2,1)S(1)} %get-tuple-element.136), channel_id=1, source_target_pairs={{0,4},{4,0},{8,12},{12,8},{1,5},{5,1},{9,13},{13,9},{2,6},{6,2},{1... | collective-permute-start | bytes 1572872 | tf_op jit(solution)/shard_map/ppermute | solution.py:96
  56.8 59.6 %collective-permute-start.3 = (bf16[2,512,768]{2,1,0:T(8,128)(2,1)S(1)}, bf16[2,512,768]{2,1,0:T(8,128)(2,1)S(1)}, u32[]{:S(2)}, u32[]{:S(2)}) collective-permute-start(bf16[2,512,768]{2,1,0:T(8,128)(2,1)S(1)} %get-tuple-element.137), channel_id=1, source_target_pairs={{0,4},{4,0},{8,12},{12,8},{1,5},{5,1},{9,13},{13,9},{2,6},{6,2},{1... | collective-permute-start | bytes 4718600 | tf_op jit(solution)/shard_map/ppermute | solution.py:96
  68.0 41.1 %collective-permute-start.5 = (bf16[32,16,512]{2,1,0:T(8,128)(2,1)}, bf16[32,16,512]{2,1,0:T(8,128)(2,1)S(1)}, u32[]{:S(2)}, u32[]{:S(2)}) collective-permute-start(bf16[32,16,512]{2,1,0:T(8,128)(2,1)} %get-tuple-element.140), channel_id=1, source_target_pairs={{0,12},{4,8},{8,4},{12,0},{1,13},{5,9},{9,5},{13,1},{2,14},{6,10},... | collective-permute-start | bytes 1572872 | tf_op jit(solution)/shard_map/ppermute | solution.py:96
  71.2 44.4 %collective-permute-start.4 = (bf16[32,16,512]{2,1,0:T(8,128)(2,1)S(1)}, bf16[32,16,512]{2,1,0:T(8,128)(2,1)S(1)}, u32[]{:S(2)}, u32[]{:S(2)}) collective-permute-start(bf16[32,16,512]{2,1,0:T(8,128)(2,1)S(1)} %get-tuple-element.139), channel_id=1, source_target_pairs={{0,8},{4,12},{8,0},{12,4},{1,9},{5,13},{9,1},{13,5},{2,10},{6,14},... | collective-permute-start | bytes 1572872 | tf_op jit(solution)/shard_map/ppermute | solution.py:96
  121.7 36.7 %collective-permute-start.6 = (bf16[512,768]{1,0:T(8,128)(2,1)S(1)}, bf16[512,768]{1,0:T(8,128)(2,1)S(1)}, u32[]{:S(2)}, u32[]{:S(2)}) collective-permute-start(bf16[512,768]{1,0:T(8,128)(2,1)S(1)} %get-tuple-element.143), channel_id=1, source_target_pairs={{0,8},{4,12},{8,0},{12,4},{1,9},{5,13},{9,1},{13,5},{2,10},{6,14},... | collective-permute-start | bytes 2359304 | tf_op jit(solution)/shard_map/ppermute | solution.py:96
  124.3 27.5 %collective-permute-start.7 = (bf16[32,16,512]{2,1,0:T(8,128)(2,1)}, bf16[32,16,512]{2,1,0:T(8,128)(2,1)}, u32[]{:S(2)}, u32[]{:S(2)}) collective-permute-start(bf16[32,16,512]{2,1,0:T(8,128)(2,1)} %get-tuple-element.145), channel_id=1, source_target_pairs={{0,4},{4,0},{8,12},{12,8},{1,5},{5,1},{9,13},{13,9},{2,6},{6,2},{1... | collective-permute-start | bytes 1572872 | tf_op jit(solution)/shard_map/ppermute | solution.py:96
  158.4 73.1 %copy-start.9 = (bf16[32,16,512]{2,1,0:T(8,128)(2,1)S(1)}, bf16[32,16,512]{2,1,0:T(8,128)(2,1)}, u32[]{:S(2)}) copy-start(bf16[32,16,512]{2,1,0:T(8,128)(2,1)} %copy-done.8) | copy-start | bytes 1572868
  158.4 77.4 %copy-start.27 = (bf16[32,16,512]{2,1,0:T(8,128)(2,1)S(1)}, bf16[32,16,512]{2,1,0:T(8,128)(2,1)}, u32[]{:S(2)}) copy-start(bf16[32,16,512]{2,1,0:T(8,128)(2,1)} %get-tuple-element.174) | copy-start | bytes 1572868
  161.6 12.5 %collective-permute-start.10 = (bf16[512,512]{1,0:T(8,128)(2,1)S(1)}, bf16[512,512]{1,0:T(8,128)(2,1)S(1)}, u32[]{:S(2)}, u32[]{:S(2)}) collective-permute-start(bf16[512,512]{1,0:T(8,128)(2,1)S(1)} %get-tuple-element.154.refs_0_), channel_id=1, source_target_pairs={{0,2},{1,3},{2,0},{3,1},{4,6},{5,7},{6,4},{7,5},{8,10},{9,11},{10,... | collective-permute-start | bytes 1572872 | tf_op jit(solution)/shard_map/ppermute | solution.py:96
  163.1 26.5 %collective-permute-start.9 = (bf16[512,512]{1,0:T(8,128)(2,1)S(1)}, bf16[512,512]{1,0:T(8,128)(2,1)S(1)}, u32[]{:S(2)}, u32[]{:S(2)}) collective-permute-start(bf16[512,512]{1,0:T(8,128)(2,1)S(1)} %get-tuple-element.154.refs_0_), channel_id=1, source_target_pairs={{0,1},{1,0},{2,3},{3,2},{4,5},{5,4},{6,7},{7,6},{8,9},{9,8},{10,11... | collective-permute-start | bytes 1572872 | tf_op jit(solution)/shard_map/ppermute | solution.py:96
  163.1 26.5 %collective-permute-start.8 = (bf16[32,16,512]{2,1,0:T(8,128)(2,1)S(1)}, bf16[32,16,512]{2,1,0:T(8,128)(2,1)S(1)}, u32[]{:S(2)}, u32[]{:S(2)}) collective-permute-start(bf16[32,16,512]{2,1,0:T(8,128)(2,1)S(1)} %copy-done.11), channel_id=1, source_target_pairs={{0,8},{4,12},{8,0},{12,4},{1,9},{5,13},{9,1},{13,5},{2,10},{6,14},... | collective-permute-start | bytes 1572872 | tf_op jit(solution)/shard_map/ppermute | solution.py:96
  174.0 15.6 %collective-permute-start.11 = (bf16[512,512]{1,0:T(8,128)(2,1)S(1)}, bf16[512,512]{1,0:T(8,128)(2,1)S(1)}, u32[]{:S(2)}, u32[]{:S(2)}) collective-permute-start(bf16[512,512]{1,0:T(8,128)(2,1)S(1)} %collective-permute-done.10.refs_2_), channel_id=1, source_target_pairs={{0,1},{1,0},{2,3},{3,2},{4,5},{5,4},{6,7},{7,6},{8,9},{9,8},{10,11... | collective-permute-start | bytes 1572872 | tf_op jit(solution)/shard_map/ppermute | solution.py:96
  189.6 87.6 %copy-start.17 = (bf16[32,16,512]{2,1,0:T(8,128)(2,1)}, bf16[32,16,512]{2,1,0:T(8,128)(2,1)S(1)}, u32[]{:S(2)}) copy-start(bf16[32,16,512]{2,1,0:T(8,128)(2,1)S(1)} %collective-permute-done.8.refs_10_) | copy-start | bytes 1572868
  189.6 15.5 %collective-permute-start.12 = (bf16[32,16,512]{2,1,0:T(8,128)(2,1)S(1)}, bf16[32,16,512]{2,1,0:T(8,128)(2,1)S(1)}, u32[]{:S(2)}, u32[]{:S(2)}) collective-permute-start(bf16[32,16,512]{2,1,0:T(8,128)(2,1)S(1)} %copy-done.28), channel_id=1, source_target_pairs={{0,12},{4,8},{8,4},{12,0},{1,13},{5,9},{9,5},{13,1},{2,14},{6,10},... | collective-permute-start | bytes 1572872 | tf_op jit(solution)/shard_map/ppermute | solution.py:96
  205.2 19.8 %collective-permute-start.14 = (bf16[512,256]{1,0:T(8,128)(2,1)S(1)}, bf16[512,256]{1,0:T(8,128)(2,1)S(1)}, u32[]{:S(2)}, u32[]{:S(2)}) collective-permute-start(bf16[512,256]{1,0:T(8,128)(2,1)S(1)} %shard_map.110.own), channel_id=1, source_target_pairs={{0,8},{4,12},{8,0},{12,4},{1,9},{5,13},{9,1},{13,5},{2,10},{6,14},... | collective-permute-start | bytes 786440 | tf_op jit(solution)/shard_map/ppermute | solution.py:96
  214.0 10.9 %collective-permute-start.13 = (bf16[512,256]{1,0:T(8,128)(2,1)S(1)}, bf16[512,256]{1,0:T(8,128)(2,1)S(1)}, u32[]{:S(2)}, u32[]{:S(2)}) collective-permute-start(bf16[512,256]{1,0:T(8,128)(2,1)S(1)} %shard_map.110.own), channel_id=1, source_target_pairs={{0,4},{4,0},{8,12},{12,8},{1,5},{5,1},{9,13},{13,9},{2,6},{6,2},{1... | collective-permute-start | bytes 786440 | tf_op jit(solution)/shard_map/ppermute | solution.py:96
  225.0 6.6 %collective-permute-start.15 = (bf16[512,256]{1,0:T(8,128)(2,1)S(1)}, bf16[512,256]{1,0:T(8,128)(2,1)S(1)}, u32[]{:S(2)}, u32[]{:S(2)}) collective-permute-start(bf16[512,256]{1,0:T(8,128)(2,1)S(1)} %collective-permute-done.14.far), channel_id=1, source_target_pairs={{0,4},{4,0},{8,12},{12,8},{1,5},{5,1},{9,13},{13,9},{2,6},{6,2},{1... | collective-permute-start | bytes 786440 | tf_op jit(solution)/shard_map/ppermute | solution.py:96
  231.5 45.7 %collective-permute-start.16 = (bf16[32,16,512]{2,1,0:T(8,128)(2,1)S(1)}, bf16[32,16,512]{2,1,0:T(8,128)(2,1)S(1)}, u32[]{:S(2)}, u32[]{:S(2)}) collective-permute-start(bf16[32,16,512]{2,1,0:T(8,128)(2,1)S(1)} %copy-done.9), channel_id=1, source_target_pairs={{0,4},{4,0},{8,12},{12,8},{1,5},{5,1},{9,13},{13,9},{2,6},{6,2},{1... | collective-permute-start | bytes 1572872 | tf_op jit(solution)/shard_map/ppermute | solution.py:96
  233.6 43.6 %collective-permute-start.17 = (bf16[32,16,512]{2,1,0:T(8,128)(2,1)S(1)}, bf16[32,16,512]{2,1,0:T(8,128)(2,1)S(1)}, u32[]{:S(2)}, u32[]{:S(2)}) collective-permute-start(bf16[32,16,512]{2,1,0:T(8,128)(2,1)S(1)} %get-tuple-element.170), channel_id=1, source_target_pairs={{0,4},{4,0},{8,12},{12,8},{1,5},{5,1},{9,13},{13,9},{2,6},{6,2},{1... | collective-permute-start | bytes 1572872 | tf_op jit(solution)/shard_map/ppermute | solution.py:96
  233.7 43.6 %collective-permute-start.18 = (bf16[32,16,512]{2,1,0:T(8,128)(2,1)S(1)}, bf16[32,16,512]{2,1,0:T(8,128)(2,1)S(1)}, u32[]{:S(2)}, u32[]{:S(2)}) collective-permute-start(bf16[32,16,512]{2,1,0:T(8,128)(2,1)S(1)} %get-tuple-element.172), channel_id=1, source_target_pairs={{0,8},{4,12},{8,0},{12,4},{1,9},{5,13},{9,1},{13,5},{2,10},{6,14},... | collective-permute-start | bytes 1572872 | tf_op jit(solution)/shard_map/ppermute | solution.py:96
  235.7 42.4 %collective-permute-start.19 = (bf16[32,16,512]{2,1,0:T(8,128)(2,1)S(1)}, bf16[32,16,512]{2,1,0:T(8,128)(2,1)S(1)}, u32[]{:S(2)}, u32[]{:S(2)}) collective-permute-start(bf16[32,16,512]{2,1,0:T(8,128)(2,1)S(1)} %copy-done.27), channel_id=1, source_target_pairs={{0,12},{4,8},{8,4},{12,0},{1,13},{5,9},{9,5},{13,1},{2,14},{6,10},... | collective-permute-start | bytes 1572872 | tf_op jit(solution)/shard_map/ppermute | solution.py:96
  327.7 51.1 %all-to-all-start.1 = ((bf16[4,16,32,512]{3,2,1,0:T(8,128)(2,1)}), bf16[4,16,32,512]{3,2,1,0:T(8,128)(2,1)}, u32[]{:S(2)}, u32[]{:S(2)}) async-start(bf16[4,16,32,512]{3,2,1,0:T(8,128)(2,1)} %get-tuple-element.176), calls=%async_computation.1 | async-start | bytes 4194304 | tf_op jit(solution)/shard_map/all_to_all | solution.py:565
  346.2 15.1 %collective-permute-start.22 = (bf16[16,64,256]{2,1,0:T(8,128)(2,1)S(1)}, bf16[16,64,256]{2,1,0:T(8,128)(2,1)S(1)}, u32[]{:S(2)}, u32[]{:S(2)}) collective-permute-start(bf16[16,64,256]{2,1,0:T(8,128)(2,1)S(1)} %get-tuple-element.202), channel_id=1, source_target_pairs={{0,1},{1,0},{2,3},{3,2},{4,5},{5,4},{6,7},{7,6},{8,9},{9,8},{10,11... | collective-permute-start | bytes 1572872 | tf_op jit(solution)/shard_map/ppermute | solution.py:96
  346.3 15.1 %collective-permute-start.23 = (bf16[16,64,256]{2,1,0:T(8,128)(2,1)S(1)}, bf16[16,64,256]{2,1,0:T(8,128)(2,1)S(1)}, u32[]{:S(2)}, u32[]{:S(2)}) collective-permute-start(bf16[16,64,256]{2,1,0:T(8,128)(2,1)S(1)} %get-tuple-element.203), channel_id=1, source_target_pairs={{0,1},{1,0},{2,3},{3,2},{4,5},{5,4},{6,7},{7,6},{8,9},{9,8},{10,11... | collective-permute-start | bytes 1572872 | tf_op jit(solution)/shard_map/ppermute | solution.py:96
  360.8 3.8 collective-permute-start.20
  360.9 3.7 collective-permute-start.21
  378.8 52.2 %all-to-all-start.2 = ((bf16[4,16,32,512]{3,2,1,0:T(8,128)(2,1)}), bf16[4,16,32,512]{3,2,1,0:T(8,128)(2,1)}, u32[]{:S(2)}, u32[]{:S(2)}) async-start(bf16[4,16,32,512]{3,2,1,0:T(8,128)(2,1)} %get-tuple-element.207), calls=%async_computation.2 | async-start | bytes 4194304 | tf_op jit(solution)/shard_map/all_to_all | solution.py:565
  383.3 14.9 %collective-permute-start.25 = (bf16[16,64,256]{2,1,0:T(8,128)(2,1)S(1)}, bf16[16,64,256]{2,1,0:T(8,128)(2,1)S(1)}, u32[]{:S(2)}, u32[]{:S(2)}) collective-permute-start(bf16[16,64,256]{2,1,0:T(8,128)(2,1)S(1)} %get-tuple-element.210), channel_id=1, source_target_pairs={{0,2},{1,3},{2,0},{3,1},{4,6},{5,7},{6,4},{7,5},{8,10},{9,11},{10,... | collective-permute-start | bytes 1572872 | tf_op jit(solution)/shard_map/ppermute | solution.py:96
  383.9 23.6 %collective-permute-start.24 = (bf16[16,64,256]{2,1,0:T(8,128)(2,1)S(1)}, bf16[16,64,256]{2,1,0:T(8,128)(2,1)S(1)}, u32[]{:S(2)}, u32[]{:S(2)}) collective-permute-start(bf16[16,64,256]{2,1,0:T(8,128)(2,1)S(1)} %get-tuple-element.208), channel_id=1, source_target_pairs={{0,2},{1,3},{2,0},{3,1},{4,6},{5,7},{6,4},{7,5},{8,10},{9,11},{10,... | collective-permute-start | bytes 1572872 | tf_op jit(solution)/shard_map/ppermute | solution.py:96
  394.7 14.3 %collective-permute-start.26 = (bf16[8,64,256]{2,1,0:T(8,128)(2,1)S(1)}, bf16[8,64,256]{2,1,0:T(8,128)(2,1)S(1)}, u32[]{:S(2)}, u32[]{:S(2)}) collective-permute-start(bf16[8,64,256]{2,1,0:T(8,128)(2,1)S(1)} %get-tuple-element.213), channel_id=1, source_target_pairs={{0,1},{1,0},{2,3},{3,2},{4,5},{5,4},{6,7},{7,6},{8,9},{9,8},{10,11... | collective-permute-start | bytes 786440 | tf_op jit(solution)/shard_map/ppermute | solution.py:96
  394.7 14.3 %collective-permute-start.27 = (bf16[8,64,256]{2,1,0:T(8,128)(2,1)S(1)}, bf16[8,64,256]{2,1,0:T(8,128)(2,1)S(1)}, u32[]{:S(2)}, u32[]{:S(2)}) collective-permute-start(bf16[8,64,256]{2,1,0:T(8,128)(2,1)S(1)} %get-tuple-element.214), channel_id=1, source_target_pairs={{0,1},{1,0},{2,3},{3,2},{4,5},{5,4},{6,7},{7,6},{8,9},{9,8},{10,11... | collective-permute-start | bytes 786440 | tf_op jit(solution)/shard_map/ppermute | solution.py:96
  431.1 40.9 %all-to-all-start.3 = ((bf16[4,12,32,512]{3,2,1,0:T(8,128)(2,1)}), bf16[4,12,32,512]{3,2,1,0:T(8,128)(2,1)}, u32[]{:S(2)}, u32[]{:S(2)}) async-start(bf16[4,12,32,512]{3,2,1,0:T(8,128)(2,1)} %get-tuple-element.218), calls=%async_computation.3 | async-start | bytes 3145728 | tf_op jit(solution)/shard_map/all_to_all | solution.py:565
  435.4 10.4 %collective-permute-start.28 = (bf16[8,64,256]{2,1,0:T(8,128)(2,1)S(1)}, bf16[8,64,256]{2,1,0:T(8,128)(2,1)S(1)}, u32[]{:S(2)}, u32[]{:S(2)}) collective-permute-start(bf16[8,64,256]{2,1,0:T(8,128)(2,1)S(1)} %get-tuple-element.219), channel_id=1, source_target_pairs={{0,2},{1,3},{2,0},{3,1},{4,6},{5,7},{6,4},{7,5},{8,10},{9,11},{10,... | collective-permute-start | bytes 786440 | tf_op jit(solution)/shard_map/ppermute | solution.py:96
  445.4 1.9 collective-permute-start.29
  445.4 1.9 collective-permute-start.30
  471.9 25.2 %all-to-all-start.4 = ((bf16[4,4,32,512]{3,2,1,0:T(8,128)(2,1)}), bf16[4,4,32,512]{3,2,1,0:T(8,128)(2,1)S(1)}, u32[]{:S(2)}, u32[]{:S(2)}) async-start(bf16[4,4,32,512]{3,2,1,0:T(8,128)(2,1)} %get-tuple-element.228), calls=%async_computation.4 | async-start | bytes 1048576 | tf_op jit(solution)/shard_map/all_to_all | solution.py:565
  484.8 8.2 %collective-permute-start.37 = (bf16[8,64,256]{2,1,0:T(8,128)(2,1)S(1)}, bf16[8,64,256]{2,1,0:T(8,128)(2,1)S(1)}, u32[]{:S(2)}, u32[]{:S(2)}) collective-permute-start(bf16[8,64,256]{2,1,0:T(8,128)(2,1)S(1)} %get-tuple-element.248), channel_id=1, source_target_pairs={{0,1},{1,0},{2,3},{3,2},{4,5},{5,4},{6,7},{7,6},{8,9},{9,8},{10,11... | collective-permute-start | bytes 786440 | tf_op jit(solution)/shard_map/ppermute | solution.py:96
  484.8 8.2 %collective-permute-start.38 = (bf16[8,64,256]{2,1,0:T(8,128)(2,1)S(1)}, bf16[8,64,256]{2,1,0:T(8,128)(2,1)S(1)}, u32[]{:S(2)}, u32[]{:S(2)}) collective-permute-start(bf16[8,64,256]{2,1,0:T(8,128)(2,1)S(1)} %get-tuple-element.249), channel_id=1, source_target_pairs={{0,1},{1,0},{2,3},{3,2},{4,5},{5,4},{6,7},{7,6},{8,9},{9,8},{10,11... | collective-permute-start | bytes 786440 | tf_op jit(solution)/shard_map/ppermute | solution.py:96
  492.0 5.1 collective-permute-start.34
  492.0 5.1 collective-permute-start.35
  492.5 12.4 %collective-permute-start.40 = (bf16[8,64,256]{2,1,0:T(8,128)(2,1)S(1)}, bf16[8,64,256]{2,1,0:T(8,128)(2,1)S(1)}, u32[]{:S(2)}, u32[]{:S(2)}) collective-permute-start(bf16[8,64,256]{2,1,0:T(8,128)(2,1)S(1)} %get-tuple-element.255), channel_id=1, source_target_pairs={{0,2},{1,3},{2,0},{3,1},{4,6},{5,7},{6,4},{7,5},{8,10},{9,11},{10,... | collective-permute-start | bytes 786440 | tf_op jit(solution)/shard_map/ppermute | solution.py:96
  495.6 11.7 %collective-permute-start.39 = (bf16[8,64,256]{2,1,0:T(8,128)(2,1)}, bf16[8,64,256]{2,1,0:T(8,128)(2,1)S(1)}, u32[]{:S(2)}, u32[]{:S(2)}) collective-permute-start(bf16[8,64,256]{2,1,0:T(8,128)(2,1)} %get-tuple-element.253), channel_id=1, source_target_pairs={{0,2},{1,3},{2,0},{3,1},{4,6},{5,7},{6,4},{7,5},{8,10},{9,11},{10,... | collective-permute-start | bytes 786440 | tf_op jit(solution)/shard_map/ppermute | solution.py:96
  497.7 14.2 %collective-permute-start.36 = (bf16[6,64,256]{2,1,0:T(8,128)(2,1)S(1)}, bf16[6,64,256]{2,1,0:T(8,128)(2,1)S(1)}, u32[]{:S(2)}, u32[]{:S(2)}) collective-permute-start(bf16[6,64,256]{2,1,0:T(8,128)(2,1)S(1)} %get-tuple-element.246), channel_id=1, source_target_pairs={{0,2},{1,3},{2,0},{3,1},{4,6},{5,7},{6,4},{7,5},{8,10},{9,11},{10,... | collective-permute-start | bytes 589832 | tf_op jit(solution)/shard_map/ppermute | solution.py:96
  501.4 1.3 collective-permute-start.31
  501.4 1.4 collective-permute-start.32
  503.3 8.6 %collective-permute-start.33 = (bf16[2,64,256]{2,1,0:T(8,128)(2,1)S(1)}, bf16[2,64,256]{2,1,0:T(8,128)(2,1)S(1)}, u32[]{:S(2)}, u32[]{:S(2)}) collective-permute-start(bf16[2,64,256]{2,1,0:T(8,128)(2,1)S(1)} %get-tuple-element.239), channel_id=1, source_target_pairs={{0,2},{1,3},{2,0},{3,1},{4,6},{5,7},{6,4},{7,5},{8,10},{9,11},{10,... | collective-permute-start | bytes 196616 | tf_op jit(solution)/shard_map/ppermute | solution.py:96
  (26 other events, 432.9 us)

commit v4 on v3

--- a/solution.py
+++ b/solution.py
@@ -121,6 +121,10 @@
     return pl.BlockSpec(shape, lambda *_: (0,) * len(shape))
 
 
+def several(count):
+    return next(group for group in (4, 2, 1) if count % group == 0)
+
+
 def array(shape, dtype):
     return jax.ShapeDtypeStruct(shape, dtype)
 
@@ -140,14 +144,20 @@
 def back_kernel(me_ref, turn_ref, second_ref, cot_ref, *refs):
     outs, held = refs[:4], refs[4]
     blocks, rows = held.shape[2], held.shape[3]
-    pair = held.shape[0] // (TILE // 2)
-    at = pl.program_id(0) % (TILE // pair)
-    back = lax.dot_general(
-        second_ref[0], cot_ref[...], (((1,), (1,)), ((), ())), preferred_element_type=F32
-    ).astype(BF16)
-    held[pl.ds(at * pair, pair)] = back.reshape(pair, 4, blocks, rows)
-
-    @pl.when(at == TILE // pair - 1)
+    group, size, _ = second_ref.shape
+    pair = size // (4 * blocks)
+    steps = TILE // (pair * group)
+    at = pl.program_id(0) % steps
+    for g in range(group):
+        back = lax.dot_general(
+            second_ref[g],
+            cot_ref[:, g * size : (g + 1) * size],
+            (((1,), (1,)), ((), ())),
+            preferred_element_type=F32,
+        ).astype(BF16)
+        held[pl.ds((at * group + g) * pair, pair)] = back.reshape(pair, 4, blocks, rows)
+
+    @pl.when(at == steps - 1)
     def _():
         for bits in range(4):
             there = me_ref[0] ^ bits
@@ -162,8 +172,9 @@
     rows = cotangent.shape[0]
     pair = size // (4 * blocks)
     count = blocks // parts
-    per = TILE // pair
-    first = part * count
+    group = several(math.gcd(count, TILE // pair))
+    steps = TILE // (pair * group)
+    first = part * count // group
     piece = array((blocks, count * pair, rows), BF16)
     return call(
         back_kernel,
@@ -171,84 +182,83 @@
         (matrix, w_second, cotangent),
         [
             whole(matrix.shape),
-            spec((1, size, size), lambda j, _: (first + j, 0, 0)),
-            spec((rows, size), lambda j, _: (0, first + j)),
+            spec((group, size, size), lambda j, _: (first + j, 0, 0)),
+            spec((rows, group * size), lambda j, _: (0, first + j)),
         ],
         [piece] * 4,
-        [spec((blocks, TILE, rows), lambda j, _: (0, j // per, 0))] * 4,
-        grid=(count,),
+        [spec((blocks, TILE, rows), lambda j, _: (0, j // steps, 0))] * 4,
+        grid=(count // group,),
         scratch=[pltpu.VMEM((TILE, 4, blocks, rows), BF16)],
     )
 
 
-def project_kernel(me_ref, value_ref, mask_ref, fill_ref, *refs):
-    weights, (masked_ref, send_ref, keep_ref), sums = refs[:3], refs[3:6], refs[6:]
+def project_kernel(me_ref, value_ref, mask_ref, fill_ref, weight_ref, *refs):
+    masked_ref, send_ref, keep_ref, total = refs
     step = pl.program_id(0)
     masked = jnp.where(
         mask_ref[...] == 1, fill_ref[...].astype(F32), value_ref[...].astype(F32)
     ).astype(BF16)
     masked_ref[...] = masked
+    width = total.shape[1] // 3
 
     @pl.when(step == 0)
     def _():
-        for total in sums:
-            total[...] = jnp.zeros_like(total)
-
-    for weight, total in zip(weights, sums):
-        total[...] += jnp.dot(masked, weight[...], preferred_element_type=F32)
+        total[...] = jnp.dot(masked, weight_ref[...], preferred_element_type=F32)
+
+    @pl.when(step > 0)
+    def _():
+        total[...] += jnp.dot(masked, weight_ref[...], preferred_element_type=F32)
 
     @pl.when(step == pl.num_programs(0) - 1)
     def _():
-        share = sums[0].shape[1] // 4
+        share = width // 4
         for out, flips in ((send_ref, (1, 3)), (keep_ref, (0, 2))):
             for slot, bits in enumerate(flips):
-                columns = pl.ds(pl.multiple_of((me_ref[0] ^ bits) * share, share), share)
-                for kind, total in enumerate(sums):
-                    out[slot, :, kind * share : (kind + 1) * share] = total[:, columns].astype(
-                        out.dtype
-                    )
+                for kind in range(3):
+                    place = pl.multiple_of(kind * width + (me_ref[0] ^ bits) * share, share)
+                    out[slot, :, kind * share : (kind + 1) * share] = total[
+                        :, pl.ds(place, share)
+                    ].astype(out.dtype)
 
 
 def project_call(me, expression, gene_mask, mask_value, w_qkv):
     rows, genes = expression.shape
-    width = w_qkv.shape[1] // 3
-    depth = min(genes, 512)
+    width = w_qkv.shape[1]
+    depth = min(genes, 1024)
     wide = spec((rows, depth), lambda i, _: (0, i))
-    shape = (2, rows, 3 * width // 4)
+    shape = (2, rows, width // 4)
     return call(
         project_kernel,
         me,
-        (expression, gene_mask, mask_value.reshape(1, genes), w_qkv, w_qkv, w_qkv),
+        (expression, gene_mask, mask_value.reshape(1, genes), w_qkv),
         [
             wide,
             wide,
             spec((1, depth), lambda i, _: (0, i)),
             spec((depth, width), lambda i, _: (i, 0)),
-            spec((depth, width), lambda i, _: (i, 1)),
-            spec((depth, width), lambda i, _: (i, 2)),
         ],
         [array((rows, genes), BF16), array(shape, BF16), array(shape, F32)],
         [wide, whole(shape), whole(shape)],
         grid=(genes // depth,),
-        scratch=[pltpu.VMEM((rows, width), F32)] * 3,
-    )
-
-
-def store_quarters(me, held, send_ref, keep_ref):
+        scratch=[pltpu.VMEM((rows, width), F32)],
+    )
+
+
+def store_quarters(me, at, held, send_ref, keep_ref):
     quarter = held.shape[0] // 4
     for bits in range(4):
         start = pl.multiple_of((me ^ bits) * quarter, quarter)
         part = held[pl.ds(start, quarter), :]
         if bits % 2:
-            send_ref[bits // 2][0] = part.astype(BF16)
+            send_ref[bits // 2][at] = part.astype(BF16)
         else:
-            keep_ref[bits // 2, 0] = part
-
-
-def quarter_outs(count, size):
+            keep_ref[bits // 2, at] = part
+
+
+def quarter_outs(count, group, size):
     shape = (count, size // 4, size)
-    one = spec((1, *shape[1:]), lambda j, _: (j, 0, 0))
-    two = spec((2, 1, *shape[1:]), lambda j, _: (0, j, 0, 0))
+    one = spec((group, *shape[1:]), lambda j, _: (j, 0, 0))
+    two = spec((2, group, *shape[1:]), lambda j, _: (0, j, 0, 0))
     return [array(shape, BF16)] * 2 + [array((2, *shape), F32)], [one, one, two]
 
 
@@ -381,10 +391,12 @@
 
 def first_kernel(me_ref, turn_ref, own, near, far, rest, w_out_ref, masked_ref, wf_ref, *refs):
     hidden_ref, outs, gathered, held = refs[0], refs[1:-2], refs[-2], refs[-1]
-    block = pl.program_id(0)
+    step = pl.program_id(0)
     share = own.shape[1]
-
-    @pl.when(block == 0)
+    group, size, _ = wf_ref.shape
+    steps = TILE // group
+
+    @pl.when(step == 0)
     def _():
         for bits, piece in enumerate((own, near, far, rest)):
             place = pl.multiple_of((me_ref[0] ^ bits) * share, share)
@@ -393,11 +405,15 @@
     added = jnp.dot(gathered[...], w_out_ref[...], preferred_element_type=F32)
     hidden = (masked_ref[...].astype(F32) + added).astype(BF16)
     hidden_ref[...] = hidden
-    held[block % TILE] = lax.dot_general(
-        wf_ref[0], hidden, (((1,), (1,)), ((), ())), preferred_element_type=F32
-    ).astype(BF16)
-
-    @pl.when(block % TILE == TILE - 1)
+    for g in range(group):
+        held[step % steps * group + g] = lax.dot_general(
+            wf_ref[g],
+            hidden[:, g * size : (g + 1) * size],
+            (((1,), (1,)), ((), ())),
+            preferred_element_type=F32,
+        ).astype(BF16)
+
+    @pl.when(step % steps == steps - 1)
     def _():
         deeps = [out.shape[1] for out in outs]
         deep = sum(deeps)
@@ -418,7 +434,9 @@
     blocks, size, _ = w_first_t.shape
     rows, genes = masked.shape
     width = w_out.shape[0]
-    wide = spec((rows, size), lambda b, _: (0, b))
+    group = several(TILE)
+    steps = TILE // group
+    wide = spec((rows, group * size), lambda b, _: (0, b))
     hidden, *first = call(
         first_kernel,
         me,
@@ -426,13 +444,14 @@
         [whole(matrix.shape)]
         + [whole(part.shape) for part in attended]
         + [
-            spec((width, size), lambda b, _: (0, b)),
+            spec((width, group * size), lambda b, _: (0, b)),
             wide,
-            spec((1, size, size), lambda b, _: (b, 0, 0)),
+            spec((group, size, size), lambda b, _: (b, 0, 0)),
         ],
         [array((rows, genes), BF16)] + [array((4, deep, blocks, rows), BF16) for deep in deeps],
-        [wide] + [spec((4, deep, TILE, rows), lambda b, _: (0, 0, b // TILE, 0)) for deep in deeps],
-        grid=(blocks,),
+        [wide]
+        + [spec((4, deep, TILE, rows), lambda b, _: (0, 0, b // steps, 0)) for deep in deeps],
+        grid=(blocks // group,),
         scratch=[pltpu.VMEM((rows, width), BF16), pltpu.VMEM((TILE, size, rows), BF16)],
     )
     return hidden, first
@@ -440,17 +459,20 @@
 
 def second_kernel(me_ref, *refs):
     piece, w_ref, cot_ref, hidden_ref = refs[:4]
-    out_ref, *send_ref, keep_ref, held, square = refs[-6:]
-    for source in range(4):
-        held[:, source] = piece[source]
-    size = w_ref.shape[1]
-    permuted = held[...].reshape(size, held.shape[3])
-    square[...] = jnp.dot(permuted, cot_ref[...], preferred_element_type=F32)
-    store_quarters(me_ref[1], square, send_ref, keep_ref)
-    mixed = lax.dot_general(
-        permuted, w_ref[0], (((0,), (0,)), ((), ())), preferred_element_type=F32
-    )
-    out_ref[...] = (hidden_ref[...].astype(F32) + mixed).astype(BF16)
+    out_ref, *send_ref, keep_ref, square = refs[-5:]
+    group, size, _ = w_ref.shape
+    pair = piece.shape[1] // group
+    for g in range(group):
+        at = slice(g * size, (g + 1) * size)
+        permuted = jnp.concatenate(
+            [piece[s, g * pair + o] for o in range(pair) for s in range(4)], axis=0
+        )
+        square[g] = jnp.dot(permuted, cot_ref[:, at], preferred_element_type=F32)
+        store_quarters(me_ref[1], g, square.at[g], send_ref, keep_ref)
+        mixed = lax.dot_general(
+            permuted, w_ref[g], (((0,), (0,)), ((), ())), preferred_element_type=F32
+        )
+        out_ref[:, at] = (hidden_ref[:, at].astype(F32) + mixed).astype(BF16)
 
 
 def second_call(me, piece, w_second, cotangent, hidden, denoised, start):
@@ -458,11 +480,18 @@
     _, deep, _, rows = piece.shape
     pair = size // (4 * blocks)
     count = deep // pair
-    wide = spec((rows, size), lambda j, _: (0, start + j))
-    square = spec((1, size, size), lambda j, _: (start + j, 0, 0))
+    group = several(math.gcd(count, start) if start else count)
+    begin = start // group
+    wide = spec((rows, group * size), lambda j, _: (0, begin + j))
+    square = spec((group, size, size), lambda j, _: (begin + j, 0, 0))
     args = [piece, w_second, cotangent, hidden]
-    in_specs = [spec((4, pair, blocks, rows), lambda j, _: (0, j, 0, 0)), square, wide, wide]
-    quarters = quarter_outs(count, size)
+    in_specs = [
+        spec((4, group * pair, blocks, rows), lambda j, _: (0, j, 0, 0)),
+        square,
+        wide,
+        wide,
+    ]
+    quarters = quarter_outs(count, group, size)
     aliases = {}
     if denoised is not None:
         args.append(denoised)
@@ -475,35 +504,40 @@
         in_specs,
         [array(hidden.shape, BF16), *quarters[0]],
         [wide, *quarters[1]],
-        grid=(count,),
-        scratch=[pltpu.VMEM((pair, 4, blocks, rows), BF16), pltpu.VMEM((size, size), F32)],
+        grid=(count // group,),
+        scratch=[pltpu.VMEM((group, size, size), F32)],
         aliases=aliases,
     )
 
 
 def grad_first_kernel(me_ref, *refs):
     pieces, (hidden_ref, *send_ref, keep_ref, held, square) = refs[:-6], refs[-6:]
-    for half in range(len(pieces) // 4):
-        for bits in range(4):
-            held[me_ref[0] ^ bits, half] = pieces[half * 4 + bits][0]
-    back = held[...].reshape(-1, held.shape[3])
-    square[...] = jnp.dot(back, hidden_ref[...], preferred_element_type=F32).T
-    store_quarters(me_ref[1], square, send_ref, keep_ref)
+    group, size, _ = square.shape
+    for g in range(group):
+        for part in range(len(pieces) // 4):
+            for bits in range(4):
+                held[g, me_ref[0] ^ bits, part] = pieces[part * 4 + bits][g]
+        back = held[g].reshape(size, held.shape[4])
+        hidden = hidden_ref[:, g * size : (g + 1) * size]
+        square[g] = jnp.dot(back, hidden, preferred_element_type=F32).T
+        store_quarters(me_ref[1], g, square.at[g], send_ref, keep_ref)
 
 
 def grad_first_call(me, pieces, hidden, size, start, count):
     _, deep, rows = pieces[0].shape
+    group = several(math.gcd(count, start) if start else count)
+    begin = start // group
     return call(
         grad_first_kernel,
         me,
         (*pieces, hidden),
-        [spec((1, deep, rows), lambda b, _: (start + b, 0, 0))] * len(pieces)
-        + [spec((rows, size), lambda b, _: (0, start + b))],
-        *quarter_outs(count, size),
-        grid=(count,),
+        [spec((group, deep, rows), lambda b, _: (begin + b, 0, 0))] * len(pieces)
+        + [spec((rows, group * size), lambda b, _: (0, begin + b))],
+        *quarter_outs(count, group, size),
+        grid=(count // group,),
         scratch=[
-            pltpu.VMEM((4, len(pieces) // 4, deep, rows), BF16),
-            pltpu.VMEM((size, size), F32),
+            pltpu.VMEM((group, 4, len(pieces) // 4, deep, rows), BF16),
+            pltpu.VMEM((group, size, size), F32),
         ],
     )
 
@@ -513,7 +547,7 @@
     blocks, size, _ = w_first.shape
     parts = 4
     deep = size // 4
-    deeps = [deep // 4] * 3 + [3 * deep // 16, deep // 16]
+    deeps = [deep // 2, 3 * deep // 8, deep // 8]
     matrix = grid_turn()
     sends, back = [None] * parts, [[None] * 4 for _ in range(parts)]
 
@@ -545,18 +579,18 @@
     across = flip(key_value, "cell", 2)
     beside = flip(key_value, "cell", 1)
     corner = flip(across, "cell", 1)
-    beside_keys = [begin(2, 2, key_value)]
+    beside_keys = [begin(2, 2, last), begin(2, 1, last)]
     queries = after(queries, *beside_keys, beside, across, corner)
     attended = attend_call(me, queries, (key_value, beside, across, corner))
-    attended = after(attended, begin(2, 3, queries))
+    attended = after(attended, begin(2, 3, queries), begin(3, 1, queries))
     near = flip(attended, "gene", 1)
     far = flip(attended, "gene", 2)
     rest = flip(after(far, near), "gene", 1)
+    rest = after(rest, begin(3, 2, attended))
     hidden, first = first_call(
         me, matrix, (attended, near, far, rest), w_out, masked, w_first_t, deeps
     )
-    for part, bits in ((3, 2), (3, 3), (2, 1), (3, 1)):
-        begin(part, bits, rest)
+    begin(3, 3, rest)
 
     got = []
 
@@ -564,46 +598,30 @@
         piece = after(first[t], *earlier)
         got.append(lax.all_to_all(piece, "gene", split_axis=0, concat_axis=0, tiled=True))
 
-    launch(0, back[2][1], *back[3][1:])
-    denoised, shares, made, added = None, [None, None], [], []
-    some = blocks // 2
+    launch(0, back[3][3])
+    denoised, shares = None, [None, None]
     back = sum(back, [])
 
-    def make_first(part, *earlier):
-        *send, keep = grad_first_call(
-            me, after(back, *earlier), hidden, size, part * some, some
-        )
-        made.append((0, part * some, [flip(piece, "cell", 1) for piece in send], keep))
-
-    def settle(*earlier):
-        pins = []
-        for which, start, mine, last in added:
-            shares[which] = finish_call(
-                me, mine, after(last, *earlier), shares[which], start, blocks
-            )
-        pins += [shares[which] for which in {entry[0]: 0 for entry in added}]
-        added.clear()
-        for which, start, came, keep in made:
-            mine, other = pair_call(me, keep, after(came, *earlier))
-            added.append((which, start, mine, flip(other, "cell", 2)))
-            pins.append(mine)
-        made.clear()
-        return pins
-
-    make_first(0)
-    make_first(1)
-    pins = []
+    def sum_cells(which, start, send, keep):
+        came = [flip(piece, "cell", 1) for piece in send]
+        mine, other = pair_call(me, keep, came)
+        last = flip(other, "cell", 2)
+        shares[which] = finish_call(me, mine, last, shares[which], start, blocks)
+
+    *send, keep = grad_first_call(me, back, hidden, size, 0, blocks // 2)
+    *send_next, keep_next = grad_first_call(me, back, hidden, size, blocks // 2, blocks // 2)
+    sum_cells(0, 0, send, keep)
+    sum_cells(0, blocks // 2, send_next, keep_next)
+    pin = shares[0]
     for t in range(len(deeps)):
         if t + 1 < len(deeps):
-            launch(t + 1, got[t], *pins)
-        pins = settle(got[t])
+            launch(t + 1, got[t], pin)
         start = sum(deeps[:t]) * blocks // deep
         denoised, *send, keep = second_call(
             me, got[t], w_second, cotangent, hidden, denoised, start
         )
-        made.append((1, start, [flip(piece, "cell", 1) for piece in send], keep))
-    settle()
-    settle()
+        sum_cells(1, start, send, keep)
+        pin = shares[1]
     return (denoised, *shares)
 
 

time: 518 us -> 493 us (0.952)
  waiting for transfers between devices: 173 us -> 269 us
  Pallas kernels: 213 us -> 151 us
  blocking collectives: 49.5 us -> 0 us
  starting transfers between devices: 62.6 us -> 53.2 us
    pallas_call x30 -> x24, Pallas kernels: 213 us -> 151 us  [call(): pl.pallas_call(body, out_shape=outs, grid_spec=pltpu.PrefetchScalarGridSp...]
    ppermute x41 -> x35, waiting for transfers between devices: 119 us -> 174 us  [flip(): return lax.ppermute(value, axis, pairs)]
    all_to_all x1 -> x0, blocking collectives: 49.5 us -> none  [launch(): lax.all_to_all(piece, 'gene', split_axis=0, concat_axis=0, tiled=True)]
    all_to_all x4 -> x3, waiting for transfers between devices: 53.9 us -> 94.9 us  [launch(): lax.all_to_all(piece, 'gene', split_axis=0, concat_axis=0, tiled=True)]
    ppermute x41 -> x35, starting transfers between devices: 45.8 us -> 41.1 us  [flip(): return lax.ppermute(value, axis, pairs)]
    all_to_all x4 -> x3, starting transfers between devices: 16.8 us -> 12.1 us  [launch(): lax.all_to_all(piece, 'gene', split_axis=0, concat_axis=0, tiled=True)]
    unnamed x58 -> x50, local copies, waits for them, and re-layouts: 8.94 us -> 10.9 us
  transfers between devices with their start and end apart: 45 -> 38, of which waited for: 20 -> 25; matrix products, arithmetic and copies ran while one was open for 1% -> 1% of each run, Pallas kernels for 38% -> 28%
where the time goes in v4:
time: 493 us; the launch traced here: 492 us
  waiting for transfers between devices  269 us (55%)
  Pallas kernels  151 us (31%)
  starting transfers between devices  53.2 us (11%)
  local copies, waits for them, and re-layouts  17.3 us (4%)
    ppermute x35, waiting for transfers between devices, flip(): return lax.ppermute(value, axis, pairs)  174 us
    pallas_call x24, Pallas kernels, call(): pl.pallas_call(body, out_shape=outs, grid_spec=pltpu.PrefetchScalarGridSp...  151 us
    all_to_all x3, waiting for transfers between devices, launch(): lax.all_to_all(piece, 'gene', split_axis=0, concat_axis=0, tiled=True)  94.9 us
    ppermute x35, starting transfers between devices, flip(): return lax.ppermute(value, axis, pairs)  41.1 us
    all_to_all x3, starting transfers between devices, launch(): lax.all_to_all(piece, 'gene', split_axis=0, concat_axis=0, tiled=True)  12.1 us
    unnamed x50, local copies, waits for them, and re-layouts  10.9 us
  transfers between devices with their start and end apart: 38, of which 25 were waited for; matrix products, arithmetic and copies ran while one was open for 1% of the time, Pallas kernels for 28%

profile of v4, /device:TPU:0, one launch (start us, length us, event | category | flops | bytes accessed | tf_op | source)
XLA Modules:
  0.0 491.9 jit_solution(7287016273346838706)
XLA Ops:
  1.0 4.4 shard_map.103
  5.5 4.0 collective-permute-start.1
  11.1 37.8 %shard_map.104 = (bf16[512,8192]{1,0:T(8,128)(2,1)}, bf16[2,512,768]{2,1,0:T(8,128)(2,1)S(1)}, f32[2,512,768]{2,1,0:T(8,128)}) custom-call(s32[2]{0:T(128)S(1)} %pad_add_fusion.me_ref._, bf16[512,8192]{1,0:T(8,128)(2,1)} %value_ref, s32[512,8192]{1,0:T(8,128)} %mask_ref.1, bf16[1,8192]{1,0:T(2,128)(2,1)S(1)} %reshape.9.fill_ref, bf16[8192,3072]{1,0:T(8,128)(2,1)} %weight_ref.1), custom_call_target="tpu_custom_call" | custom-call | flops 1 | bytes 1 | tf_op jit(solution)/shard_map/pallas_call | solution.py:100
  49.7 6.4 %collective-permute-start.3 = (bf16[2,512,768]{2,1,0:T(8,128)(2,1)S(1)}, bf16[2,512,768]{2,1,0:T(8,128)(2,1)S(1)}, u32[]{:S(2)}, u32[]{:S(2)}) collective-permute-start(bf16[2,512,768]{2,1,0:T(8,128)(2,1)S(1)} %get-tuple-element.87), channel_id=1, source_target_pairs={{0,4},{4,0},{8,12},{12,8},{1,5},{5,1},{9,13},{13,9},{2,6},{6,2},{1... | collective-permute-start | bytes 4718600 | tf_op jit(solution)/shard_map/ppermute | solution.py:96
  56.1 4.6 shard_map.105
  61.5 3.3 collective-permute-start.5
  64.8 41.1 %collective-permute-done.5.refs_7_ = bf16[32,16,512]{2,1,0:T(8,128)(2,1)S(1)} collective-permute-done((bf16[32,16,512]{2,1,0:T(8,128)(2,1)}, bf16[32,16,512]{2,1,0:T(8,128)(2,1)S(1)}, u32[]{:S(2)}, u32[]{:S(2)}) %collective-permute-start.5) | collective-permute-done | bytes 524320 | tf_op jit(solution)/shard_map/ppermute | solution.py:96
  105.9 6.5 %collective-permute-done.4.refs_6_ = bf16[32,16,512]{2,1,0:T(8,128)(2,1)S(1)} collective-permute-done((bf16[32,16,512]{2,1,0:T(8,128)(2,1)S(1)}, bf16[32,16,512]{2,1,0:T(8,128)(2,1)S(1)}, u32[]{:S(2)}, u32[]{:S(2)}) %collective-permute-start.4) | collective-permute-done | bytes 524320 | tf_op jit(solution)/shard_map/ppermute | solution.py:96
  114.3 4.2 shard_map.106
  118.5 2.7 collective-permute-start.6
  122.3 4.5 shard_map.107
  129.2 4.4 shard_map.108
  134.4 6.5 %copy.16 = bf16[32,256,256]{1,2,0:T(8,128)(2,1)} copy(bf16[32,256,256]{2,1,0:T(8,128)(2,1)} %param.13) | data formatting | bytes 8388608 | tf_op jit(solution)/shard_map/optimization_barrier | solution.py:91
  140.9 7.8 %collective-permute-done.7.refs_5_ = bf16[32,16,512]{2,1,0:T(8,128)(2,1)} collective-permute-done((bf16[32,16,512]{2,1,0:T(8,128)(2,1)}, bf16[32,16,512]{2,1,0:T(8,128)(2,1)}, u32[]{:S(2)}, u32[]{:S(2)}) %collective-permute-start.7) | collective-permute-done | bytes 524320 | tf_op jit(solution)/shard_map/ppermute | solution.py:96
  148.6 6.5 %collective-permute-done.6.came_ref = bf16[512,768]{1,0:T(8,128)(2,1)S(1)} collective-permute-done((bf16[512,768]{1,0:T(8,128)(2,1)S(1)}, bf16[512,768]{1,0:T(8,128)(2,1)S(1)}, u32[]{:S(2)}, u32[]{:S(2)}) %collective-permute-start.6) | collective-permute-done | bytes 786464 | tf_op jit(solution)/shard_map/ppermute | solution.py:96
  155.1 3.2 shard_map.109
  160.3 3.4 collective-permute-start.8
  163.7 7.1 %collective-permute-done.11.refs_2_ = bf16[512,512]{1,0:T(8,128)(2,1)S(1)} collective-permute-done((bf16[512,512]{1,0:T(8,128)(2,1)S(1)}, bf16[512,512]{1,0:T(8,128)(2,1)S(1)}, u32[]{:S(2)}, u32[]{:S(2)}) %collective-permute-start.11) | collective-permute-done | bytes 524320 | tf_op jit(solution)/shard_map/ppermute | solution.py:96
  170.8 14.6 %collective-permute-done.9.refs_9_ = bf16[32,16,512]{2,1,0:T(8,128)(2,1)S(1)} collective-permute-done((bf16[32,16,512]{2,1,0:T(8,128)(2,1)}, bf16[32,16,512]{2,1,0:T(8,128)(2,1)S(1)}, u32[]{:S(2)}, u32[]{:S(2)}) %collective-permute-start.9) | collective-permute-done | bytes 524320 | tf_op jit(solution)/shard_map/ppermute | solution.py:96
  185.4 2.1 collective-permute-done.8.refs_10_
  187.5 2.4 collective-permute-start.13
  190.0 7.1 %shard_map.110.own = bf16[512,256]{1,0:T(8,128)(2,1)S(1)} custom-call(s32[2]{0:T(128)S(1)} %pad_add_fusion.me_ref._, bf16[512,256]{1,0:T(8,128)(2,1)S(1)} %get-tuple-element.108.query_ref, bf16[512,512]{1,0:T(8,128)(2,1)S(1)} %get-tuple-element.107.refs_0_, bf16[512,512]{1,0:T(8,128)(2,1)S(1)} %collective-permute-done.10.refs_1_, ...), custom_call_target="tpu_custom_call" | custom-call | flops 1 | bytes 1 | tf_op jit(solution)/shard_map/pallas_call | solution.py:100
  197.1 7.4 %collective-permute-done.13.refs_11_ = bf16[32,16,512]{2,1,0:T(8,128)(2,1)S(1)} collective-permute-done((bf16[32,16,512]{2,1,0:T(8,128)(2,1)}, bf16[32,16,512]{2,1,0:T(8,128)(2,1)S(1)}, u32[]{:S(2)}, u32[]{:S(2)}) %collective-permute-start.13) | collective-permute-done | bytes 524320 | tf_op jit(solution)/shard_map/ppermute | solution.py:96
  204.5 8.8 %collective-permute-done.14.refs_13_ = bf16[32,16,512]{2,1,0:T(8,128)(2,1)S(1)} collective-permute-done((bf16[32,16,512]{2,1,0:T(8,128)(2,1)S(1)}, bf16[32,16,512]{2,1,0:T(8,128)(2,1)S(1)}, u32[]{:S(2)}, u32[]{:S(2)}) %collective-permute-start.14) | collective-permute-done | bytes 524320 | tf_op jit(solution)/shard_map/ppermute | solution.py:96
  215.4 2.5 collective-permute-start.18
  217.9 12.3 %collective-permute-done.16.far = bf16[512,256]{1,0:T(8,128)(2,1)S(1)} collective-permute-done((bf16[512,256]{1,0:T(8,128)(2,1)S(1)}, bf16[512,256]{1,0:T(8,128)(2,1)S(1)}, u32[]{:S(2)}, u32[]{:S(2)}) %collective-permute-start.16) | collective-permute-done | bytes 262176 | tf_op jit(solution)/shard_map/ppermute | solution.py:96
  230.3 20.3 %collective-permute-done.18.refs_14_ = bf16[32,16,512]{2,1,0:T(8,128)(2,1)S(1)} collective-permute-done((bf16[32,16,512]{2,1,0:T(8,128)(2,1)S(1)}, bf16[32,16,512]{2,1,0:T(8,128)(2,1)S(1)}, u32[]{:S(2)}, u32[]{:S(2)}) %collective-permute-start.18) | collective-permute-done | bytes 524320 | tf_op jit(solution)/shard_map/ppermute | solution.py:96
  250.5 3.1 collective-permute-start.19
  253.7 24.5 %shard_map.111 = (bf16[512,8192]{1,0:T(8,128)(2,1)}, bf16[4,32,32,512]{3,2,1,0:T(8,128)(2,1)}, bf16[4,24,32,512]{3,2,1,0:T(8,128)(2,1)}, bf16[4,8,32,512]{3,2,1,0:T(8,128)(2,1)}) custom-call(s32[2]{0:T(128)S(1)} %pad_add_fusion.me_ref._, bf16[256,256]{1,0:T(8,128)(2,1)S(1)} %fusion.turn_ref, bf16[512,256]{1,0:T(8,128)(2,1)S(1)} %shard_map.110.own, ...), custom_call_target="tpu_custom_call" | custom-call | flops 1 | bytes 1 | tf_op jit(solution)/shard_map/pallas_call | solution.py:100
  279.1 4.9 all-to-all-start
  283.9 7.0 %shard_map.114 = (bf16[16,64,256]{2,1,0:T(8,128)(2,1)S(1)}, bf16[16,64,256]{2,1,0:T(8,128)(2,1)S(1)}, f32[2,16,64,256]{3,2,1,0:T(8,128)}) custom-call(s32[2]{0:T(128)S(1)} %pad_add_fusion.me_ref._, bf16[32,16,512]{2,1,0:T(8,128)(2,1)S(1)} %get-tuple-element.80.refs_0_, bf16[32,16,512]{2,1,0:T(8,128)(2,1)} %copy-done.11, bf16[32,16,512]{2,1,0:T(8,128)(2,1)} %copy-done.9, ...), custom_call_target="tpu_custom_call" | custom-call | flops 1 | bytes 1 | tf_op jit(solution)/shard_map/pallas_call | solution.py:100
  291.5 7.0 %shard_map.112 = (bf16[16,64,256]{2,1,0:T(8,128)(2,1)S(1)}, bf16[16,64,256]{2,1,0:T(8,128)(2,1)S(1)}, f32[2,16,64,256]{3,2,1,0:T(8,128)}) custom-call(s32[2]{0:T(128)S(1)} %pad_add_fusion.me_ref._, bf16[32,16,512]{2,1,0:T(8,128)(2,1)S(1)} %get-tuple-element.80.refs_0_, bf16[32,16,512]{2,1,0:T(8,128)(2,1)} %copy-done.11, bf16[32,16,512]{2,1,0:T(8,128)(2,1)} %copy-done.9, ...), custom_call_target="tpu_custom_call" | custom-call | flops 1 | bytes 1 | tf_op jit(solution)/shard_map/pallas_call | solution.py:100
  299.1 3.2 shard_map.115
  302.9 3.2 shard_map.113
  307.6 9.5 %collective-permute-done.25.came_ref = bf16[16,64,256]{2,1,0:T(8,128)(2,1)S(1)} collective-permute-done((bf16[16,64,256]{2,1,0:T(8,128)(2,1)S(1)}, bf16[16,64,256]{2,1,0:T(8,128)(2,1)S(1)}, u32[]{:S(2)}, u32[]{:S(2)}) %collective-permute-start.25) | collective-permute-done | bytes 524320 | tf_op jit(solution)/shard_map/ppermute | solution.py:96
  320.0 7.5 %collective-permute-done.22.came_ref = bf16[16,64,256]{2,1,0:T(8,128)(2,1)S(1)} collective-permute-done((bf16[16,64,256]{2,1,0:T(8,128)(2,1)S(1)}, bf16[16,64,256]{2,1,0:T(8,128)(2,1)S(1)}, u32[]{:S(2)}, u32[]{:S(2)}) %collective-permute-start.22) | collective-permute-done | bytes 524320 | tf_op jit(solution)/shard_map/ppermute | solution.py:96
  329.1 45.4 %all-to-all-done.refs_0_ = bf16[4,32,32,512]{3,2,1,0:T(8,128)(2,1)} async-done(((bf16[4,32,32,512]{3,2,1,0:T(8,128)(2,1)}), bf16[4,32,32,512]{3,2,1,0:T(8,128)(2,1)}, u32[]{:S(2)}, u32[]{:S(2)}) %all-to-all-start) | async-done | bytes 4194336 | tf_op jit(solution)/shard_map/all_to_all | solution.py:599
  374.5 3.7 all-to-all-start.1
  378.2 9.6 %shard_map.118 = (bf16[512,8192]{1,0:T(8,128)(2,1)}, bf16[16,64,256]{2,1,0:T(8,128)(2,1)S(1)}, bf16[16,64,256]{2,1,0:T(8,128)(2,1)S(1)}, f32[2,16,64,256]{3,2,1,0:T(8,128)}) custom-call(s32[2]{0:T(128)S(1)} %pad_add_fusion.me_ref._, bf16[4,32,32,512]{3,2,1,0:T(8,128)(2,1)} %all-to-all-done.refs_0_, bf16[32,256,256]{2,1,0:T(8,128)(2,1)} %refs_1_.5, ...), custom_call_target="tpu_custom_call" | custom-call | flops 1 | bytes 1 | tf_op jit(solution)/shard_map/pallas_call | solution.py:100
  390.5 3.2 shard_map.119
  394.3 13.4 %collective-permute-done.28.came_ref = bf16[16,64,256]{2,1,0:T(8,128)(2,1)S(1)} collective-permute-done((bf16[16,64,256]{2,1,0:T(8,128)(2,1)S(1)}, bf16[16,64,256]{2,1,0:T(8,128)(2,1)S(1)}, u32[]{:S(2)}, u32[]{:S(2)}) %collective-permute-start.28) | collective-permute-done | bytes 524320 | tf_op jit(solution)/shard_map/ppermute | solution.py:96
  410.5 37.8 %all-to-all-done.1.refs_0_ = bf16[4,24,32,512]{3,2,1,0:T(8,128)(2,1)S(1)} async-done(((bf16[4,24,32,512]{3,2,1,0:T(8,128)(2,1)}), bf16[4,24,32,512]{3,2,1,0:T(8,128)(2,1)S(1)}, u32[]{:S(2)}, u32[]{:S(2)}) %all-to-all-start.1) | async-done | bytes 3145760 | tf_op jit(solution)/shard_map/all_to_all | solution.py:599
  450.0 3.5 all-to-all-start.2
  453.5 8.5 %shard_map.121 = (bf16[512,8192]{1,0:T(8,128)(2,1)}, bf16[12,64,256]{2,1,0:T(8,128)(2,1)S(1)}, bf16[12,64,256]{2,1,0:T(8,128)(2,1)S(1)}, f32[2,12,64,256]{3,2,1,0:T(8,128)}) custom-call(s32[2]{0:T(128)S(1)} %pad_add_fusion.me_ref._, bf16[4,24,32,512]{3,2,1,0:T(8,128)(2,1)} %copy-done.8, ...), custom_call_target="tpu_custom_call", output_to_operand_aliasing={{0}: (5, {})} | custom-call | flops 1 | bytes 1 | tf_op jit(solution)/shard_map/pallas_call | solution.py:100
  464.3 2.1 shard_map.124
  467.0 11.7 %all-to-all-done.2.refs_0_ = bf16[4,8,32,512]{3,2,1,0:T(8,128)(2,1)S(1)} async-done(((bf16[4,8,32,512]{3,2,1,0:T(8,128)(2,1)}), bf16[4,8,32,512]{3,2,1,0:T(8,128)(2,1)S(1)}, u32[]{:S(2)}, u32[]{:S(2)}) %all-to-all-start.2) | async-done | bytes 1048608 | tf_op jit(solution)/shard_map/all_to_all | solution.py:599
  478.7 4.0 shard_map.122
  487.5 3.2 collective-permute-done.31.came_ref
  (109 shorter events, 38.8 us)
Async XLA Ops:
  5.5 43.4 %collective-permute-start.1 = (bf16[32,16,512]{2,1,0:T(8,128)(2,1)S(1)}, bf16[32,16,512]{2,1,0:T(8,128)(2,1)S(1)}, u32[]{:S(2)}, u32[]{:S(2)}) collective-permute-start(bf16[32,16,512]{2,1,0:T(8,128)(2,1)S(1)} %get-tuple-element.85), channel_id=1, source_target_pairs={{0,8},{4,12},{8,0},{12,4},{1,9},{5,13},{9,1},{13,5},{2,10},{6,14},... | collective-permute-start | bytes 1572872 | tf_op jit(solution)/shard_map/ppermute | solution.py:96
  9.5 39.4 %collective-permute-start = (bf16[32,16,512]{2,1,0:T(8,128)(2,1)}, bf16[32,16,512]{2,1,0:T(8,128)(2,1)S(1)}, u32[]{:S(2)}, u32[]{:S(2)}) collective-permute-start(bf16[32,16,512]{2,1,0:T(8,128)(2,1)} %get-tuple-element.84), channel_id=1, source_target_pairs={{0,12},{4,8},{8,4},{12,0},{1,13},{5,9},{9,5},{13,1},{2,14},{6,10},... | collective-permute-start | bytes 1572872 | tf_op jit(solution)/shard_map/ppermute | solution.py:96
  10.9 38.1 %collective-permute-start.2 = (bf16[32,16,512]{2,1,0:T(8,128)(2,1)S(1)}, bf16[32,16,512]{2,1,0:T(8,128)(2,1)S(1)}, u32[]{:S(2)}, u32[]{:S(2)}) collective-permute-start(bf16[32,16,512]{2,1,0:T(8,128)(2,1)S(1)} %get-tuple-element.86), channel_id=1, source_target_pairs={{0,4},{4,0},{8,12},{12,8},{1,5},{5,1},{9,13},{13,9},{2,6},{6,2},{1... | collective-permute-start | bytes 1572872 | tf_op jit(solution)/shard_map/ppermute | solution.py:96
  48.9 11.8 %copy-start.10 = (bf16[32,16,512]{2,1,0:T(8,128)(2,1)}, bf16[32,16,512]{2,1,0:T(8,128)(2,1)S(1)}, u32[]{:S(2)}) copy-start(bf16[32,16,512]{2,1,0:T(8,128)(2,1)S(1)} %collective-permute-done.refs_3_) | copy-start | bytes 1572868
  49.7 63.4 %collective-permute-start.3 = (bf16[2,512,768]{2,1,0:T(8,128)(2,1)S(1)}, bf16[2,512,768]{2,1,0:T(8,128)(2,1)S(1)}, u32[]{:S(2)}, u32[]{:S(2)}) collective-permute-start(bf16[2,512,768]{2,1,0:T(8,128)(2,1)S(1)} %get-tuple-element.87), channel_id=1, source_target_pairs={{0,4},{4,0},{8,12},{12,8},{1,5},{5,1},{9,13},{13,9},{2,6},{6,2},{1... | collective-permute-start | bytes 4718600 | tf_op jit(solution)/shard_map/ppermute | solution.py:96
  61.5 44.4 %collective-permute-start.5 = (bf16[32,16,512]{2,1,0:T(8,128)(2,1)}, bf16[32,16,512]{2,1,0:T(8,128)(2,1)S(1)}, u32[]{:S(2)}, u32[]{:S(2)}) collective-permute-start(bf16[32,16,512]{2,1,0:T(8,128)(2,1)} %get-tuple-element.90), channel_id=1, source_target_pairs={{0,12},{4,8},{8,4},{12,0},{1,13},{5,9},{9,5},{13,1},{2,14},{6,10},... | collective-permute-start | bytes 1572872 | tf_op jit(solution)/shard_map/ppermute | solution.py:96
  64.8 47.6 %collective-permute-start.4 = (bf16[32,16,512]{2,1,0:T(8,128)(2,1)S(1)}, bf16[32,16,512]{2,1,0:T(8,128)(2,1)S(1)}, u32[]{:S(2)}, u32[]{:S(2)}) collective-permute-start(bf16[32,16,512]{2,1,0:T(8,128)(2,1)S(1)} %get-tuple-element.89), channel_id=1, source_target_pairs={{0,8},{4,12},{8,0},{12,4},{1,9},{5,13},{9,1},{13,5},{2,10},{6,14},... | collective-permute-start | bytes 1572872 | tf_op jit(solution)/shard_map/ppermute | solution.py:96
  105.9 20.9 %copy-start.12 = (bf16[32,16,512]{2,1,0:T(8,128)(2,1)}, bf16[32,16,512]{2,1,0:T(8,128)(2,1)S(1)}, u32[]{:S(2)}) copy-start(bf16[32,16,512]{2,1,0:T(8,128)(2,1)S(1)} %collective-permute-done.5.refs_7_) | copy-start | bytes 1572868
  112.4 14.3 %copy-start.13 = (bf16[32,16,512]{2,1,0:T(8,128)(2,1)}, bf16[32,16,512]{2,1,0:T(8,128)(2,1)S(1)}, u32[]{:S(2)}) copy-start(bf16[32,16,512]{2,1,0:T(8,128)(2,1)S(1)} %collective-permute-done.4.refs_6_) | copy-start | bytes 1572868
  118.5 36.7 %collective-permute-start.6 = (bf16[512,768]{1,0:T(8,128)(2,1)S(1)}, bf16[512,768]{1,0:T(8,128)(2,1)S(1)}, u32[]{:S(2)}, u32[]{:S(2)}) collective-permute-start(bf16[512,768]{1,0:T(8,128)(2,1)S(1)} %get-tuple-element.93), channel_id=1, source_target_pairs={{0,8},{4,12},{8,0},{12,4},{1,9},{5,13},{9,1},{13,5},{2,10},{6,14},... | collective-permute-start | bytes 2359304 | tf_op jit(solution)/shard_map/ppermute | solution.py:96
  121.2 27.5 %collective-permute-start.7 = (bf16[32,16,512]{2,1,0:T(8,128)(2,1)}, bf16[32,16,512]{2,1,0:T(8,128)(2,1)}, u32[]{:S(2)}, u32[]{:S(2)}) collective-permute-start(bf16[32,16,512]{2,1,0:T(8,128)(2,1)} %get-tuple-element.95), channel_id=1, source_target_pairs={{0,4},{4,0},{8,12},{12,8},{1,5},{5,1},{9,13},{13,9},{2,6},{6,2},{1... | collective-permute-start | bytes 1572872 | tf_op jit(solution)/shard_map/ppermute | solution.py:96
  140.9 109.7 %copy-start.24 = (bf16[32,16,512]{2,1,0:T(8,128)(2,1)S(1)}, bf16[32,16,512]{2,1,0:T(8,128)(2,1)}, u32[]{:S(2)}) copy-start(bf16[32,16,512]{2,1,0:T(8,128)(2,1)} %get-tuple-element.123) | copy-start | bytes 1572868
  158.3 12.5 %collective-permute-start.11 = (bf16[512,512]{1,0:T(8,128)(2,1)S(1)}, bf16[512,512]{1,0:T(8,128)(2,1)S(1)}, u32[]{:S(2)}, u32[]{:S(2)}) collective-permute-start(bf16[512,512]{1,0:T(8,128)(2,1)S(1)} %get-tuple-element.107.refs_0_), channel_id=1, source_target_pairs={{0,2},{1,3},{2,0},{3,1},{4,6},{5,7},{6,4},{7,5},{8,10},{9,11},{10,... | collective-permute-start | bytes 1572872 | tf_op jit(solution)/shard_map/ppermute | solution.py:96
  159.9 27.6 %collective-permute-start.10 = (bf16[512,512]{1,0:T(8,128)(2,1)S(1)}, bf16[512,512]{1,0:T(8,128)(2,1)S(1)}, u32[]{:S(2)}, u32[]{:S(2)}) collective-permute-start(bf16[512,512]{1,0:T(8,128)(2,1)S(1)} %get-tuple-element.107.refs_0_), channel_id=1, source_target_pairs={{0,1},{1,0},{2,3},{3,2},{4,5},{5,4},{6,7},{7,6},{8,9},{9,8},{10,11... | collective-permute-start | bytes 1572872 | tf_op jit(solution)/shard_map/ppermute | solution.py:96
  159.9 25.6 %collective-permute-start.9 = (bf16[32,16,512]{2,1,0:T(8,128)(2,1)}, bf16[32,16,512]{2,1,0:T(8,128)(2,1)S(1)}, u32[]{:S(2)}, u32[]{:S(2)}) collective-permute-start(bf16[32,16,512]{2,1,0:T(8,128)(2,1)} %copy-done.7), channel_id=1, source_target_pairs={{0,4},{4,0},{8,12},{12,8},{1,5},{5,1},{9,13},{13,9},{2,6},{6,2},{1... | collective-permute-start | bytes 1572872 | tf_op jit(solution)/shard_map/ppermute | solution.py:96
  160.3 27.2 %collective-permute-start.8 = (bf16[32,16,512]{2,1,0:T(8,128)(2,1)}, bf16[32,16,512]{2,1,0:T(8,128)(2,1)S(1)}, u32[]{:S(2)}, u32[]{:S(2)}) collective-permute-start(bf16[32,16,512]{2,1,0:T(8,128)(2,1)} %copy-done.6), channel_id=1, source_target_pairs={{0,8},{4,12},{8,0},{12,4},{1,9},{5,13},{9,1},{13,5},{2,10},{6,14},... | collective-permute-start | bytes 1572872 | tf_op jit(solution)/shard_map/ppermute | solution.py:96
  170.8 19.2 %copy-start.21 = (bf16[512,512]{1,0:T(8,128)(2,1)}, bf16[512,512]{1,0:T(8,128)(2,1)S(1)}, u32[]{:S(2)}) copy-start(bf16[512,512]{1,0:T(8,128)(2,1)S(1)} %collective-permute-done.11.refs_2_) | copy-start | bytes 1572868
  170.8 16.7 %collective-permute-start.12 = (bf16[512,512]{1,0:T(8,128)(2,1)S(1)}, bf16[512,512]{1,0:T(8,128)(2,1)S(1)}, u32[]{:S(2)}, u32[]{:S(2)}) collective-permute-start(bf16[512,512]{1,0:T(8,128)(2,1)S(1)} %collective-permute-done.11.refs_2_), channel_id=1, source_target_pairs={{0,1},{1,0},{2,3},{3,2},{4,5},{5,4},{6,7},{7,6},{8,9},{9,8},{10,11... | collective-permute-start | bytes 1572872 | tf_op jit(solution)/shard_map/ppermute | solution.py:96
  185.4 92.8 %copy-start.14 = (bf16[32,16,512]{2,1,0:T(8,128)(2,1)}, bf16[32,16,512]{2,1,0:T(8,128)(2,1)S(1)}, u32[]{:S(2)}) copy-start(bf16[32,16,512]{2,1,0:T(8,128)(2,1)S(1)} %collective-permute-done.9.refs_9_) | copy-start | bytes 1572868
  187.5 90.7 %copy-start.15 = (bf16[32,16,512]{2,1,0:T(8,128)(2,1)}, bf16[32,16,512]{2,1,0:T(8,128)(2,1)S(1)}, u32[]{:S(2)}) copy-start(bf16[32,16,512]{2,1,0:T(8,128)(2,1)S(1)} %collective-permute-done.8.refs_10_) | copy-start | bytes 1572868
  187.5 17.0 %collective-permute-start.13 = (bf16[32,16,512]{2,1,0:T(8,128)(2,1)}, bf16[32,16,512]{2,1,0:T(8,128)(2,1)S(1)}, u32[]{:S(2)}, u32[]{:S(2)}) collective-permute-start(bf16[32,16,512]{2,1,0:T(8,128)(2,1)} %get-tuple-element.110), channel_id=1, source_target_pairs={{0,12},{4,8},{8,4},{12,0},{1,13},{5,9},{9,5},{13,1},{2,14},{6,10},... | collective-permute-start | bytes 1572872 | tf_op jit(solution)/shard_map/ppermute | solution.py:96
  190.0 23.4 %collective-permute-start.14 = (bf16[32,16,512]{2,1,0:T(8,128)(2,1)S(1)}, bf16[32,16,512]{2,1,0:T(8,128)(2,1)S(1)}, u32[]{:S(2)}, u32[]{:S(2)}) collective-permute-start(bf16[32,16,512]{2,1,0:T(8,128)(2,1)S(1)} %get-tuple-element.112), channel_id=1, source_target_pairs={{0,4},{4,0},{8,12},{12,8},{1,5},{5,1},{9,13},{13,9},{2,6},{6,2},{1... | collective-permute-start | bytes 1572872 | tf_op jit(solution)/shard_map/ppermute | solution.py:96
  204.5 73.7 %copy-start.16 = (bf16[32,16,512]{2,1,0:T(8,128)(2,1)}, bf16[32,16,512]{2,1,0:T(8,128)(2,1)S(1)}, u32[]{:S(2)}) copy-start(bf16[32,16,512]{2,1,0:T(8,128)(2,1)S(1)} %collective-permute-done.13.refs_11_) | copy-start | bytes 1572868
  213.3 64.9 %copy-start.17 = (bf16[32,16,512]{2,1,0:T(8,128)(2,1)}, bf16[32,16,512]{2,1,0:T(8,128)(2,1)S(1)}, u32[]{:S(2)}) copy-start(bf16[32,16,512]{2,1,0:T(8,128)(2,1)S(1)} %collective-permute-done.14.refs_13_) | copy-start | bytes 1572868
  213.3 16.9 %collective-permute-start.16 = (bf16[512,256]{1,0:T(8,128)(2,1)S(1)}, bf16[512,256]{1,0:T(8,128)(2,1)S(1)}, u32[]{:S(2)}, u32[]{:S(2)}) collective-permute-start(bf16[512,256]{1,0:T(8,128)(2,1)S(1)} %shard_map.110.own), channel_id=1, source_target_pairs={{0,8},{4,12},{8,0},{12,4},{1,9},{5,13},{9,1},{13,5},{2,10},{6,14},... | collective-permute-start | bytes 786440 | tf_op jit(solution)/shard_map/ppermute | solution.py:96
  213.9 16.4 %collective-permute-start.15 = (bf16[512,256]{1,0:T(8,128)(2,1)S(1)}, bf16[512,256]{1,0:T(8,128)(2,1)S(1)}, u32[]{:S(2)}, u32[]{:S(2)}) collective-permute-start(bf16[512,256]{1,0:T(8,128)(2,1)S(1)} %shard_map.110.own), channel_id=1, source_target_pairs={{0,4},{4,0},{8,12},{12,8},{1,5},{5,1},{9,13},{13,9},{2,6},{6,2},{1... | collective-permute-start | bytes 786440 | tf_op jit(solution)/shard_map/ppermute | solution.py:96
  215.4 35.1 %collective-permute-start.18 = (bf16[32,16,512]{2,1,0:T(8,128)(2,1)S(1)}, bf16[32,16,512]{2,1,0:T(8,128)(2,1)S(1)}, u32[]{:S(2)}, u32[]{:S(2)}) collective-permute-start(bf16[32,16,512]{2,1,0:T(8,128)(2,1)S(1)} %get-tuple-element.116), channel_id=1, source_target_pairs={{0,8},{4,12},{8,0},{12,4},{1,9},{5,13},{9,1},{13,5},{2,10},{6,14},... | collective-permute-start | bytes 1572872 | tf_op jit(solution)/shard_map/ppermute | solution.py:96
  230.3 20.3 %collective-permute-start.17 = (bf16[512,256]{1,0:T(8,128)(2,1)S(1)}, bf16[512,256]{1,0:T(8,128)(2,1)S(1)}, u32[]{:S(2)}, u32[]{:S(2)}) collective-permute-start(bf16[512,256]{1,0:T(8,128)(2,1)S(1)} %collective-permute-done.16.far), channel_id=1, source_target_pairs={{0,4},{4,0},{8,12},{12,8},{1,5},{5,1},{9,13},{13,9},{2,6},{6,2},{1... | collective-permute-start | bytes 786440 | tf_op jit(solution)/shard_map/ppermute | solution.py:96
  250.5 27.7 %copy-start.18 = (bf16[32,16,512]{2,1,0:T(8,128)(2,1)}, bf16[32,16,512]{2,1,0:T(8,128)(2,1)S(1)}, u32[]{:S(2)}) copy-start(bf16[32,16,512]{2,1,0:T(8,128)(2,1)S(1)} %collective-permute-done.18.refs_14_) | copy-start | bytes 1572868
  250.5 27.7 %collective-permute-start.19 = (bf16[32,16,512]{2,1,0:T(8,128)(2,1)S(1)}, bf16[32,16,512]{2,1,0:T(8,128)(2,1)S(1)}, u32[]{:S(2)}, u32[]{:S(2)}) collective-permute-start(bf16[32,16,512]{2,1,0:T(8,128)(2,1)S(1)} %copy-done.24), channel_id=1, source_target_pairs={{0,12},{4,8},{8,4},{12,0},{1,13},{5,9},{9,5},{13,1},{2,14},{6,10},... | collective-permute-start | bytes 1572872 | tf_op jit(solution)/shard_map/ppermute | solution.py:96
  279.1 95.5 %all-to-all-start = ((bf16[4,32,32,512]{3,2,1,0:T(8,128)(2,1)}), bf16[4,32,32,512]{3,2,1,0:T(8,128)(2,1)}, u32[]{:S(2)}, u32[]{:S(2)}) async-start(bf16[4,32,32,512]{3,2,1,0:T(8,128)(2,1)} %get-tuple-element.124), calls=%async_computation | async-start | bytes 8388608 | tf_op jit(solution)/shard_map/all_to_all | solution.py:599
  290.9 8.2 %collective-permute-start.23 = (bf16[16,64,256]{2,1,0:T(8,128)(2,1)S(1)}, bf16[16,64,256]{2,1,0:T(8,128)(2,1)S(1)}, u32[]{:S(2)}, u32[]{:S(2)}) collective-permute-start(bf16[16,64,256]{2,1,0:T(8,128)(2,1)S(1)} %get-tuple-element.133), channel_id=1, source_target_pairs={{0,1},{1,0},{2,3},{3,2},{4,5},{5,4},{6,7},{7,6},{8,9},{9,8},{10,11... | collective-permute-start | bytes 1572872 | tf_op jit(solution)/shard_map/ppermute | solution.py:96
  291.0 8.1 %collective-permute-start.24 = (bf16[16,64,256]{2,1,0:T(8,128)(2,1)S(1)}, bf16[16,64,256]{2,1,0:T(8,128)(2,1)S(1)}, u32[]{:S(2)}, u32[]{:S(2)}) collective-permute-start(bf16[16,64,256]{2,1,0:T(8,128)(2,1)S(1)} %get-tuple-element.134), channel_id=1, source_target_pairs={{0,1},{1,0},{2,3},{3,2},{4,5},{5,4},{6,7},{7,6},{8,9},{9,8},{10,11... | collective-permute-start | bytes 1572872 | tf_op jit(solution)/shard_map/ppermute | solution.py:96
  298.5 4.4 collective-permute-start.20
  298.7 4.2 collective-permute-start.21
  302.4 14.8 %collective-permute-start.25 = (bf16[16,64,256]{2,1,0:T(8,128)(2,1)S(1)}, bf16[16,64,256]{2,1,0:T(8,128)(2,1)S(1)}, u32[]{:S(2)}, u32[]{:S(2)}) collective-permute-start(bf16[16,64,256]{2,1,0:T(8,128)(2,1)S(1)} %get-tuple-element.136), channel_id=1, source_target_pairs={{0,2},{1,3},{2,0},{3,1},{4,6},{5,7},{6,4},{7,5},{8,10},{9,11},{10,... | collective-permute-start | bytes 1572872 | tf_op jit(solution)/shard_map/ppermute | solution.py:96
  306.1 21.4 %collective-permute-start.22 = (bf16[16,64,256]{2,1,0:T(8,128)(2,1)S(1)}, bf16[16,64,256]{2,1,0:T(8,128)(2,1)S(1)}, u32[]{:S(2)}, u32[]{:S(2)}) collective-permute-start(bf16[16,64,256]{2,1,0:T(8,128)(2,1)S(1)} %get-tuple-element.131), channel_id=1, source_target_pairs={{0,2},{1,3},{2,0},{3,1},{4,6},{5,7},{6,4},{7,5},{8,10},{9,11},{10,... | collective-permute-start | bytes 1572872 | tf_op jit(solution)/shard_map/ppermute | solution.py:96
  374.5 73.8 %all-to-all-start.1 = ((bf16[4,24,32,512]{3,2,1,0:T(8,128)(2,1)}), bf16[4,24,32,512]{3,2,1,0:T(8,128)(2,1)S(1)}, u32[]{:S(2)}, u32[]{:S(2)}) async-start(bf16[4,24,32,512]{3,2,1,0:T(8,128)(2,1)} %get-tuple-element.137), calls=%async_computation.1 | async-start | bytes 6291456 | tf_op jit(solution)/shard_map/all_to_all | solution.py:599
  387.9 1.9 collective-permute-start.26
  387.9 2.7 collective-permute-start.27
  393.7 14.0 %collective-permute-start.28 = (bf16[16,64,256]{2,1,0:T(8,128)(2,1)S(1)}, bf16[16,64,256]{2,1,0:T(8,128)(2,1)S(1)}, u32[]{:S(2)}, u32[]{:S(2)}) collective-permute-start(bf16[16,64,256]{2,1,0:T(8,128)(2,1)S(1)} %get-tuple-element.142), channel_id=1, source_target_pairs={{0,2},{1,3},{2,0},{3,1},{4,6},{5,7},{6,4},{7,5},{8,10},{9,11},{10,... | collective-permute-start | bytes 1572872 | tf_op jit(solution)/shard_map/ppermute | solution.py:96
  450.0 28.7 %all-to-all-start.2 = ((bf16[4,8,32,512]{3,2,1,0:T(8,128)(2,1)}), bf16[4,8,32,512]{3,2,1,0:T(8,128)(2,1)S(1)}, u32[]{:S(2)}, u32[]{:S(2)}) async-start(bf16[4,8,32,512]{3,2,1,0:T(8,128)(2,1)} %get-tuple-element.143), calls=%async_computation.2 | async-start | bytes 2097152 | tf_op jit(solution)/shard_map/all_to_all | solution.py:599
  462.0 1.7 collective-permute-start.32
  462.0 2.3 collective-permute-start.33
  466.4 19.0 %collective-permute-start.34 = (bf16[12,64,256]{2,1,0:T(8,128)(2,1)S(1)}, bf16[12,64,256]{2,1,0:T(8,128)(2,1)S(1)}, u32[]{:S(2)}, u32[]{:S(2)}) collective-permute-start(bf16[12,64,256]{2,1,0:T(8,128)(2,1)S(1)} %get-tuple-element.156), channel_id=1, source_target_pairs={{0,2},{1,3},{2,0},{3,1},{4,6},{5,7},{6,4},{7,5},{8,10},{9,11},{10,... | collective-permute-start | bytes 1179656 | tf_op jit(solution)/shard_map/ppermute | solution.py:96
  482.7 1.3 collective-permute-start.29
  482.7 1.5 collective-permute-start.30
  484.9 5.8 %collective-permute-start.31 = (bf16[4,64,256]{2,1,0:T(8,128)(2,1)S(1)}, bf16[4,64,256]{2,1,0:T(8,128)(2,1)S(1)}, u32[]{:S(2)}, u32[]{:S(2)}) collective-permute-start(bf16[4,64,256]{2,1,0:T(8,128)(2,1)S(1)} %get-tuple-element.151), channel_id=1, source_target_pairs={{0,2},{1,3},{2,0},{3,1},{4,6},{5,7},{6,4},{7,5},{8,10},{9,11},{10,... | collective-permute-start | bytes 393224 | tf_op jit(solution)/shard_map/ppermute | solution.py:96
  (15 other events, 44.3 us)

commit v5 on v4

--- a/solution.py
+++ b/solution.py
@@ -268,14 +268,18 @@
 
 
 def add_call(me, keep, came):
-    shape = keep.shape
+    _, rows, columns = keep.shape
+    some = rows // 4
+    two = spec((2, some, columns), lambda i, _: (0, i, 0))
+    one = spec((some, columns), lambda i, _: (i, 0))
     return call(
         add_kernel,
         me,
         (keep, came),
-        [whole(shape), whole(shape)],
-        [array(shape[1:], F32), array(shape[1:], BF16)],
-        [whole(shape[1:])] * 2,
+        [two, two],
+        [array((rows, columns), F32), array((rows, columns), BF16)],
+        [one, one],
+        grid=(4,),
     )
 
 
@@ -342,14 +346,16 @@
 
 def split_call(me, mine, came):
     rows, columns = mine.shape
-    shapes = ((rows, columns // 3), (rows, 2 * columns // 3))
+    wides = (columns // 3, 2 * columns // 3)
+    some = rows // 4
     return call(
         split_kernel,
         me,
         (mine, came),
-        [whole(mine.shape)] * 2,
-        [array(shape, BF16) for shape in shapes],
-        [whole(shape) for shape in shapes],
+        [spec((some, columns), lambda i, _: (i, 0))] * 2,
+        [array((rows, wide), BF16) for wide in wides],
+        [spec((some, wide), lambda i, _: (i, 0)) for wide in wides],
+        grid=(4,),
     )
 
 
@@ -559,38 +565,45 @@
         back[part][bits] = flip(after(sends[part][bits], *earlier), "gene", bits)
         return back[part][bits]
 
+    def begin_pair(part, pair, *earlier):
+        ends = [pair, pair[::-1]]
+        return lax.ppermute(after(sends[part][3], *earlier), "gene", ends)
+
     prepare(0)
-    first_part = [begin(0, bits) for bits in (3, 2, 1)]
+    beside_qkv = [begin(0, bits) for bits in (3, 2, 1)]
+    prepare(1, sends[0][0])
     masked, send, keep = project_call(
-        me, after(expression, sends[0][0]), gene_mask, mask_value, w_qkv
-    )
-    came = flip(after(send, *first_part), "gene", 1)
-    prepare(1, send)
-    beside_sum = [begin(1, 2), begin(1, 3)]
-    mine, other = add_call(me, keep, after(came, *beside_sum))
+        me, after(expression, sends[1][0]), gene_mask, mask_value, w_qkv
+    )
+    came = flip(after(send, *beside_qkv), "gene", 1)
+    beside_sum = [begin(1, bits, send, *beside_qkv) for bits in (2, 3)]
+    prepare(2, send)
+    middle = begin_pair(2, (1, 2))
+    prepare(3, sends[2][0])
+    w_first_t = jnp.swapaxes(after(w_first, send), 1, 2)
+    mine, other = add_call(
+        me, keep, after(came, *beside_sum, middle, sends[3][0], w_first_t)
+    )
     last = flip(other, "gene", 2)
-    prepare(2, other)
-    prepare(3, sends[2][0])
-    w_first_t = jnp.swapaxes(after(w_first, other), 1, 2)
-    beside_sum = [begin(1, 1, other)]
-    queries, key_value = split_call(
-        me, mine, after(last, *beside_sum, sends[3][0], w_first_t)
-    )
+    beside_sum = [begin(2, 2, other), begin(1, 1, other)]
+    queries, key_value = split_call(me, mine, after(last, *beside_sum))
     across = flip(key_value, "cell", 2)
     beside = flip(key_value, "cell", 1)
     corner = flip(across, "cell", 1)
-    beside_keys = [begin(2, 2, last), begin(2, 1, last)]
-    queries = after(queries, *beside_keys, beside, across, corner)
+    outer = begin_pair(2, (0, 3), last)
+    inner = (me[0] == 1) | (me[0] == 2)
+    back[2][3] = jnp.where(inner, middle, outer)
+    queries = after(queries, outer, begin(2, 1, last), beside, across, corner)
     attended = attend_call(me, queries, (key_value, beside, across, corner))
-    attended = after(attended, begin(2, 3, queries), begin(3, 1, queries))
     near = flip(attended, "gene", 1)
     far = flip(attended, "gene", 2)
     rest = flip(after(far, near), "gene", 1)
-    rest = after(rest, begin(3, 2, attended))
+    rest = after(rest, begin(3, 2, queries))
     hidden, first = first_call(
         me, matrix, (attended, near, far, rest), w_out, masked, w_first_t, deeps
     )
     begin(3, 3, rest)
+    begin(3, 1, rest)
 
     got = []
 
@@ -598,7 +611,7 @@
         piece = after(first[t], *earlier)
         got.append(lax.all_to_all(piece, "gene", split_axis=0, concat_axis=0, tiled=True))
 
-    launch(0, back[3][3])
+    launch(0, back[3][3], back[3][1])
     denoised, shares = None, [None, None]
     back = sum(back, [])
 

time: 493 us -> 510 us (1.034)
  waiting for transfers between devices: 269 us -> 283 us
    ppermute x0 -> x2, waiting for transfers between devices: none -> 7.37 us  [begin_pair(): return lax.ppermute(after(sends[part][3], *earlier), 'gene', ends)]
    ppermute x35 -> x34, waiting for transfers between devices: 174 us -> 179 us  [flip(): return lax.ppermute(value, axis, pairs)]
    ppermute x35 -> x34, starting transfers between devices: 41.1 us -> 38 us  [flip(): return lax.ppermute(value, axis, pairs)]
    unnamed x50 -> x56, local copies, waits for them, and re-layouts: 10.9 us -> 8.13 us
  transfers between devices with their start and end apart: 38 -> 39, of which waited for: 25 -> 22; matrix products, arithmetic and copies ran while one was open for 1% -> 1% of each run, Pallas kernels for 28% -> 26%
where the time goes in v5:
time: 510 us; the launch traced here: 509 us
  waiting for transfers between devices  283 us (55%)
  Pallas kernels  153 us (30%)
  starting transfers between devices  56.2 us (11%)
  local copies, waits for them, and re-layouts  14.6 us (3%)
    ppermute x34, waiting for transfers between devices, flip(): return lax.ppermute(value, axis, pairs)  179 us
    pallas_call x24, Pallas kernels, call(): pl.pallas_call(body, out_shape=outs, grid_spec=pltpu.PrefetchScalarGridSp...  153 us
    all_to_all x3, waiting for transfers between devices, launch(): lax.all_to_all(piece, 'gene', split_axis=0, concat_axis=0, tiled=True)  97 us
    ppermute x34, starting transfers between devices, flip(): return lax.ppermute(value, axis, pairs)  38 us
    all_to_all x3, starting transfers between devices, launch(): lax.all_to_all(piece, 'gene', split_axis=0, concat_axis=0, tiled=True)  13.4 us
  transfers between devices with their start and end apart: 39, of which 22 were waited for; matrix products, arithmetic and copies ran while one was open for 1% of the time, Pallas kernels for 26%

profile of v5, /device:TPU:0, one launch (start us, length us, event | category | flops | bytes accessed | tf_op | source)
XLA Modules:
  0.0 509.0 jit_solution(5910037290464844053)
XLA Ops:
  1.0 4.4 shard_map.103
  5.5 4.0 collective-permute-start.1
  11.1 4.6 shard_map.104
  16.5 37.8 %shard_map.105 = (bf16[512,8192]{1,0:T(8,128)(2,1)}, bf16[2,512,768]{2,1,0:T(8,128)(2,1)S(1)}, f32[2,512,768]{2,1,0:T(8,128)}) custom-call(s32[2]{0:T(128)S(1)} %pad_add_fusion.me_ref._, bf16[512,8192]{1,0:T(8,128)(2,1)} %value_ref, s32[512,8192]{1,0:T(8,128)} %mask_ref.1, bf16[1,8192]{1,0:T(2,128)(2,1)S(1)} %reshape.9.fill_ref, bf16[8192,3072]{1,0:T(8,128)(2,1)} %weight_ref.1), custom_call_target="tpu_custom_call" | custom-call | flops 1 | bytes 1 | tf_op jit(solution)/shard_map/pallas_call | solution.py:100
  54.4 1.9 collective-permute-start.3
  56.2 4.5 shard_map.106
  64.5 2.4 collective-permute-start.4
  66.9 2.9 collective-permute-start.5
  69.8 4.5 shard_map.107
  75.1 6.5 %copy.16 = bf16[32,256,256]{1,2,0:T(8,128)(2,1)} copy(bf16[32,256,256]{2,1,0:T(8,128)(2,1)} %param.13) | data formatting | bytes 8388608 | tf_op jit(solution)/shard_map/optimization_barrier | solution.py:91
  81.6 20.8 %collective-permute-done.4.refs_6_ = bf16[32,16,512]{2,1,0:T(8,128)(2,1)} collective-permute-done((bf16[32,16,512]{2,1,0:T(8,128)(2,1)}, bf16[32,16,512]{2,1,0:T(8,128)(2,1)}, u32[]{:S(2)}, u32[]{:S(2)}) %collective-permute-start.4) | collective-permute-done | bytes 524320 | tf_op jit(solution)/shard_map/ppermute | solution.py:96
  102.4 13.9 %collective-permute-done.5.refs_7_ = bf16[32,16,512]{2,1,0:T(8,128)(2,1)} collective-permute-done((bf16[32,16,512]{2,1,0:T(8,128)(2,1)}, bf16[32,16,512]{2,1,0:T(8,128)(2,1)}, u32[]{:S(2)}, u32[]{:S(2)}) %collective-permute-start.5) | collective-permute-done | bytes 524320 | tf_op jit(solution)/shard_map/ppermute | solution.py:96
  116.3 4.7 shard_map.108
  121.0 9.5 %collective-permute-start.7 = (bf16[512,768]{1,0:T(8,128)(2,1)S(1)}, bf16[512,768]{1,0:T(8,128)(2,1)S(1)}, u32[]{:S(2)}, u32[]{:S(2)}) collective-permute-start(bf16[512,768]{1,0:T(8,128)(2,1)S(1)} %get-tuple-element.103), channel_id=1, source_target_pairs={{0,8},{4,12},{8,0},{12,4},{1,9},{5,13},{9,1},{13,5},{2,10},{6,14},... | collective-permute-start | bytes 2359304 | tf_op jit(solution)/shard_map/ppermute | solution.py:96
  130.6 1.7 collective-permute-start.9
  132.3 54.4 %collective-permute-done.8.refs_10_ = bf16[32,16,512]{2,1,0:T(8,128)(2,1)S(1)} collective-permute-done((bf16[32,16,512]{2,1,0:T(8,128)(2,1)S(1)}, bf16[32,16,512]{2,1,0:T(8,128)(2,1)S(1)}, u32[]{:S(2)}, u32[]{:S(2)}) %collective-permute-start.8) | collective-permute-done | bytes 524320 | tf_op jit(solution)/shard_map/ppermute | solution.py:96
  186.7 3.9 shard_map.109
  192.2 3.4 collective-permute-start.10
  195.7 7.5 %collective-permute-done.13.refs_2_ = bf16[512,512]{1,0:T(8,128)(2,1)S(1)} collective-permute-done((bf16[512,512]{1,0:T(8,128)(2,1)S(1)}, bf16[512,512]{1,0:T(8,128)(2,1)S(1)}, u32[]{:S(2)}, u32[]{:S(2)}) %collective-permute-start.13) | collective-permute-done | bytes 524320 | tf_op jit(solution)/shard_map/ppermute | solution.py:96
  203.2 7.4 %collective-permute-done.10 = bf16[32,16,512]{2,1,0:T(8,128)(2,1)S(1)} collective-permute-done((bf16[32,16,512]{2,1,0:T(8,128)(2,1)S(1)}, bf16[32,16,512]{2,1,0:T(8,128)(2,1)S(1)}, u32[]{:S(2)}, u32[]{:S(2)}) %collective-permute-start.10) | collective-permute-done | bytes 524320 | tf_op jit(solution)/shard_map/ppermute | solution.py:570
  210.6 10.4 %collective-permute-done.11.refs_9_ = bf16[32,16,512]{2,1,0:T(8,128)(2,1)S(1)} collective-permute-done((bf16[32,16,512]{2,1,0:T(8,128)(2,1)S(1)}, bf16[32,16,512]{2,1,0:T(8,128)(2,1)S(1)}, u32[]{:S(2)}, u32[]{:S(2)}) %collective-permute-start.11) | collective-permute-done | bytes 524320 | tf_op jit(solution)/shard_map/ppermute | solution.py:96
  221.8 7.1 %shard_map.110.own = bf16[512,256]{1,0:T(8,128)(2,1)S(1)} custom-call(s32[2]{0:T(128)S(1)} %pad_add_fusion.me_ref._, bf16[512,256]{1,0:T(8,128)(2,1)S(1)} %get-tuple-element.114.query_ref, bf16[512,512]{1,0:T(8,128)(2,1)S(1)} %get-tuple-element.113.refs_0_, bf16[512,512]{1,0:T(8,128)(2,1)S(1)} %collective-permute-done.12.refs_1_, ...), custom_call_target="tpu_custom_call" | custom-call | flops 1 | bytes 1 | tf_op jit(solution)/shard_map/pallas_call | solution.py:100
  232.1 12.4 %collective-permute-done.16.far = bf16[512,256]{1,0:T(8,128)(2,1)S(1)} collective-permute-done((bf16[512,256]{1,0:T(8,128)(2,1)S(1)}, bf16[512,256]{1,0:T(8,128)(2,1)S(1)}, u32[]{:S(2)}, u32[]{:S(2)}) %collective-permute-start.16) | collective-permute-done | bytes 262176 | tf_op jit(solution)/shard_map/ppermute | solution.py:96
  244.9 20.7 %collective-permute-done.18.refs_14_ = bf16[32,16,512]{2,1,0:T(8,128)(2,1)S(1)} collective-permute-done((bf16[32,16,512]{2,1,0:T(8,128)(2,1)S(1)}, bf16[32,16,512]{2,1,0:T(8,128)(2,1)S(1)}, u32[]{:S(2)}, u32[]{:S(2)}) %collective-permute-start.18) | collective-permute-done | bytes 524320 | tf_op jit(solution)/shard_map/ppermute | solution.py:96
  265.7 2.3 collective-permute-start.19
  268.0 24.5 %shard_map.111 = (bf16[512,8192]{1,0:T(8,128)(2,1)}, bf16[4,32,32,512]{3,2,1,0:T(8,128)(2,1)}, bf16[4,24,32,512]{3,2,1,0:T(8,128)(2,1)}, bf16[4,8,32,512]{3,2,1,0:T(8,128)(2,1)}) custom-call(s32[2]{0:T(128)S(1)} %pad_add_fusion.me_ref._, bf16[256,256]{1,0:T(8,128)(2,1)S(1)} %fusion.turn_ref, bf16[512,256]{1,0:T(8,128)(2,1)S(1)} %shard_map.110.own, ...), custom_call_target="tpu_custom_call" | custom-call | flops 1 | bytes 1 | tf_op jit(solution)/shard_map/pallas_call | solution.py:100
  293.6 5.0 all-to-all-start
  299.5 7.0 %shard_map.114 = (bf16[16,64,256]{2,1,0:T(8,128)(2,1)S(1)}, bf16[16,64,256]{2,1,0:T(8,128)(2,1)S(1)}, f32[2,16,64,256]{3,2,1,0:T(8,128)}) custom-call(s32[2]{0:T(128)S(1)} %pad_add_fusion.me_ref._, bf16[32,16,512]{2,1,0:T(8,128)(2,1)S(1)} %get-tuple-element.81.refs_0_, bf16[32,16,512]{2,1,0:T(8,128)(2,1)} %copy-done.14, bf16[32,16,512]{2,1,0:T(8,128)(2,1)} %copy-done.12, ...), custom_call_target="tpu_custom_call" | custom-call | flops 1 | bytes 1 | tf_op jit(solution)/shard_map/pallas_call | solution.py:100
  307.0 7.0 %shard_map.112 = (bf16[16,64,256]{2,1,0:T(8,128)(2,1)S(1)}, bf16[16,64,256]{2,1,0:T(8,128)(2,1)S(1)}, f32[2,16,64,256]{3,2,1,0:T(8,128)}) custom-call(s32[2]{0:T(128)S(1)} %pad_add_fusion.me_ref._, bf16[32,16,512]{2,1,0:T(8,128)(2,1)S(1)} %get-tuple-element.81.refs_0_, bf16[32,16,512]{2,1,0:T(8,128)(2,1)} %copy-done.14, bf16[32,16,512]{2,1,0:T(8,128)(2,1)} %copy-done.12, ...), custom_call_target="tpu_custom_call" | custom-call | flops 1 | bytes 1 | tf_op jit(solution)/shard_map/pallas_call | solution.py:100
  314.6 3.2 shard_map.115
  318.4 3.2 shard_map.113
  323.1 9.5 %collective-permute-done.26.came_ref = bf16[16,64,256]{2,1,0:T(8,128)(2,1)S(1)} collective-permute-done((bf16[16,64,256]{2,1,0:T(8,128)(2,1)S(1)}, bf16[16,64,256]{2,1,0:T(8,128)(2,1)S(1)}, u32[]{:S(2)}, u32[]{:S(2)}) %collective-permute-start.26) | collective-permute-done | bytes 524320 | tf_op jit(solution)/shard_map/ppermute | solution.py:96
  333.9 1.6 shard_map.116.refs_0_
  335.5 7.5 %collective-permute-done.23.came_ref = bf16[16,64,256]{2,1,0:T(8,128)(2,1)S(1)} collective-permute-done((bf16[16,64,256]{2,1,0:T(8,128)(2,1)S(1)}, bf16[16,64,256]{2,1,0:T(8,128)(2,1)S(1)}, u32[]{:S(2)}, u32[]{:S(2)}) %collective-permute-start.23) | collective-permute-done | bytes 524320 | tf_op jit(solution)/shard_map/ppermute | solution.py:96
  343.0 1.6 shard_map.117
  344.6 47.6 %all-to-all-done.refs_0_ = bf16[4,32,32,512]{3,2,1,0:T(8,128)(2,1)} async-done(((bf16[4,32,32,512]{3,2,1,0:T(8,128)(2,1)}), bf16[4,32,32,512]{3,2,1,0:T(8,128)(2,1)}, u32[]{:S(2)}, u32[]{:S(2)}) %all-to-all-start) | async-done | bytes 4194336 | tf_op jit(solution)/shard_map/all_to_all | solution.py:612
  392.2 4.9 all-to-all-start.1
  397.0 9.6 %shard_map.118 = (bf16[512,8192]{1,0:T(8,128)(2,1)}, bf16[16,64,256]{2,1,0:T(8,128)(2,1)S(1)}, bf16[16,64,256]{2,1,0:T(8,128)(2,1)S(1)}, f32[2,16,64,256]{3,2,1,0:T(8,128)}) custom-call(s32[2]{0:T(128)S(1)} %pad_add_fusion.me_ref._, bf16[4,32,32,512]{3,2,1,0:T(8,128)(2,1)} %all-to-all-done.refs_0_, bf16[32,256,256]{2,1,0:T(8,128)(2,1)} %refs_1_.5, ...), custom_call_target="tpu_custom_call" | custom-call | flops 1 | bytes 1 | tf_op jit(solution)/shard_map/pallas_call | solution.py:100
  409.3 3.3 shard_map.119
  413.1 13.4 %collective-permute-done.29.came_ref = bf16[16,64,256]{2,1,0:T(8,128)(2,1)S(1)} collective-permute-done((bf16[16,64,256]{2,1,0:T(8,128)(2,1)S(1)}, bf16[16,64,256]{2,1,0:T(8,128)(2,1)S(1)}, u32[]{:S(2)}, u32[]{:S(2)}) %collective-permute-start.29) | collective-permute-done | bytes 524320 | tf_op jit(solution)/shard_map/ppermute | solution.py:96
  429.4 37.8 %all-to-all-done.1.refs_0_ = bf16[4,24,32,512]{3,2,1,0:T(8,128)(2,1)} async-done(((bf16[4,24,32,512]{3,2,1,0:T(8,128)(2,1)}), bf16[4,24,32,512]{3,2,1,0:T(8,128)(2,1)}, u32[]{:S(2)}, u32[]{:S(2)}) %all-to-all-start.1) | async-done | bytes 3145760 | tf_op jit(solution)/shard_map/all_to_all | solution.py:612
  467.1 3.5 all-to-all-start.2
  470.6 8.5 %shard_map.121 = (bf16[512,8192]{1,0:T(8,128)(2,1)}, bf16[12,64,256]{2,1,0:T(8,128)(2,1)S(1)}, bf16[12,64,256]{2,1,0:T(8,128)(2,1)S(1)}, f32[2,12,64,256]{3,2,1,0:T(8,128)}) custom-call(s32[2]{0:T(128)S(1)} %pad_add_fusion.me_ref._, bf16[4,24,32,512]{3,2,1,0:T(8,128)(2,1)} %all-to-all-done.1.refs_0_, ...), custom_call_target="tpu_custom_call", output_to_operand_aliasing={{0}: (5, {})} | custom-call | flops 1 | bytes 1 | tf_op jit(solution)/shard_map/pallas_call | solution.py:100
  481.4 2.1 shard_map.124
  484.1 11.7 %all-to-all-done.2.refs_0_ = bf16[4,8,32,512]{3,2,1,0:T(8,128)(2,1)S(1)} async-done(((bf16[4,8,32,512]{3,2,1,0:T(8,128)(2,1)}), bf16[4,8,32,512]{3,2,1,0:T(8,128)(2,1)S(1)}, u32[]{:S(2)}, u32[]{:S(2)}) %all-to-all-start.2) | async-done | bytes 1048608 | tf_op jit(solution)/shard_map/all_to_all | solution.py:612
  495.8 4.0 shard_map.122
  502.6 2.0 shard_map.125.refs_0_
  504.6 3.2 collective-permute-done.32.came_ref
  (118 shorter events, 32.8 us)
Async XLA Ops:
  5.5 48.8 %collective-permute-start.1 = (bf16[32,16,512]{2,1,0:T(8,128)(2,1)S(1)}, bf16[32,16,512]{2,1,0:T(8,128)(2,1)S(1)}, u32[]{:S(2)}, u32[]{:S(2)}) collective-permute-start(bf16[32,16,512]{2,1,0:T(8,128)(2,1)S(1)} %get-tuple-element.88), channel_id=1, source_target_pairs={{0,8},{4,12},{8,0},{12,4},{1,9},{5,13},{9,1},{13,5},{2,10},{6,14},... | collective-permute-start | bytes 1572872 | tf_op jit(solution)/shard_map/ppermute | solution.py:96
  9.5 44.8 %collective-permute-start = (bf16[32,16,512]{2,1,0:T(8,128)(2,1)}, bf16[32,16,512]{2,1,0:T(8,128)(2,1)S(1)}, u32[]{:S(2)}, u32[]{:S(2)}) collective-permute-start(bf16[32,16,512]{2,1,0:T(8,128)(2,1)} %get-tuple-element.87), channel_id=1, source_target_pairs={{0,12},{4,8},{8,4},{12,0},{1,13},{5,9},{9,5},{13,1},{2,14},{6,10},... | collective-permute-start | bytes 1572872 | tf_op jit(solution)/shard_map/ppermute | solution.py:96
  10.9 43.5 %collective-permute-start.2 = (bf16[32,16,512]{2,1,0:T(8,128)(2,1)S(1)}, bf16[32,16,512]{2,1,0:T(8,128)(2,1)S(1)}, u32[]{:S(2)}, u32[]{:S(2)}) collective-permute-start(bf16[32,16,512]{2,1,0:T(8,128)(2,1)S(1)} %get-tuple-element.89), channel_id=1, source_target_pairs={{0,4},{4,0},{8,12},{12,8},{1,5},{5,1},{9,13},{13,9},{2,6},{6,2},{1... | collective-permute-start | bytes 1572872 | tf_op jit(solution)/shard_map/ppermute | solution.py:96
  54.4 62.0 %collective-permute-start.3 = (bf16[2,512,768]{2,1,0:T(8,128)(2,1)S(1)}, bf16[2,512,768]{2,1,0:T(8,128)(2,1)}, u32[]{:S(2)}, u32[]{:S(2)}) collective-permute-start(bf16[2,512,768]{2,1,0:T(8,128)(2,1)S(1)} %get-tuple-element.90), channel_id=1, source_target_pairs={{0,4},{4,0},{8,12},{12,8},{1,5},{5,1},{9,13},{13,9},{2,6},{6,2},{1... | collective-permute-start | bytes 4718600 | tf_op jit(solution)/shard_map/ppermute | solution.py:96
  63.1 18.5 %collective-permute-start.6 = (bf16[32,16,512]{2,1,0:T(8,128)(2,1)}, bf16[32,16,512]{2,1,0:T(8,128)(2,1)}, u32[]{:S(2)}, u32[]{:S(2)}) collective-permute-start(bf16[32,16,512]{2,1,0:T(8,128)(2,1)} %get-tuple-element.110), channel_id=1, source_target_pairs={{4,8},{8,4},{5,9},{9,5},{6,10},{10,6},{7,11},{11,7},{20,24},{24,20... | collective-permute-start | bytes 1572872 | tf_op jit(solution)/shard_map/ppermute | solution.py:570
  64.5 37.9 %collective-permute-start.4 = (bf16[32,16,512]{2,1,0:T(8,128)(2,1)}, bf16[32,16,512]{2,1,0:T(8,128)(2,1)}, u32[]{:S(2)}, u32[]{:S(2)}) collective-permute-start(bf16[32,16,512]{2,1,0:T(8,128)(2,1)} %get-tuple-element.92), channel_id=1, source_target_pairs={{0,8},{4,12},{8,0},{12,4},{1,9},{5,13},{9,1},{13,5},{2,10},{6,14},... | collective-permute-start | bytes 1572872 | tf_op jit(solution)/shard_map/ppermute | solution.py:96
  66.9 49.4 %collective-permute-start.5 = (bf16[32,16,512]{2,1,0:T(8,128)(2,1)}, bf16[32,16,512]{2,1,0:T(8,128)(2,1)}, u32[]{:S(2)}, u32[]{:S(2)}) collective-permute-start(bf16[32,16,512]{2,1,0:T(8,128)(2,1)} %get-tuple-element.94), channel_id=1, source_target_pairs={{0,12},{4,8},{8,4},{12,0},{1,13},{5,9},{9,5},{13,1},{2,14},{6,10},... | collective-permute-start | bytes 1572872 | tf_op jit(solution)/shard_map/ppermute | solution.py:96
  81.6 48.9 %copy-start.11 = (bf16[32,16,512]{2,1,0:T(8,128)(2,1)S(1)}, bf16[32,16,512]{2,1,0:T(8,128)(2,1)}, u32[]{:S(2)}) copy-start(bf16[32,16,512]{2,1,0:T(8,128)(2,1)} %copy-done.10) | copy-start | bytes 1572868
  81.6 49.0 %copy-start.9 = (bf16[32,16,512]{2,1,0:T(8,128)(2,1)S(1)}, bf16[32,16,512]{2,1,0:T(8,128)(2,1)}, u32[]{:S(2)}) copy-start(bf16[32,16,512]{2,1,0:T(8,128)(2,1)} %copy-done.8) | copy-start | bytes 1572868
  81.6 110.6 %copy-start.27 = (bf16[32,16,512]{2,1,0:T(8,128)(2,1)S(1)}, bf16[32,16,512]{2,1,0:T(8,128)(2,1)}, u32[]{:S(2)}) copy-start(bf16[32,16,512]{2,1,0:T(8,128)(2,1)} %get-tuple-element.110) | copy-start | bytes 1572868
  81.6 114.1 %copy-start.7 = (bf16[32,16,512]{2,1,0:T(8,128)(2,1)S(1)}, bf16[32,16,512]{2,1,0:T(8,128)(2,1)}, u32[]{:S(2)}) copy-start(bf16[32,16,512]{2,1,0:T(8,128)(2,1)} %copy-done.6) | copy-start | bytes 1572868
  116.3 149.3 %copy-start.26 = (bf16[32,16,512]{2,1,0:T(8,128)(2,1)S(1)}, bf16[32,16,512]{2,1,0:T(8,128)(2,1)}, u32[]{:S(2)}) copy-start(bf16[32,16,512]{2,1,0:T(8,128)(2,1)} %get-tuple-element.124) | copy-start | bytes 1572868
  121.0 65.6 %collective-permute-start.7 = (bf16[512,768]{1,0:T(8,128)(2,1)S(1)}, bf16[512,768]{1,0:T(8,128)(2,1)S(1)}, u32[]{:S(2)}, u32[]{:S(2)}) collective-permute-start(bf16[512,768]{1,0:T(8,128)(2,1)S(1)} %get-tuple-element.103), channel_id=1, source_target_pairs={{0,8},{4,12},{8,0},{12,4},{1,9},{5,13},{9,1},{13,5},{2,10},{6,14},... | collective-permute-start | bytes 2359304 | tf_op jit(solution)/shard_map/ppermute | solution.py:96
  130.5 56.2 %collective-permute-start.8 = (bf16[32,16,512]{2,1,0:T(8,128)(2,1)S(1)}, bf16[32,16,512]{2,1,0:T(8,128)(2,1)S(1)}, u32[]{:S(2)}, u32[]{:S(2)}) collective-permute-start(bf16[32,16,512]{2,1,0:T(8,128)(2,1)S(1)} %copy-done.11), channel_id=1, source_target_pairs={{0,8},{4,12},{8,0},{12,4},{1,9},{5,13},{9,1},{13,5},{2,10},{6,14},... | collective-permute-start | bytes 1572872 | tf_op jit(solution)/shard_map/ppermute | solution.py:96
  130.6 56.1 %collective-permute-start.9 = (bf16[32,16,512]{2,1,0:T(8,128)(2,1)S(1)}, bf16[32,16,512]{2,1,0:T(8,128)(2,1)S(1)}, u32[]{:S(2)}, u32[]{:S(2)}) collective-permute-start(bf16[32,16,512]{2,1,0:T(8,128)(2,1)S(1)} %copy-done.9), channel_id=1, source_target_pairs={{0,4},{4,0},{8,12},{12,8},{1,5},{5,1},{9,13},{13,9},{2,6},{6,2},{1... | collective-permute-start | bytes 1572872 | tf_op jit(solution)/shard_map/ppermute | solution.py:96
  186.7 105.8 %copy-start.15 = (bf16[32,16,512]{2,1,0:T(8,128)(2,1)}, bf16[32,16,512]{2,1,0:T(8,128)(2,1)S(1)}, u32[]{:S(2)}) copy-start(bf16[32,16,512]{2,1,0:T(8,128)(2,1)S(1)} %collective-permute-done.8.refs_10_) | copy-start | bytes 1572868
  186.7 105.8 %copy-start.16 = (bf16[32,16,512]{2,1,0:T(8,128)(2,1)}, bf16[32,16,512]{2,1,0:T(8,128)(2,1)S(1)}, u32[]{:S(2)}) copy-start(bf16[32,16,512]{2,1,0:T(8,128)(2,1)S(1)} %collective-permute-done.9.refs_5_) | copy-start | bytes 1572868
  190.6 12.6 %collective-permute-start.13 = (bf16[512,512]{1,0:T(8,128)(2,1)S(1)}, bf16[512,512]{1,0:T(8,128)(2,1)S(1)}, u32[]{:S(2)}, u32[]{:S(2)}) collective-permute-start(bf16[512,512]{1,0:T(8,128)(2,1)S(1)} %get-tuple-element.113.refs_0_), channel_id=1, source_target_pairs={{0,2},{1,3},{2,0},{3,1},{4,6},{5,7},{6,4},{7,5},{8,10},{9,11},{10,... | collective-permute-start | bytes 1572872 | tf_op jit(solution)/shard_map/ppermute | solution.py:96
  192.2 11.0 %collective-permute-start.12 = (bf16[512,512]{1,0:T(8,128)(2,1)S(1)}, bf16[512,512]{1,0:T(8,128)(2,1)S(1)}, u32[]{:S(2)}, u32[]{:S(2)}) collective-permute-start(bf16[512,512]{1,0:T(8,128)(2,1)S(1)} %get-tuple-element.113.refs_0_), channel_id=1, source_target_pairs={{0,1},{1,0},{2,3},{3,2},{4,5},{5,4},{6,7},{7,6},{8,9},{9,8},{10,11... | collective-permute-start | bytes 1572872 | tf_op jit(solution)/shard_map/ppermute | solution.py:96
  192.2 18.4 %collective-permute-start.10 = (bf16[32,16,512]{2,1,0:T(8,128)(2,1)S(1)}, bf16[32,16,512]{2,1,0:T(8,128)(2,1)S(1)}, u32[]{:S(2)}, u32[]{:S(2)}) collective-permute-start(bf16[32,16,512]{2,1,0:T(8,128)(2,1)S(1)} %copy-done.27), channel_id=1, source_target_pairs={{0,12},{12,0},{1,13},{13,1},{2,14},{14,2},{3,15},{15,3},{16,28},{2... | collective-permute-start | bytes 1572872 | tf_op jit(solution)/shard_map/ppermute | solution.py:570
  195.6 25.4 %collective-permute-start.11 = (bf16[32,16,512]{2,1,0:T(8,128)(2,1)S(1)}, bf16[32,16,512]{2,1,0:T(8,128)(2,1)S(1)}, u32[]{:S(2)}, u32[]{:S(2)}) collective-permute-start(bf16[32,16,512]{2,1,0:T(8,128)(2,1)S(1)} %copy-done.7), channel_id=1, source_target_pairs={{0,4},{4,0},{8,12},{12,8},{1,5},{5,1},{9,13},{13,9},{2,6},{6,2},{1... | collective-permute-start | bytes 1572872 | tf_op jit(solution)/shard_map/ppermute | solution.py:96
  203.2 17.8 %collective-permute-start.14 = (bf16[512,512]{1,0:T(8,128)(2,1)S(1)}, bf16[512,512]{1,0:T(8,128)(2,1)S(1)}, u32[]{:S(2)}, u32[]{:S(2)}) collective-permute-start(bf16[512,512]{1,0:T(8,128)(2,1)S(1)} %collective-permute-done.13.refs_2_), channel_id=1, source_target_pairs={{0,1},{1,0},{2,3},{3,2},{4,5},{5,4},{6,7},{7,6},{8,9},{9,8},{10,11... | collective-permute-start | bytes 1572872 | tf_op jit(solution)/shard_map/ppermute | solution.py:96
  210.6 55.0 %copy-start.21 = (bf16[32,16,512]{2,1,0:T(8,128)(2,1)}, bf16[32,16,512]{2,1,0:T(8,128)(2,1)S(1)}, u32[]{:S(2)}) copy-start(bf16[32,16,512]{2,1,0:T(8,128)(2,1)S(1)} %collective-permute-done.10) | copy-start | bytes 1572868
  221.0 71.5 %copy-start.17 = (bf16[32,16,512]{2,1,0:T(8,128)(2,1)}, bf16[32,16,512]{2,1,0:T(8,128)(2,1)S(1)}, u32[]{:S(2)}) copy-start(bf16[32,16,512]{2,1,0:T(8,128)(2,1)S(1)} %collective-permute-done.11.refs_9_) | copy-start | bytes 1572868
  229.0 15.6 %collective-permute-start.16 = (bf16[512,256]{1,0:T(8,128)(2,1)S(1)}, bf16[512,256]{1,0:T(8,128)(2,1)S(1)}, u32[]{:S(2)}, u32[]{:S(2)}) collective-permute-start(bf16[512,256]{1,0:T(8,128)(2,1)S(1)} %shard_map.110.own), channel_id=1, source_target_pairs={{0,8},{4,12},{8,0},{12,4},{1,9},{5,13},{9,1},{13,5},{2,10},{6,14},... | collective-permute-start | bytes 786440 | tf_op jit(solution)/shard_map/ppermute | solution.py:96
  230.1 14.5 %collective-permute-start.15 = (bf16[512,256]{1,0:T(8,128)(2,1)S(1)}, bf16[512,256]{1,0:T(8,128)(2,1)S(1)}, u32[]{:S(2)}, u32[]{:S(2)}) collective-permute-start(bf16[512,256]{1,0:T(8,128)(2,1)S(1)} %shard_map.110.own), channel_id=1, source_target_pairs={{0,4},{4,0},{8,12},{12,8},{1,5},{5,1},{9,13},{13,9},{2,6},{6,2},{1... | collective-permute-start | bytes 786440 | tf_op jit(solution)/shard_map/ppermute | solution.py:96
  231.6 34.1 %collective-permute-start.18 = (bf16[32,16,512]{2,1,0:T(8,128)(2,1)S(1)}, bf16[32,16,512]{2,1,0:T(8,128)(2,1)S(1)}, u32[]{:S(2)}, u32[]{:S(2)}) collective-permute-start(bf16[32,16,512]{2,1,0:T(8,128)(2,1)S(1)} %get-tuple-element.117), channel_id=1, source_target_pairs={{0,8},{4,12},{8,0},{12,4},{1,9},{5,13},{9,1},{13,5},{2,10},{6,14},... | collective-permute-start | bytes 1572872 | tf_op jit(solution)/shard_map/ppermute | solution.py:96
  244.5 21.1 %collective-permute-start.17 = (bf16[512,256]{1,0:T(8,128)(2,1)S(1)}, bf16[512,256]{1,0:T(8,128)(2,1)S(1)}, u32[]{:S(2)}, u32[]{:S(2)}) collective-permute-start(bf16[512,256]{1,0:T(8,128)(2,1)S(1)} %collective-permute-done.16.far), channel_id=1, source_target_pairs={{0,4},{4,0},{8,12},{12,8},{1,5},{5,1},{9,13},{13,9},{2,6},{6,2},{1... | collective-permute-start | bytes 786440 | tf_op jit(solution)/shard_map/ppermute | solution.py:96
  265.7 26.9 %collective-permute-start.19 = (bf16[32,16,512]{2,1,0:T(8,128)(2,1)S(1)}, bf16[32,16,512]{2,1,0:T(8,128)(2,1)S(1)}, u32[]{:S(2)}, u32[]{:S(2)}) collective-permute-start(bf16[32,16,512]{2,1,0:T(8,128)(2,1)S(1)} %copy-done.26), channel_id=1, source_target_pairs={{0,12},{4,8},{8,4},{12,0},{1,13},{5,9},{9,5},{13,1},{2,14},{6,10},... | collective-permute-start | bytes 1572872 | tf_op jit(solution)/shard_map/ppermute | solution.py:96
  268.0 24.7 %collective-permute-start.20 = (bf16[32,16,512]{2,1,0:T(8,128)(2,1)S(1)}, bf16[32,16,512]{2,1,0:T(8,128)(2,1)S(1)}, u32[]{:S(2)}, u32[]{:S(2)}) collective-permute-start(bf16[32,16,512]{2,1,0:T(8,128)(2,1)S(1)} %get-tuple-element.126), channel_id=1, source_target_pairs={{0,4},{4,0},{8,12},{12,8},{1,5},{5,1},{9,13},{13,9},{2,6},{6,2},{1... | collective-permute-start | bytes 1572872 | tf_op jit(solution)/shard_map/ppermute | solution.py:96
  293.6 98.6 %all-to-all-start = ((bf16[4,32,32,512]{3,2,1,0:T(8,128)(2,1)}), bf16[4,32,32,512]{3,2,1,0:T(8,128)(2,1)}, u32[]{:S(2)}, u32[]{:S(2)}) async-start(bf16[4,32,32,512]{3,2,1,0:T(8,128)(2,1)} %get-tuple-element.127), calls=%async_computation | async-start | bytes 8388608 | tf_op jit(solution)/shard_map/all_to_all | solution.py:612
  306.5 8.2 %collective-permute-start.24 = (bf16[16,64,256]{2,1,0:T(8,128)(2,1)S(1)}, bf16[16,64,256]{2,1,0:T(8,128)(2,1)S(1)}, u32[]{:S(2)}, u32[]{:S(2)}) collective-permute-start(bf16[16,64,256]{2,1,0:T(8,128)(2,1)S(1)} %get-tuple-element.135), channel_id=1, source_target_pairs={{0,1},{1,0},{2,3},{3,2},{4,5},{5,4},{6,7},{7,6},{8,9},{9,8},{10,11... | collective-permute-start | bytes 1572872 | tf_op jit(solution)/shard_map/ppermute | solution.py:96
  306.6 8.1 %collective-permute-start.25 = (bf16[16,64,256]{2,1,0:T(8,128)(2,1)S(1)}, bf16[16,64,256]{2,1,0:T(8,128)(2,1)S(1)}, u32[]{:S(2)}, u32[]{:S(2)}) collective-permute-start(bf16[16,64,256]{2,1,0:T(8,128)(2,1)S(1)} %get-tuple-element.136), channel_id=1, source_target_pairs={{0,1},{1,0},{2,3},{3,2},{4,5},{5,4},{6,7},{7,6},{8,9},{9,8},{10,11... | collective-permute-start | bytes 1572872 | tf_op jit(solution)/shard_map/ppermute | solution.py:96
  314.1 4.3 collective-permute-start.21
  314.2 4.2 collective-permute-start.22
  317.9 14.8 %collective-permute-start.26 = (bf16[16,64,256]{2,1,0:T(8,128)(2,1)S(1)}, bf16[16,64,256]{2,1,0:T(8,128)(2,1)S(1)}, u32[]{:S(2)}, u32[]{:S(2)}) collective-permute-start(bf16[16,64,256]{2,1,0:T(8,128)(2,1)S(1)} %get-tuple-element.138), channel_id=1, source_target_pairs={{0,2},{1,3},{2,0},{3,1},{4,6},{5,7},{6,4},{7,5},{8,10},{9,11},{10,... | collective-permute-start | bytes 1572872 | tf_op jit(solution)/shard_map/ppermute | solution.py:96
  321.6 21.4 %collective-permute-start.23 = (bf16[16,64,256]{2,1,0:T(8,128)(2,1)S(1)}, bf16[16,64,256]{2,1,0:T(8,128)(2,1)S(1)}, u32[]{:S(2)}, u32[]{:S(2)}) collective-permute-start(bf16[16,64,256]{2,1,0:T(8,128)(2,1)S(1)} %get-tuple-element.133), channel_id=1, source_target_pairs={{0,2},{1,3},{2,0},{3,1},{4,6},{5,7},{6,4},{7,5},{8,10},{9,11},{10,... | collective-permute-start | bytes 1572872 | tf_op jit(solution)/shard_map/ppermute | solution.py:96
  392.2 75.0 %all-to-all-start.1 = ((bf16[4,24,32,512]{3,2,1,0:T(8,128)(2,1)}), bf16[4,24,32,512]{3,2,1,0:T(8,128)(2,1)}, u32[]{:S(2)}, u32[]{:S(2)}) async-start(bf16[4,24,32,512]{3,2,1,0:T(8,128)(2,1)} %get-tuple-element.139), calls=%async_computation.1 | async-start | bytes 6291456 | tf_op jit(solution)/shard_map/all_to_all | solution.py:612
  406.6 1.9 collective-permute-start.27
  406.6 2.7 collective-permute-start.28
  412.6 14.0 %collective-permute-start.29 = (bf16[16,64,256]{2,1,0:T(8,128)(2,1)S(1)}, bf16[16,64,256]{2,1,0:T(8,128)(2,1)S(1)}, u32[]{:S(2)}, u32[]{:S(2)}) collective-permute-start(bf16[16,64,256]{2,1,0:T(8,128)(2,1)S(1)} %get-tuple-element.144), channel_id=1, source_target_pairs={{0,2},{1,3},{2,0},{3,1},{4,6},{5,7},{6,4},{7,5},{8,10},{9,11},{10,... | collective-permute-start | bytes 1572872 | tf_op jit(solution)/shard_map/ppermute | solution.py:96
  467.1 28.7 %all-to-all-start.2 = ((bf16[4,8,32,512]{3,2,1,0:T(8,128)(2,1)}), bf16[4,8,32,512]{3,2,1,0:T(8,128)(2,1)S(1)}, u32[]{:S(2)}, u32[]{:S(2)}) async-start(bf16[4,8,32,512]{3,2,1,0:T(8,128)(2,1)} %get-tuple-element.145), calls=%async_computation.2 | async-start | bytes 2097152 | tf_op jit(solution)/shard_map/all_to_all | solution.py:612
  479.1 1.7 collective-permute-start.33
  479.1 2.3 collective-permute-start.34
  483.5 19.0 %collective-permute-start.35 = (bf16[12,64,256]{2,1,0:T(8,128)(2,1)S(1)}, bf16[12,64,256]{2,1,0:T(8,128)(2,1)S(1)}, u32[]{:S(2)}, u32[]{:S(2)}) collective-permute-start(bf16[12,64,256]{2,1,0:T(8,128)(2,1)S(1)} %get-tuple-element.158), channel_id=1, source_target_pairs={{0,2},{1,3},{2,0},{3,1},{4,6},{5,7},{6,4},{7,5},{8,10},{9,11},{10,... | collective-permute-start | bytes 1179656 | tf_op jit(solution)/shard_map/ppermute | solution.py:96
  499.8 1.3 collective-permute-start.30
  499.8 1.5 collective-permute-start.31
  502.0 5.8 %collective-permute-start.32 = (bf16[4,64,256]{2,1,0:T(8,128)(2,1)S(1)}, bf16[4,64,256]{2,1,0:T(8,128)(2,1)S(1)}, u32[]{:S(2)}, u32[]{:S(2)}) collective-permute-start(bf16[4,64,256]{2,1,0:T(8,128)(2,1)S(1)} %get-tuple-element.153), channel_id=1, source_target_pairs={{0,2},{1,3},{2,0},{3,1},{4,6},{5,7},{6,4},{7,5},{8,10},{9,11},{10,... | collective-permute-start | bytes 393224 | tf_op jit(solution)/shard_map/ppermute | solution.py:96
  (19 other events, 130.1 us)

commit v6 on v4

--- a/solution.py
+++ b/solution.py
@@ -141,8 +141,8 @@
     return jnp.dot(matrix, flat, preferred_element_type=F32).astype(BF16).reshape(TILE, TILE, rows)
 
 
-def back_kernel(me_ref, turn_ref, second_ref, cot_ref, *refs):
-    outs, held = refs[:4], refs[4]
+def back_kernel(_, turn_ref, second_ref, cot_ref, *refs):
+    out, held = refs
     blocks, rows = held.shape[2], held.shape[3]
     group, size, _ = second_ref.shape
     pair = size // (4 * blocks)
@@ -159,10 +159,9 @@
 
     @pl.when(at == steps - 1)
     def _():
-        for bits in range(4):
-            there = me_ref[0] ^ bits
+        for there in range(4):
             for low in range(0, blocks, TILE):
-                outs[bits][low : low + TILE] = turn(
+                out[there, low : low + TILE] = turn(
                     turn_ref[...], held[:, there, low : low + TILE, :]
                 )
 
@@ -175,7 +174,6 @@
     group = several(math.gcd(count, TILE // pair))
     steps = TILE // (pair * group)
     first = part * count // group
-    piece = array((blocks, count * pair, rows), BF16)
     return call(
         back_kernel,
         me,
@@ -185,8 +183,8 @@
             spec((group, size, size), lambda j, _: (first + j, 0, 0)),
             spec((rows, group * size), lambda j, _: (0, first + j)),
         ],
-        [piece] * 4,
-        [spec((blocks, TILE, rows), lambda j, _: (0, j // steps, 0))] * 4,
+        array((4, blocks, count * pair, rows), BF16),
+        spec((4, blocks, TILE, rows), lambda j, _: (0, 0, j // steps, 0)),
         grid=(count // group,),
         scratch=[pltpu.VMEM((TILE, 4, blocks, rows), BF16)],
     )
@@ -511,96 +509,72 @@
 
 
 def grad_first_kernel(me_ref, *refs):
-    pieces, (hidden_ref, *send_ref, keep_ref, held, square) = refs[:-6], refs[-6:]
+    pieces, (hidden_ref, *send_ref, keep_ref, square) = refs[:-5], refs[-5:]
     group, size, _ = square.shape
     for g in range(group):
-        for part in range(len(pieces) // 4):
-            for bits in range(4):
-                held[g, me_ref[0] ^ bits, part] = pieces[part * 4 + bits][g]
-        back = held[g].reshape(size, held.shape[4])
+        back = jnp.concatenate([piece[s, g] for s in range(4) for piece in pieces], axis=0)
         hidden = hidden_ref[:, g * size : (g + 1) * size]
         square[g] = jnp.dot(back, hidden, preferred_element_type=F32).T
         store_quarters(me_ref[1], g, square.at[g], send_ref, keep_ref)
 
 
 def grad_first_call(me, pieces, hidden, size, start, count):
-    _, deep, rows = pieces[0].shape
+    _, _, deep, rows = pieces[0].shape
     group = several(math.gcd(count, start) if start else count)
     begin = start // group
     return call(
         grad_first_kernel,
         me,
         (*pieces, hidden),
-        [spec((group, deep, rows), lambda b, _: (begin + b, 0, 0))] * len(pieces)
+        [spec((4, group, deep, rows), lambda b, _: (0, begin + b, 0, 0))] * len(pieces)
         + [spec((rows, group * size), lambda b, _: (0, begin + b))],
         *quarter_outs(count, group, size),
         grid=(count // group,),
-        scratch=[
-            pltpu.VMEM((group, 4, len(pieces) // 4, deep, rows), BF16),
-            pltpu.VMEM((group, size, size), F32),
-        ],
+        scratch=[pltpu.VMEM((group, size, size), F32)],
     )
 
 
 def on_device_four(expression, gene_mask, mask_value, w_qkv, w_out, w_first, w_second, cotangent):
     me = jnp.stack([lax.axis_index("gene"), lax.axis_index("cell")]).astype(jnp.int32)
     blocks, size, _ = w_first.shape
-    parts = 4
     deep = size // 4
     deeps = [deep // 2, 3 * deep // 8, deep // 8]
     matrix = grid_turn()
-    sends, back = [None] * parts, [[None] * 4 for _ in range(parts)]
-
-    def prepare(part, *earlier):
-        sends[part] = back_call(me, matrix, w_second, after(cotangent, *earlier), part, parts)
-        back[part][0] = sends[part][0]
-
-    def begin(part, bits, *earlier):
-        back[part][bits] = flip(after(sends[part][bits], *earlier), "gene", bits)
-        return back[part][bits]
-
-    prepare(0)
-    first_part = [begin(0, bits) for bits in (3, 2, 1)]
+
+    def swap_genes(piece, *earlier):
+        piece = after(piece, *earlier)
+        return lax.all_to_all(piece, "gene", split_axis=0, concat_axis=0, tiled=True)
+
+    back_send = back_call(me, matrix, w_second, cotangent, 0, 2)
+    back = [swap_genes(back_send)]
     masked, send, keep = project_call(
-        me, after(expression, sends[0][0]), gene_mask, mask_value, w_qkv
-    )
-    came = flip(after(send, *first_part), "gene", 1)
-    prepare(1, send)
-    beside_sum = [begin(1, 2), begin(1, 3)]
-    mine, other = add_call(me, keep, after(came, *beside_sum))
+        me, after(expression, back_send), gene_mask, mask_value, w_qkv
+    )
+    came = flip(send, "gene", 1)
+    back_send = back_call(me, matrix, w_second, after(cotangent, send), 1, 2)
+    w_first_t = jnp.swapaxes(after(w_first, send), 1, 2)
+    mine, other = add_call(me, keep, after(came, *back, back_send, w_first_t))
     last = flip(other, "gene", 2)
-    prepare(2, other)
-    prepare(3, sends[2][0])
-    w_first_t = jnp.swapaxes(after(w_first, other), 1, 2)
-    beside_sum = [begin(1, 1, other)]
-    queries, key_value = split_call(
-        me, mine, after(last, *beside_sum, sends[3][0], w_first_t)
-    )
+    queries, key_value = split_call(me, mine, last)
+    back.append(swap_genes(back_send, last))
     across = flip(key_value, "cell", 2)
     beside = flip(key_value, "cell", 1)
     corner = flip(across, "cell", 1)
-    beside_keys = [begin(2, 2, last), begin(2, 1, last)]
-    queries = after(queries, *beside_keys, beside, across, corner)
     attended = attend_call(me, queries, (key_value, beside, across, corner))
-    attended = after(attended, begin(2, 3, queries), begin(3, 1, queries))
     near = flip(attended, "gene", 1)
     far = flip(attended, "gene", 2)
     rest = flip(after(far, near), "gene", 1)
-    rest = after(rest, begin(3, 2, attended))
     hidden, first = first_call(
         me, matrix, (attended, near, far, rest), w_out, masked, w_first_t, deeps
     )
-    begin(3, 3, rest)
 
     got = []
 
     def launch(t, *earlier):
-        piece = after(first[t], *earlier)
-        got.append(lax.all_to_all(piece, "gene", split_axis=0, concat_axis=0, tiled=True))
-
-    launch(0, back[3][3])
+        got.append(swap_genes(first[t], *earlier))
+
+    launch(0, back[1])
     denoised, shares = None, [None, None]
-    back = sum(back, [])
 
     def sum_cells(which, start, send, keep):
         came = [flip(piece, "cell", 1) for piece in send]

time: 493 us -> 518 us (1.051)
  waiting for transfers between devices: 269 us -> 311 us
  starting transfers between devices: 53.2 us -> 42.3 us
    ppermute x35 -> x23, waiting for transfers between devices: 174 us -> 215 us  [flip(): return lax.ppermute(value, axis, pairs)]
    ppermute x35 -> x23, starting transfers between devices: 41.1 us -> 18.7 us  [flip(): return lax.ppermute(value, axis, pairs)]
    all_to_all x3 -> x5, starting transfers between devices: 12.1 us -> 23.6 us  [swap_genes(): lax.all_to_all(piece, 'gene', split_axis=0, concat_axis=0, tiled=True)]
    unnamed x50 -> x16, local copies, waits for them, and re-layouts: 10.9 us -> 6.01 us
    pallas_call x24 -> x22, Pallas kernels: 151 us -> 150 us  [call(): pl.pallas_call(body, out_shape=outs, grid_spec=pltpu.PrefetchScalarGridSp...]
    all_to_all x3 -> x5, waiting for transfers between devices: 94.9 us -> 96.3 us  [swap_genes(): lax.all_to_all(piece, 'gene', split_axis=0, concat_axis=0, tiled=True)]
  transfers between devices with their start and end apart: 38 -> 28, of which waited for: 25 -> 19; matrix products, arithmetic and copies ran while one was open for 1% -> 1% of each run, Pallas kernels for 28% -> 26%
where the time goes in v6:
time: 518 us; the launch traced here: 517 us
  waiting for transfers between devices  311 us (60%)
  Pallas kernels  150 us (29%)
  starting transfers between devices  42.3 us (8%)
  local copies, waits for them, and re-layouts  12.5 us (2%)
    ppermute x23, waiting for transfers between devices, flip(): return lax.ppermute(value, axis, pairs)  215 us
    pallas_call x22, Pallas kernels, call(): pl.pallas_call(body, out_shape=outs, grid_spec=pltpu.PrefetchScalarGridSp...  150 us
    all_to_all x5, waiting for transfers between devices, swap_genes(): lax.all_to_all(piece, 'gene', split_axis=0, concat_axis=0, tiled=True)  96.3 us
    all_to_all x5, starting transfers between devices, swap_genes(): lax.all_to_all(piece, 'gene', split_axis=0, concat_axis=0, tiled=True)  23.6 us
    ppermute x23, starting transfers between devices, flip(): return lax.ppermute(value, axis, pairs)  18.7 us
  transfers between devices with their start and end apart: 28, of which 19 were waited for; matrix products, arithmetic and copies ran while one was open for 1% of the time, Pallas kernels for 26%

profile of v6, /device:TPU:0, one launch (start us, length us, event | category | flops | bytes accessed | tf_op | source)
XLA Modules:
  0.0 516.8 jit_solution(1141503639960601655)
XLA Ops:
  1.0 8.4 %shard_map.103 = bf16[4,32,32,512]{3,2,1,0:T(8,128)(2,1)} custom-call(s32[2]{0:T(128)S(1)} %pad_add_fusion._.me_ref, bf16[256,256]{1,0:T(8,128)(2,1)S(1)} %fusion.turn_ref, bf16[32,256,256]{2,1,0:T(8,128)(2,1)} %refs_1_.5, bf16[512,8192]{1,0:T(8,128)(2,1)} %refs_2_.5), custom_call_target="tpu_custom_call" | custom-call | flops 1 | bytes 1 | tf_op jit(solution)/shard_map/pallas_call | solution.py:100
  9.4 6.5 %all-to-all-start = ((bf16[4,32,32,512]{3,2,1,0:T(8,128)(2,1)}), bf16[4,32,32,512]{3,2,1,0:T(8,128)(2,1)}, u32[]{:S(2)}, u32[]{:S(2)}) async-start(bf16[4,32,32,512]{3,2,1,0:T(8,128)(2,1)} %shard_map.103), calls=%async_computation | async-start | bytes 8388608 | tf_op jit(solution)/shard_map/all_to_all | solution.py:546
  15.9 37.8 %shard_map.104 = (bf16[512,8192]{1,0:T(8,128)(2,1)}, bf16[2,512,768]{2,1,0:T(8,128)(2,1)S(1)}, f32[2,512,768]{2,1,0:T(8,128)}) custom-call(s32[2]{0:T(128)S(1)} %pad_add_fusion._.me_ref, bf16[512,8192]{1,0:T(8,128)(2,1)} %value_ref, s32[512,8192]{1,0:T(8,128)} %mask_ref.1, bf16[1,8192]{1,0:T(2,128)(2,1)S(1)} %reshape.9.fill_ref, bf16[8192,3072]{1,0:T(8,128)(2,1)} %weight_ref.1), custom_call_target="tpu_custom_call" | custom-call | flops 1 | bytes 1 | tf_op jit(solution)/shard_map/pallas_call | solution.py:100
  53.7 2.0 collective-permute-start
  55.7 8.4 %shard_map.105 = bf16[4,32,32,512]{3,2,1,0:T(8,128)(2,1)} custom-call(s32[2]{0:T(128)S(1)} %pad_add_fusion._.me_ref, bf16[256,256]{1,0:T(8,128)(2,1)S(1)} %fusion.turn_ref, bf16[32,256,256]{2,1,0:T(8,128)(2,1)} %refs_1_.5, bf16[512,8192]{1,0:T(8,128)(2,1)} %refs_2_.5), custom_call_target="tpu_custom_call" | custom-call | flops 1 | bytes 1 | tf_op jit(solution)/shard_map/pallas_call | solution.py:100
  64.1 6.5 %copy.16 = bf16[32,256,256]{1,2,0:T(8,128)(2,1)} copy(bf16[32,256,256]{2,1,0:T(8,128)(2,1)} %param.13) | data formatting | bytes 8388608 | tf_op jit(solution)/shard_map/optimization_barrier | solution.py:91
  70.6 48.8 %collective-permute-done.came_ref = bf16[2,512,768]{2,1,0:T(8,128)(2,1)S(1)} collective-permute-done((bf16[2,512,768]{2,1,0:T(8,128)(2,1)S(1)}, bf16[2,512,768]{2,1,0:T(8,128)(2,1)S(1)}, u32[]{:S(2)}, u32[]{:S(2)}) %collective-permute-start) | collective-permute-done | bytes 1572896 | tf_op jit(solution)/shard_map/ppermute | solution.py:96
  120.5 4.2 shard_map.106
  124.7 2.7 collective-permute-start.1
  127.4 33.6 %collective-permute-done.1.came_ref = bf16[512,768]{1,0:T(8,128)(2,1)S(1)} collective-permute-done((bf16[512,768]{1,0:T(8,128)(2,1)S(1)}, bf16[512,768]{1,0:T(8,128)(2,1)S(1)}, u32[]{:S(2)}, u32[]{:S(2)}) %collective-permute-start.1) | collective-permute-done | bytes 786464 | tf_op jit(solution)/shard_map/ppermute | solution.py:96
  161.0 5.0 all-to-all-start.1
  166.0 3.2 shard_map.107
  169.2 1.6 collective-permute-start.3
  170.9 12.3 %collective-permute-done.3.refs_2_ = bf16[512,512]{1,0:T(8,128)(2,1)S(1)} collective-permute-done((bf16[512,512]{1,0:T(8,128)(2,1)S(1)}, bf16[512,512]{1,0:T(8,128)(2,1)S(1)}, u32[]{:S(2)}, u32[]{:S(2)}) %collective-permute-start.3) | collective-permute-done | bytes 524320 | tf_op jit(solution)/shard_map/ppermute | solution.py:96
  183.1 1.9 collective-permute-done.4.refs_3_
  185.8 7.1 %shard_map.108.own = bf16[512,256]{1,0:T(8,128)(2,1)S(1)} custom-call(s32[2]{0:T(128)S(1)} %pad_add_fusion._.me_ref, bf16[512,256]{1,0:T(8,128)(2,1)S(1)} %get-tuple-element.59.query_ref, bf16[512,512]{1,0:T(8,128)(2,1)S(1)} %get-tuple-element.60.refs_0_, bf16[512,512]{1,0:T(8,128)(2,1)S(1)} %collective-permute-done.2.refs_1_, bf16[512,512]{1,0:T(8,128)(2,1)} %copy-done.5, ...), custom_call_target="tpu_custom_call" | custom-call | flops 1 | bytes 1 | tf_op jit(solution)/shard_map/pallas_call | solution.py:100
  193.0 2.5 collective-permute-start.6
  195.5 1.5 collective-permute-start.5
  196.9 73.7 %collective-permute-done.6.far = bf16[512,256]{1,0:T(8,128)(2,1)S(1)} collective-permute-done((bf16[512,256]{1,0:T(8,128)(2,1)S(1)}, bf16[512,256]{1,0:T(8,128)(2,1)S(1)}, u32[]{:S(2)}, u32[]{:S(2)}) %collective-permute-start.6) | collective-permute-done | bytes 262176 | tf_op jit(solution)/shard_map/ppermute | solution.py:96
  270.7 7.4 %collective-permute-done.7.rest = bf16[512,256]{1,0:T(8,128)(2,1)S(1)} collective-permute-done((bf16[512,256]{1,0:T(8,128)(2,1)S(1)}, bf16[512,256]{1,0:T(8,128)(2,1)S(1)}, u32[]{:S(2)}, u32[]{:S(2)}) %collective-permute-start.7) | collective-permute-done | bytes 262176 | tf_op jit(solution)/shard_map/ppermute | solution.py:96
  278.0 24.6 %shard_map.109 = (bf16[512,8192]{1,0:T(8,128)(2,1)}, bf16[4,32,32,512]{3,2,1,0:T(8,128)(2,1)}, bf16[4,24,32,512]{3,2,1,0:T(8,128)(2,1)}, bf16[4,8,32,512]{3,2,1,0:T(8,128)(2,1)}) custom-call(s32[2]{0:T(128)S(1)} %pad_add_fusion._.me_ref, bf16[256,256]{1,0:T(8,128)(2,1)S(1)} %fusion.turn_ref, bf16[512,256]{1,0:T(8,128)(2,1)S(1)} %shard_map.108.own, ...), custom_call_target="tpu_custom_call" | custom-call | flops 1 | bytes 1 | tf_op jit(solution)/shard_map/pallas_call | solution.py:100
  302.6 4.9 all-to-all-start.2
  307.5 6.8 %shard_map.112 = (bf16[16,64,256]{2,1,0:T(8,128)(2,1)S(1)}, bf16[16,64,256]{2,1,0:T(8,128)(2,1)S(1)}, f32[2,16,64,256]{3,2,1,0:T(8,128)}) custom-call(s32[2]{0:T(128)S(1)} %pad_add_fusion._.me_ref, bf16[4,32,32,512]{3,2,1,0:T(8,128)(2,1)} %all-to-all-done.refs_0_, bf16[4,32,32,512]{3,2,1,0:T(8,128)(2,1)} %all-to-all-done.1.refs_1_, ...), custom_call_target="tpu_custom_call" | custom-call | flops 1 | bytes 1 | tf_op jit(solution)/shard_map/pallas_call | solution.py:100
  314.8 6.8 %shard_map.110 = (bf16[16,64,256]{2,1,0:T(8,128)(2,1)S(1)}, bf16[16,64,256]{2,1,0:T(8,128)(2,1)S(1)}, f32[2,16,64,256]{3,2,1,0:T(8,128)}) custom-call(s32[2]{0:T(128)S(1)} %pad_add_fusion._.me_ref, bf16[4,32,32,512]{3,2,1,0:T(8,128)(2,1)} %all-to-all-done.refs_0_, bf16[4,32,32,512]{3,2,1,0:T(8,128)(2,1)} %all-to-all-done.1.refs_1_, ...), custom_call_target="tpu_custom_call" | custom-call | flops 1 | bytes 1 | tf_op jit(solution)/shard_map/pallas_call | solution.py:100
  322.2 3.2 shard_map.113
  325.4 1.3 collective-permute-start.13
  326.7 3.2 shard_map.111
  330.6 9.5 %collective-permute-done.13.came_ref = bf16[16,64,256]{2,1,0:T(8,128)(2,1)S(1)} collective-permute-done((bf16[16,64,256]{2,1,0:T(8,128)(2,1)S(1)}, bf16[16,64,256]{2,1,0:T(8,128)(2,1)S(1)}, u32[]{:S(2)}, u32[]{:S(2)}) %collective-permute-start.13) | collective-permute-done | bytes 524320 | tf_op jit(solution)/shard_map/ppermute | solution.py:96
  341.4 1.6 shard_map.114.refs_0_
  343.0 7.5 %collective-permute-done.10.came_ref = bf16[16,64,256]{2,1,0:T(8,128)(2,1)S(1)} collective-permute-done((bf16[16,64,256]{2,1,0:T(8,128)(2,1)S(1)}, bf16[16,64,256]{2,1,0:T(8,128)(2,1)S(1)}, u32[]{:S(2)}, u32[]{:S(2)}) %collective-permute-start.10) | collective-permute-done | bytes 524320 | tf_op jit(solution)/shard_map/ppermute | solution.py:96
  350.4 1.6 shard_map.115
  352.0 47.4 %all-to-all-done.2.refs_0_ = bf16[4,32,32,512]{3,2,1,0:T(8,128)(2,1)} async-done(((bf16[4,32,32,512]{3,2,1,0:T(8,128)(2,1)}), bf16[4,32,32,512]{3,2,1,0:T(8,128)(2,1)}, u32[]{:S(2)}, u32[]{:S(2)}) %all-to-all-start.2) | async-done | bytes 4194336 | tf_op jit(solution)/shard_map/all_to_all | solution.py:546
  399.4 3.7 all-to-all-start.3
  403.1 9.6 %shard_map.116 = (bf16[512,8192]{1,0:T(8,128)(2,1)}, bf16[16,64,256]{2,1,0:T(8,128)(2,1)S(1)}, bf16[16,64,256]{2,1,0:T(8,128)(2,1)S(1)}, f32[2,16,64,256]{3,2,1,0:T(8,128)}) custom-call(s32[2]{0:T(128)S(1)} %pad_add_fusion._.me_ref, bf16[4,32,32,512]{3,2,1,0:T(8,128)(2,1)} %all-to-all-done.2.refs_0_, bf16[32,256,256]{2,1,0:T(8,128)(2,1)} %refs_1_.5, ...), custom_call_target="tpu_custom_call" | custom-call | flops 1 | bytes 1 | tf_op jit(solution)/shard_map/pallas_call | solution.py:100
  413.3 1.4 collective-permute-done.14.came_ref
  415.4 3.2 shard_map.117
  419.8 12.8 %collective-permute-done.16.came_ref = bf16[16,64,256]{2,1,0:T(8,128)(2,1)S(1)} collective-permute-done((bf16[16,64,256]{2,1,0:T(8,128)(2,1)S(1)}, bf16[16,64,256]{2,1,0:T(8,128)(2,1)S(1)}, u32[]{:S(2)}, u32[]{:S(2)}) %collective-permute-start.16) | collective-permute-done | bytes 524320 | tf_op jit(solution)/shard_map/ppermute | solution.py:96
  433.8 1.6 shard_map.118.refs_0_
  435.4 37.9 %all-to-all-done.3.refs_0_ = bf16[4,24,32,512]{3,2,1,0:T(8,128)(2,1)S(1)} async-done(((bf16[4,24,32,512]{3,2,1,0:T(8,128)(2,1)}), bf16[4,24,32,512]{3,2,1,0:T(8,128)(2,1)S(1)}, u32[]{:S(2)}, u32[]{:S(2)}) %all-to-all-start.3) | async-done | bytes 3145760 | tf_op jit(solution)/shard_map/all_to_all | solution.py:546
  473.3 1.6 copy-done.3
  474.9 3.5 all-to-all-start.4
  478.4 8.5 %shard_map.119 = (bf16[512,8192]{1,0:T(8,128)(2,1)}, bf16[12,64,256]{2,1,0:T(8,128)(2,1)S(1)}, bf16[12,64,256]{2,1,0:T(8,128)(2,1)S(1)}, f32[2,12,64,256]{3,2,1,0:T(8,128)}) custom-call(s32[2]{0:T(128)S(1)} %pad_add_fusion._.me_ref, bf16[4,24,32,512]{3,2,1,0:T(8,128)(2,1)} %copy-done.3, ...), custom_call_target="tpu_custom_call", output_to_operand_aliasing={{0}: (5, {})} | custom-call | flops 1 | bytes 1 | tf_op jit(solution)/shard_map/pallas_call | solution.py:100
  489.2 2.1 shard_map.122
  491.3 1.3 collective-permute-start.22
  492.6 11.0 %all-to-all-done.4.refs_0_ = bf16[4,8,32,512]{3,2,1,0:T(8,128)(2,1)S(1)} async-done(((bf16[4,8,32,512]{3,2,1,0:T(8,128)(2,1)}), bf16[4,8,32,512]{3,2,1,0:T(8,128)(2,1)S(1)}, u32[]{:S(2)}, u32[]{:S(2)}) %all-to-all-start.4) | async-done | bytes 1048608 | tf_op jit(solution)/shard_map/all_to_all | solution.py:546
  503.6 4.0 shard_map.120
  511.0 2.0 shard_map.123.refs_0_
  513.0 2.5 collective-permute-done.19.came_ref
  (53 shorter events, 16.0 us)
Async XLA Ops:
  9.4 6.5 %copy-start.7 = (bf16[8192]{0:T(1024)(128)(2,1)S(1)}, bf16[8192]{0:T(1024)(128)(2,1)}, u32[]{:S(2)}) copy-start(bf16[8192]{0:T(1024)(128)(2,1)} %param.10) | copy-start | bytes 49156
  9.4 110.0 %all-to-all-start = ((bf16[4,32,32,512]{3,2,1,0:T(8,128)(2,1)}), bf16[4,32,32,512]{3,2,1,0:T(8,128)(2,1)}, u32[]{:S(2)}, u32[]{:S(2)}) async-start(bf16[4,32,32,512]{3,2,1,0:T(8,128)(2,1)} %shard_map.103), calls=%async_computation | async-start | bytes 8388608 | tf_op jit(solution)/shard_map/all_to_all | solution.py:546
  53.7 65.7 %collective-permute-start = (bf16[2,512,768]{2,1,0:T(8,128)(2,1)S(1)}, bf16[2,512,768]{2,1,0:T(8,128)(2,1)S(1)}, u32[]{:S(2)}, u32[]{:S(2)}) collective-permute-start(bf16[2,512,768]{2,1,0:T(8,128)(2,1)S(1)} %get-tuple-element.53), channel_id=1, source_target_pairs={{0,4},{4,0},{8,12},{12,8},{1,5},{5,1},{9,13},{13,9},{2,6},{6,2},{1... | collective-permute-start | bytes 4718600 | tf_op jit(solution)/shard_map/ppermute | solution.py:96
  119.4 1.1 copy-start.4
  124.7 36.3 %collective-permute-start.1 = (bf16[512,768]{1,0:T(8,128)(2,1)S(1)}, bf16[512,768]{1,0:T(8,128)(2,1)S(1)}, u32[]{:S(2)}, u32[]{:S(2)}) collective-permute-start(bf16[512,768]{1,0:T(8,128)(2,1)S(1)} %get-tuple-element.58), channel_id=1, source_target_pairs={{0,8},{4,12},{8,0},{12,4},{1,9},{5,13},{9,1},{13,5},{2,10},{6,14},... | collective-permute-start | bytes 2359304 | tf_op jit(solution)/shard_map/ppermute | solution.py:96
  161.0 141.6 %all-to-all-start.1 = ((bf16[4,32,32,512]{3,2,1,0:T(8,128)(2,1)}), bf16[4,32,32,512]{3,2,1,0:T(8,128)(2,1)}, u32[]{:S(2)}, u32[]{:S(2)}) async-start(bf16[4,32,32,512]{3,2,1,0:T(8,128)(2,1)} %shard_map.105), calls=%async_computation.1 | async-start | bytes 8388608 | tf_op jit(solution)/shard_map/all_to_all | solution.py:546
  169.2 13.9 %collective-permute-start.3 = (bf16[512,512]{1,0:T(8,128)(2,1)S(1)}, bf16[512,512]{1,0:T(8,128)(2,1)S(1)}, u32[]{:S(2)}, u32[]{:S(2)}) collective-permute-start(bf16[512,512]{1,0:T(8,128)(2,1)S(1)} %get-tuple-element.60.refs_0_), channel_id=1, source_target_pairs={{0,2},{1,3},{2,0},{3,1},{4,6},{5,7},{6,4},{7,5},{8,10},{9,11},{10,... | collective-permute-start | bytes 1572872 | tf_op jit(solution)/shard_map/ppermute | solution.py:96
  170.9 12.3 %collective-permute-start.2 = (bf16[512,512]{1,0:T(8,128)(2,1)S(1)}, bf16[512,512]{1,0:T(8,128)(2,1)S(1)}, u32[]{:S(2)}, u32[]{:S(2)}) collective-permute-start(bf16[512,512]{1,0:T(8,128)(2,1)S(1)} %get-tuple-element.60.refs_0_), channel_id=1, source_target_pairs={{0,1},{1,0},{2,3},{3,2},{4,5},{5,4},{6,7},{7,6},{8,9},{9,8},{10,11... | collective-permute-start | bytes 1572872 | tf_op jit(solution)/shard_map/ppermute | solution.py:96
  183.1 1.9 copy-start.5
  183.1 1.9 collective-permute-start.4
  185.1 0.8 copy-start.6
  193.0 77.7 %collective-permute-start.6 = (bf16[512,256]{1,0:T(8,128)(2,1)S(1)}, bf16[512,256]{1,0:T(8,128)(2,1)S(1)}, u32[]{:S(2)}, u32[]{:S(2)}) collective-permute-start(bf16[512,256]{1,0:T(8,128)(2,1)S(1)} %shard_map.108.own), channel_id=1, source_target_pairs={{0,8},{4,12},{8,0},{12,4},{1,9},{5,13},{9,1},{13,5},{2,10},{6,14},... | collective-permute-start | bytes 786440 | tf_op jit(solution)/shard_map/ppermute | solution.py:96
  195.5 75.2 %collective-permute-start.5 = (bf16[512,256]{1,0:T(8,128)(2,1)S(1)}, bf16[512,256]{1,0:T(8,128)(2,1)S(1)}, u32[]{:S(2)}, u32[]{:S(2)}) collective-permute-start(bf16[512,256]{1,0:T(8,128)(2,1)S(1)} %shard_map.108.own), channel_id=1, source_target_pairs={{0,4},{4,0},{8,12},{12,8},{1,5},{5,1},{9,13},{13,9},{2,6},{6,2},{1... | collective-permute-start | bytes 786440 | tf_op jit(solution)/shard_map/ppermute | solution.py:96
  270.6 7.4 %collective-permute-start.7 = (bf16[512,256]{1,0:T(8,128)(2,1)S(1)}, bf16[512,256]{1,0:T(8,128)(2,1)S(1)}, u32[]{:S(2)}, u32[]{:S(2)}) collective-permute-start(bf16[512,256]{1,0:T(8,128)(2,1)S(1)} %collective-permute-done.6.far), channel_id=1, source_target_pairs={{0,4},{4,0},{8,12},{12,8},{1,5},{5,1},{9,13},{13,9},{2,6},{6,2},{1... | collective-permute-start | bytes 786440 | tf_op jit(solution)/shard_map/ppermute | solution.py:96
  302.6 96.8 %all-to-all-start.2 = ((bf16[4,32,32,512]{3,2,1,0:T(8,128)(2,1)}), bf16[4,32,32,512]{3,2,1,0:T(8,128)(2,1)}, u32[]{:S(2)}, u32[]{:S(2)}) async-start(bf16[4,32,32,512]{3,2,1,0:T(8,128)(2,1)} %get-tuple-element.67), calls=%async_computation.2 | async-start | bytes 8388608 | tf_op jit(solution)/shard_map/all_to_all | solution.py:546
  314.3 7.8 %collective-permute-start.11 = (bf16[16,64,256]{2,1,0:T(8,128)(2,1)S(1)}, bf16[16,64,256]{2,1,0:T(8,128)(2,1)S(1)}, u32[]{:S(2)}, u32[]{:S(2)}) collective-permute-start(bf16[16,64,256]{2,1,0:T(8,128)(2,1)S(1)} %get-tuple-element.75), channel_id=1, source_target_pairs={{0,1},{1,0},{2,3},{3,2},{4,5},{5,4},{6,7},{7,6},{8,9},{9,8},{10,11... | collective-permute-start | bytes 1572872 | tf_op jit(solution)/shard_map/ppermute | solution.py:96
  314.3 7.8 %collective-permute-start.12 = (bf16[16,64,256]{2,1,0:T(8,128)(2,1)S(1)}, bf16[16,64,256]{2,1,0:T(8,128)(2,1)S(1)}, u32[]{:S(2)}, u32[]{:S(2)}) collective-permute-start(bf16[16,64,256]{2,1,0:T(8,128)(2,1)S(1)} %get-tuple-element.76), channel_id=1, source_target_pairs={{0,1},{1,0},{2,3},{3,2},{4,5},{5,4},{6,7},{7,6},{8,9},{9,8},{10,11... | collective-permute-start | bytes 1572872 | tf_op jit(solution)/shard_map/ppermute | solution.py:96
  321.6 5.0 collective-permute-start.8
  321.7 5.0 collective-permute-start.9
  325.4 14.8 %collective-permute-start.13 = (bf16[16,64,256]{2,1,0:T(8,128)(2,1)S(1)}, bf16[16,64,256]{2,1,0:T(8,128)(2,1)S(1)}, u32[]{:S(2)}, u32[]{:S(2)}) collective-permute-start(bf16[16,64,256]{2,1,0:T(8,128)(2,1)S(1)} %get-tuple-element.78), channel_id=1, source_target_pairs={{0,2},{1,3},{2,0},{3,1},{4,6},{5,7},{6,4},{7,5},{8,10},{9,11},{10,... | collective-permute-start | bytes 1572872 | tf_op jit(solution)/shard_map/ppermute | solution.py:96
  329.9 20.5 %collective-permute-start.10 = (bf16[16,64,256]{2,1,0:T(8,128)(2,1)S(1)}, bf16[16,64,256]{2,1,0:T(8,128)(2,1)S(1)}, u32[]{:S(2)}, u32[]{:S(2)}) collective-permute-start(bf16[16,64,256]{2,1,0:T(8,128)(2,1)S(1)} %get-tuple-element.73), channel_id=1, source_target_pairs={{0,2},{1,3},{2,0},{3,1},{4,6},{5,7},{6,4},{7,5},{8,10},{9,11},{10,... | collective-permute-start | bytes 1572872 | tf_op jit(solution)/shard_map/ppermute | solution.py:96
  340.2 1.2 copy-start
  341.4 9.1 %copy-start.1 = (f32[16,64,256]{2,1,0:T(8,128)S(1)}, f32[16,64,256]{2,1,0:T(8,128)}, u32[]{:S(2)}) copy-start(f32[16,64,256]{2,1,0:T(8,128)} %get-tuple-element.72.mine_ref) | copy-start | bytes 3145732
  399.4 73.8 %all-to-all-start.3 = ((bf16[4,24,32,512]{3,2,1,0:T(8,128)(2,1)}), bf16[4,24,32,512]{3,2,1,0:T(8,128)(2,1)S(1)}, u32[]{:S(2)}, u32[]{:S(2)}) async-start(bf16[4,24,32,512]{3,2,1,0:T(8,128)(2,1)} %get-tuple-element.79), calls=%async_computation.3 | async-start | bytes 6291456 | tf_op jit(solution)/shard_map/all_to_all | solution.py:546
  412.7 1.9 collective-permute-start.14
  412.7 2.7 collective-permute-start.15
  418.6 14.0 %collective-permute-start.16 = (bf16[16,64,256]{2,1,0:T(8,128)(2,1)S(1)}, bf16[16,64,256]{2,1,0:T(8,128)(2,1)S(1)}, u32[]{:S(2)}, u32[]{:S(2)}) collective-permute-start(bf16[16,64,256]{2,1,0:T(8,128)(2,1)S(1)} %get-tuple-element.84), channel_id=1, source_target_pairs={{0,2},{1,3},{2,0},{3,1},{4,6},{5,7},{6,4},{7,5},{8,10},{9,11},{10,... | collective-permute-start | bytes 1572872 | tf_op jit(solution)/shard_map/ppermute | solution.py:96
  432.6 1.2 copy-start.2
  473.3 1.6 copy-start.3
  474.9 28.7 %all-to-all-start.4 = ((bf16[4,8,32,512]{3,2,1,0:T(8,128)(2,1)}), bf16[4,8,32,512]{3,2,1,0:T(8,128)(2,1)S(1)}, u32[]{:S(2)}, u32[]{:S(2)}) async-start(bf16[4,8,32,512]{3,2,1,0:T(8,128)(2,1)} %get-tuple-element.85), calls=%async_computation.4 | async-start | bytes 2097152 | tf_op jit(solution)/shard_map/all_to_all | solution.py:546
  486.9 1.7 collective-permute-start.20
  486.9 2.3 collective-permute-start.21
  491.3 19.7 %collective-permute-start.22 = (bf16[12,64,256]{2,1,0:T(8,128)(2,1)S(1)}, bf16[12,64,256]{2,1,0:T(8,128)(2,1)S(1)}, u32[]{:S(2)}, u32[]{:S(2)}) collective-permute-start(bf16[12,64,256]{2,1,0:T(8,128)(2,1)S(1)} %get-tuple-element.98), channel_id=1, source_target_pairs={{0,2},{1,3},{2,0},{3,1},{4,6},{5,7},{6,4},{7,5},{8,10},{9,11},{10,... | collective-permute-start | bytes 1179656 | tf_op jit(solution)/shard_map/ppermute | solution.py:96
  507.6 1.3 collective-permute-start.17
  507.6 1.5 collective-permute-start.18
  509.7 5.8 %collective-permute-start.19 = (bf16[4,64,256]{2,1,0:T(8,128)(2,1)S(1)}, bf16[4,64,256]{2,1,0:T(8,128)(2,1)S(1)}, u32[]{:S(2)}, u32[]{:S(2)}) collective-permute-start(bf16[4,64,256]{2,1,0:T(8,128)(2,1)S(1)} %get-tuple-element.93), channel_id=1, source_target_pairs={{0,2},{1,3},{2,0},{3,1},{4,6},{5,7},{6,4},{7,5},{8,10},{9,11},{10,... | collective-permute-start | bytes 393224 | tf_op jit(solution)/shard_map/ppermute | solution.py:96

commit v7 on v4

--- a/solution.py
+++ b/solution.py
@@ -167,14 +167,13 @@
                 )
 
 
-def back_call(me, matrix, w_second, cotangent, part, parts):
+def back_call(me, matrix, w_second, cotangent, start, count):
     blocks, size, _ = w_second.shape
     rows = cotangent.shape[0]
     pair = size // (4 * blocks)
-    count = blocks // parts
     group = several(math.gcd(count, TILE // pair))
     steps = TILE // (pair * group)
-    first = part * count // group
+    first = start // group
     piece = array((blocks, count * pair, rows), BF16)
     return call(
         back_kernel,
@@ -415,28 +414,43 @@
 
     @pl.when(step % steps == steps - 1)
     def _():
-        deeps = [out.shape[1] for out in outs]
-        deep = sum(deeps)
-        for there in range(4):
+        chunks = []
+        rest = list(outs)
+        while rest:
+            swapped = len(rest[0].shape) == 4
+            refs = rest[: 1 if swapped else 4]
+            rest = rest[len(refs) :]
+            chunks.append((refs, refs[0].shape[1 if swapped else 0]))
+        deep = sum(count for _, count in chunks)
+        for bits in range(4):
+            there = me_ref[0] ^ bits
             for low in range(0, deep, TILE):
-                start = there * deep + low
-                tile = turn(turn_ref[...], held[:, start : start + TILE, :])
-                for chunk, count in enumerate(deeps):
-                    begin = sum(deeps[:chunk])
+                start = pl.multiple_of(there * deep + low, TILE)
+                tile = turn(turn_ref[...], held[:, pl.ds(start, TILE), :])
+                begin = 0
+                for refs, count in chunks:
                     least, most = max(begin, low), min(begin + count, low + TILE)
                     if least < most:
-                        outs[chunk][there, least - begin : most - begin] = tile[
-                            least - low : most - low
-                        ]
-
-
-def first_call(me, matrix, attended, w_out, masked, w_first_t, deeps):
+                        target = refs[0].at[there] if len(refs) == 1 else refs[bits]
+                        target[least - begin : most - begin] = tile[least - low : most - low]
+                    begin += count
+
+
+def first_call(me, matrix, attended, w_out, masked, w_first_t, chunks):
     blocks, size, _ = w_first_t.shape
     rows, genes = masked.shape
     width = w_out.shape[0]
     group = several(TILE)
     steps = TILE // group
     wide = spec((rows, group * size), lambda b, _: (0, b))
+    outs, places = [array((rows, genes), BF16)], [wide]
+    for deep, swapped in chunks:
+        if swapped:
+            outs.append(array((4, deep, blocks, rows), BF16))
+            places.append(spec((4, deep, TILE, rows), lambda b, _: (0, 0, b // steps, 0)))
+        else:
+            outs += [array((deep, blocks, rows), BF16)] * 4
+            places += [spec((deep, TILE, rows), lambda b, _: (0, b // steps, 0))] * 4
     hidden, *first = call(
         first_kernel,
         me,
@@ -448,25 +462,35 @@
             wide,
             spec((group, size, size), lambda b, _: (b, 0, 0)),
         ],
-        [array((rows, genes), BF16)] + [array((4, deep, blocks, rows), BF16) for deep in deeps],
-        [wide]
-        + [spec((4, deep, TILE, rows), lambda b, _: (0, 0, b // steps, 0)) for deep in deeps],
+        outs,
+        places,
         grid=(blocks // group,),
         scratch=[pltpu.VMEM((rows, width), BF16), pltpu.VMEM((TILE, size, rows), BF16)],
     )
-    return hidden, first
+    taken = []
+    for _, swapped in chunks:
+        wanted = 1 if swapped else 4
+        taken.append(first[:wanted])
+        first = first[wanted:]
+    return hidden, taken
 
 
 def second_kernel(me_ref, *refs):
-    piece, w_ref, cot_ref, hidden_ref = refs[:4]
-    out_ref, *send_ref, keep_ref, square = refs[-5:]
+    pieces = refs[: 1 if len(refs[0].shape) == 4 else 4]
+    w_ref, cot_ref, hidden_ref = refs[len(pieces) : len(pieces) + 3]
+    out_ref, *send_ref, keep_ref, square, held = refs[-6:]
     group, size, _ = w_ref.shape
-    pair = piece.shape[1] // group
+    pair = held.shape[1]
     for g in range(group):
         at = slice(g * size, (g + 1) * size)
-        permuted = jnp.concatenate(
-            [piece[s, g * pair + o] for o in range(pair) for s in range(4)], axis=0
-        )
+        mine = slice(g * pair, (g + 1) * pair)
+        if len(pieces) == 1:
+            for source in range(4):
+                held[g, :, source] = pieces[0][source, mine]
+        else:
+            for bits in range(4):
+                held[g, :, me_ref[0] ^ bits] = pieces[bits][mine]
+        permuted = held[g].reshape(size, held.shape[4])
         square[g] = jnp.dot(permuted, cot_ref[:, at], preferred_element_type=F32)
         store_quarters(me_ref[1], g, square.at[g], send_ref, keep_ref)
         mixed = lax.dot_general(
@@ -475,22 +499,22 @@
         out_ref[:, at] = (hidden_ref[:, at].astype(F32) + mixed).astype(BF16)
 
 
-def second_call(me, piece, w_second, cotangent, hidden, denoised, start):
+def second_call(me, pieces, w_second, cotangent, hidden, denoised, start):
     blocks, size, _ = w_second.shape
-    _, deep, _, rows = piece.shape
+    deep, _, rows = pieces[0].shape[-3:]
     pair = size // (4 * blocks)
     count = deep // pair
     group = several(math.gcd(count, start) if start else count)
     begin = start // group
     wide = spec((rows, group * size), lambda j, _: (0, begin + j))
     square = spec((group, size, size), lambda j, _: (begin + j, 0, 0))
-    args = [piece, w_second, cotangent, hidden]
-    in_specs = [
-        spec((4, group * pair, blocks, rows), lambda j, _: (0, j, 0, 0)),
-        square,
-        wide,
-        wide,
-    ]
+    args = [*pieces, w_second, cotangent, hidden]
+    part = (group * pair, blocks, rows)
+    if len(pieces) == 1:
+        in_specs = [spec((4, *part), lambda j, _: (0, j, 0, 0))]
+    else:
+        in_specs = [spec(part, lambda j, _: (j, 0, 0))] * 4
+    in_specs += [square, wide, wide]
     quarters = quarter_outs(count, group, size)
     aliases = {}
     if denoised is not None:
@@ -505,7 +529,10 @@
         [array(hidden.shape, BF16), *quarters[0]],
         [wide, *quarters[1]],
         grid=(count // group,),
-        scratch=[pltpu.VMEM((group, size, size), F32)],
+        scratch=[
+            pltpu.VMEM((group, size, size), F32),
+            pltpu.VMEM((group, pair, 4, blocks, rows), BF16),
+        ],
         aliases=aliases,
     )
 
@@ -514,29 +541,32 @@
     pieces, (hidden_ref, *send_ref, keep_ref, held, square) = refs[:-6], refs[-6:]
     group, size, _ = square.shape
     for g in range(group):
-        for part in range(len(pieces) // 4):
+        low = 0
+        for part in range(0, len(pieces), 4):
+            deep = pieces[part].shape[1]
             for bits in range(4):
-                held[g, me_ref[0] ^ bits, part] = pieces[part * 4 + bits][g]
-        back = held[g].reshape(size, held.shape[4])
+                held[g, me_ref[0] ^ bits, low : low + deep] = pieces[part + bits][g]
+            low += deep
+        back = held[g].reshape(size, held.shape[3])
         hidden = hidden_ref[:, g * size : (g + 1) * size]
         square[g] = jnp.dot(back, hidden, preferred_element_type=F32).T
         store_quarters(me_ref[1], g, square.at[g], send_ref, keep_ref)
 
 
 def grad_first_call(me, pieces, hidden, size, start, count):
-    _, deep, rows = pieces[0].shape
+    rows = hidden.shape[0]
     group = several(math.gcd(count, start) if start else count)
     begin = start // group
     return call(
         grad_first_kernel,
         me,
         (*pieces, hidden),
-        [spec((group, deep, rows), lambda b, _: (begin + b, 0, 0))] * len(pieces)
+        [spec((group, *piece.shape[1:]), lambda b, _: (begin + b, 0, 0)) for piece in pieces]
         + [spec((rows, group * size), lambda b, _: (0, begin + b))],
         *quarter_outs(count, group, size),
         grid=(count // group,),
         scratch=[
-            pltpu.VMEM((group, 4, len(pieces) // 4, deep, rows), BF16),
+            pltpu.VMEM((group, 4, size // 4, rows), BF16),
             pltpu.VMEM((group, size, size), F32),
         ],
     )
@@ -545,14 +575,16 @@
 def on_device_four(expression, gene_mask, mask_value, w_qkv, w_out, w_first, w_second, cotangent):
     me = jnp.stack([lax.axis_index("gene"), lax.axis_index("cell")]).astype(jnp.int32)
     blocks, size, _ = w_first.shape
-    parts = 4
     deep = size // 4
-    deeps = [deep // 2, 3 * deep // 8, deep // 8]
+    counts = [blocks // 4, blocks // 2, blocks // 4]
+    chunks = [(deep // 2, True), (3 * deep // 8, True), (deep // 8, True)]
     matrix = grid_turn()
-    sends, back = [None] * parts, [[None] * 4 for _ in range(parts)]
+    sends, back = [None] * 3, [[None] * 4 for _ in range(3)]
 
     def prepare(part, *earlier):
-        sends[part] = back_call(me, matrix, w_second, after(cotangent, *earlier), part, parts)
+        sends[part] = back_call(
+            me, matrix, w_second, after(cotangent, *earlier), sum(counts[:part]), counts[part]
+        )
         back[part][0] = sends[part][0]
 
     def begin(part, bits, *earlier):
@@ -560,45 +592,44 @@
         return back[part][bits]
 
     prepare(0)
-    first_part = [begin(0, bits) for bits in (3, 2, 1)]
+    beside_qkv = [begin(0, bits) for bits in (3, 2, 1)]
+    prepare(1, sends[0][0])
     masked, send, keep = project_call(
-        me, after(expression, sends[0][0]), gene_mask, mask_value, w_qkv
-    )
-    came = flip(after(send, *first_part), "gene", 1)
-    prepare(1, send)
-    beside_sum = [begin(1, 2), begin(1, 3)]
-    mine, other = add_call(me, keep, after(came, *beside_sum))
+        me, after(expression, sends[1][0]), gene_mask, mask_value, w_qkv
+    )
+    came = flip(after(send, *beside_qkv), "gene", 1)
+    beside_sum = begin(1, 3, send, *beside_qkv)
+    prepare(2, send)
+    w_first_t = jnp.swapaxes(after(w_first, send), 1, 2)
+    mine, other = add_call(me, keep, after(came, sends[2][0], w_first_t))
     last = flip(other, "gene", 2)
-    prepare(2, other)
-    prepare(3, sends[2][0])
-    w_first_t = jnp.swapaxes(after(w_first, other), 1, 2)
-    beside_sum = [begin(1, 1, other)]
-    queries, key_value = split_call(
-        me, mine, after(last, *beside_sum, sends[3][0], w_first_t)
-    )
+    queries, key_value = split_call(me, mine, after(last, beside_sum))
     across = flip(key_value, "cell", 2)
     beside = flip(key_value, "cell", 1)
     corner = flip(across, "cell", 1)
-    beside_keys = [begin(2, 2, last), begin(2, 1, last)]
-    queries = after(queries, *beside_keys, beside, across, corner)
+    beside_keys = [begin(1, 2, last), begin(1, 1, last)]
     attended = attend_call(me, queries, (key_value, beside, across, corner))
-    attended = after(attended, begin(2, 3, queries), begin(3, 1, queries))
+    attended = after(attended, *beside_keys)
     near = flip(attended, "gene", 1)
     far = flip(attended, "gene", 2)
     rest = flip(after(far, near), "gene", 1)
-    rest = after(rest, begin(3, 2, attended))
+    rest = after(rest, begin(2, 2, attended))
     hidden, first = first_call(
-        me, matrix, (attended, near, far, rest), w_out, masked, w_first_t, deeps
-    )
-    begin(3, 3, rest)
+        me, matrix, (attended, near, far, rest), w_out, masked, w_first_t, chunks
+    )
+    begin(2, 3, rest)
+    begin(2, 1, rest)
 
     got = []
 
     def launch(t, *earlier):
-        piece = after(first[t], *earlier)
-        got.append(lax.all_to_all(piece, "gene", split_axis=0, concat_axis=0, tiled=True))
-
-    launch(0, back[3][3])
+        pieces = after(first[t], *earlier)
+        if chunks[t][1]:
+            got.append([lax.all_to_all(pieces[0], "gene", split_axis=0, concat_axis=0, tiled=True)])
+        else:
+            got.append([pieces[0]] + [flip(pieces[bits], "gene", bits) for bits in (1, 2, 3)])
+
+    launch(0, back[2][3], back[2][1])
     denoised, shares = None, [None, None]
     back = sum(back, [])
 
@@ -613,10 +644,10 @@
     sum_cells(0, 0, send, keep)
     sum_cells(0, blocks // 2, send_next, keep_next)
     pin = shares[0]
-    for t in range(len(deeps)):
-        if t + 1 < len(deeps):
-            launch(t + 1, got[t], pin)
-        start = sum(deeps[:t]) * blocks // deep
+    for t in range(len(chunks)):
+        start = sum(count for count, _ in chunks[:t]) * blocks // deep
+        if t + 1 < len(chunks):
+            launch(t + 1, *got[t], pin)
         denoised, *send, keep = second_call(
             me, got[t], w_second, cotangent, hidden, denoised, start
         )

time: 493 us -> 484 us (0.982)
  starting transfers between devices: 53.2 us -> 41 us
  waiting for transfers between devices: 269 us -> 278 us
  local copies, waits for them, and re-layouts: 17.3 us -> 12.3 us
    ppermute x35 -> x32, starting transfers between devices: 41.1 us -> 28 us  [flip(): return lax.ppermute(value, axis, pairs)]
    ppermute x35 -> x32, waiting for transfers between devices: 174 us -> 180 us  [flip(): return lax.ppermute(value, axis, pairs)]
    unnamed x50 -> x38, local copies, waits for them, and re-layouts: 10.9 us -> 5.86 us
    pallas_call x24 -> x23, Pallas kernels: 151 us -> 151 us  [call(): pl.pallas_call(body, out_shape=outs, grid_spec=pltpu.PrefetchScalarGridSp...]
  transfers between devices with their start and end apart: 38 -> 35, of which waited for: 25 -> 22; matrix products, arithmetic and copies ran while one was open for 1% -> 1% of each run, Pallas kernels for 28% -> 29%
where the time goes in v7:
time: 484 us; the launch traced here: 483 us
  waiting for transfers between devices  278 us (57%)
  Pallas kernels  151 us (31%)
  starting transfers between devices  41 us (8%)
  local copies, waits for them, and re-layouts  12.3 us (3%)
    ppermute x32, waiting for transfers between devices, flip(): return lax.ppermute(value, axis, pairs)  180 us
    pallas_call x23, Pallas kernels, call(): pl.pallas_call(body, out_shape=outs, grid_spec=pltpu.PrefetchScalarGridSp...  151 us
    all_to_all x3, waiting for transfers between devices, launch(): lax.all_to_all(pieces[0], 'gene', split_axis=0, concat_axis=0, tiled=True)  98.1 us
    ppermute x32, starting transfers between devices, flip(): return lax.ppermute(value, axis, pairs)  28 us
    all_to_all x3, starting transfers between devices, launch(): lax.all_to_all(pieces[0], 'gene', split_axis=0, concat_axis=0, tiled=True)  13 us
  transfers between devices with their start and end apart: 35, of which 22 were waited for; matrix products, arithmetic and copies ran while one was open for 1% of the time, Pallas kernels for 29%

profile of v7, /device:TPU:0, one launch (start us, length us, event | category | flops | bytes accessed | tf_op | source)
XLA Modules:
  0.0 482.9 jit_solution(15594027836183329362)
XLA Ops:
  1.0 4.4 shard_map.103
  5.5 4.0 collective-permute-start.1
  11.1 8.1 %shard_map.104 = (bf16[32,32,512]{2,1,0:T(8,128)(2,1)S(1)}, bf16[32,32,512]{2,1,0:T(8,128)(2,1)}, bf16[32,32,512]{2,1,0:T(8,128)(2,1)}, bf16[32,32,512]{2,1,0:T(8,128)(2,1)}) custom-call(s32[2]{0:T(128)S(1)} %pad_add_fusion.me_ref._, bf16[256,256]{1,0:T(8,128)(2,1)S(1)} %fusion.turn_ref, bf16[32,256,256]{2,1,0:T(8,128)(2,1)} %refs_1_.5, ...), custom_call_target="tpu_custom_call" | custom-call | flops 1 | bytes 1 | tf_op jit(solution)/shard_map/pallas_call | solution.py:100
  20.2 37.8 %shard_map.105 = (bf16[512,8192]{1,0:T(8,128)(2,1)}, bf16[2,512,768]{2,1,0:T(8,128)(2,1)S(1)}, f32[2,512,768]{2,1,0:T(8,128)}) custom-call(s32[2]{0:T(128)S(1)} %pad_add_fusion.me_ref._, bf16[512,8192]{1,0:T(8,128)(2,1)} %value_ref, s32[512,8192]{1,0:T(8,128)} %mask_ref.1, bf16[1,8192]{1,0:T(2,128)(2,1)S(1)} %reshape.9.fill_ref, bf16[8192,3072]{1,0:T(8,128)(2,1)} %weight_ref.1), custom_call_target="tpu_custom_call" | custom-call | flops 1 | bytes 1 | tf_op jit(solution)/shard_map/pallas_call | solution.py:100
  58.0 1.9 collective-permute-start.3
  59.9 2.5 collective-permute-start.5
  62.4 4.5 shard_map.106
  67.7 6.5 %copy.16 = bf16[32,256,256]{1,2,0:T(8,128)(2,1)} copy(bf16[32,256,256]{2,1,0:T(8,128)(2,1)} %param.13) | data formatting | bytes 8388608 | tf_op jit(solution)/shard_map/optimization_barrier | solution.py:91
  74.1 20.6 %collective-permute-done.3.came_ref = bf16[2,512,768]{2,1,0:T(8,128)(2,1)} collective-permute-done((bf16[2,512,768]{2,1,0:T(8,128)(2,1)S(1)}, bf16[2,512,768]{2,1,0:T(8,128)(2,1)}, u32[]{:S(2)}, u32[]{:S(2)}) %collective-permute-start.3) | collective-permute-done | bytes 1572896 | tf_op jit(solution)/shard_map/ppermute | solution.py:96
  94.8 4.2 shard_map.107
  98.9 3.6 collective-permute-start.4
  102.5 49.3 %collective-permute-done.4.came_ref = bf16[512,768]{1,0:T(8,128)(2,1)S(1)} collective-permute-done((bf16[512,768]{1,0:T(8,128)(2,1)S(1)}, bf16[512,768]{1,0:T(8,128)(2,1)S(1)}, u32[]{:S(2)}, u32[]{:S(2)}) %collective-permute-start.4) | collective-permute-done | bytes 786464 | tf_op jit(solution)/shard_map/ppermute | solution.py:96
  151.8 3.2 shard_map.108
  155.0 1.6 collective-permute-start.7
  156.6 1.9 collective-permute-start.10
  158.5 10.4 %collective-permute-done.7.refs_2_ = bf16[512,512]{1,0:T(8,128)(2,1)S(1)} collective-permute-done((bf16[512,512]{1,0:T(8,128)(2,1)S(1)}, bf16[512,512]{1,0:T(8,128)(2,1)S(1)}, u32[]{:S(2)}, u32[]{:S(2)}) %collective-permute-start.7) | collective-permute-done | bytes 524320 | tf_op jit(solution)/shard_map/ppermute | solution.py:96
  168.9 1.9 collective-permute-done.8.refs_3_
  171.6 7.3 %shard_map.109.own = bf16[512,256]{1,0:T(8,128)(2,1)S(1)} custom-call(s32[2]{0:T(128)S(1)} %pad_add_fusion.me_ref._, bf16[512,256]{1,0:T(8,128)(2,1)S(1)} %get-tuple-element.92.query_ref, bf16[512,512]{1,0:T(8,128)(2,1)S(1)} %get-tuple-element.93.refs_0_, bf16[512,512]{1,0:T(8,128)(2,1)S(1)} %collective-permute-done.6.refs_1_, bf16[512,512]{1,0:T(8,128)(2,1)} %copy-done.13, ...), custom_call_target="tpu_custom_call" | custom-call | flops 1 | bytes 1 | tf_op jit(solution)/shard_map/pallas_call | solution.py:100
  179.0 24.6 %collective-permute-done.9.refs_6_ = bf16[32,32,512]{2,1,0:T(8,128)(2,1)S(1)} collective-permute-done((bf16[32,32,512]{2,1,0:T(8,128)(2,1)S(1)}, bf16[32,32,512]{2,1,0:T(8,128)(2,1)S(1)}, u32[]{:S(2)}, u32[]{:S(2)}) %collective-permute-start.9) | collective-permute-done | bytes 1048608 | tf_op jit(solution)/shard_map/ppermute | solution.py:96
  204.1 2.7 collective-permute-start.11
  207.1 12.4 %collective-permute-done.12.far = bf16[512,256]{1,0:T(8,128)(2,1)S(1)} collective-permute-done((bf16[512,256]{1,0:T(8,128)(2,1)S(1)}, bf16[512,256]{1,0:T(8,128)(2,1)S(1)}, u32[]{:S(2)}, u32[]{:S(2)}) %collective-permute-start.12) | collective-permute-done | bytes 262176 | tf_op jit(solution)/shard_map/ppermute | solution.py:96
  219.5 21.2 %collective-permute-done.14.refs_10_ = bf16[32,16,512]{2,1,0:T(8,128)(2,1)S(1)} collective-permute-done((bf16[32,16,512]{2,1,0:T(8,128)(2,1)S(1)}, bf16[32,16,512]{2,1,0:T(8,128)(2,1)S(1)}, u32[]{:S(2)}, u32[]{:S(2)}) %collective-permute-start.14) | collective-permute-done | bytes 524320 | tf_op jit(solution)/shard_map/ppermute | solution.py:96
  240.7 1.4 collective-permute-start.15
  242.1 24.5 %shard_map.110 = (bf16[512,8192]{1,0:T(8,128)(2,1)}, bf16[4,32,32,512]{3,2,1,0:T(8,128)(2,1)}, bf16[4,24,32,512]{3,2,1,0:T(8,128)(2,1)}, bf16[4,8,32,512]{3,2,1,0:T(8,128)(2,1)}) custom-call(s32[2]{0:T(128)S(1)} %pad_add_fusion.me_ref._, bf16[256,256]{1,0:T(8,128)(2,1)S(1)} %fusion.turn_ref, bf16[512,256]{1,0:T(8,128)(2,1)S(1)} %shard_map.109.own, ...), custom_call_target="tpu_custom_call" | custom-call | flops 1 | bytes 1 | tf_op jit(solution)/shard_map/pallas_call | solution.py:100
  267.7 4.8 %all-to-all-start = ((bf16[4,32,32,512]{3,2,1,0:T(8,128)(2,1)}), bf16[4,32,32,512]{3,2,1,0:T(8,128)(2,1)}, u32[]{:S(2)}, u32[]{:S(2)}) async-start(bf16[4,32,32,512]{3,2,1,0:T(8,128)(2,1)} %get-tuple-element.111), calls=%async_computation | async-start | bytes 8388608 | tf_op jit(solution)/shard_map/all_to_all | solution.py:628
  272.5 7.0 %shard_map.113 = (bf16[16,64,256]{2,1,0:T(8,128)(2,1)S(1)}, bf16[16,64,256]{2,1,0:T(8,128)(2,1)S(1)}, f32[2,16,64,256]{3,2,1,0:T(8,128)}) custom-call(s32[2]{0:T(128)S(1)} %pad_add_fusion.me_ref._, bf16[32,16,512]{2,1,0:T(8,128)(2,1)S(1)} %get-tuple-element.73.refs_0_, bf16[32,16,512]{2,1,0:T(8,128)(2,1)} %copy-done.9, bf16[32,16,512]{2,1,0:T(8,128)(2,1)} %copy-done.7, ...), custom_call_target="tpu_custom_call" | custom-call | flops 1 | bytes 1 | tf_op jit(solution)/shard_map/pallas_call | solution.py:100
  280.1 7.0 %shard_map.111 = (bf16[16,64,256]{2,1,0:T(8,128)(2,1)S(1)}, bf16[16,64,256]{2,1,0:T(8,128)(2,1)S(1)}, f32[2,16,64,256]{3,2,1,0:T(8,128)}) custom-call(s32[2]{0:T(128)S(1)} %pad_add_fusion.me_ref._, bf16[32,16,512]{2,1,0:T(8,128)(2,1)S(1)} %get-tuple-element.73.refs_0_, bf16[32,16,512]{2,1,0:T(8,128)(2,1)} %copy-done.9, bf16[32,16,512]{2,1,0:T(8,128)(2,1)} %copy-done.7, ...), custom_call_target="tpu_custom_call" | custom-call | flops 1 | bytes 1 | tf_op jit(solution)/shard_map/pallas_call | solution.py:100
  287.7 3.2 shard_map.114
  291.5 3.2 shard_map.112
  294.7 1.5 collective-permute-start.19
  296.2 9.5 %collective-permute-done.22.came_ref = bf16[16,64,256]{2,1,0:T(8,128)(2,1)S(1)} collective-permute-done((bf16[16,64,256]{2,1,0:T(8,128)(2,1)S(1)}, bf16[16,64,256]{2,1,0:T(8,128)(2,1)S(1)}, u32[]{:S(2)}, u32[]{:S(2)}) %collective-permute-start.22) | collective-permute-done | bytes 524320 | tf_op jit(solution)/shard_map/ppermute | solution.py:96
  306.9 1.6 shard_map.115.refs_0_
  308.5 7.5 %collective-permute-done.19.came_ref = bf16[16,64,256]{2,1,0:T(8,128)(2,1)S(1)} collective-permute-done((bf16[16,64,256]{2,1,0:T(8,128)(2,1)S(1)}, bf16[16,64,256]{2,1,0:T(8,128)(2,1)S(1)}, u32[]{:S(2)}, u32[]{:S(2)}) %collective-permute-start.19) | collective-permute-done | bytes 524320 | tf_op jit(solution)/shard_map/ppermute | solution.py:96
  316.1 1.6 shard_map.116
  317.6 48.3 %all-to-all-done.refs_0_ = bf16[4,32,32,512]{3,2,1,0:T(8,128)(2,1)} async-done(((bf16[4,32,32,512]{3,2,1,0:T(8,128)(2,1)}), bf16[4,32,32,512]{3,2,1,0:T(8,128)(2,1)}, u32[]{:S(2)}, u32[]{:S(2)}) %all-to-all-start) | async-done | bytes 4194336 | tf_op jit(solution)/shard_map/all_to_all | solution.py:628
  366.0 4.6 all-to-all-start.1
  370.6 9.6 %shard_map.117 = (bf16[512,8192]{1,0:T(8,128)(2,1)}, bf16[16,64,256]{2,1,0:T(8,128)(2,1)S(1)}, bf16[16,64,256]{2,1,0:T(8,128)(2,1)S(1)}, f32[2,16,64,256]{3,2,1,0:T(8,128)}) custom-call(s32[2]{0:T(128)S(1)} %pad_add_fusion.me_ref._, bf16[4,32,32,512]{3,2,1,0:T(8,128)(2,1)} %all-to-all-done.refs_0_, bf16[32,256,256]{2,1,0:T(8,128)(2,1)} %refs_1_.5, ...), custom_call_target="tpu_custom_call" | custom-call | flops 1 | bytes 1 | tf_op jit(solution)/shard_map/pallas_call | solution.py:100
  382.9 3.3 shard_map.118
  386.7 13.4 %collective-permute-done.25.came_ref = bf16[16,64,256]{2,1,0:T(8,128)(2,1)S(1)} collective-permute-done((bf16[16,64,256]{2,1,0:T(8,128)(2,1)S(1)}, bf16[16,64,256]{2,1,0:T(8,128)(2,1)S(1)}, u32[]{:S(2)}, u32[]{:S(2)}) %collective-permute-start.25) | collective-permute-done | bytes 524320 | tf_op jit(solution)/shard_map/ppermute | solution.py:96
  401.4 1.6 shard_map.119.refs_0_
  403.0 38.0 %all-to-all-done.1.refs_0_ = bf16[4,24,32,512]{3,2,1,0:T(8,128)(2,1)} async-done(((bf16[4,24,32,512]{3,2,1,0:T(8,128)(2,1)}), bf16[4,24,32,512]{3,2,1,0:T(8,128)(2,1)}, u32[]{:S(2)}, u32[]{:S(2)}) %all-to-all-start.1) | async-done | bytes 3145760 | tf_op jit(solution)/shard_map/all_to_all | solution.py:628
  441.0 3.5 all-to-all-start.2
  444.6 8.5 %shard_map.120 = (bf16[512,8192]{1,0:T(8,128)(2,1)}, bf16[12,64,256]{2,1,0:T(8,128)(2,1)S(1)}, bf16[12,64,256]{2,1,0:T(8,128)(2,1)S(1)}, f32[2,12,64,256]{3,2,1,0:T(8,128)}) custom-call(s32[2]{0:T(128)S(1)} %pad_add_fusion.me_ref._, bf16[4,24,32,512]{3,2,1,0:T(8,128)(2,1)} %all-to-all-done.1.refs_0_, ...), custom_call_target="tpu_custom_call", output_to_operand_aliasing={{0}: (5, {})} | custom-call | flops 1 | bytes 1 | tf_op jit(solution)/shard_map/pallas_call | solution.py:100
  455.3 2.1 shard_map.123
  458.0 11.7 %all-to-all-done.2.refs_0_ = bf16[4,8,32,512]{3,2,1,0:T(8,128)(2,1)S(1)} async-done(((bf16[4,8,32,512]{3,2,1,0:T(8,128)(2,1)}), bf16[4,8,32,512]{3,2,1,0:T(8,128)(2,1)S(1)}, u32[]{:S(2)}, u32[]{:S(2)}) %all-to-all-start.2) | async-done | bytes 1048608 | tf_op jit(solution)/shard_map/all_to_all | solution.py:628
  469.7 4.0 shard_map.121
  476.5 2.0 shard_map.124.refs_0_
  478.5 3.2 collective-permute-done.28.came_ref
  (90 shorter events, 20.6 us)
Async XLA Ops:
  5.5 52.5 %collective-permute-start.1 = (bf16[32,16,512]{2,1,0:T(8,128)(2,1)S(1)}, bf16[32,16,512]{2,1,0:T(8,128)(2,1)S(1)}, u32[]{:S(2)}, u32[]{:S(2)}) collective-permute-start(bf16[32,16,512]{2,1,0:T(8,128)(2,1)S(1)} %get-tuple-element.80), channel_id=1, source_target_pairs={{0,8},{4,12},{8,0},{12,4},{1,9},{5,13},{9,1},{13,5},{2,10},{6,14},... | collective-permute-start | bytes 1572872 | tf_op jit(solution)/shard_map/ppermute | solution.py:96
  9.5 48.5 %collective-permute-start = (bf16[32,16,512]{2,1,0:T(8,128)(2,1)}, bf16[32,16,512]{2,1,0:T(8,128)(2,1)S(1)}, u32[]{:S(2)}, u32[]{:S(2)}) collective-permute-start(bf16[32,16,512]{2,1,0:T(8,128)(2,1)} %get-tuple-element.79), channel_id=1, source_target_pairs={{0,12},{4,8},{8,4},{12,0},{1,13},{5,9},{9,5},{13,1},{2,14},{6,10},... | collective-permute-start | bytes 1572872 | tf_op jit(solution)/shard_map/ppermute | solution.py:96
  10.9 47.2 %collective-permute-start.2 = (bf16[32,16,512]{2,1,0:T(8,128)(2,1)S(1)}, bf16[32,16,512]{2,1,0:T(8,128)(2,1)S(1)}, u32[]{:S(2)}, u32[]{:S(2)}) collective-permute-start(bf16[32,16,512]{2,1,0:T(8,128)(2,1)S(1)} %get-tuple-element.81), channel_id=1, source_target_pairs={{0,4},{4,0},{8,12},{12,8},{1,5},{5,1},{9,13},{13,9},{2,6},{6,2},{1... | collective-permute-start | bytes 1572872 | tf_op jit(solution)/shard_map/ppermute | solution.py:96
  11.1 9.1 %copy-start.15 = (bf16[8192]{0:T(1024)(128)(2,1)S(1)}, bf16[8192]{0:T(1024)(128)(2,1)}, u32[]{:S(2)}) copy-start(bf16[8192]{0:T(1024)(128)(2,1)} %param.10) | copy-start | bytes 49156
  58.0 1.9 copy-start.7
  58.0 4.4 copy-start.8
  58.0 4.4 copy-start.9
  58.0 36.7 %collective-permute-start.3 = (bf16[2,512,768]{2,1,0:T(8,128)(2,1)S(1)}, bf16[2,512,768]{2,1,0:T(8,128)(2,1)}, u32[]{:S(2)}, u32[]{:S(2)}) collective-permute-start(bf16[2,512,768]{2,1,0:T(8,128)(2,1)S(1)} %get-tuple-element.82), channel_id=1, source_target_pairs={{0,4},{4,0},{8,12},{12,8},{1,5},{5,1},{9,13},{13,9},{2,6},{6,2},{1... | collective-permute-start | bytes 4718600 | tf_op jit(solution)/shard_map/ppermute | solution.py:96
  59.9 91.9 %collective-permute-start.5 = (bf16[32,32,512]{2,1,0:T(8,128)(2,1)}, bf16[32,32,512]{2,1,0:T(8,128)(2,1)}, u32[]{:S(2)}, u32[]{:S(2)}) collective-permute-start(bf16[32,32,512]{2,1,0:T(8,128)(2,1)} %get-tuple-element.90), channel_id=1, source_target_pairs={{0,12},{4,8},{8,4},{12,0},{1,13},{5,9},{9,5},{13,1},{2,14},{6,10},... | collective-permute-start | bytes 3145736 | tf_op jit(solution)/shard_map/ppermute | solution.py:96
  74.1 82.5 %copy-start.17 = (bf16[32,32,512]{2,1,0:T(8,128)(2,1)S(1)}, bf16[32,32,512]{2,1,0:T(8,128)(2,1)}, u32[]{:S(2)}) copy-start(bf16[32,32,512]{2,1,0:T(8,128)(2,1)} %get-tuple-element.95) | copy-start | bytes 3145732
  74.1 82.5 %copy-start.16 = (bf16[32,32,512]{2,1,0:T(8,128)(2,1)S(1)}, bf16[32,32,512]{2,1,0:T(8,128)(2,1)}, u32[]{:S(2)}) copy-start(bf16[32,32,512]{2,1,0:T(8,128)(2,1)} %get-tuple-element.97) | copy-start | bytes 3145732
  94.8 145.9 %copy-start.18 = (bf16[32,16,512]{2,1,0:T(8,128)(2,1)S(1)}, bf16[32,16,512]{2,1,0:T(8,128)(2,1)}, u32[]{:S(2)}) copy-start(bf16[32,16,512]{2,1,0:T(8,128)(2,1)} %get-tuple-element.108) | copy-start | bytes 1572868
  98.9 52.9 %collective-permute-start.4 = (bf16[512,768]{1,0:T(8,128)(2,1)S(1)}, bf16[512,768]{1,0:T(8,128)(2,1)S(1)}, u32[]{:S(2)}, u32[]{:S(2)}) collective-permute-start(bf16[512,768]{1,0:T(8,128)(2,1)S(1)} %get-tuple-element.88), channel_id=1, source_target_pairs={{0,8},{4,12},{8,0},{12,4},{1,9},{5,13},{9,1},{13,5},{2,10},{6,14},... | collective-permute-start | bytes 2359304 | tf_op jit(solution)/shard_map/ppermute | solution.py:96
  155.0 13.9 %collective-permute-start.7 = (bf16[512,512]{1,0:T(8,128)(2,1)S(1)}, bf16[512,512]{1,0:T(8,128)(2,1)S(1)}, u32[]{:S(2)}, u32[]{:S(2)}) collective-permute-start(bf16[512,512]{1,0:T(8,128)(2,1)S(1)} %get-tuple-element.93.refs_0_), channel_id=1, source_target_pairs={{0,2},{1,3},{2,0},{3,1},{4,6},{5,7},{6,4},{7,5},{8,10},{9,11},{10,... | collective-permute-start | bytes 1572872 | tf_op jit(solution)/shard_map/ppermute | solution.py:96
  156.6 47.0 %collective-permute-start.9 = (bf16[32,32,512]{2,1,0:T(8,128)(2,1)S(1)}, bf16[32,32,512]{2,1,0:T(8,128)(2,1)S(1)}, u32[]{:S(2)}, u32[]{:S(2)}) collective-permute-start(bf16[32,32,512]{2,1,0:T(8,128)(2,1)S(1)} %copy-done.17), channel_id=1, source_target_pairs={{0,8},{4,12},{8,0},{12,4},{1,9},{5,13},{9,1},{13,5},{2,10},{6,14},... | collective-permute-start | bytes 3145736 | tf_op jit(solution)/shard_map/ppermute | solution.py:96
  156.6 47.3 %collective-permute-start.10 = (bf16[32,32,512]{2,1,0:T(8,128)(2,1)S(1)}, bf16[32,32,512]{2,1,0:T(8,128)(2,1)S(1)}, u32[]{:S(2)}, u32[]{:S(2)}) collective-permute-start(bf16[32,32,512]{2,1,0:T(8,128)(2,1)S(1)} %copy-done.16), channel_id=1, source_target_pairs={{0,4},{4,0},{8,12},{12,8},{1,5},{5,1},{9,13},{13,9},{2,6},{6,2},{1... | collective-permute-start | bytes 3145736 | tf_op jit(solution)/shard_map/ppermute | solution.py:96
  158.5 10.4 %collective-permute-start.6 = (bf16[512,512]{1,0:T(8,128)(2,1)S(1)}, bf16[512,512]{1,0:T(8,128)(2,1)S(1)}, u32[]{:S(2)}, u32[]{:S(2)}) collective-permute-start(bf16[512,512]{1,0:T(8,128)(2,1)S(1)} %get-tuple-element.93.refs_0_), channel_id=1, source_target_pairs={{0,1},{1,0},{2,3},{3,2},{4,5},{5,4},{6,7},{7,6},{8,9},{9,8},{10,11... | collective-permute-start | bytes 1572872 | tf_op jit(solution)/shard_map/ppermute | solution.py:96
  168.9 1.9 copy-start.13
  168.9 1.9 collective-permute-start.8
  203.6 63.1 %copy-start.5 = (bf16[32,32,512]{2,1,0:T(8,128)(2,1)}, bf16[32,32,512]{2,1,0:T(8,128)(2,1)S(1)}, u32[]{:S(2)}) copy-start(bf16[32,32,512]{2,1,0:T(8,128)(2,1)S(1)} %collective-permute-done.9.refs_6_) | copy-start | bytes 3145732
  203.9 62.7 %copy-start.6 = (bf16[32,32,512]{2,1,0:T(8,128)(2,1)}, bf16[32,32,512]{2,1,0:T(8,128)(2,1)S(1)}, u32[]{:S(2)}) copy-start(bf16[32,32,512]{2,1,0:T(8,128)(2,1)S(1)} %collective-permute-done.10.refs_5_) | copy-start | bytes 3145732
  203.9 15.6 %collective-permute-start.12 = (bf16[512,256]{1,0:T(8,128)(2,1)S(1)}, bf16[512,256]{1,0:T(8,128)(2,1)S(1)}, u32[]{:S(2)}, u32[]{:S(2)}) collective-permute-start(bf16[512,256]{1,0:T(8,128)(2,1)S(1)} %shard_map.109.own), channel_id=1, source_target_pairs={{0,8},{4,12},{8,0},{12,4},{1,9},{5,13},{9,1},{13,5},{2,10},{6,14},... | collective-permute-start | bytes 786440 | tf_op jit(solution)/shard_map/ppermute | solution.py:96
  204.1 15.4 %collective-permute-start.11 = (bf16[512,256]{1,0:T(8,128)(2,1)S(1)}, bf16[512,256]{1,0:T(8,128)(2,1)S(1)}, u32[]{:S(2)}, u32[]{:S(2)}) collective-permute-start(bf16[512,256]{1,0:T(8,128)(2,1)S(1)} %shard_map.109.own), channel_id=1, source_target_pairs={{0,4},{4,0},{8,12},{12,8},{1,5},{5,1},{9,13},{13,9},{2,6},{6,2},{1... | collective-permute-start | bytes 786440 | tf_op jit(solution)/shard_map/ppermute | solution.py:96
  206.8 33.9 %collective-permute-start.14 = (bf16[32,16,512]{2,1,0:T(8,128)(2,1)S(1)}, bf16[32,16,512]{2,1,0:T(8,128)(2,1)S(1)}, u32[]{:S(2)}, u32[]{:S(2)}) collective-permute-start(bf16[32,16,512]{2,1,0:T(8,128)(2,1)S(1)} %get-tuple-element.101), channel_id=1, source_target_pairs={{0,8},{4,12},{8,0},{12,4},{1,9},{5,13},{9,1},{13,5},{2,10},{6,14},... | collective-permute-start | bytes 1572872 | tf_op jit(solution)/shard_map/ppermute | solution.py:96
  219.5 21.2 %collective-permute-start.13 = (bf16[512,256]{1,0:T(8,128)(2,1)S(1)}, bf16[512,256]{1,0:T(8,128)(2,1)S(1)}, u32[]{:S(2)}, u32[]{:S(2)}) collective-permute-start(bf16[512,256]{1,0:T(8,128)(2,1)S(1)} %collective-permute-done.12.far), channel_id=1, source_target_pairs={{0,4},{4,0},{8,12},{12,8},{1,5},{5,1},{9,13},{13,9},{2,6},{6,2},{1... | collective-permute-start | bytes 786440 | tf_op jit(solution)/shard_map/ppermute | solution.py:96
  240.7 26.0 %copy-start.10 = (bf16[32,16,512]{2,1,0:T(8,128)(2,1)}, bf16[32,16,512]{2,1,0:T(8,128)(2,1)S(1)}, u32[]{:S(2)}) copy-start(bf16[32,16,512]{2,1,0:T(8,128)(2,1)S(1)} %collective-permute-done.14.refs_10_) | copy-start | bytes 1572868
  240.7 26.0 %collective-permute-start.15 = (bf16[32,16,512]{2,1,0:T(8,128)(2,1)S(1)}, bf16[32,16,512]{2,1,0:T(8,128)(2,1)S(1)}, u32[]{:S(2)}, u32[]{:S(2)}) collective-permute-start(bf16[32,16,512]{2,1,0:T(8,128)(2,1)S(1)} %copy-done.18), channel_id=1, source_target_pairs={{0,12},{4,8},{8,4},{12,0},{1,13},{5,9},{9,5},{13,1},{2,14},{6,10},... | collective-permute-start | bytes 1572872 | tf_op jit(solution)/shard_map/ppermute | solution.py:96
  242.1 24.8 %collective-permute-start.16 = (bf16[32,16,512]{2,1,0:T(8,128)(2,1)S(1)}, bf16[32,16,512]{2,1,0:T(8,128)(2,1)S(1)}, u32[]{:S(2)}, u32[]{:S(2)}) collective-permute-start(bf16[32,16,512]{2,1,0:T(8,128)(2,1)S(1)} %get-tuple-element.110), channel_id=1, source_target_pairs={{0,4},{4,0},{8,12},{12,8},{1,5},{5,1},{9,13},{13,9},{2,6},{6,2},{1... | collective-permute-start | bytes 1572872 | tf_op jit(solution)/shard_map/ppermute | solution.py:96
  267.7 98.3 %all-to-all-start = ((bf16[4,32,32,512]{3,2,1,0:T(8,128)(2,1)}), bf16[4,32,32,512]{3,2,1,0:T(8,128)(2,1)}, u32[]{:S(2)}, u32[]{:S(2)}) async-start(bf16[4,32,32,512]{3,2,1,0:T(8,128)(2,1)} %get-tuple-element.111), calls=%async_computation | async-start | bytes 8388608 | tf_op jit(solution)/shard_map/all_to_all | solution.py:628
  279.5 8.1 %collective-permute-start.20 = (bf16[16,64,256]{2,1,0:T(8,128)(2,1)S(1)}, bf16[16,64,256]{2,1,0:T(8,128)(2,1)S(1)}, u32[]{:S(2)}, u32[]{:S(2)}) collective-permute-start(bf16[16,64,256]{2,1,0:T(8,128)(2,1)S(1)} %get-tuple-element.119), channel_id=1, source_target_pairs={{0,1},{1,0},{2,3},{3,2},{4,5},{5,4},{6,7},{7,6},{8,9},{9,8},{10,11... | collective-permute-start | bytes 1572872 | tf_op jit(solution)/shard_map/ppermute | solution.py:96
  279.6 8.1 %collective-permute-start.21 = (bf16[16,64,256]{2,1,0:T(8,128)(2,1)S(1)}, bf16[16,64,256]{2,1,0:T(8,128)(2,1)S(1)}, u32[]{:S(2)}, u32[]{:S(2)}) collective-permute-start(bf16[16,64,256]{2,1,0:T(8,128)(2,1)S(1)} %get-tuple-element.120), channel_id=1, source_target_pairs={{0,1},{1,0},{2,3},{3,2},{4,5},{5,4},{6,7},{7,6},{8,9},{9,8},{10,11... | collective-permute-start | bytes 1572872 | tf_op jit(solution)/shard_map/ppermute | solution.py:96
  287.1 4.4 collective-permute-start.17
  287.2 4.2 collective-permute-start.18
  290.9 14.8 %collective-permute-start.22 = (bf16[16,64,256]{2,1,0:T(8,128)(2,1)S(1)}, bf16[16,64,256]{2,1,0:T(8,128)(2,1)S(1)}, u32[]{:S(2)}, u32[]{:S(2)}) collective-permute-start(bf16[16,64,256]{2,1,0:T(8,128)(2,1)S(1)} %get-tuple-element.122), channel_id=1, source_target_pairs={{0,2},{1,3},{2,0},{3,1},{4,6},{5,7},{6,4},{7,5},{8,10},{9,11},{10,... | collective-permute-start | bytes 1572872 | tf_op jit(solution)/shard_map/ppermute | solution.py:96
  294.7 21.4 %collective-permute-start.19 = (bf16[16,64,256]{2,1,0:T(8,128)(2,1)S(1)}, bf16[16,64,256]{2,1,0:T(8,128)(2,1)S(1)}, u32[]{:S(2)}, u32[]{:S(2)}) collective-permute-start(bf16[16,64,256]{2,1,0:T(8,128)(2,1)S(1)} %get-tuple-element.117), channel_id=1, source_target_pairs={{0,2},{1,3},{2,0},{3,1},{4,6},{5,7},{6,4},{7,5},{8,10},{9,11},{10,... | collective-permute-start | bytes 1572872 | tf_op jit(solution)/shard_map/ppermute | solution.py:96
  305.7 1.2 copy-start.2
  306.9 9.1 %copy-start.3 = (f32[16,64,256]{2,1,0:T(8,128)S(1)}, f32[16,64,256]{2,1,0:T(8,128)}, u32[]{:S(2)}) copy-start(f32[16,64,256]{2,1,0:T(8,128)} %get-tuple-element.116.mine_ref) | copy-start | bytes 3145732
  366.0 75.0 %all-to-all-start.1 = ((bf16[4,24,32,512]{3,2,1,0:T(8,128)(2,1)}), bf16[4,24,32,512]{3,2,1,0:T(8,128)(2,1)}, u32[]{:S(2)}, u32[]{:S(2)}) async-start(bf16[4,24,32,512]{3,2,1,0:T(8,128)(2,1)} %get-tuple-element.123), calls=%async_computation.1 | async-start | bytes 6291456 | tf_op jit(solution)/shard_map/all_to_all | solution.py:628
  380.3 1.9 collective-permute-start.23
  380.3 2.7 collective-permute-start.24
  386.2 14.0 %collective-permute-start.25 = (bf16[16,64,256]{2,1,0:T(8,128)(2,1)S(1)}, bf16[16,64,256]{2,1,0:T(8,128)(2,1)S(1)}, u32[]{:S(2)}, u32[]{:S(2)}) collective-permute-start(bf16[16,64,256]{2,1,0:T(8,128)(2,1)S(1)} %get-tuple-element.128), channel_id=1, source_target_pairs={{0,2},{1,3},{2,0},{3,1},{4,6},{5,7},{6,4},{7,5},{8,10},{9,11},{10,... | collective-permute-start | bytes 1572872 | tf_op jit(solution)/shard_map/ppermute | solution.py:96
  441.0 28.7 %all-to-all-start.2 = ((bf16[4,8,32,512]{3,2,1,0:T(8,128)(2,1)}), bf16[4,8,32,512]{3,2,1,0:T(8,128)(2,1)S(1)}, u32[]{:S(2)}, u32[]{:S(2)}) async-start(bf16[4,8,32,512]{3,2,1,0:T(8,128)(2,1)} %get-tuple-element.129), calls=%async_computation.2 | async-start | bytes 2097152 | tf_op jit(solution)/shard_map/all_to_all | solution.py:628
  453.0 1.7 collective-permute-start.29
  453.0 2.3 collective-permute-start.30
  457.4 19.0 %collective-permute-start.31 = (bf16[12,64,256]{2,1,0:T(8,128)(2,1)S(1)}, bf16[12,64,256]{2,1,0:T(8,128)(2,1)S(1)}, u32[]{:S(2)}, u32[]{:S(2)}) collective-permute-start(bf16[12,64,256]{2,1,0:T(8,128)(2,1)S(1)} %get-tuple-element.142), channel_id=1, source_target_pairs={{0,2},{1,3},{2,0},{3,1},{4,6},{5,7},{6,4},{7,5},{8,10},{9,11},{10,... | collective-permute-start | bytes 1179656 | tf_op jit(solution)/shard_map/ppermute | solution.py:96
  473.7 1.3 collective-permute-start.26
  473.7 1.5 collective-permute-start.27
  475.9 5.8 %collective-permute-start.28 = (bf16[4,64,256]{2,1,0:T(8,128)(2,1)S(1)}, bf16[4,64,256]{2,1,0:T(8,128)(2,1)S(1)}, u32[]{:S(2)}, u32[]{:S(2)}) collective-permute-start(bf16[4,64,256]{2,1,0:T(8,128)(2,1)S(1)} %get-tuple-element.137), channel_id=1, source_target_pairs={{0,2},{1,3},{2,0},{3,1},{4,6},{5,7},{6,4},{7,5},{8,10},{9,11},{10,... | collective-permute-start | bytes 393224 | tf_op jit(solution)/shard_map/ppermute | solution.py:96
  (6 other events, 5.4 us)

commit v8 on v7

--- a/solution.py
+++ b/solution.py
@@ -331,17 +331,17 @@
     )
 
 
-def split_kernel(_, mine_ref, came_ref, query_ref, out_ref):
+def split_kernel(_, mine_ref, came_ref, query_ref, key_ref, value_ref):
     total = mine_ref[...] + came_ref[...].astype(F32)
     share = total.shape[1] // 3
     query_ref[...] = normalize_heads(total[:, :share])
-    out_ref[:, :share] = normalize_heads(total[:, share : 2 * share])
-    out_ref[:, share:] = total[:, 2 * share :].astype(BF16)
+    key_ref[...] = normalize_heads(total[:, share : 2 * share])
+    value_ref[...] = total[:, 2 * share :].astype(BF16)
 
 
 def split_call(me, mine, came):
     rows, columns = mine.shape
-    shapes = ((rows, columns // 3), (rows, 2 * columns // 3))
+    shapes = ((rows, columns // 3),) * 3
     return call(
         split_kernel,
         me,
@@ -353,7 +353,8 @@
 
 
 def attend_kernel(_, query_ref, *refs):
-    pieces, out_ref = refs[:-1], refs[-1]
+    count = len(refs) // 2
+    keys, values, out_ref = refs[:count], refs[count:-1], refs[-1]
     queries = query_ref[...]
     rows, share = queries.shape
     head_of = lax.broadcasted_iota(jnp.int32, (rows, share), 1) // HEAD_DIM
@@ -362,13 +363,13 @@
         query = jnp.where(head_of == head, queries.astype(F32) * HEAD_DIM**-0.5, 0.0).astype(BF16)
         numer = jnp.zeros((rows, share), F32)
         denom = jnp.zeros((rows, 1), F32)
-        for piece in pieces:
+        for key, value in zip(keys, values):
             scores = lax.dot_general(
-                query, piece[:, :share], (((1,), (1,)), ((), ())), preferred_element_type=F32
+                query, key[...], (((1,), (1,)), ((), ())), preferred_element_type=F32
             )
             expw = jnp.exp(scores).astype(BF16)
             denom += jnp.sum(expw.astype(F32), axis=1, keepdims=True)
-            numer += jnp.dot(expw, piece[:, share:], preferred_element_type=F32)
+            numer += jnp.dot(expw, value[...], preferred_element_type=F32)
         out = jnp.where(head_of == head, numer / denom, out)
     out_ref[...] = out.astype(BF16)
 
@@ -577,7 +578,7 @@
     blocks, size, _ = w_first.shape
     deep = size // 4
     counts = [blocks // 4, blocks // 2, blocks // 4]
-    chunks = [(deep // 2, True), (3 * deep // 8, True), (deep // 8, True)]
+    chunks = [(3 * deep // 4, True), (deep // 4, True)]
     matrix = grid_turn()
     sends, back = [None] * 3, [[None] * 4 for _ in range(3)]
 
@@ -603,17 +604,18 @@
     w_first_t = jnp.swapaxes(after(w_first, send), 1, 2)
     mine, other = add_call(me, keep, after(came, sends[2][0], w_first_t))
     last = flip(other, "gene", 2)
-    queries, key_value = split_call(me, mine, after(last, beside_sum))
-    across = flip(key_value, "cell", 2)
-    beside = flip(key_value, "cell", 1)
-    corner = flip(across, "cell", 1)
-    beside_keys = [begin(1, 2, last), begin(1, 1, last)]
-    attended = attend_call(me, queries, (key_value, beside, across, corner))
+    queries, *own = split_call(me, mine, after(last, beside_sum))
+    across = [flip(piece, "cell", 2) for piece in own]
+    beside = [flip(piece, "cell", 1) for piece in own]
+    corner = [flip(piece, "cell", 1) for piece in across]
+    beside_keys = [begin(1, bits, last, beside_sum) for bits in (2, 1)]
+    gathered = [piece for kind in zip(own, beside, across, corner) for piece in kind]
+    attended = attend_call(me, queries, gathered)
     attended = after(attended, *beside_keys)
     near = flip(attended, "gene", 1)
     far = flip(attended, "gene", 2)
     rest = flip(after(far, near), "gene", 1)
-    rest = after(rest, begin(2, 2, attended))
+    begin(2, 2, attended)
     hidden, first = first_call(
         me, matrix, (attended, near, far, rest), w_out, masked, w_first_t, chunks
     )
@@ -629,7 +631,7 @@
         else:
             got.append([pieces[0]] + [flip(pieces[bits], "gene", bits) for bits in (1, 2, 3)])
 
-    launch(0, back[2][3], back[2][1])
+    launch(0, *back[2][1:])
     denoised, shares = None, [None, None]
     back = sum(back, [])
 

time: 484 us -> 477 us (0.986)
  waiting for transfers between devices: 278 us -> 271 us
    ppermute x32, waiting for transfers between devices: 180 us -> 153 us  [flip(): return lax.ppermute(value, axis, pairs)]
    all_to_all x3 -> x2, waiting for transfers between devices: 98.1 us -> 118 us  [launch(): lax.all_to_all(pieces[0], 'gene', split_axis=0, concat_axis=0, tiled=True)]
    pallas_call x23 -> x20, Pallas kernels: 151 us -> 147 us  [call(): pl.pallas_call(body, out_shape=outs, grid_spec=pltpu.PrefetchScalarGridSp...]
    all_to_all x3 -> x2, starting transfers between devices: 13 us -> 11 us  [launch(): lax.all_to_all(pieces[0], 'gene', split_axis=0, concat_axis=0, tiled=True)]
  transfers between devices with their start and end apart: 35 -> 34, of which waited for: 22 -> 21; matrix products, arithmetic and copies ran while one was open for 1% -> 1% of each run, Pallas kernels for 29% -> 30%
where the time goes in v8:
time: 477 us; the launch traced here: 476 us
  waiting for transfers between devices  271 us (57%)
  Pallas kernels  147 us (31%)
  starting transfers between devices  43.7 us (9%)
  local copies, waits for them, and re-layouts  13.2 us (3%)
    ppermute x32, waiting for transfers between devices, flip(): return lax.ppermute(value, axis, pairs)  153 us
    pallas_call x20, Pallas kernels, call(): pl.pallas_call(body, out_shape=outs, grid_spec=pltpu.PrefetchScalarGridSp...  147 us
    all_to_all x2, waiting for transfers between devices, launch(): lax.all_to_all(pieces[0], 'gene', split_axis=0, concat_axis=0, tiled=True)  118 us
    ppermute x32, starting transfers between devices, flip(): return lax.ppermute(value, axis, pairs)  32.6 us
    all_to_all x2, starting transfers between devices, launch(): lax.all_to_all(pieces[0], 'gene', split_axis=0, concat_axis=0, tiled=True)  11 us
  transfers between devices with their start and end apart: 34, of which 21 were waited for; matrix products, arithmetic and copies ran while one was open for 1% of the time, Pallas kernels for 30%

profile of v8, /device:TPU:0, one launch (start us, length us, event | category | flops | bytes accessed | tf_op | source)
XLA Modules:
  0.0 476.3 jit_solution(11094518953686606197)
XLA Ops:
  1.0 4.4 shard_map.103
  5.5 4.0 collective-permute-start.1
  11.1 8.1 %shard_map.104 = (bf16[32,32,512]{2,1,0:T(8,128)(2,1)S(1)}, bf16[32,32,512]{2,1,0:T(8,128)(2,1)}, bf16[32,32,512]{2,1,0:T(8,128)(2,1)}, bf16[32,32,512]{2,1,0:T(8,128)(2,1)}) custom-call(s32[2]{0:T(128)S(1)} %pad_add_fusion.me_ref._, bf16[256,256]{1,0:T(8,128)(2,1)S(1)} %fusion.turn_ref, bf16[32,256,256]{2,1,0:T(8,128)(2,1)} %refs_1_.3, ...), custom_call_target="tpu_custom_call" | custom-call | flops 1 | bytes 1 | tf_op jit(solution)/shard_map/pallas_call | solution.py:100
  20.2 37.8 %shard_map.105 = (bf16[512,8192]{1,0:T(8,128)(2,1)}, bf16[2,512,768]{2,1,0:T(8,128)(2,1)S(1)}, f32[2,512,768]{2,1,0:T(8,128)}) custom-call(s32[2]{0:T(128)S(1)} %pad_add_fusion.me_ref._, bf16[512,8192]{1,0:T(8,128)(2,1)} %value_ref, s32[512,8192]{1,0:T(8,128)} %mask_ref.1, bf16[1,8192]{1,0:T(2,128)(2,1)S(1)} %reshape.9.fill_ref, bf16[8192,3072]{1,0:T(8,128)(2,1)} %weight_ref.1), custom_call_target="tpu_custom_call" | custom-call | flops 1 | bytes 1 | tf_op jit(solution)/shard_map/pallas_call | solution.py:100
  58.0 1.9 collective-permute-start.3
  59.9 2.5 collective-permute-start.5
  62.4 4.5 shard_map.106
  67.6 6.5 %copy.14 = bf16[32,256,256]{1,2,0:T(8,128)(2,1)} copy(bf16[32,256,256]{2,1,0:T(8,128)(2,1)} %param.13) | data formatting | bytes 8388608 | tf_op jit(solution)/shard_map/optimization_barrier | solution.py:91
  74.2 20.6 %collective-permute-done.3.came_ref = bf16[2,512,768]{2,1,0:T(8,128)(2,1)} collective-permute-done((bf16[2,512,768]{2,1,0:T(8,128)(2,1)S(1)}, bf16[2,512,768]{2,1,0:T(8,128)(2,1)}, u32[]{:S(2)}, u32[]{:S(2)}) %collective-permute-start.3) | collective-permute-done | bytes 1572896 | tf_op jit(solution)/shard_map/ppermute | solution.py:96
  94.8 4.2 shard_map.107
  98.9 3.6 collective-permute-start.4
  102.5 17.8 %collective-permute-done.5.refs_7_ = bf16[32,32,512]{2,1,0:T(8,128)(2,1)} collective-permute-done((bf16[32,32,512]{2,1,0:T(8,128)(2,1)}, bf16[32,32,512]{2,1,0:T(8,128)(2,1)}, u32[]{:S(2)}, u32[]{:S(2)}) %collective-permute-start.5) | collective-permute-done | bytes 1048608 | tf_op jit(solution)/shard_map/ppermute | solution.py:96
  120.4 31.5 %collective-permute-done.4.came_ref = bf16[512,768]{1,0:T(8,128)(2,1)S(1)} collective-permute-done((bf16[512,768]{1,0:T(8,128)(2,1)S(1)}, bf16[512,768]{1,0:T(8,128)(2,1)S(1)}, u32[]{:S(2)}, u32[]{:S(2)}) %collective-permute-start.4) | collective-permute-done | bytes 786464 | tf_op jit(solution)/shard_map/ppermute | solution.py:96
  151.8 1.9 collective-permute-start.13
  153.7 3.2 shard_map.108
  156.9 1.6 collective-permute-start.7
  159.0 7.2 %collective-permute-done.7.refs_2_ = bf16[512,256]{1,0:T(8,128)(2,1)S(1)} collective-permute-done((bf16[512,256]{1,0:T(8,128)(2,1)S(1)}, bf16[512,256]{1,0:T(8,128)(2,1)S(1)}, u32[]{:S(2)}, u32[]{:S(2)}) %collective-permute-start.7) | collective-permute-done | bytes 262176 | tf_op jit(solution)/shard_map/ppermute | solution.py:96
  166.8 3.5 collective-permute-done.10.refs_6_
  170.3 1.5 collective-permute-done.11.refs_7_
  172.5 7.2 %shard_map.109.own = bf16[512,256]{1,0:T(8,128)(2,1)S(1)} custom-call(s32[2]{0:T(128)S(1)} %pad_add_fusion.me_ref._, bf16[512,256]{1,0:T(8,128)(2,1)S(1)} %get-tuple-element.84.query_ref, bf16[512,256]{1,0:T(8,128)(2,1)S(1)} %get-tuple-element.85.refs_0_, bf16[512,256]{1,0:T(8,128)(2,1)S(1)} %collective-permute-done.6.refs_1_, ...), custom_call_target="tpu_custom_call" | custom-call | flops 1 | bytes 1 | tf_op jit(solution)/shard_map/pallas_call | solution.py:100
  179.8 19.3 %collective-permute-done.12.refs_6_ = bf16[32,32,512]{2,1,0:T(8,128)(2,1)S(1)} collective-permute-done((bf16[32,32,512]{2,1,0:T(8,128)(2,1)S(1)}, bf16[32,32,512]{2,1,0:T(8,128)(2,1)S(1)}, u32[]{:S(2)}, u32[]{:S(2)}) %collective-permute-start.12) | collective-permute-done | bytes 1048608 | tf_op jit(solution)/shard_map/ppermute | solution.py:96
  199.6 2.7 collective-permute-start.14
  202.3 11.5 %collective-permute-done.15.far = bf16[512,256]{1,0:T(8,128)(2,1)S(1)} collective-permute-done((bf16[512,256]{1,0:T(8,128)(2,1)S(1)}, bf16[512,256]{1,0:T(8,128)(2,1)S(1)}, u32[]{:S(2)}, u32[]{:S(2)}) %collective-permute-start.15) | collective-permute-done | bytes 262176 | tf_op jit(solution)/shard_map/ppermute | solution.py:96
  214.0 2.1 collective-permute-start.18
  216.1 10.3 %collective-permute-done.16.rest = bf16[512,256]{1,0:T(8,128)(2,1)S(1)} collective-permute-done((bf16[512,256]{1,0:T(8,128)(2,1)S(1)}, bf16[512,256]{1,0:T(8,128)(2,1)S(1)}, u32[]{:S(2)}, u32[]{:S(2)}) %collective-permute-start.16) | collective-permute-done | bytes 262176 | tf_op jit(solution)/shard_map/ppermute | solution.py:96
  226.3 2.4 collective-permute-start.19
  228.7 24.5 %shard_map.110 = (bf16[512,8192]{1,0:T(8,128)(2,1)}, bf16[4,48,32,512]{3,2,1,0:T(8,128)(2,1)}, bf16[4,16,32,512]{3,2,1,0:T(8,128)(2,1)}) custom-call(s32[2]{0:T(128)S(1)} %pad_add_fusion.me_ref._, bf16[256,256]{1,0:T(8,128)(2,1)S(1)} %fusion.turn_ref, bf16[512,256]{1,0:T(8,128)(2,1)S(1)} %shard_map.109.own, ...), custom_call_target="tpu_custom_call" | custom-call | flops 1 | bytes 1 | tf_op jit(solution)/shard_map/pallas_call | solution.py:100
  253.2 4.1 collective-permute-done.17.refs_9_
  258.4 6.6 %all-to-all-start = ((bf16[4,48,32,512]{3,2,1,0:T(8,128)(2,1)}), bf16[4,48,32,512]{3,2,1,0:T(8,128)(2,1)}, u32[]{:S(2)}, u32[]{:S(2)}) async-start(bf16[4,48,32,512]{3,2,1,0:T(8,128)(2,1)} %get-tuple-element.102), calls=%async_computation | async-start | bytes 12582912 | tf_op jit(solution)/shard_map/all_to_all | solution.py:630
  264.9 7.0 %shard_map.113 = (bf16[16,64,256]{2,1,0:T(8,128)(2,1)S(1)}, bf16[16,64,256]{2,1,0:T(8,128)(2,1)S(1)}, f32[2,16,64,256]{3,2,1,0:T(8,128)}) custom-call(s32[2]{0:T(128)S(1)} %pad_add_fusion.me_ref._, bf16[32,16,512]{2,1,0:T(8,128)(2,1)S(1)} %get-tuple-element.65.refs_0_, bf16[32,16,512]{2,1,0:T(8,128)(2,1)} %copy-done.9, bf16[32,16,512]{2,1,0:T(8,128)(2,1)} %copy-done.7, ...), custom_call_target="tpu_custom_call" | custom-call | flops 1 | bytes 1 | tf_op jit(solution)/shard_map/pallas_call | solution.py:100
  272.5 7.0 %shard_map.111 = (bf16[16,64,256]{2,1,0:T(8,128)(2,1)S(1)}, bf16[16,64,256]{2,1,0:T(8,128)(2,1)S(1)}, f32[2,16,64,256]{3,2,1,0:T(8,128)}) custom-call(s32[2]{0:T(128)S(1)} %pad_add_fusion.me_ref._, bf16[32,16,512]{2,1,0:T(8,128)(2,1)S(1)} %get-tuple-element.65.refs_0_, bf16[32,16,512]{2,1,0:T(8,128)(2,1)} %copy-done.9, bf16[32,16,512]{2,1,0:T(8,128)(2,1)} %copy-done.7, ...), custom_call_target="tpu_custom_call" | custom-call | flops 1 | bytes 1 | tf_op jit(solution)/shard_map/pallas_call | solution.py:100
  280.1 3.2 shard_map.114
  284.8 3.2 shard_map.112
  288.6 9.5 %collective-permute-done.25.came_ref = bf16[16,64,256]{2,1,0:T(8,128)(2,1)S(1)} collective-permute-done((bf16[16,64,256]{2,1,0:T(8,128)(2,1)S(1)}, bf16[16,64,256]{2,1,0:T(8,128)(2,1)S(1)}, u32[]{:S(2)}, u32[]{:S(2)}) %collective-permute-start.25) | collective-permute-done | bytes 524320 | tf_op jit(solution)/shard_map/ppermute | solution.py:96
  299.3 1.6 shard_map.115.refs_0_
  300.9 7.5 %collective-permute-done.22.came_ref = bf16[16,64,256]{2,1,0:T(8,128)(2,1)S(1)} collective-permute-done((bf16[16,64,256]{2,1,0:T(8,128)(2,1)S(1)}, bf16[16,64,256]{2,1,0:T(8,128)(2,1)S(1)}, u32[]{:S(2)}, u32[]{:S(2)}) %collective-permute-start.22) | collective-permute-done | bytes 524320 | tf_op jit(solution)/shard_map/ppermute | solution.py:96
  308.5 1.6 shard_map.116
  310.1 93.1 %all-to-all-done.refs_0_ = bf16[4,48,32,512]{3,2,1,0:T(8,128)(2,1)} async-done(((bf16[4,48,32,512]{3,2,1,0:T(8,128)(2,1)}), bf16[4,48,32,512]{3,2,1,0:T(8,128)(2,1)}, u32[]{:S(2)}, u32[]{:S(2)}) %all-to-all-start) | async-done | bytes 6291488 | tf_op jit(solution)/shard_map/all_to_all | solution.py:630
  403.1 4.5 all-to-all-start.1
  407.6 13.6 %shard_map.117 = (bf16[512,8192]{1,0:T(8,128)(2,1)}, bf16[24,64,256]{2,1,0:T(8,128)(2,1)S(1)}, bf16[24,64,256]{2,1,0:T(8,128)(2,1)S(1)}, f32[2,24,64,256]{3,2,1,0:T(8,128)}) custom-call(s32[2]{0:T(128)S(1)} %pad_add_fusion.me_ref._, bf16[4,48,32,512]{3,2,1,0:T(8,128)(2,1)} %all-to-all-done.refs_0_, bf16[32,256,256]{2,1,0:T(8,128)(2,1)} %refs_1_.3, ...), custom_call_target="tpu_custom_call" | custom-call | flops 1 | bytes 1 | tf_op jit(solution)/shard_map/pallas_call | solution.py:100
  421.7 1.8 collective-permute-done.29.came_ref
  425.5 3.9 shard_map.120
  430.9 25.4 %all-to-all-done.1.refs_0_ = bf16[4,16,32,512]{3,2,1,0:T(8,128)(2,1)} async-done(((bf16[4,16,32,512]{3,2,1,0:T(8,128)(2,1)}), bf16[4,16,32,512]{3,2,1,0:T(8,128)(2,1)}, u32[]{:S(2)}, u32[]{:S(2)}) %all-to-all-start.1) | async-done | bytes 2097184 | tf_op jit(solution)/shard_map/all_to_all | solution.py:630
  456.3 5.4 %shard_map.118 = (bf16[512,8192]{1,0:T(8,128)(2,1)}, bf16[8,64,256]{2,1,0:T(8,128)(2,1)S(1)}, bf16[8,64,256]{2,1,0:T(8,128)(2,1)S(1)}, f32[2,8,64,256]{3,2,1,0:T(8,128)S(1)}) custom-call(s32[2]{0:T(128)S(1)} %pad_add_fusion.me_ref._, bf16[4,16,32,512]{3,2,1,0:T(8,128)(2,1)} %all-to-all-done.1.refs_0_, ...), custom_call_target="tpu_custom_call", output_to_operand_aliasing={{0}: (5, {})} | custom-call | flops 1 | bytes 1 | tf_op jit(solution)/shard_map/pallas_call | solution.py:100
  464.6 1.9 shard_map.119
  466.5 1.6 collective-permute-start.28
  468.1 3.2 shard_map.121.refs_0_
  471.3 3.6 collective-permute-done.28.came_ref
  (89 shorter events, 19.9 us)
Async XLA Ops:
  5.5 52.5 %collective-permute-start.1 = (bf16[32,16,512]{2,1,0:T(8,128)(2,1)S(1)}, bf16[32,16,512]{2,1,0:T(8,128)(2,1)S(1)}, u32[]{:S(2)}, u32[]{:S(2)}) collective-permute-start(bf16[32,16,512]{2,1,0:T(8,128)(2,1)S(1)} %get-tuple-element.72), channel_id=1, source_target_pairs={{0,8},{4,12},{8,0},{12,4},{1,9},{5,13},{9,1},{13,5},{2,10},{6,14},... | collective-permute-start | bytes 1572872 | tf_op jit(solution)/shard_map/ppermute | solution.py:96
  9.5 48.5 %collective-permute-start = (bf16[32,16,512]{2,1,0:T(8,128)(2,1)}, bf16[32,16,512]{2,1,0:T(8,128)(2,1)S(1)}, u32[]{:S(2)}, u32[]{:S(2)}) collective-permute-start(bf16[32,16,512]{2,1,0:T(8,128)(2,1)} %get-tuple-element.71), channel_id=1, source_target_pairs={{0,12},{4,8},{8,4},{12,0},{1,13},{5,9},{9,5},{13,1},{2,14},{6,10},... | collective-permute-start | bytes 1572872 | tf_op jit(solution)/shard_map/ppermute | solution.py:96
  10.9 47.2 %collective-permute-start.2 = (bf16[32,16,512]{2,1,0:T(8,128)(2,1)S(1)}, bf16[32,16,512]{2,1,0:T(8,128)(2,1)S(1)}, u32[]{:S(2)}, u32[]{:S(2)}) collective-permute-start(bf16[32,16,512]{2,1,0:T(8,128)(2,1)S(1)} %get-tuple-element.73), channel_id=1, source_target_pairs={{0,4},{4,0},{8,12},{12,8},{1,5},{5,1},{9,13},{13,9},{2,6},{6,2},{1... | collective-permute-start | bytes 1572872 | tf_op jit(solution)/shard_map/ppermute | solution.py:96
  11.1 9.1 %copy-start.17 = (bf16[8192]{0:T(1024)(128)(2,1)S(1)}, bf16[8192]{0:T(1024)(128)(2,1)}, u32[]{:S(2)}) copy-start(bf16[8192]{0:T(1024)(128)(2,1)} %param.10) | copy-start | bytes 49156
  58.0 1.9 copy-start.7
  58.0 4.4 copy-start.8
  58.0 4.4 copy-start.9
  58.0 36.7 %collective-permute-start.3 = (bf16[2,512,768]{2,1,0:T(8,128)(2,1)S(1)}, bf16[2,512,768]{2,1,0:T(8,128)(2,1)}, u32[]{:S(2)}, u32[]{:S(2)}) collective-permute-start(bf16[2,512,768]{2,1,0:T(8,128)(2,1)S(1)} %get-tuple-element.74), channel_id=1, source_target_pairs={{0,4},{4,0},{8,12},{12,8},{1,5},{5,1},{9,13},{13,9},{2,6},{6,2},{1... | collective-permute-start | bytes 4718600 | tf_op jit(solution)/shard_map/ppermute | solution.py:96
  59.9 60.4 %collective-permute-start.5 = (bf16[32,32,512]{2,1,0:T(8,128)(2,1)}, bf16[32,32,512]{2,1,0:T(8,128)(2,1)}, u32[]{:S(2)}, u32[]{:S(2)}) collective-permute-start(bf16[32,32,512]{2,1,0:T(8,128)(2,1)} %get-tuple-element.82), channel_id=1, source_target_pairs={{0,12},{4,8},{8,4},{12,0},{1,13},{5,9},{9,5},{13,1},{2,14},{6,10},... | collective-permute-start | bytes 3145736 | tf_op jit(solution)/shard_map/ppermute | solution.py:96
  74.2 77.7 %copy-start.19 = (bf16[32,32,512]{2,1,0:T(8,128)(2,1)S(1)}, bf16[32,32,512]{2,1,0:T(8,128)(2,1)}, u32[]{:S(2)}) copy-start(bf16[32,32,512]{2,1,0:T(8,128)(2,1)} %get-tuple-element.88) | copy-start | bytes 3145732
  74.2 77.7 %copy-start.18 = (bf16[32,32,512]{2,1,0:T(8,128)(2,1)S(1)}, bf16[32,32,512]{2,1,0:T(8,128)(2,1)}, u32[]{:S(2)}) copy-start(bf16[32,32,512]{2,1,0:T(8,128)(2,1)} %get-tuple-element.90) | copy-start | bytes 3145732
  94.8 131.6 %copy-start.20 = (bf16[32,16,512]{2,1,0:T(8,128)(2,1)S(1)}, bf16[32,16,512]{2,1,0:T(8,128)(2,1)}, u32[]{:S(2)}) copy-start(bf16[32,16,512]{2,1,0:T(8,128)(2,1)} %get-tuple-element.101) | copy-start | bytes 1572868
  98.9 52.9 %collective-permute-start.4 = (bf16[512,768]{1,0:T(8,128)(2,1)S(1)}, bf16[512,768]{1,0:T(8,128)(2,1)S(1)}, u32[]{:S(2)}, u32[]{:S(2)}) collective-permute-start(bf16[512,768]{1,0:T(8,128)(2,1)S(1)} %get-tuple-element.80), channel_id=1, source_target_pairs={{0,8},{4,12},{8,0},{12,4},{1,9},{5,13},{9,1},{13,5},{2,10},{6,14},... | collective-permute-start | bytes 2359304 | tf_op jit(solution)/shard_map/ppermute | solution.py:96
  151.8 47.3 %collective-permute-start.12 = (bf16[32,32,512]{2,1,0:T(8,128)(2,1)S(1)}, bf16[32,32,512]{2,1,0:T(8,128)(2,1)S(1)}, u32[]{:S(2)}, u32[]{:S(2)}) collective-permute-start(bf16[32,32,512]{2,1,0:T(8,128)(2,1)S(1)} %copy-done.19), channel_id=1, source_target_pairs={{0,8},{4,12},{8,0},{12,4},{1,9},{5,13},{9,1},{13,5},{2,10},{6,14},... | collective-permute-start | bytes 3145736 | tf_op jit(solution)/shard_map/ppermute | solution.py:96
  151.8 47.6 %collective-permute-start.13 = (bf16[32,32,512]{2,1,0:T(8,128)(2,1)S(1)}, bf16[32,32,512]{2,1,0:T(8,128)(2,1)S(1)}, u32[]{:S(2)}, u32[]{:S(2)}) collective-permute-start(bf16[32,32,512]{2,1,0:T(8,128)(2,1)S(1)} %copy-done.18), channel_id=1, source_target_pairs={{0,4},{4,0},{8,12},{12,8},{1,5},{5,1},{9,13},{13,9},{2,6},{6,2},{1... | collective-permute-start | bytes 3145736 | tf_op jit(solution)/shard_map/ppermute | solution.py:96
  156.9 9.3 %collective-permute-start.7 = (bf16[512,256]{1,0:T(8,128)(2,1)S(1)}, bf16[512,256]{1,0:T(8,128)(2,1)S(1)}, u32[]{:S(2)}, u32[]{:S(2)}) collective-permute-start(bf16[512,256]{1,0:T(8,128)(2,1)S(1)} %get-tuple-element.85.refs_0_), channel_id=1, source_target_pairs={{0,2},{1,3},{2,0},{3,1},{4,6},{5,7},{6,4},{7,5},{8,10},{9,11},{10,... | collective-permute-start | bytes 786440 | tf_op jit(solution)/shard_map/ppermute | solution.py:96
  158.5 7.8 %collective-permute-start.6 = (bf16[512,256]{1,0:T(8,128)(2,1)S(1)}, bf16[512,256]{1,0:T(8,128)(2,1)S(1)}, u32[]{:S(2)}, u32[]{:S(2)}) collective-permute-start(bf16[512,256]{1,0:T(8,128)(2,1)S(1)} %get-tuple-element.85.refs_0_), channel_id=1, source_target_pairs={{0,1},{1,0},{2,3},{3,2},{4,5},{5,4},{6,7},{7,6},{8,9},{9,8},{10,11... | collective-permute-start | bytes 786440 | tf_op jit(solution)/shard_map/ppermute | solution.py:96
  158.5 11.8 %collective-permute-start.10 = (bf16[512,256]{1,0:T(8,128)(2,1)S(1)}, bf16[512,256]{1,0:T(8,128)(2,1)S(1)}, u32[]{:S(2)}, u32[]{:S(2)}) collective-permute-start(bf16[512,256]{1,0:T(8,128)(2,1)S(1)} %get-tuple-element.86.refs_4_), channel_id=1, source_target_pairs={{0,2},{1,3},{2,0},{3,1},{4,6},{5,7},{6,4},{7,5},{8,10},{9,11},{10,... | collective-permute-start | bytes 786440 | tf_op jit(solution)/shard_map/ppermute | solution.py:96
  166.2 4.1 collective-permute-start.9
  166.2 4.1 collective-permute-start.8
  170.3 1.5 copy-start.14
  170.3 1.5 collective-permute-start.11
  170.3 1.5 copy-start.15
  199.1 54.1 %copy-start.5 = (bf16[32,32,512]{2,1,0:T(8,128)(2,1)}, bf16[32,32,512]{2,1,0:T(8,128)(2,1)S(1)}, u32[]{:S(2)}) copy-start(bf16[32,32,512]{2,1,0:T(8,128)(2,1)S(1)} %collective-permute-done.12.refs_6_) | copy-start | bytes 3145732
  199.5 53.8 %copy-start.6 = (bf16[32,32,512]{2,1,0:T(8,128)(2,1)}, bf16[32,32,512]{2,1,0:T(8,128)(2,1)S(1)}, u32[]{:S(2)}) copy-start(bf16[32,32,512]{2,1,0:T(8,128)(2,1)S(1)} %collective-permute-done.13.refs_5_) | copy-start | bytes 3145732
  199.5 14.3 %collective-permute-start.15 = (bf16[512,256]{1,0:T(8,128)(2,1)S(1)}, bf16[512,256]{1,0:T(8,128)(2,1)S(1)}, u32[]{:S(2)}, u32[]{:S(2)}) collective-permute-start(bf16[512,256]{1,0:T(8,128)(2,1)S(1)} %shard_map.109.own), channel_id=1, source_target_pairs={{0,8},{4,12},{8,0},{12,4},{1,9},{5,13},{9,1},{13,5},{2,10},{6,14},... | collective-permute-start | bytes 786440 | tf_op jit(solution)/shard_map/ppermute | solution.py:96
  199.6 14.4 %collective-permute-start.14 = (bf16[512,256]{1,0:T(8,128)(2,1)S(1)}, bf16[512,256]{1,0:T(8,128)(2,1)S(1)}, u32[]{:S(2)}, u32[]{:S(2)}) collective-permute-start(bf16[512,256]{1,0:T(8,128)(2,1)S(1)} %shard_map.109.own), channel_id=1, source_target_pairs={{0,4},{4,0},{8,12},{12,8},{1,5},{5,1},{9,13},{13,9},{2,6},{6,2},{1... | collective-permute-start | bytes 786440 | tf_op jit(solution)/shard_map/ppermute | solution.py:96
  214.0 12.4 %collective-permute-start.16 = (bf16[512,256]{1,0:T(8,128)(2,1)S(1)}, bf16[512,256]{1,0:T(8,128)(2,1)S(1)}, u32[]{:S(2)}, u32[]{:S(2)}) collective-permute-start(bf16[512,256]{1,0:T(8,128)(2,1)S(1)} %collective-permute-done.15.far), channel_id=1, source_target_pairs={{0,4},{4,0},{8,12},{12,8},{1,5},{5,1},{9,13},{13,9},{2,6},{6,2},{1... | collective-permute-start | bytes 786440 | tf_op jit(solution)/shard_map/ppermute | solution.py:96
  214.0 39.3 %collective-permute-start.18 = (bf16[32,16,512]{2,1,0:T(8,128)(2,1)S(1)}, bf16[32,16,512]{2,1,0:T(8,128)(2,1)S(1)}, u32[]{:S(2)}, u32[]{:S(2)}) collective-permute-start(bf16[32,16,512]{2,1,0:T(8,128)(2,1)S(1)} %get-tuple-element.99), channel_id=1, source_target_pairs={{0,8},{4,12},{8,0},{12,4},{1,9},{5,13},{9,1},{13,5},{2,10},{6,14},... | collective-permute-start | bytes 1572872 | tf_op jit(solution)/shard_map/ppermute | solution.py:96
  226.3 31.0 %collective-permute-start.17 = (bf16[32,16,512]{2,1,0:T(8,128)(2,1)S(1)}, bf16[32,16,512]{2,1,0:T(8,128)(2,1)S(1)}, u32[]{:S(2)}, u32[]{:S(2)}) collective-permute-start(bf16[32,16,512]{2,1,0:T(8,128)(2,1)S(1)} %get-tuple-element.97), channel_id=1, source_target_pairs={{0,4},{4,0},{8,12},{12,8},{1,5},{5,1},{9,13},{13,9},{2,6},{6,2},{1... | collective-permute-start | bytes 1572872 | tf_op jit(solution)/shard_map/ppermute | solution.py:96
  226.3 31.0 %collective-permute-start.19 = (bf16[32,16,512]{2,1,0:T(8,128)(2,1)S(1)}, bf16[32,16,512]{2,1,0:T(8,128)(2,1)S(1)}, u32[]{:S(2)}, u32[]{:S(2)}) collective-permute-start(bf16[32,16,512]{2,1,0:T(8,128)(2,1)S(1)} %copy-done.20), channel_id=1, source_target_pairs={{0,12},{4,8},{8,4},{12,0},{1,13},{5,9},{9,5},{13,1},{2,14},{6,10},... | collective-permute-start | bytes 1572872 | tf_op jit(solution)/shard_map/ppermute | solution.py:96
  253.2 4.1 copy-start.10
  258.4 144.8 %all-to-all-start = ((bf16[4,48,32,512]{3,2,1,0:T(8,128)(2,1)}), bf16[4,48,32,512]{3,2,1,0:T(8,128)(2,1)}, u32[]{:S(2)}, u32[]{:S(2)}) async-start(bf16[4,48,32,512]{3,2,1,0:T(8,128)(2,1)} %get-tuple-element.102), calls=%async_computation | async-start | bytes 12582912 | tf_op jit(solution)/shard_map/all_to_all | solution.py:630
  271.9 8.1 %collective-permute-start.23 = (bf16[16,64,256]{2,1,0:T(8,128)(2,1)S(1)}, bf16[16,64,256]{2,1,0:T(8,128)(2,1)S(1)}, u32[]{:S(2)}, u32[]{:S(2)}) collective-permute-start(bf16[16,64,256]{2,1,0:T(8,128)(2,1)S(1)} %get-tuple-element.110), channel_id=1, source_target_pairs={{0,1},{1,0},{2,3},{3,2},{4,5},{5,4},{6,7},{7,6},{8,9},{9,8},{10,11... | collective-permute-start | bytes 1572872 | tf_op jit(solution)/shard_map/ppermute | solution.py:96
  272.0 8.1 %collective-permute-start.24 = (bf16[16,64,256]{2,1,0:T(8,128)(2,1)S(1)}, bf16[16,64,256]{2,1,0:T(8,128)(2,1)S(1)}, u32[]{:S(2)}, u32[]{:S(2)}) collective-permute-start(bf16[16,64,256]{2,1,0:T(8,128)(2,1)S(1)} %get-tuple-element.111), channel_id=1, source_target_pairs={{0,1},{1,0},{2,3},{3,2},{4,5},{5,4},{6,7},{7,6},{8,9},{9,8},{10,11... | collective-permute-start | bytes 1572872 | tf_op jit(solution)/shard_map/ppermute | solution.py:96
  279.5 5.3 %collective-permute-start.20 = (bf16[16,64,256]{2,1,0:T(8,128)(2,1)S(1)}, bf16[16,64,256]{2,1,0:T(8,128)(2,1)S(1)}, u32[]{:S(2)}, u32[]{:S(2)}) collective-permute-start(bf16[16,64,256]{2,1,0:T(8,128)(2,1)S(1)} %get-tuple-element.105), channel_id=1, source_target_pairs={{0,1},{1,0},{2,3},{3,2},{4,5},{5,4},{6,7},{7,6},{8,9},{9,8},{10,11... | collective-permute-start | bytes 1572872 | tf_op jit(solution)/shard_map/ppermute | solution.py:96
  279.6 5.2 %collective-permute-start.21 = (bf16[16,64,256]{2,1,0:T(8,128)(2,1)S(1)}, bf16[16,64,256]{2,1,0:T(8,128)(2,1)S(1)}, u32[]{:S(2)}, u32[]{:S(2)}) collective-permute-start(bf16[16,64,256]{2,1,0:T(8,128)(2,1)S(1)} %get-tuple-element.106), channel_id=1, source_target_pairs={{0,1},{1,0},{2,3},{3,2},{4,5},{5,4},{6,7},{7,6},{8,9},{9,8},{10,11... | collective-permute-start | bytes 1572872 | tf_op jit(solution)/shard_map/ppermute | solution.py:96
  283.3 14.8 %collective-permute-start.25 = (bf16[16,64,256]{2,1,0:T(8,128)(2,1)S(1)}, bf16[16,64,256]{2,1,0:T(8,128)(2,1)S(1)}, u32[]{:S(2)}, u32[]{:S(2)}) collective-permute-start(bf16[16,64,256]{2,1,0:T(8,128)(2,1)S(1)} %get-tuple-element.113), channel_id=1, source_target_pairs={{0,2},{1,3},{2,0},{3,1},{4,6},{5,7},{6,4},{7,5},{8,10},{9,11},{10,... | collective-permute-start | bytes 1572872 | tf_op jit(solution)/shard_map/ppermute | solution.py:96
  288.0 20.4 %collective-permute-start.22 = (bf16[16,64,256]{2,1,0:T(8,128)(2,1)S(1)}, bf16[16,64,256]{2,1,0:T(8,128)(2,1)S(1)}, u32[]{:S(2)}, u32[]{:S(2)}) collective-permute-start(bf16[16,64,256]{2,1,0:T(8,128)(2,1)S(1)} %get-tuple-element.108), channel_id=1, source_target_pairs={{0,2},{1,3},{2,0},{3,1},{4,6},{5,7},{6,4},{7,5},{8,10},{9,11},{10,... | collective-permute-start | bytes 1572872 | tf_op jit(solution)/shard_map/ppermute | solution.py:96
  298.1 1.2 copy-start.3
  299.3 9.1 %copy-start.4 = (f32[16,64,256]{2,1,0:T(8,128)S(1)}, f32[16,64,256]{2,1,0:T(8,128)}, u32[]{:S(2)}) copy-start(f32[16,64,256]{2,1,0:T(8,128)} %get-tuple-element.107.mine_ref) | copy-start | bytes 3145732
  403.1 53.2 %all-to-all-start.1 = ((bf16[4,16,32,512]{3,2,1,0:T(8,128)(2,1)}), bf16[4,16,32,512]{3,2,1,0:T(8,128)(2,1)}, u32[]{:S(2)}, u32[]{:S(2)}) async-start(bf16[4,16,32,512]{3,2,1,0:T(8,128)(2,1)} %get-tuple-element.114), calls=%async_computation.1 | async-start | bytes 4194304 | tf_op jit(solution)/shard_map/all_to_all | solution.py:630
  421.2 2.3 collective-permute-start.29
  421.2 3.4 collective-permute-start.30
  429.4 38.6 %collective-permute-start.31 = (bf16[24,64,256]{2,1,0:T(8,128)(2,1)S(1)}, bf16[24,64,256]{2,1,0:T(8,128)(2,1)S(1)}, u32[]{:S(2)}, u32[]{:S(2)}) collective-permute-start(bf16[24,64,256]{2,1,0:T(8,128)(2,1)S(1)} %get-tuple-element.126), channel_id=1, source_target_pairs={{0,2},{1,3},{2,0},{3,1},{4,6},{5,7},{6,4},{7,5},{8,10},{9,11},{10,... | collective-permute-start | bytes 2359304 | tf_op jit(solution)/shard_map/ppermute | solution.py:96
  462.7 1.5 collective-permute-start.26
  462.7 1.9 collective-permute-start.27
  466.5 8.4 %collective-permute-start.28 = (bf16[8,64,256]{2,1,0:T(8,128)(2,1)S(1)}, bf16[8,64,256]{2,1,0:T(8,128)(2,1)S(1)}, u32[]{:S(2)}, u32[]{:S(2)}) collective-permute-start(bf16[8,64,256]{2,1,0:T(8,128)(2,1)S(1)} %get-tuple-element.121), channel_id=1, source_target_pairs={{0,2},{1,3},{2,0},{3,1},{4,6},{5,7},{6,4},{7,5},{8,10},{9,11},{10,... | collective-permute-start | bytes 786440 | tf_op jit(solution)/shard_map/ppermute | solution.py:96
  (7 other events, 6.1 us)

commit v9 on v8

--- a/solution.py
+++ b/solution.py
@@ -608,13 +608,12 @@
     across = [flip(piece, "cell", 2) for piece in own]
     beside = [flip(piece, "cell", 1) for piece in own]
     corner = [flip(piece, "cell", 1) for piece in across]
-    beside_keys = [begin(1, bits, last, beside_sum) for bits in (2, 1)]
+    beside_keys = [begin(1, bits, other) for bits in (2, 1)]
     gathered = [piece for kind in zip(own, beside, across, corner) for piece in kind]
     attended = attend_call(me, queries, gathered)
-    attended = after(attended, *beside_keys)
     near = flip(attended, "gene", 1)
     far = flip(attended, "gene", 2)
-    rest = flip(after(far, near), "gene", 1)
+    rest = flip(after(far, near, *beside_keys), "gene", 1)
     begin(2, 2, attended)
     hidden, first = first_call(
         me, matrix, (attended, near, far, rest), w_out, masked, w_first_t, chunks

time: 477 us -> 479 us (level)
  transfers between devices with their start and end apart: 34 -> 34, of which waited for: 21 -> 19; matrix products, arithmetic and copies ran while one was open for 1% -> 1% of each run, Pallas kernels for 30% -> 29%
where the time goes in v9:
time: 479 us; the launch traced here: 478 us
  waiting for transfers between devices  273 us (57%)
  Pallas kernels  147 us (31%)
  starting transfers between devices  43.8 us (9%)
  local copies, waits for them, and re-layouts  13.2 us (3%)
    ppermute x32, waiting for transfers between devices, flip(): return lax.ppermute(value, axis, pairs)  155 us
    pallas_call x20, Pallas kernels, call(): pl.pallas_call(body, out_shape=outs, grid_spec=pltpu.PrefetchScalarGridSp...  147 us
    all_to_all x2, waiting for transfers between devices, launch(): lax.all_to_all(pieces[0], 'gene', split_axis=0, concat_axis=0, tiled=True)  118 us
    ppermute x32, starting transfers between devices, flip(): return lax.ppermute(value, axis, pairs)  31.6 us
    all_to_all x2, starting transfers between devices, launch(): lax.all_to_all(pieces[0], 'gene', split_axis=0, concat_axis=0, tiled=True)  12.2 us
  transfers between devices with their start and end apart: 34, of which 19 were waited for; matrix products, arithmetic and copies ran while one was open for 1% of the time, Pallas kernels for 29%

profile of v9, /device:TPU:0, one launch (start us, length us, event | category | flops | bytes accessed | tf_op | source)
XLA Modules:
  0.0 478.2 jit_solution(9162677888158019021)
XLA Ops:
  1.0 4.4 shard_map.103
  5.5 4.0 collective-permute-start.1
  11.1 8.1 %shard_map.104 = (bf16[32,32,512]{2,1,0:T(8,128)(2,1)S(1)}, bf16[32,32,512]{2,1,0:T(8,128)(2,1)}, bf16[32,32,512]{2,1,0:T(8,128)(2,1)}, bf16[32,32,512]{2,1,0:T(8,128)(2,1)}) custom-call(s32[2]{0:T(128)S(1)} %pad_add_fusion.me_ref._, bf16[256,256]{1,0:T(8,128)(2,1)S(1)} %fusion.turn_ref, bf16[32,256,256]{2,1,0:T(8,128)(2,1)} %refs_1_.3, ...), custom_call_target="tpu_custom_call" | custom-call | flops 1 | bytes 1 | tf_op jit(solution)/shard_map/pallas_call | solution.py:100
  20.2 37.8 %shard_map.105 = (bf16[512,8192]{1,0:T(8,128)(2,1)}, bf16[2,512,768]{2,1,0:T(8,128)(2,1)S(1)}, f32[2,512,768]{2,1,0:T(8,128)}) custom-call(s32[2]{0:T(128)S(1)} %pad_add_fusion.me_ref._, bf16[512,8192]{1,0:T(8,128)(2,1)} %value_ref, s32[512,8192]{1,0:T(8,128)} %mask_ref.1, bf16[1,8192]{1,0:T(2,128)(2,1)S(1)} %reshape.9.fill_ref, bf16[8192,3072]{1,0:T(8,128)(2,1)} %weight_ref.1), custom_call_target="tpu_custom_call" | custom-call | flops 1 | bytes 1 | tf_op jit(solution)/shard_map/pallas_call | solution.py:100
  58.0 1.9 collective-permute-start.3
  59.9 2.5 collective-permute-start.5
  62.4 4.5 shard_map.106
  67.6 6.5 %copy.14 = bf16[32,256,256]{1,2,0:T(8,128)(2,1)} copy(bf16[32,256,256]{2,1,0:T(8,128)(2,1)} %param.13) | data formatting | bytes 8388608 | tf_op jit(solution)/shard_map/optimization_barrier | solution.py:91
  74.2 20.6 %collective-permute-done.3.came_ref = bf16[2,512,768]{2,1,0:T(8,128)(2,1)} collective-permute-done((bf16[2,512,768]{2,1,0:T(8,128)(2,1)S(1)}, bf16[2,512,768]{2,1,0:T(8,128)(2,1)}, u32[]{:S(2)}, u32[]{:S(2)}) %collective-permute-start.3) | collective-permute-done | bytes 1572896 | tf_op jit(solution)/shard_map/ppermute | solution.py:96
  94.8 4.2 shard_map.107
  98.9 3.6 collective-permute-start.4
  102.6 1.9 collective-permute-start.15
  104.4 16.0 %collective-permute-done.5.refs_7_ = bf16[32,32,512]{2,1,0:T(8,128)(2,1)} collective-permute-done((bf16[32,32,512]{2,1,0:T(8,128)(2,1)}, bf16[32,32,512]{2,1,0:T(8,128)(2,1)}, u32[]{:S(2)}, u32[]{:S(2)}) %collective-permute-start.5) | collective-permute-done | bytes 1048608 | tf_op jit(solution)/shard_map/ppermute | solution.py:96
  120.4 54.0 %collective-permute-done.4.came_ref = bf16[512,768]{1,0:T(8,128)(2,1)S(1)} collective-permute-done((bf16[512,768]{1,0:T(8,128)(2,1)S(1)}, bf16[512,768]{1,0:T(8,128)(2,1)S(1)}, u32[]{:S(2)}, u32[]{:S(2)}) %collective-permute-start.4) | collective-permute-done | bytes 786464 | tf_op jit(solution)/shard_map/ppermute | solution.py:96
  174.4 3.2 shard_map.108
  177.6 1.6 collective-permute-start.7
  179.7 7.2 %collective-permute-done.7.refs_2_ = bf16[512,256]{1,0:T(8,128)(2,1)S(1)} collective-permute-done((bf16[512,256]{1,0:T(8,128)(2,1)S(1)}, bf16[512,256]{1,0:T(8,128)(2,1)S(1)}, u32[]{:S(2)}, u32[]{:S(2)}) %collective-permute-start.7) | collective-permute-done | bytes 262176 | tf_op jit(solution)/shard_map/ppermute | solution.py:96
  187.4 4.1 collective-permute-done.10.refs_6_
  191.5 1.5 collective-permute-done.11.refs_7_
  193.7 7.2 %shard_map.109.own = bf16[512,256]{1,0:T(8,128)(2,1)S(1)} custom-call(s32[2]{0:T(128)S(1)} %pad_add_fusion.me_ref._, bf16[512,256]{1,0:T(8,128)(2,1)S(1)} %get-tuple-element.83.query_ref, bf16[512,256]{1,0:T(8,128)(2,1)S(1)} %get-tuple-element.84.refs_0_, bf16[512,256]{1,0:T(8,128)(2,1)S(1)} %collective-permute-done.6.refs_1_, ...), custom_call_target="tpu_custom_call" | custom-call | flops 1 | bytes 1 | tf_op jit(solution)/shard_map/pallas_call | solution.py:100
  201.0 1.9 collective-permute-start.12
  202.9 11.7 %collective-permute-done.13.far = bf16[512,256]{1,0:T(8,128)(2,1)S(1)} collective-permute-done((bf16[512,256]{1,0:T(8,128)(2,1)S(1)}, bf16[512,256]{1,0:T(8,128)(2,1)S(1)}, u32[]{:S(2)}, u32[]{:S(2)}) %collective-permute-start.13) | collective-permute-done | bytes 262176 | tf_op jit(solution)/shard_map/ppermute | solution.py:96
  215.3 2.6 collective-permute-start.18
  217.9 10.4 %collective-permute-done.16.rest = bf16[512,256]{1,0:T(8,128)(2,1)S(1)} collective-permute-done((bf16[512,256]{1,0:T(8,128)(2,1)S(1)}, bf16[512,256]{1,0:T(8,128)(2,1)S(1)}, u32[]{:S(2)}, u32[]{:S(2)}) %collective-permute-start.16) | collective-permute-done | bytes 262176 | tf_op jit(solution)/shard_map/ppermute | solution.py:96
  229.7 24.5 %shard_map.110 = (bf16[512,8192]{1,0:T(8,128)(2,1)}, bf16[4,48,32,512]{3,2,1,0:T(8,128)(2,1)}, bf16[4,16,32,512]{3,2,1,0:T(8,128)(2,1)}) custom-call(s32[2]{0:T(128)S(1)} %pad_add_fusion.me_ref._, bf16[256,256]{1,0:T(8,128)(2,1)S(1)} %fusion.turn_ref, bf16[512,256]{1,0:T(8,128)(2,1)S(1)} %shard_map.109.own, ...), custom_call_target="tpu_custom_call" | custom-call | flops 1 | bytes 1 | tf_op jit(solution)/shard_map/pallas_call | solution.py:100
  254.2 3.9 collective-permute-done.17.refs_9_
  259.1 7.7 %all-to-all-start = ((bf16[4,48,32,512]{3,2,1,0:T(8,128)(2,1)}), bf16[4,48,32,512]{3,2,1,0:T(8,128)(2,1)}, u32[]{:S(2)}, u32[]{:S(2)}) async-start(bf16[4,48,32,512]{3,2,1,0:T(8,128)(2,1)} %get-tuple-element.100), calls=%async_computation | async-start | bytes 12582912 | tf_op jit(solution)/shard_map/all_to_all | solution.py:629
  266.8 7.0 %shard_map.113 = (bf16[16,64,256]{2,1,0:T(8,128)(2,1)S(1)}, bf16[16,64,256]{2,1,0:T(8,128)(2,1)S(1)}, f32[2,16,64,256]{3,2,1,0:T(8,128)}) custom-call(s32[2]{0:T(128)S(1)} %pad_add_fusion.me_ref._, bf16[32,16,512]{2,1,0:T(8,128)(2,1)S(1)} %get-tuple-element.64.refs_0_, bf16[32,16,512]{2,1,0:T(8,128)(2,1)} %copy-done.9, bf16[32,16,512]{2,1,0:T(8,128)(2,1)} %copy-done.7, ...), custom_call_target="tpu_custom_call" | custom-call | flops 1 | bytes 1 | tf_op jit(solution)/shard_map/pallas_call | solution.py:100
  274.4 7.0 %shard_map.111 = (bf16[16,64,256]{2,1,0:T(8,128)(2,1)S(1)}, bf16[16,64,256]{2,1,0:T(8,128)(2,1)S(1)}, f32[2,16,64,256]{3,2,1,0:T(8,128)}) custom-call(s32[2]{0:T(128)S(1)} %pad_add_fusion.me_ref._, bf16[32,16,512]{2,1,0:T(8,128)(2,1)S(1)} %get-tuple-element.64.refs_0_, bf16[32,16,512]{2,1,0:T(8,128)(2,1)} %copy-done.9, bf16[32,16,512]{2,1,0:T(8,128)(2,1)} %copy-done.7, ...), custom_call_target="tpu_custom_call" | custom-call | flops 1 | bytes 1 | tf_op jit(solution)/shard_map/pallas_call | solution.py:100
  282.0 3.2 shard_map.114
  285.2 1.5 collective-permute-start.25
  286.7 3.2 shard_map.112
  290.4 9.5 %collective-permute-done.25.came_ref = bf16[16,64,256]{2,1,0:T(8,128)(2,1)S(1)} collective-permute-done((bf16[16,64,256]{2,1,0:T(8,128)(2,1)S(1)}, bf16[16,64,256]{2,1,0:T(8,128)(2,1)S(1)}, u32[]{:S(2)}, u32[]{:S(2)}) %collective-permute-start.25) | collective-permute-done | bytes 524320 | tf_op jit(solution)/shard_map/ppermute | solution.py:96
  301.2 1.6 shard_map.115.refs_0_
  302.8 7.5 %collective-permute-done.22.came_ref = bf16[16,64,256]{2,1,0:T(8,128)(2,1)S(1)} collective-permute-done((bf16[16,64,256]{2,1,0:T(8,128)(2,1)S(1)}, bf16[16,64,256]{2,1,0:T(8,128)(2,1)S(1)}, u32[]{:S(2)}, u32[]{:S(2)}) %collective-permute-start.22) | collective-permute-done | bytes 524320 | tf_op jit(solution)/shard_map/ppermute | solution.py:96
  310.3 1.6 shard_map.116
  311.9 93.1 %all-to-all-done.refs_0_ = bf16[4,48,32,512]{3,2,1,0:T(8,128)(2,1)} async-done(((bf16[4,48,32,512]{3,2,1,0:T(8,128)(2,1)}), bf16[4,48,32,512]{3,2,1,0:T(8,128)(2,1)}, u32[]{:S(2)}, u32[]{:S(2)}) %all-to-all-start) | async-done | bytes 6291488 | tf_op jit(solution)/shard_map/all_to_all | solution.py:629
  405.1 4.5 all-to-all-start.1
  409.5 13.6 %shard_map.117 = (bf16[512,8192]{1,0:T(8,128)(2,1)}, bf16[24,64,256]{2,1,0:T(8,128)(2,1)S(1)}, bf16[24,64,256]{2,1,0:T(8,128)(2,1)S(1)}, f32[2,24,64,256]{3,2,1,0:T(8,128)}) custom-call(s32[2]{0:T(128)S(1)} %pad_add_fusion.me_ref._, bf16[4,48,32,512]{3,2,1,0:T(8,128)(2,1)} %all-to-all-done.refs_0_, bf16[32,256,256]{2,1,0:T(8,128)(2,1)} %refs_1_.3, ...), custom_call_target="tpu_custom_call" | custom-call | flops 1 | bytes 1 | tf_op jit(solution)/shard_map/pallas_call | solution.py:100
  423.7 1.8 collective-permute-done.29.came_ref
  427.5 3.9 shard_map.120
  431.4 1.5 collective-permute-start.31
  432.9 25.4 %all-to-all-done.1.refs_0_ = bf16[4,16,32,512]{3,2,1,0:T(8,128)(2,1)} async-done(((bf16[4,16,32,512]{3,2,1,0:T(8,128)(2,1)}), bf16[4,16,32,512]{3,2,1,0:T(8,128)(2,1)}, u32[]{:S(2)}, u32[]{:S(2)}) %all-to-all-start.1) | async-done | bytes 2097184 | tf_op jit(solution)/shard_map/all_to_all | solution.py:629
  458.2 5.4 %shard_map.118 = (bf16[512,8192]{1,0:T(8,128)(2,1)}, bf16[8,64,256]{2,1,0:T(8,128)(2,1)S(1)}, bf16[8,64,256]{2,1,0:T(8,128)(2,1)S(1)}, f32[2,8,64,256]{3,2,1,0:T(8,128)S(1)}) custom-call(s32[2]{0:T(128)S(1)} %pad_add_fusion.me_ref._, bf16[4,16,32,512]{3,2,1,0:T(8,128)(2,1)} %all-to-all-done.1.refs_0_, ...), custom_call_target="tpu_custom_call", output_to_operand_aliasing={{0}: (5, {})} | custom-call | flops 1 | bytes 1 | tf_op jit(solution)/shard_map/pallas_call | solution.py:100
  466.5 1.9 shard_map.119
  468.4 1.6 collective-permute-start.28
  470.0 3.2 shard_map.121.refs_0_
  473.2 3.6 collective-permute-done.28.came_ref
  (89 shorter events, 18.4 us)
Async XLA Ops:
  5.5 52.5 %collective-permute-start.1 = (bf16[32,16,512]{2,1,0:T(8,128)(2,1)S(1)}, bf16[32,16,512]{2,1,0:T(8,128)(2,1)S(1)}, u32[]{:S(2)}, u32[]{:S(2)}) collective-permute-start(bf16[32,16,512]{2,1,0:T(8,128)(2,1)S(1)} %get-tuple-element.71), channel_id=1, source_target_pairs={{0,8},{4,12},{8,0},{12,4},{1,9},{5,13},{9,1},{13,5},{2,10},{6,14},... | collective-permute-start | bytes 1572872 | tf_op jit(solution)/shard_map/ppermute | solution.py:96
  9.5 48.5 %collective-permute-start = (bf16[32,16,512]{2,1,0:T(8,128)(2,1)}, bf16[32,16,512]{2,1,0:T(8,128)(2,1)S(1)}, u32[]{:S(2)}, u32[]{:S(2)}) collective-permute-start(bf16[32,16,512]{2,1,0:T(8,128)(2,1)} %get-tuple-element.70), channel_id=1, source_target_pairs={{0,12},{4,8},{8,4},{12,0},{1,13},{5,9},{9,5},{13,1},{2,14},{6,10},... | collective-permute-start | bytes 1572872 | tf_op jit(solution)/shard_map/ppermute | solution.py:96
  10.9 47.2 %collective-permute-start.2 = (bf16[32,16,512]{2,1,0:T(8,128)(2,1)S(1)}, bf16[32,16,512]{2,1,0:T(8,128)(2,1)S(1)}, u32[]{:S(2)}, u32[]{:S(2)}) collective-permute-start(bf16[32,16,512]{2,1,0:T(8,128)(2,1)S(1)} %get-tuple-element.72), channel_id=1, source_target_pairs={{0,4},{4,0},{8,12},{12,8},{1,5},{5,1},{9,13},{13,9},{2,6},{6,2},{1... | collective-permute-start | bytes 1572872 | tf_op jit(solution)/shard_map/ppermute | solution.py:96
  11.1 9.1 %copy-start.17 = (bf16[8192]{0:T(1024)(128)(2,1)S(1)}, bf16[8192]{0:T(1024)(128)(2,1)}, u32[]{:S(2)}) copy-start(bf16[8192]{0:T(1024)(128)(2,1)} %param.10) | copy-start | bytes 49156
  58.0 1.9 copy-start.7
  58.0 4.4 copy-start.8
  58.0 4.4 copy-start.9
  58.0 36.7 %collective-permute-start.3 = (bf16[2,512,768]{2,1,0:T(8,128)(2,1)S(1)}, bf16[2,512,768]{2,1,0:T(8,128)(2,1)}, u32[]{:S(2)}, u32[]{:S(2)}) collective-permute-start(bf16[2,512,768]{2,1,0:T(8,128)(2,1)S(1)} %get-tuple-element.73), channel_id=1, source_target_pairs={{0,4},{4,0},{8,12},{12,8},{1,5},{5,1},{9,13},{13,9},{2,6},{6,2},{1... | collective-permute-start | bytes 4718600 | tf_op jit(solution)/shard_map/ppermute | solution.py:96
  59.9 60.5 %collective-permute-start.5 = (bf16[32,32,512]{2,1,0:T(8,128)(2,1)}, bf16[32,32,512]{2,1,0:T(8,128)(2,1)}, u32[]{:S(2)}, u32[]{:S(2)}) collective-permute-start(bf16[32,32,512]{2,1,0:T(8,128)(2,1)} %get-tuple-element.81), channel_id=1, source_target_pairs={{0,12},{4,8},{8,4},{12,0},{1,13},{5,9},{9,5},{13,1},{2,14},{6,10},... | collective-permute-start | bytes 3145736 | tf_op jit(solution)/shard_map/ppermute | solution.py:96
  74.2 28.4 %copy-start.19 = (bf16[32,32,512]{2,1,0:T(8,128)(2,1)S(1)}, bf16[32,32,512]{2,1,0:T(8,128)(2,1)}, u32[]{:S(2)}) copy-start(bf16[32,32,512]{2,1,0:T(8,128)(2,1)} %get-tuple-element.87) | copy-start | bytes 3145732
  74.2 28.4 %copy-start.18 = (bf16[32,32,512]{2,1,0:T(8,128)(2,1)S(1)}, bf16[32,32,512]{2,1,0:T(8,128)(2,1)}, u32[]{:S(2)}) copy-start(bf16[32,32,512]{2,1,0:T(8,128)(2,1)} %get-tuple-element.89) | copy-start | bytes 3145732
  94.8 133.5 %copy-start.20 = (bf16[32,16,512]{2,1,0:T(8,128)(2,1)S(1)}, bf16[32,16,512]{2,1,0:T(8,128)(2,1)}, u32[]{:S(2)}) copy-start(bf16[32,16,512]{2,1,0:T(8,128)(2,1)} %get-tuple-element.99) | copy-start | bytes 1572868
  98.9 75.5 %collective-permute-start.4 = (bf16[512,768]{1,0:T(8,128)(2,1)S(1)}, bf16[512,768]{1,0:T(8,128)(2,1)S(1)}, u32[]{:S(2)}, u32[]{:S(2)}) collective-permute-start(bf16[512,768]{1,0:T(8,128)(2,1)S(1)} %get-tuple-element.79), channel_id=1, source_target_pairs={{0,8},{4,12},{8,0},{12,4},{1,9},{5,13},{9,1},{13,5},{2,10},{6,14},... | collective-permute-start | bytes 2359304 | tf_op jit(solution)/shard_map/ppermute | solution.py:96
  102.5 100.4 %collective-permute-start.14 = (bf16[32,32,512]{2,1,0:T(8,128)(2,1)S(1)}, bf16[32,32,512]{2,1,0:T(8,128)(2,1)S(1)}, u32[]{:S(2)}, u32[]{:S(2)}) collective-permute-start(bf16[32,32,512]{2,1,0:T(8,128)(2,1)S(1)} %copy-done.19), channel_id=1, source_target_pairs={{0,8},{4,12},{8,0},{12,4},{1,9},{5,13},{9,1},{13,5},{2,10},{6,14},... | collective-permute-start | bytes 3145736 | tf_op jit(solution)/shard_map/ppermute | solution.py:96
  102.6 100.3 %collective-permute-start.15 = (bf16[32,32,512]{2,1,0:T(8,128)(2,1)S(1)}, bf16[32,32,512]{2,1,0:T(8,128)(2,1)S(1)}, u32[]{:S(2)}, u32[]{:S(2)}) collective-permute-start(bf16[32,32,512]{2,1,0:T(8,128)(2,1)S(1)} %copy-done.18), channel_id=1, source_target_pairs={{0,4},{4,0},{8,12},{12,8},{1,5},{5,1},{9,13},{13,9},{2,6},{6,2},{1... | collective-permute-start | bytes 3145736 | tf_op jit(solution)/shard_map/ppermute | solution.py:96
  177.6 9.2 %collective-permute-start.7 = (bf16[512,256]{1,0:T(8,128)(2,1)S(1)}, bf16[512,256]{1,0:T(8,128)(2,1)S(1)}, u32[]{:S(2)}, u32[]{:S(2)}) collective-permute-start(bf16[512,256]{1,0:T(8,128)(2,1)S(1)} %get-tuple-element.84.refs_0_), channel_id=1, source_target_pairs={{0,2},{1,3},{2,0},{3,1},{4,6},{5,7},{6,4},{7,5},{8,10},{9,11},{10,... | collective-permute-start | bytes 786440 | tf_op jit(solution)/shard_map/ppermute | solution.py:96
  179.2 7.7 %collective-permute-start.6 = (bf16[512,256]{1,0:T(8,128)(2,1)S(1)}, bf16[512,256]{1,0:T(8,128)(2,1)S(1)}, u32[]{:S(2)}, u32[]{:S(2)}) collective-permute-start(bf16[512,256]{1,0:T(8,128)(2,1)S(1)} %get-tuple-element.84.refs_0_), channel_id=1, source_target_pairs={{0,1},{1,0},{2,3},{3,2},{4,5},{5,4},{6,7},{7,6},{8,9},{9,8},{10,11... | collective-permute-start | bytes 786440 | tf_op jit(solution)/shard_map/ppermute | solution.py:96
  179.2 12.3 %collective-permute-start.10 = (bf16[512,256]{1,0:T(8,128)(2,1)S(1)}, bf16[512,256]{1,0:T(8,128)(2,1)S(1)}, u32[]{:S(2)}, u32[]{:S(2)}) collective-permute-start(bf16[512,256]{1,0:T(8,128)(2,1)S(1)} %get-tuple-element.85.refs_4_), channel_id=1, source_target_pairs={{0,2},{1,3},{2,0},{3,1},{4,6},{5,7},{6,4},{7,5},{8,10},{9,11},{10,... | collective-permute-start | bytes 786440 | tf_op jit(solution)/shard_map/ppermute | solution.py:96
  186.9 4.6 collective-permute-start.9
  186.9 4.6 collective-permute-start.8
  191.4 1.5 copy-start.14
  191.4 1.5 collective-permute-start.11
  191.4 1.5 copy-start.15
  200.9 13.7 %collective-permute-start.13 = (bf16[512,256]{1,0:T(8,128)(2,1)S(1)}, bf16[512,256]{1,0:T(8,128)(2,1)S(1)}, u32[]{:S(2)}, u32[]{:S(2)}) collective-permute-start(bf16[512,256]{1,0:T(8,128)(2,1)S(1)} %shard_map.109.own), channel_id=1, source_target_pairs={{0,8},{4,12},{8,0},{12,4},{1,9},{5,13},{9,1},{13,5},{2,10},{6,14},... | collective-permute-start | bytes 786440 | tf_op jit(solution)/shard_map/ppermute | solution.py:96
  201.0 14.0 %collective-permute-start.12 = (bf16[512,256]{1,0:T(8,128)(2,1)S(1)}, bf16[512,256]{1,0:T(8,128)(2,1)S(1)}, u32[]{:S(2)}, u32[]{:S(2)}) collective-permute-start(bf16[512,256]{1,0:T(8,128)(2,1)S(1)} %shard_map.109.own), channel_id=1, source_target_pairs={{0,4},{4,0},{8,12},{12,8},{1,5},{5,1},{9,13},{13,9},{2,6},{6,2},{1... | collective-permute-start | bytes 786440 | tf_op jit(solution)/shard_map/ppermute | solution.py:96
  202.9 51.3 %copy-start.5 = (bf16[32,32,512]{2,1,0:T(8,128)(2,1)}, bf16[32,32,512]{2,1,0:T(8,128)(2,1)S(1)}, u32[]{:S(2)}) copy-start(bf16[32,32,512]{2,1,0:T(8,128)(2,1)S(1)} %collective-permute-done.14.refs_6_) | copy-start | bytes 3145732
  202.9 51.3 %copy-start.6 = (bf16[32,32,512]{2,1,0:T(8,128)(2,1)}, bf16[32,32,512]{2,1,0:T(8,128)(2,1)S(1)}, u32[]{:S(2)}) copy-start(bf16[32,32,512]{2,1,0:T(8,128)(2,1)S(1)} %collective-permute-done.15.refs_5_) | copy-start | bytes 3145732
  215.0 13.2 %collective-permute-start.16 = (bf16[512,256]{1,0:T(8,128)(2,1)S(1)}, bf16[512,256]{1,0:T(8,128)(2,1)S(1)}, u32[]{:S(2)}, u32[]{:S(2)}) collective-permute-start(bf16[512,256]{1,0:T(8,128)(2,1)S(1)} %collective-permute-done.13.far), channel_id=1, source_target_pairs={{0,4},{4,0},{8,12},{12,8},{1,5},{5,1},{9,13},{13,9},{2,6},{6,2},{1... | collective-permute-start | bytes 786440 | tf_op jit(solution)/shard_map/ppermute | solution.py:96
  215.3 38.9 %collective-permute-start.18 = (bf16[32,16,512]{2,1,0:T(8,128)(2,1)S(1)}, bf16[32,16,512]{2,1,0:T(8,128)(2,1)S(1)}, u32[]{:S(2)}, u32[]{:S(2)}) collective-permute-start(bf16[32,16,512]{2,1,0:T(8,128)(2,1)S(1)} %get-tuple-element.97), channel_id=1, source_target_pairs={{0,8},{4,12},{8,0},{12,4},{1,9},{5,13},{9,1},{13,5},{2,10},{6,14},... | collective-permute-start | bytes 1572872 | tf_op jit(solution)/shard_map/ppermute | solution.py:96
  228.2 29.9 %collective-permute-start.17 = (bf16[32,16,512]{2,1,0:T(8,128)(2,1)S(1)}, bf16[32,16,512]{2,1,0:T(8,128)(2,1)S(1)}, u32[]{:S(2)}, u32[]{:S(2)}) collective-permute-start(bf16[32,16,512]{2,1,0:T(8,128)(2,1)S(1)} %get-tuple-element.95), channel_id=1, source_target_pairs={{0,4},{4,0},{8,12},{12,8},{1,5},{5,1},{9,13},{13,9},{2,6},{6,2},{1... | collective-permute-start | bytes 1572872 | tf_op jit(solution)/shard_map/ppermute | solution.py:96
  228.2 29.9 %collective-permute-start.19 = (bf16[32,16,512]{2,1,0:T(8,128)(2,1)S(1)}, bf16[32,16,512]{2,1,0:T(8,128)(2,1)S(1)}, u32[]{:S(2)}, u32[]{:S(2)}) collective-permute-start(bf16[32,16,512]{2,1,0:T(8,128)(2,1)S(1)} %copy-done.20), channel_id=1, source_target_pairs={{0,12},{4,8},{8,4},{12,0},{1,13},{5,9},{9,5},{13,1},{2,14},{6,10},... | collective-permute-start | bytes 1572872 | tf_op jit(solution)/shard_map/ppermute | solution.py:96
  254.2 3.9 copy-start.10
  259.1 145.9 %all-to-all-start = ((bf16[4,48,32,512]{3,2,1,0:T(8,128)(2,1)}), bf16[4,48,32,512]{3,2,1,0:T(8,128)(2,1)}, u32[]{:S(2)}, u32[]{:S(2)}) async-start(bf16[4,48,32,512]{3,2,1,0:T(8,128)(2,1)} %get-tuple-element.100), calls=%async_computation | async-start | bytes 12582912 | tf_op jit(solution)/shard_map/all_to_all | solution.py:629
  273.8 8.1 %collective-permute-start.23 = (bf16[16,64,256]{2,1,0:T(8,128)(2,1)S(1)}, bf16[16,64,256]{2,1,0:T(8,128)(2,1)S(1)}, u32[]{:S(2)}, u32[]{:S(2)}) collective-permute-start(bf16[16,64,256]{2,1,0:T(8,128)(2,1)S(1)} %get-tuple-element.108), channel_id=1, source_target_pairs={{0,1},{1,0},{2,3},{3,2},{4,5},{5,4},{6,7},{7,6},{8,9},{9,8},{10,11... | collective-permute-start | bytes 1572872 | tf_op jit(solution)/shard_map/ppermute | solution.py:96
  273.9 8.1 %collective-permute-start.24 = (bf16[16,64,256]{2,1,0:T(8,128)(2,1)S(1)}, bf16[16,64,256]{2,1,0:T(8,128)(2,1)S(1)}, u32[]{:S(2)}, u32[]{:S(2)}) collective-permute-start(bf16[16,64,256]{2,1,0:T(8,128)(2,1)S(1)} %get-tuple-element.109), channel_id=1, source_target_pairs={{0,1},{1,0},{2,3},{3,2},{4,5},{5,4},{6,7},{7,6},{8,9},{9,8},{10,11... | collective-permute-start | bytes 1572872 | tf_op jit(solution)/shard_map/ppermute | solution.py:96
  281.4 5.3 %collective-permute-start.20 = (bf16[16,64,256]{2,1,0:T(8,128)(2,1)S(1)}, bf16[16,64,256]{2,1,0:T(8,128)(2,1)S(1)}, u32[]{:S(2)}, u32[]{:S(2)}) collective-permute-start(bf16[16,64,256]{2,1,0:T(8,128)(2,1)S(1)} %get-tuple-element.103), channel_id=1, source_target_pairs={{0,1},{1,0},{2,3},{3,2},{4,5},{5,4},{6,7},{7,6},{8,9},{9,8},{10,11... | collective-permute-start | bytes 1572872 | tf_op jit(solution)/shard_map/ppermute | solution.py:96
  281.5 5.2 %collective-permute-start.21 = (bf16[16,64,256]{2,1,0:T(8,128)(2,1)S(1)}, bf16[16,64,256]{2,1,0:T(8,128)(2,1)S(1)}, u32[]{:S(2)}, u32[]{:S(2)}) collective-permute-start(bf16[16,64,256]{2,1,0:T(8,128)(2,1)S(1)} %get-tuple-element.104), channel_id=1, source_target_pairs={{0,1},{1,0},{2,3},{3,2},{4,5},{5,4},{6,7},{7,6},{8,9},{9,8},{10,11... | collective-permute-start | bytes 1572872 | tf_op jit(solution)/shard_map/ppermute | solution.py:96
  285.2 14.8 %collective-permute-start.25 = (bf16[16,64,256]{2,1,0:T(8,128)(2,1)S(1)}, bf16[16,64,256]{2,1,0:T(8,128)(2,1)S(1)}, u32[]{:S(2)}, u32[]{:S(2)}) collective-permute-start(bf16[16,64,256]{2,1,0:T(8,128)(2,1)S(1)} %get-tuple-element.111), channel_id=1, source_target_pairs={{0,2},{1,3},{2,0},{3,1},{4,6},{5,7},{6,4},{7,5},{8,10},{9,11},{10,... | collective-permute-start | bytes 1572872 | tf_op jit(solution)/shard_map/ppermute | solution.py:96
  289.9 20.4 %collective-permute-start.22 = (bf16[16,64,256]{2,1,0:T(8,128)(2,1)S(1)}, bf16[16,64,256]{2,1,0:T(8,128)(2,1)S(1)}, u32[]{:S(2)}, u32[]{:S(2)}) collective-permute-start(bf16[16,64,256]{2,1,0:T(8,128)(2,1)S(1)} %get-tuple-element.106), channel_id=1, source_target_pairs={{0,2},{1,3},{2,0},{3,1},{4,6},{5,7},{6,4},{7,5},{8,10},{9,11},{10,... | collective-permute-start | bytes 1572872 | tf_op jit(solution)/shard_map/ppermute | solution.py:96
  300.0 1.2 copy-start.3
  301.2 9.1 %copy-start.4 = (f32[16,64,256]{2,1,0:T(8,128)S(1)}, f32[16,64,256]{2,1,0:T(8,128)}, u32[]{:S(2)}) copy-start(f32[16,64,256]{2,1,0:T(8,128)} %get-tuple-element.105.mine_ref) | copy-start | bytes 3145732
  405.1 53.2 %all-to-all-start.1 = ((bf16[4,16,32,512]{3,2,1,0:T(8,128)(2,1)}), bf16[4,16,32,512]{3,2,1,0:T(8,128)(2,1)}, u32[]{:S(2)}, u32[]{:S(2)}) async-start(bf16[4,16,32,512]{3,2,1,0:T(8,128)(2,1)} %get-tuple-element.112), calls=%async_computation.1 | async-start | bytes 4194304 | tf_op jit(solution)/shard_map/all_to_all | solution.py:629
  423.1 2.3 collective-permute-start.29
  423.2 3.4 collective-permute-start.30
  431.4 38.6 %collective-permute-start.31 = (bf16[24,64,256]{2,1,0:T(8,128)(2,1)S(1)}, bf16[24,64,256]{2,1,0:T(8,128)(2,1)S(1)}, u32[]{:S(2)}, u32[]{:S(2)}) collective-permute-start(bf16[24,64,256]{2,1,0:T(8,128)(2,1)S(1)} %get-tuple-element.124), channel_id=1, source_target_pairs={{0,2},{1,3},{2,0},{3,1},{4,6},{5,7},{6,4},{7,5},{8,10},{9,11},{10,... | collective-permute-start | bytes 2359304 | tf_op jit(solution)/shard_map/ppermute | solution.py:96
  464.6 1.5 collective-permute-start.26
  464.6 1.9 collective-permute-start.27
  468.4 8.4 %collective-permute-start.28 = (bf16[8,64,256]{2,1,0:T(8,128)(2,1)S(1)}, bf16[8,64,256]{2,1,0:T(8,128)(2,1)S(1)}, u32[]{:S(2)}, u32[]{:S(2)}) collective-permute-start(bf16[8,64,256]{2,1,0:T(8,128)(2,1)S(1)} %get-tuple-element.119), channel_id=1, source_target_pairs={{0,2},{1,3},{2,0},{3,1},{4,6},{5,7},{6,4},{7,5},{8,10},{9,11},{10,... | collective-permute-start | bytes 786440 | tf_op jit(solution)/shard_map/ppermute | solution.py:96
  (7 other events, 6.1 us)

commit v10 on v9

--- a/solution.py
+++ b/solution.py
@@ -500,21 +500,20 @@
         out_ref[:, at] = (hidden_ref[:, at].astype(F32) + mixed).astype(BF16)
 
 
-def second_call(me, pieces, w_second, cotangent, hidden, denoised, start):
+def second_call(me, pieces, w_second, cotangent, hidden, denoised, start, low, count):
     blocks, size, _ = w_second.shape
-    deep, _, rows = pieces[0].shape[-3:]
+    rows = hidden.shape[0]
     pair = size // (4 * blocks)
-    count = deep // pair
-    group = several(math.gcd(count, start) if start else count)
-    begin = start // group
+    group = several(math.gcd(count, start, low))
+    begin, low = start // group, low // group
     wide = spec((rows, group * size), lambda j, _: (0, begin + j))
     square = spec((group, size, size), lambda j, _: (begin + j, 0, 0))
     args = [*pieces, w_second, cotangent, hidden]
     part = (group * pair, blocks, rows)
     if len(pieces) == 1:
-        in_specs = [spec((4, *part), lambda j, _: (0, j, 0, 0))]
+        in_specs = [spec((4, *part), lambda j, _: (0, low + j, 0, 0))]
     else:
-        in_specs = [spec(part, lambda j, _: (j, 0, 0))] * 4
+        in_specs = [spec(part, lambda j, _: (low + j, 0, 0))] * 4
     in_specs += [square, wide, wide]
     quarters = quarter_outs(count, group, size)
     aliases = {}
@@ -608,7 +607,7 @@
     across = [flip(piece, "cell", 2) for piece in own]
     beside = [flip(piece, "cell", 1) for piece in own]
     corner = [flip(piece, "cell", 1) for piece in across]
-    beside_keys = [begin(1, bits, other) for bits in (2, 1)]
+    beside_keys = [begin(1, bits, last, beside_sum) for bits in (2, 1)]
     gathered = [piece for kind in zip(own, beside, across, corner) for piece in kind]
     attended = attend_call(me, queries, gathered)
     near = flip(attended, "gene", 1)
@@ -646,13 +645,16 @@
     sum_cells(0, blocks // 2, send_next, keep_next)
     pin = shares[0]
     for t in range(len(chunks)):
-        start = sum(count for count, _ in chunks[:t]) * blocks // deep
         if t + 1 < len(chunks):
             launch(t + 1, *got[t], pin)
-        denoised, *send, keep = second_call(
-            me, got[t], w_second, cotangent, hidden, denoised, start
-        )
-        sum_cells(1, start, send, keep)
+        start, count = (n * blocks // deep for n in (sum(n for n, _ in chunks[:t]), chunks[t][0]))
+        calls = 2 if t == len(chunks) - 1 else 1
+        count //= calls
+        for low in range(0, calls * count, count):
+            denoised, *send, keep = second_call(
+                me, got[t], w_second, cotangent, hidden, denoised, start + low, low, count
+            )
+            sum_cells(1, start + low, send, keep)
         pin = shares[1]
     return (denoised, *shares)
 

time: 479 us -> 475 us (level)
  waiting for transfers between devices: 273 us -> 264 us
    ppermute x32 -> x35, waiting for transfers between devices: 155 us -> 146 us  [flip(): return lax.ppermute(value, axis, pairs)]
    pallas_call x20 -> x23, Pallas kernels: 147 us -> 151 us  [call(): pl.pallas_call(body, out_shape=outs, grid_spec=pltpu.PrefetchScalarGridSp...]
    ppermute x32 -> x35, starting transfers between devices: 31.6 us -> 33.8 us  [flip(): return lax.ppermute(value, axis, pairs)]
  transfers between devices with their start and end apart: 34 -> 37, of which waited for: 19 -> 18; matrix products, arithmetic and copies ran while one was open for 1% -> 1% of each run, Pallas kernels for 29% -> 31%
where the time goes in v10:
time: 475 us; the launch traced here: 474 us
  waiting for transfers between devices  264 us (56%)
  Pallas kernels  151 us (32%)
  starting transfers between devices  46 us (10%)
  local copies, waits for them, and re-layouts  12.2 us (3%)
    pallas_call x23, Pallas kernels, call(): pl.pallas_call(body, out_shape=outs, grid_spec=pltpu.PrefetchScalarGridSp...  151 us
    ppermute x35, waiting for transfers between devices, flip(): return lax.ppermute(value, axis, pairs)  146 us
    all_to_all x2, waiting for transfers between devices, launch(): lax.all_to_all(pieces[0], 'gene', split_axis=0, concat_axis=0, tiled=True)  119 us
    ppermute x35, starting transfers between devices, flip(): return lax.ppermute(value, axis, pairs)  33.8 us
    all_to_all x2, starting transfers between devices, launch(): lax.all_to_all(pieces[0], 'gene', split_axis=0, concat_axis=0, tiled=True)  12.2 us
  transfers between devices with their start and end apart: 37, of which 18 were waited for; matrix products, arithmetic and copies ran while one was open for 1% of the time, Pallas kernels for 31%

profile of v10, /device:TPU:0, one launch (start us, length us, event | category | flops | bytes accessed | tf_op | source)
XLA Modules:
  0.0 474.2 jit_solution(12829617384797472889)
XLA Ops:
  1.0 4.4 shard_map.103
  5.5 4.0 collective-permute-start.1
  11.1 8.1 %shard_map.104 = (bf16[32,32,512]{2,1,0:T(8,128)(2,1)S(1)}, bf16[32,32,512]{2,1,0:T(8,128)(2,1)}, bf16[32,32,512]{2,1,0:T(8,128)(2,1)}, bf16[32,32,512]{2,1,0:T(8,128)(2,1)}) custom-call(s32[2]{0:T(128)S(1)} %pad_add_fusion.me_ref._, bf16[256,256]{1,0:T(8,128)(2,1)S(1)} %fusion.turn_ref, bf16[32,256,256]{2,1,0:T(8,128)(2,1)} %refs_1_.5, ...), custom_call_target="tpu_custom_call" | custom-call | flops 1 | bytes 1 | tf_op jit(solution)/shard_map/pallas_call | solution.py:100
  20.2 37.8 %shard_map.105 = (bf16[512,8192]{1,0:T(8,128)(2,1)}, bf16[2,512,768]{2,1,0:T(8,128)(2,1)S(1)}, f32[2,512,768]{2,1,0:T(8,128)}) custom-call(s32[2]{0:T(128)S(1)} %pad_add_fusion.me_ref._, bf16[512,8192]{1,0:T(8,128)(2,1)} %value_ref, s32[512,8192]{1,0:T(8,128)} %mask_ref.1, bf16[1,8192]{1,0:T(2,128)(2,1)S(1)} %reshape.9.fill_ref, bf16[8192,3072]{1,0:T(8,128)(2,1)} %weight_ref.1), custom_call_target="tpu_custom_call" | custom-call | flops 1 | bytes 1 | tf_op jit(solution)/shard_map/pallas_call | solution.py:100
  58.1 1.9 collective-permute-start.3
  59.9 2.5 collective-permute-start.5
  62.4 4.5 shard_map.106
  67.7 6.5 %copy.16 = bf16[32,256,256]{1,2,0:T(8,128)(2,1)} copy(bf16[32,256,256]{2,1,0:T(8,128)(2,1)} %param.13) | data formatting | bytes 8388608 | tf_op jit(solution)/shard_map/optimization_barrier | solution.py:91
  74.1 20.6 %collective-permute-done.3.came_ref = bf16[2,512,768]{2,1,0:T(8,128)(2,1)} collective-permute-done((bf16[2,512,768]{2,1,0:T(8,128)(2,1)S(1)}, bf16[2,512,768]{2,1,0:T(8,128)(2,1)}, u32[]{:S(2)}, u32[]{:S(2)}) %collective-permute-start.3) | collective-permute-done | bytes 1572896 | tf_op jit(solution)/shard_map/ppermute | solution.py:96
  94.8 4.2 shard_map.107
  98.9 3.6 collective-permute-start.4
  102.5 17.8 %collective-permute-done.5.refs_7_ = bf16[32,32,512]{2,1,0:T(8,128)(2,1)} collective-permute-done((bf16[32,32,512]{2,1,0:T(8,128)(2,1)}, bf16[32,32,512]{2,1,0:T(8,128)(2,1)}, u32[]{:S(2)}, u32[]{:S(2)}) %collective-permute-start.5) | collective-permute-done | bytes 1048608 | tf_op jit(solution)/shard_map/ppermute | solution.py:96
  120.4 31.5 %collective-permute-done.4.came_ref = bf16[512,768]{1,0:T(8,128)(2,1)S(1)} collective-permute-done((bf16[512,768]{1,0:T(8,128)(2,1)S(1)}, bf16[512,768]{1,0:T(8,128)(2,1)S(1)}, u32[]{:S(2)}, u32[]{:S(2)}) %collective-permute-start.4) | collective-permute-done | bytes 786464 | tf_op jit(solution)/shard_map/ppermute | solution.py:96
  151.9 1.9 collective-permute-start.15
  153.8 3.2 shard_map.108
  157.0 1.5 collective-permute-start.7
  159.0 7.2 %collective-permute-done.7.refs_2_ = bf16[512,256]{1,0:T(8,128)(2,1)S(1)} collective-permute-done((bf16[512,256]{1,0:T(8,128)(2,1)S(1)}, bf16[512,256]{1,0:T(8,128)(2,1)S(1)}, u32[]{:S(2)}, u32[]{:S(2)}) %collective-permute-start.7) | collective-permute-done | bytes 262176 | tf_op jit(solution)/shard_map/ppermute | solution.py:96
  166.8 3.5 collective-permute-done.10.refs_6_
  170.3 1.5 collective-permute-done.11.refs_7_
  172.5 7.2 %shard_map.109.own = bf16[512,256]{1,0:T(8,128)(2,1)S(1)} custom-call(s32[2]{0:T(128)S(1)} %pad_add_fusion.me_ref._, bf16[512,256]{1,0:T(8,128)(2,1)S(1)} %get-tuple-element.89.query_ref, bf16[512,256]{1,0:T(8,128)(2,1)S(1)} %get-tuple-element.90.refs_0_, bf16[512,256]{1,0:T(8,128)(2,1)S(1)} %collective-permute-done.6.refs_1_, ...), custom_call_target="tpu_custom_call" | custom-call | flops 1 | bytes 1 | tf_op jit(solution)/shard_map/pallas_call | solution.py:100
  181.1 1.7 collective-permute-start.12
  182.9 27.5 %collective-permute-done.13.far = bf16[512,256]{1,0:T(8,128)(2,1)S(1)} collective-permute-done((bf16[512,256]{1,0:T(8,128)(2,1)S(1)}, bf16[512,256]{1,0:T(8,128)(2,1)S(1)}, u32[]{:S(2)}, u32[]{:S(2)}) %collective-permute-start.13) | collective-permute-done | bytes 262176 | tf_op jit(solution)/shard_map/ppermute | solution.py:96
  211.1 2.5 collective-permute-start.18
  213.6 10.6 %collective-permute-done.16.rest = bf16[512,256]{1,0:T(8,128)(2,1)S(1)} collective-permute-done((bf16[512,256]{1,0:T(8,128)(2,1)S(1)}, bf16[512,256]{1,0:T(8,128)(2,1)S(1)}, u32[]{:S(2)}, u32[]{:S(2)}) %collective-permute-start.16) | collective-permute-done | bytes 262176 | tf_op jit(solution)/shard_map/ppermute | solution.py:96
  224.2 1.4 collective-permute-start.19
  225.6 24.5 %shard_map.110 = (bf16[512,8192]{1,0:T(8,128)(2,1)}, bf16[4,48,32,512]{3,2,1,0:T(8,128)(2,1)}, bf16[4,16,32,512]{3,2,1,0:T(8,128)(2,1)}) custom-call(s32[2]{0:T(128)S(1)} %pad_add_fusion.me_ref._, bf16[256,256]{1,0:T(8,128)(2,1)S(1)} %fusion.turn_ref, bf16[512,256]{1,0:T(8,128)(2,1)S(1)} %shard_map.109.own, ...), custom_call_target="tpu_custom_call" | custom-call | flops 1 | bytes 1 | tf_op jit(solution)/shard_map/pallas_call | solution.py:100
  250.1 4.0 collective-permute-done.17.refs_9_
  255.1 7.7 %all-to-all-start = ((bf16[4,48,32,512]{3,2,1,0:T(8,128)(2,1)}), bf16[4,48,32,512]{3,2,1,0:T(8,128)(2,1)}, u32[]{:S(2)}, u32[]{:S(2)}) async-start(bf16[4,48,32,512]{3,2,1,0:T(8,128)(2,1)} %get-tuple-element.106), calls=%async_computation | async-start | bytes 12582912 | tf_op jit(solution)/shard_map/all_to_all | solution.py:628
  262.9 7.0 %shard_map.113 = (bf16[16,64,256]{2,1,0:T(8,128)(2,1)S(1)}, bf16[16,64,256]{2,1,0:T(8,128)(2,1)S(1)}, f32[2,16,64,256]{3,2,1,0:T(8,128)}) custom-call(s32[2]{0:T(128)S(1)} %pad_add_fusion.me_ref._, bf16[32,16,512]{2,1,0:T(8,128)(2,1)S(1)} %get-tuple-element.70.refs_0_, bf16[32,16,512]{2,1,0:T(8,128)(2,1)} %copy-done.8, bf16[32,16,512]{2,1,0:T(8,128)(2,1)} %copy-done.6, ...), custom_call_target="tpu_custom_call" | custom-call | flops 1 | bytes 1 | tf_op jit(solution)/shard_map/pallas_call | solution.py:100
  270.4 7.0 %shard_map.111 = (bf16[16,64,256]{2,1,0:T(8,128)(2,1)S(1)}, bf16[16,64,256]{2,1,0:T(8,128)(2,1)S(1)}, f32[2,16,64,256]{3,2,1,0:T(8,128)}) custom-call(s32[2]{0:T(128)S(1)} %pad_add_fusion.me_ref._, bf16[32,16,512]{2,1,0:T(8,128)(2,1)S(1)} %get-tuple-element.70.refs_0_, bf16[32,16,512]{2,1,0:T(8,128)(2,1)} %copy-done.8, bf16[32,16,512]{2,1,0:T(8,128)(2,1)} %copy-done.6, ...), custom_call_target="tpu_custom_call" | custom-call | flops 1 | bytes 1 | tf_op jit(solution)/shard_map/pallas_call | solution.py:100
  278.0 3.3 shard_map.114
  281.3 1.5 collective-permute-start.25
  282.8 3.2 shard_map.112
  286.5 9.5 %collective-permute-done.25.came_ref = bf16[16,64,256]{2,1,0:T(8,128)(2,1)S(1)} collective-permute-done((bf16[16,64,256]{2,1,0:T(8,128)(2,1)S(1)}, bf16[16,64,256]{2,1,0:T(8,128)(2,1)S(1)}, u32[]{:S(2)}, u32[]{:S(2)}) %collective-permute-start.25) | collective-permute-done | bytes 524320 | tf_op jit(solution)/shard_map/ppermute | solution.py:96
  297.3 1.6 shard_map.115.refs_0_
  298.9 7.5 %collective-permute-done.22.came_ref = bf16[16,64,256]{2,1,0:T(8,128)(2,1)S(1)} collective-permute-done((bf16[16,64,256]{2,1,0:T(8,128)(2,1)S(1)}, bf16[16,64,256]{2,1,0:T(8,128)(2,1)S(1)}, u32[]{:S(2)}, u32[]{:S(2)}) %collective-permute-start.22) | collective-permute-done | bytes 524320 | tf_op jit(solution)/shard_map/ppermute | solution.py:96
  306.4 1.6 shard_map.116
  308.0 93.3 %all-to-all-done.refs_0_ = bf16[4,48,32,512]{3,2,1,0:T(8,128)(2,1)} async-done(((bf16[4,48,32,512]{3,2,1,0:T(8,128)(2,1)}), bf16[4,48,32,512]{3,2,1,0:T(8,128)(2,1)}, u32[]{:S(2)}, u32[]{:S(2)}) %all-to-all-start) | async-done | bytes 6291488 | tf_op jit(solution)/shard_map/all_to_all | solution.py:628
  401.3 4.5 all-to-all-start.1
  405.8 13.6 %shard_map.117 = (bf16[512,8192]{1,0:T(8,128)(2,1)}, bf16[24,64,256]{2,1,0:T(8,128)(2,1)S(1)}, bf16[24,64,256]{2,1,0:T(8,128)(2,1)S(1)}, f32[2,24,64,256]{3,2,1,0:T(8,128)}) custom-call(s32[2]{0:T(128)S(1)} %pad_add_fusion.me_ref._, bf16[4,48,32,512]{3,2,1,0:T(8,128)(2,1)} %all-to-all-done.refs_0_, bf16[32,256,256]{2,1,0:T(8,128)(2,1)} %refs_1_.5, ...), custom_call_target="tpu_custom_call" | custom-call | flops 1 | bytes 1 | tf_op jit(solution)/shard_map/pallas_call | solution.py:100
  419.9 1.8 collective-permute-done.32.came_ref
  423.7 3.9 shard_map.122
  427.6 1.5 collective-permute-start.34
  429.1 25.4 %all-to-all-done.1.refs_0_ = bf16[4,16,32,512]{3,2,1,0:T(8,128)(2,1)} async-done(((bf16[4,16,32,512]{3,2,1,0:T(8,128)(2,1)}), bf16[4,16,32,512]{3,2,1,0:T(8,128)(2,1)}, u32[]{:S(2)}, u32[]{:S(2)}) %all-to-all-start.1) | async-done | bytes 2097184 | tf_op jit(solution)/shard_map/all_to_all | solution.py:628
  454.5 4.3 shard_map.118
  459.3 4.3 shard_map.119
  464.7 1.6 collective-permute-start.31
  467.4 3.2 shard_map.123.refs_0_
  (96 shorter events, 20.5 us)
Async XLA Ops:
  5.5 52.5 %collective-permute-start.1 = (bf16[32,16,512]{2,1,0:T(8,128)(2,1)S(1)}, bf16[32,16,512]{2,1,0:T(8,128)(2,1)S(1)}, u32[]{:S(2)}, u32[]{:S(2)}) collective-permute-start(bf16[32,16,512]{2,1,0:T(8,128)(2,1)S(1)} %get-tuple-element.77), channel_id=1, source_target_pairs={{0,8},{4,12},{8,0},{12,4},{1,9},{5,13},{9,1},{13,5},{2,10},{6,14},... | collective-permute-start | bytes 1572872 | tf_op jit(solution)/shard_map/ppermute | solution.py:96
  9.5 48.5 %collective-permute-start = (bf16[32,16,512]{2,1,0:T(8,128)(2,1)}, bf16[32,16,512]{2,1,0:T(8,128)(2,1)S(1)}, u32[]{:S(2)}, u32[]{:S(2)}) collective-permute-start(bf16[32,16,512]{2,1,0:T(8,128)(2,1)} %get-tuple-element.76), channel_id=1, source_target_pairs={{0,12},{4,8},{8,4},{12,0},{1,13},{5,9},{9,5},{13,1},{2,14},{6,10},... | collective-permute-start | bytes 1572872 | tf_op jit(solution)/shard_map/ppermute | solution.py:96
  10.9 47.2 %collective-permute-start.2 = (bf16[32,16,512]{2,1,0:T(8,128)(2,1)S(1)}, bf16[32,16,512]{2,1,0:T(8,128)(2,1)S(1)}, u32[]{:S(2)}, u32[]{:S(2)}) collective-permute-start(bf16[32,16,512]{2,1,0:T(8,128)(2,1)S(1)} %get-tuple-element.78), channel_id=1, source_target_pairs={{0,4},{4,0},{8,12},{12,8},{1,5},{5,1},{9,13},{13,9},{2,6},{6,2},{1... | collective-permute-start | bytes 1572872 | tf_op jit(solution)/shard_map/ppermute | solution.py:96
  11.1 9.1 %copy-start.16 = (bf16[8192]{0:T(1024)(128)(2,1)S(1)}, bf16[8192]{0:T(1024)(128)(2,1)}, u32[]{:S(2)}) copy-start(bf16[8192]{0:T(1024)(128)(2,1)} %param.10) | copy-start | bytes 49156
  58.0 1.9 copy-start.6
  58.0 4.4 copy-start.7
  58.0 4.4 copy-start.8
  58.1 36.7 %collective-permute-start.3 = (bf16[2,512,768]{2,1,0:T(8,128)(2,1)S(1)}, bf16[2,512,768]{2,1,0:T(8,128)(2,1)}, u32[]{:S(2)}, u32[]{:S(2)}) collective-permute-start(bf16[2,512,768]{2,1,0:T(8,128)(2,1)S(1)} %get-tuple-element.79), channel_id=1, source_target_pairs={{0,4},{4,0},{8,12},{12,8},{1,5},{5,1},{9,13},{13,9},{2,6},{6,2},{1... | collective-permute-start | bytes 4718600 | tf_op jit(solution)/shard_map/ppermute | solution.py:96
  59.9 60.4 %collective-permute-start.5 = (bf16[32,32,512]{2,1,0:T(8,128)(2,1)}, bf16[32,32,512]{2,1,0:T(8,128)(2,1)}, u32[]{:S(2)}, u32[]{:S(2)}) collective-permute-start(bf16[32,32,512]{2,1,0:T(8,128)(2,1)} %get-tuple-element.87), channel_id=1, source_target_pairs={{0,12},{4,8},{8,4},{12,0},{1,13},{5,9},{9,5},{13,1},{2,14},{6,10},... | collective-permute-start | bytes 3145736 | tf_op jit(solution)/shard_map/ppermute | solution.py:96
  74.1 77.7 %copy-start.18 = (bf16[32,32,512]{2,1,0:T(8,128)(2,1)S(1)}, bf16[32,32,512]{2,1,0:T(8,128)(2,1)}, u32[]{:S(2)}) copy-start(bf16[32,32,512]{2,1,0:T(8,128)(2,1)} %get-tuple-element.93) | copy-start | bytes 3145732
  74.1 77.7 %copy-start.17 = (bf16[32,32,512]{2,1,0:T(8,128)(2,1)S(1)}, bf16[32,32,512]{2,1,0:T(8,128)(2,1)}, u32[]{:S(2)}) copy-start(bf16[32,32,512]{2,1,0:T(8,128)(2,1)} %get-tuple-element.95) | copy-start | bytes 3145732
  94.8 129.4 %copy-start.19 = (bf16[32,16,512]{2,1,0:T(8,128)(2,1)S(1)}, bf16[32,16,512]{2,1,0:T(8,128)(2,1)}, u32[]{:S(2)}) copy-start(bf16[32,16,512]{2,1,0:T(8,128)(2,1)} %get-tuple-element.105) | copy-start | bytes 1572868
  98.9 52.9 %collective-permute-start.4 = (bf16[512,768]{1,0:T(8,128)(2,1)S(1)}, bf16[512,768]{1,0:T(8,128)(2,1)S(1)}, u32[]{:S(2)}, u32[]{:S(2)}) collective-permute-start(bf16[512,768]{1,0:T(8,128)(2,1)S(1)} %get-tuple-element.85), channel_id=1, source_target_pairs={{0,8},{4,12},{8,0},{12,4},{1,9},{5,13},{9,1},{13,5},{2,10},{6,14},... | collective-permute-start | bytes 2359304 | tf_op jit(solution)/shard_map/ppermute | solution.py:96
  151.8 58.9 %collective-permute-start.14 = (bf16[32,32,512]{2,1,0:T(8,128)(2,1)S(1)}, bf16[32,32,512]{2,1,0:T(8,128)(2,1)S(1)}, u32[]{:S(2)}, u32[]{:S(2)}) collective-permute-start(bf16[32,32,512]{2,1,0:T(8,128)(2,1)S(1)} %copy-done.18), channel_id=1, source_target_pairs={{0,8},{4,12},{8,0},{12,4},{1,9},{5,13},{9,1},{13,5},{2,10},{6,14},... | collective-permute-start | bytes 3145736 | tf_op jit(solution)/shard_map/ppermute | solution.py:96
  151.9 58.9 %collective-permute-start.15 = (bf16[32,32,512]{2,1,0:T(8,128)(2,1)S(1)}, bf16[32,32,512]{2,1,0:T(8,128)(2,1)S(1)}, u32[]{:S(2)}, u32[]{:S(2)}) collective-permute-start(bf16[32,32,512]{2,1,0:T(8,128)(2,1)S(1)} %copy-done.17), channel_id=1, source_target_pairs={{0,4},{4,0},{8,12},{12,8},{1,5},{5,1},{9,13},{13,9},{2,6},{6,2},{1... | collective-permute-start | bytes 3145736 | tf_op jit(solution)/shard_map/ppermute | solution.py:96
  157.0 9.3 %collective-permute-start.7 = (bf16[512,256]{1,0:T(8,128)(2,1)S(1)}, bf16[512,256]{1,0:T(8,128)(2,1)S(1)}, u32[]{:S(2)}, u32[]{:S(2)}) collective-permute-start(bf16[512,256]{1,0:T(8,128)(2,1)S(1)} %get-tuple-element.90.refs_0_), channel_id=1, source_target_pairs={{0,2},{1,3},{2,0},{3,1},{4,6},{5,7},{6,4},{7,5},{8,10},{9,11},{10,... | collective-permute-start | bytes 786440 | tf_op jit(solution)/shard_map/ppermute | solution.py:96
  158.5 7.8 %collective-permute-start.6 = (bf16[512,256]{1,0:T(8,128)(2,1)S(1)}, bf16[512,256]{1,0:T(8,128)(2,1)S(1)}, u32[]{:S(2)}, u32[]{:S(2)}) collective-permute-start(bf16[512,256]{1,0:T(8,128)(2,1)S(1)} %get-tuple-element.90.refs_0_), channel_id=1, source_target_pairs={{0,1},{1,0},{2,3},{3,2},{4,5},{5,4},{6,7},{7,6},{8,9},{9,8},{10,11... | collective-permute-start | bytes 786440 | tf_op jit(solution)/shard_map/ppermute | solution.py:96
  158.5 11.8 %collective-permute-start.10 = (bf16[512,256]{1,0:T(8,128)(2,1)S(1)}, bf16[512,256]{1,0:T(8,128)(2,1)S(1)}, u32[]{:S(2)}, u32[]{:S(2)}) collective-permute-start(bf16[512,256]{1,0:T(8,128)(2,1)S(1)} %get-tuple-element.91.refs_4_), channel_id=1, source_target_pairs={{0,2},{1,3},{2,0},{3,1},{4,6},{5,7},{6,4},{7,5},{8,10},{9,11},{10,... | collective-permute-start | bytes 786440 | tf_op jit(solution)/shard_map/ppermute | solution.py:96
  166.3 4.1 collective-permute-start.9
  166.3 4.1 collective-permute-start.8
  170.3 1.5 collective-permute-start.11
  179.8 30.6 %collective-permute-start.13 = (bf16[512,256]{1,0:T(8,128)(2,1)S(1)}, bf16[512,256]{1,0:T(8,128)(2,1)S(1)}, u32[]{:S(2)}, u32[]{:S(2)}) collective-permute-start(bf16[512,256]{1,0:T(8,128)(2,1)S(1)} %shard_map.109.own), channel_id=1, source_target_pairs={{0,8},{4,12},{8,0},{12,4},{1,9},{5,13},{9,1},{13,5},{2,10},{6,14},... | collective-permute-start | bytes 786440 | tf_op jit(solution)/shard_map/ppermute | solution.py:96
  181.1 29.6 %collective-permute-start.12 = (bf16[512,256]{1,0:T(8,128)(2,1)S(1)}, bf16[512,256]{1,0:T(8,128)(2,1)S(1)}, u32[]{:S(2)}, u32[]{:S(2)}) collective-permute-start(bf16[512,256]{1,0:T(8,128)(2,1)S(1)} %shard_map.109.own), channel_id=1, source_target_pairs={{0,4},{4,0},{8,12},{12,8},{1,5},{5,1},{9,13},{13,9},{2,6},{6,2},{1... | collective-permute-start | bytes 786440 | tf_op jit(solution)/shard_map/ppermute | solution.py:96
  210.7 39.4 %copy-start.4 = (bf16[32,32,512]{2,1,0:T(8,128)(2,1)}, bf16[32,32,512]{2,1,0:T(8,128)(2,1)S(1)}, u32[]{:S(2)}) copy-start(bf16[32,32,512]{2,1,0:T(8,128)(2,1)S(1)} %collective-permute-done.14.refs_6_) | copy-start | bytes 3145732
  210.7 39.4 %copy-start.5 = (bf16[32,32,512]{2,1,0:T(8,128)(2,1)}, bf16[32,32,512]{2,1,0:T(8,128)(2,1)S(1)}, u32[]{:S(2)}) copy-start(bf16[32,32,512]{2,1,0:T(8,128)(2,1)S(1)} %collective-permute-done.15.refs_5_) | copy-start | bytes 3145732
  210.7 13.5 %collective-permute-start.16 = (bf16[512,256]{1,0:T(8,128)(2,1)S(1)}, bf16[512,256]{1,0:T(8,128)(2,1)S(1)}, u32[]{:S(2)}, u32[]{:S(2)}) collective-permute-start(bf16[512,256]{1,0:T(8,128)(2,1)S(1)} %collective-permute-done.13.far), channel_id=1, source_target_pairs={{0,4},{4,0},{8,12},{12,8},{1,5},{5,1},{9,13},{13,9},{2,6},{6,2},{1... | collective-permute-start | bytes 786440 | tf_op jit(solution)/shard_map/ppermute | solution.py:96
  211.1 39.0 %collective-permute-start.18 = (bf16[32,16,512]{2,1,0:T(8,128)(2,1)S(1)}, bf16[32,16,512]{2,1,0:T(8,128)(2,1)S(1)}, u32[]{:S(2)}, u32[]{:S(2)}) collective-permute-start(bf16[32,16,512]{2,1,0:T(8,128)(2,1)S(1)} %get-tuple-element.103), channel_id=1, source_target_pairs={{0,8},{4,12},{8,0},{12,4},{1,9},{5,13},{9,1},{13,5},{2,10},{6,14},... | collective-permute-start | bytes 1572872 | tf_op jit(solution)/shard_map/ppermute | solution.py:96
  224.2 29.9 %collective-permute-start.17 = (bf16[32,16,512]{2,1,0:T(8,128)(2,1)S(1)}, bf16[32,16,512]{2,1,0:T(8,128)(2,1)S(1)}, u32[]{:S(2)}, u32[]{:S(2)}) collective-permute-start(bf16[32,16,512]{2,1,0:T(8,128)(2,1)S(1)} %get-tuple-element.101), channel_id=1, source_target_pairs={{0,4},{4,0},{8,12},{12,8},{1,5},{5,1},{9,13},{13,9},{2,6},{6,2},{1... | collective-permute-start | bytes 1572872 | tf_op jit(solution)/shard_map/ppermute | solution.py:96
  224.2 29.9 %collective-permute-start.19 = (bf16[32,16,512]{2,1,0:T(8,128)(2,1)S(1)}, bf16[32,16,512]{2,1,0:T(8,128)(2,1)S(1)}, u32[]{:S(2)}, u32[]{:S(2)}) collective-permute-start(bf16[32,16,512]{2,1,0:T(8,128)(2,1)S(1)} %copy-done.19), channel_id=1, source_target_pairs={{0,12},{4,8},{8,4},{12,0},{1,13},{5,9},{9,5},{13,1},{2,14},{6,10},... | collective-permute-start | bytes 1572872 | tf_op jit(solution)/shard_map/ppermute | solution.py:96
  250.1 4.0 copy-start.9
  255.1 146.1 %all-to-all-start = ((bf16[4,48,32,512]{3,2,1,0:T(8,128)(2,1)}), bf16[4,48,32,512]{3,2,1,0:T(8,128)(2,1)}, u32[]{:S(2)}, u32[]{:S(2)}) async-start(bf16[4,48,32,512]{3,2,1,0:T(8,128)(2,1)} %get-tuple-element.106), calls=%async_computation | async-start | bytes 12582912 | tf_op jit(solution)/shard_map/all_to_all | solution.py:628
  269.9 8.1 %collective-permute-start.23 = (bf16[16,64,256]{2,1,0:T(8,128)(2,1)S(1)}, bf16[16,64,256]{2,1,0:T(8,128)(2,1)S(1)}, u32[]{:S(2)}, u32[]{:S(2)}) collective-permute-start(bf16[16,64,256]{2,1,0:T(8,128)(2,1)S(1)} %get-tuple-element.114), channel_id=1, source_target_pairs={{0,1},{1,0},{2,3},{3,2},{4,5},{5,4},{6,7},{7,6},{8,9},{9,8},{10,11... | collective-permute-start | bytes 1572872 | tf_op jit(solution)/shard_map/ppermute | solution.py:96
  269.9 8.1 %collective-permute-start.24 = (bf16[16,64,256]{2,1,0:T(8,128)(2,1)S(1)}, bf16[16,64,256]{2,1,0:T(8,128)(2,1)S(1)}, u32[]{:S(2)}, u32[]{:S(2)}) collective-permute-start(bf16[16,64,256]{2,1,0:T(8,128)(2,1)S(1)} %get-tuple-element.115), channel_id=1, source_target_pairs={{0,1},{1,0},{2,3},{3,2},{4,5},{5,4},{6,7},{7,6},{8,9},{9,8},{10,11... | collective-permute-start | bytes 1572872 | tf_op jit(solution)/shard_map/ppermute | solution.py:96
  277.4 5.3 %collective-permute-start.20 = (bf16[16,64,256]{2,1,0:T(8,128)(2,1)S(1)}, bf16[16,64,256]{2,1,0:T(8,128)(2,1)S(1)}, u32[]{:S(2)}, u32[]{:S(2)}) collective-permute-start(bf16[16,64,256]{2,1,0:T(8,128)(2,1)S(1)} %get-tuple-element.109), channel_id=1, source_target_pairs={{0,1},{1,0},{2,3},{3,2},{4,5},{5,4},{6,7},{7,6},{8,9},{9,8},{10,11... | collective-permute-start | bytes 1572872 | tf_op jit(solution)/shard_map/ppermute | solution.py:96
  277.6 5.2 %collective-permute-start.21 = (bf16[16,64,256]{2,1,0:T(8,128)(2,1)S(1)}, bf16[16,64,256]{2,1,0:T(8,128)(2,1)S(1)}, u32[]{:S(2)}, u32[]{:S(2)}) collective-permute-start(bf16[16,64,256]{2,1,0:T(8,128)(2,1)S(1)} %get-tuple-element.110), channel_id=1, source_target_pairs={{0,1},{1,0},{2,3},{3,2},{4,5},{5,4},{6,7},{7,6},{8,9},{9,8},{10,11... | collective-permute-start | bytes 1572872 | tf_op jit(solution)/shard_map/ppermute | solution.py:96
  281.3 14.8 %collective-permute-start.25 = (bf16[16,64,256]{2,1,0:T(8,128)(2,1)S(1)}, bf16[16,64,256]{2,1,0:T(8,128)(2,1)S(1)}, u32[]{:S(2)}, u32[]{:S(2)}) collective-permute-start(bf16[16,64,256]{2,1,0:T(8,128)(2,1)S(1)} %get-tuple-element.117), channel_id=1, source_target_pairs={{0,2},{1,3},{2,0},{3,1},{4,6},{5,7},{6,4},{7,5},{8,10},{9,11},{10,... | collective-permute-start | bytes 1572872 | tf_op jit(solution)/shard_map/ppermute | solution.py:96
  286.0 20.4 %collective-permute-start.22 = (bf16[16,64,256]{2,1,0:T(8,128)(2,1)S(1)}, bf16[16,64,256]{2,1,0:T(8,128)(2,1)S(1)}, u32[]{:S(2)}, u32[]{:S(2)}) collective-permute-start(bf16[16,64,256]{2,1,0:T(8,128)(2,1)S(1)} %get-tuple-element.112), channel_id=1, source_target_pairs={{0,2},{1,3},{2,0},{3,1},{4,6},{5,7},{6,4},{7,5},{8,10},{9,11},{10,... | collective-permute-start | bytes 1572872 | tf_op jit(solution)/shard_map/ppermute | solution.py:96
  297.3 9.1 %copy-start.3 = (f32[16,64,256]{2,1,0:T(8,128)S(1)}, f32[16,64,256]{2,1,0:T(8,128)}, u32[]{:S(2)}) copy-start(f32[16,64,256]{2,1,0:T(8,128)} %get-tuple-element.111.mine_ref) | copy-start | bytes 3145732
  401.3 53.2 %all-to-all-start.1 = ((bf16[4,16,32,512]{3,2,1,0:T(8,128)(2,1)}), bf16[4,16,32,512]{3,2,1,0:T(8,128)(2,1)}, u32[]{:S(2)}, u32[]{:S(2)}) async-start(bf16[4,16,32,512]{3,2,1,0:T(8,128)(2,1)} %get-tuple-element.118), calls=%async_computation.1 | async-start | bytes 4194304 | tf_op jit(solution)/shard_map/all_to_all | solution.py:628
  419.4 2.3 collective-permute-start.32
  419.4 3.4 collective-permute-start.33
  427.6 39.8 %collective-permute-start.34 = (bf16[24,64,256]{2,1,0:T(8,128)(2,1)S(1)}, bf16[24,64,256]{2,1,0:T(8,128)(2,1)S(1)}, u32[]{:S(2)}, u32[]{:S(2)}) collective-permute-start(bf16[24,64,256]{2,1,0:T(8,128)(2,1)S(1)} %get-tuple-element.136), channel_id=1, source_target_pairs={{0,2},{1,3},{2,0},{3,1},{4,6},{5,7},{6,4},{7,5},{8,10},{9,11},{10,... | collective-permute-start | bytes 2359304 | tf_op jit(solution)/shard_map/ppermute | solution.py:96
  458.8 5.3 %collective-permute-start.29 = (bf16[4,64,256]{2,1,0:T(8,128)(2,1)S(1)}, bf16[4,64,256]{2,1,0:T(8,128)(2,1)S(1)}, u32[]{:S(2)}, u32[]{:S(2)}) collective-permute-start(bf16[4,64,256]{2,1,0:T(8,128)(2,1)S(1)} %get-tuple-element.128), channel_id=1, source_target_pairs={{0,1},{1,0},{2,3},{3,2},{4,5},{5,4},{6,7},{7,6},{8,9},{9,8},{10,11... | collective-permute-start | bytes 393224 | tf_op jit(solution)/shard_map/ppermute | solution.py:96
  458.8 5.3 %collective-permute-start.30 = (bf16[4,64,256]{2,1,0:T(8,128)(2,1)S(1)}, bf16[4,64,256]{2,1,0:T(8,128)(2,1)S(1)}, u32[]{:S(2)}, u32[]{:S(2)}) collective-permute-start(bf16[4,64,256]{2,1,0:T(8,128)(2,1)S(1)} %get-tuple-element.129), channel_id=1, source_target_pairs={{0,1},{1,0},{2,3},{3,2},{4,5},{5,4},{6,7},{7,6},{8,9},{9,8},{10,11... | collective-permute-start | bytes 393224 | tf_op jit(solution)/shard_map/ppermute | solution.py:96
  463.5 2.7 collective-permute-start.26
  463.6 2.7 collective-permute-start.27
  464.7 6.4 %collective-permute-start.31 = (bf16[4,64,256]{2,1,0:T(8,128)(2,1)S(1)}, bf16[4,64,256]{2,1,0:T(8,128)(2,1)S(1)}, u32[]{:S(2)}, u32[]{:S(2)}) collective-permute-start(bf16[4,64,256]{2,1,0:T(8,128)(2,1)S(1)} %get-tuple-element.131), channel_id=1, source_target_pairs={{0,2},{1,3},{2,0},{3,1},{4,6},{5,7},{6,4},{7,5},{8,10},{9,11},{10,... | collective-permute-start | bytes 393224 | tf_op jit(solution)/shard_map/ppermute | solution.py:96
  466.8 6.1 %collective-permute-start.28 = (bf16[4,64,256]{2,1,0:T(8,128)(2,1)S(1)}, bf16[4,64,256]{2,1,0:T(8,128)(2,1)S(1)}, u32[]{:S(2)}, u32[]{:S(2)}) collective-permute-start(bf16[4,64,256]{2,1,0:T(8,128)(2,1)S(1)} %get-tuple-element.126), channel_id=1, source_target_pairs={{0,2},{1,3},{2,0},{3,1},{4,6},{5,7},{6,4},{7,5},{8,10},{9,11},{10,... | collective-permute-start | bytes 393224 | tf_op jit(solution)/shard_map/ppermute | solution.py:96
  (9 other events, 9.6 us)

commit v11 on v10

--- a/solution.py
+++ b/solution.py
@@ -603,7 +603,7 @@
     w_first_t = jnp.swapaxes(after(w_first, send), 1, 2)
     mine, other = add_call(me, keep, after(came, sends[2][0], w_first_t))
     last = flip(other, "gene", 2)
-    queries, *own = split_call(me, mine, after(last, beside_sum))
+    queries, *own = split_call(me, mine, after(last, beside_sum, begin(2, 1, other)))
     across = [flip(piece, "cell", 2) for piece in own]
     beside = [flip(piece, "cell", 1) for piece in own]
     corner = [flip(piece, "cell", 1) for piece in across]
@@ -618,7 +618,6 @@
         me, matrix, (attended, near, far, rest), w_out, masked, w_first_t, chunks
     )
     begin(2, 3, rest)
-    begin(2, 1, rest)
 
     got = []
 
@@ -629,7 +628,7 @@
         else:
             got.append([pieces[0]] + [flip(pieces[bits], "gene", bits) for bits in (1, 2, 3)])
 
-    launch(0, *back[2][1:])
+    launch(0, *back[2][2:])
     denoised, shares = None, [None, None]
     back = sum(back, [])
 
@@ -648,11 +647,12 @@
         if t + 1 < len(chunks):
             launch(t + 1, *got[t], pin)
         start, count = (n * blocks // deep for n in (sum(n for n, _ in chunks[:t]), chunks[t][0]))
+        pieces = got[t] if t + 1 < len(chunks) else after(got[t], pin)
         calls = 2 if t == len(chunks) - 1 else 1
         count //= calls
         for low in range(0, calls * count, count):
             denoised, *send, keep = second_call(
-                me, got[t], w_second, cotangent, hidden, denoised, start + low, low, count
+                me, pieces, w_second, cotangent, hidden, denoised, start + low, low, count
             )
             sum_cells(1, start + low, send, keep)
         pin = shares[1]

time: 475 us -> 475 us (level)
    all_to_all x2, waiting for transfers between devices: 119 us -> 97.2 us  [launch(): lax.all_to_all(pieces[0], 'gene', split_axis=0, concat_axis=0, tiled=True)]
    ppermute x35, waiting for transfers between devices: 146 us -> 163 us  [flip(): return lax.ppermute(value, axis, pairs)]
  transfers between devices with their start and end apart: 37 -> 37, of which waited for: 18 -> 18; matrix products, arithmetic and copies ran while one was open for 1% -> 1% of each run, Pallas kernels for 31% -> 30%
where the time goes in v11:
time: 475 us
  waiting for transfers between devices  260 us (55%)
  Pallas kernels  151 us (32%)
  starting transfers between devices  49.2 us (10%)
  local copies, waits for them, and re-layouts  13.4 us (3%)
    ppermute x35, waiting for transfers between devices, flip(): return lax.ppermute(value, axis, pairs)  163 us
    pallas_call x23, Pallas kernels, call(): pl.pallas_call(body, out_shape=outs, grid_spec=pltpu.PrefetchScalarGridSp...  151 us
    all_to_all x2, waiting for transfers between devices, launch(): lax.all_to_all(pieces[0], 'gene', split_axis=0, concat_axis=0, tiled=True)  97.2 us
    ppermute x35, starting transfers between devices, flip(): return lax.ppermute(value, axis, pairs)  33.8 us
    all_to_all x2, starting transfers between devices, launch(): lax.all_to_all(pieces[0], 'gene', split_axis=0, concat_axis=0, tiled=True)  15.4 us
  transfers between devices with their start and end apart: 37, of which 18 were waited for; matrix products, arithmetic and copies ran while one was open for 1% of the time, Pallas kernels for 30%

profile of v11, /device:TPU:0, one launch (start us, length us, event | category | flops | bytes accessed | tf_op | source)
XLA Modules:
  0.0 474.5 jit_solution(362395901815931247)
XLA Ops:
  1.0 4.4 shard_map.103
  5.5 4.0 collective-permute-start.1
  11.1 8.1 %shard_map.104 = (bf16[32,32,512]{2,1,0:T(8,128)(2,1)S(1)}, bf16[32,32,512]{2,1,0:T(8,128)(2,1)}, bf16[32,32,512]{2,1,0:T(8,128)(2,1)}, bf16[32,32,512]{2,1,0:T(8,128)(2,1)}) custom-call(s32[2]{0:T(128)S(1)} %pad_add_fusion.me_ref._, bf16[256,256]{1,0:T(8,128)(2,1)S(1)} %fusion.turn_ref, bf16[32,256,256]{2,1,0:T(8,128)(2,1)} %refs_1_.5, ...), custom_call_target="tpu_custom_call" | custom-call | flops 1 | bytes 1 | tf_op jit(solution)/shard_map/pallas_call | solution.py:100
  20.2 37.8 %shard_map.105 = (bf16[512,8192]{1,0:T(8,128)(2,1)}, bf16[2,512,768]{2,1,0:T(8,128)(2,1)S(1)}, f32[2,512,768]{2,1,0:T(8,128)}) custom-call(s32[2]{0:T(128)S(1)} %pad_add_fusion.me_ref._, bf16[512,8192]{1,0:T(8,128)(2,1)} %value_ref, s32[512,8192]{1,0:T(8,128)} %mask_ref.1, bf16[1,8192]{1,0:T(2,128)(2,1)S(1)} %reshape.9.fill_ref, bf16[8192,3072]{1,0:T(8,128)(2,1)} %weight_ref.1), custom_call_target="tpu_custom_call" | custom-call | flops 1 | bytes 1 | tf_op jit(solution)/shard_map/pallas_call | solution.py:100
  58.1 1.9 collective-permute-start.3
  59.9 2.5 collective-permute-start.5
  62.4 4.5 shard_map.106
  67.7 6.4 %copy.16 = bf16[32,256,256]{1,2,0:T(8,128)(2,1)} copy(bf16[32,256,256]{2,1,0:T(8,128)(2,1)} %param.13) | data formatting | bytes 8388608 | tf_op jit(solution)/shard_map/optimization_barrier | solution.py:91
  74.2 20.6 %collective-permute-done.3.came_ref = bf16[2,512,768]{2,1,0:T(8,128)(2,1)} collective-permute-done((bf16[2,512,768]{2,1,0:T(8,128)(2,1)S(1)}, bf16[2,512,768]{2,1,0:T(8,128)(2,1)}, u32[]{:S(2)}, u32[]{:S(2)}) %collective-permute-start.3) | collective-permute-done | bytes 1572896 | tf_op jit(solution)/shard_map/ppermute | solution.py:96
  94.8 4.2 shard_map.107
  99.0 3.6 collective-permute-start.4
  102.6 17.9 %collective-permute-done.5.refs_7_ = bf16[32,32,512]{2,1,0:T(8,128)(2,1)} collective-permute-done((bf16[32,32,512]{2,1,0:T(8,128)(2,1)}, bf16[32,32,512]{2,1,0:T(8,128)(2,1)}, u32[]{:S(2)}, u32[]{:S(2)}) %collective-permute-start.5) | collective-permute-done | bytes 1048608 | tf_op jit(solution)/shard_map/ppermute | solution.py:96
  120.4 31.5 %collective-permute-done.4.came_ref = bf16[512,768]{1,0:T(8,128)(2,1)S(1)} collective-permute-done((bf16[512,768]{1,0:T(8,128)(2,1)S(1)}, bf16[512,768]{1,0:T(8,128)(2,1)S(1)}, u32[]{:S(2)}, u32[]{:S(2)}) %collective-permute-start.4) | collective-permute-done | bytes 786464 | tf_op jit(solution)/shard_map/ppermute | solution.py:96
  151.9 1.9 collective-permute-start.16
  153.8 3.2 shard_map.108
  157.0 1.6 collective-permute-start.8
  159.1 7.2 %collective-permute-done.8.refs_2_ = bf16[512,256]{1,0:T(8,128)(2,1)S(1)} collective-permute-done((bf16[512,256]{1,0:T(8,128)(2,1)S(1)}, bf16[512,256]{1,0:T(8,128)(2,1)S(1)}, u32[]{:S(2)}, u32[]{:S(2)}) %collective-permute-start.8) | collective-permute-done | bytes 262176 | tf_op jit(solution)/shard_map/ppermute | solution.py:96
  166.8 3.5 collective-permute-done.11.refs_6_
  170.4 1.5 collective-permute-done.12.refs_7_
  172.6 7.2 %shard_map.109.own = bf16[512,256]{1,0:T(8,128)(2,1)S(1)} custom-call(s32[2]{0:T(128)S(1)} %pad_add_fusion.me_ref._, bf16[512,256]{1,0:T(8,128)(2,1)S(1)} %get-tuple-element.92.query_ref, bf16[512,256]{1,0:T(8,128)(2,1)S(1)} %get-tuple-element.93.refs_0_, bf16[512,256]{1,0:T(8,128)(2,1)S(1)} %collective-permute-done.7.refs_1_, ...), custom_call_target="tpu_custom_call" | custom-call | flops 1 | bytes 1 | tf_op jit(solution)/shard_map/pallas_call | solution.py:100
  181.2 1.7 collective-permute-start.13
  183.0 27.5 %collective-permute-done.14.far = bf16[512,256]{1,0:T(8,128)(2,1)S(1)} collective-permute-done((bf16[512,256]{1,0:T(8,128)(2,1)S(1)}, bf16[512,256]{1,0:T(8,128)(2,1)S(1)}, u32[]{:S(2)}, u32[]{:S(2)}) %collective-permute-start.14) | collective-permute-done | bytes 262176 | tf_op jit(solution)/shard_map/ppermute | solution.py:96
  211.1 2.5 collective-permute-start.18
  213.7 10.6 %collective-permute-done.17.rest = bf16[512,256]{1,0:T(8,128)(2,1)S(1)} collective-permute-done((bf16[512,256]{1,0:T(8,128)(2,1)S(1)}, bf16[512,256]{1,0:T(8,128)(2,1)S(1)}, u32[]{:S(2)}, u32[]{:S(2)}) %collective-permute-start.17) | collective-permute-done | bytes 262176 | tf_op jit(solution)/shard_map/ppermute | solution.py:96
  225.6 24.5 %shard_map.110 = (bf16[512,8192]{1,0:T(8,128)(2,1)}, bf16[4,48,32,512]{3,2,1,0:T(8,128)(2,1)}, bf16[4,16,32,512]{3,2,1,0:T(8,128)(2,1)}) custom-call(s32[2]{0:T(128)S(1)} %pad_add_fusion.me_ref._, bf16[256,256]{1,0:T(8,128)(2,1)S(1)} %fusion.turn_ref, bf16[512,256]{1,0:T(8,128)(2,1)S(1)} %shard_map.109.own, ...), custom_call_target="tpu_custom_call" | custom-call | flops 1 | bytes 1 | tf_op jit(solution)/shard_map/pallas_call | solution.py:100
  251.1 11.8 %all-to-all-start = ((bf16[4,48,32,512]{3,2,1,0:T(8,128)(2,1)}), bf16[4,48,32,512]{3,2,1,0:T(8,128)(2,1)}, u32[]{:S(2)}, u32[]{:S(2)}) async-start(bf16[4,48,32,512]{3,2,1,0:T(8,128)(2,1)} %get-tuple-element.107), calls=%async_computation | async-start | bytes 12582912 | tf_op jit(solution)/shard_map/all_to_all | solution.py:627
  262.9 7.0 %shard_map.113 = (bf16[16,64,256]{2,1,0:T(8,128)(2,1)S(1)}, bf16[16,64,256]{2,1,0:T(8,128)(2,1)S(1)}, f32[2,16,64,256]{3,2,1,0:T(8,128)}) custom-call(s32[2]{0:T(128)S(1)} %pad_add_fusion.me_ref._, bf16[32,16,512]{2,1,0:T(8,128)(2,1)S(1)} %get-tuple-element.71.refs_0_, bf16[32,16,512]{2,1,0:T(8,128)(2,1)} %copy-done.9, bf16[32,16,512]{2,1,0:T(8,128)(2,1)} %copy-done.7, ...), custom_call_target="tpu_custom_call" | custom-call | flops 1 | bytes 1 | tf_op jit(solution)/shard_map/pallas_call | solution.py:100
  270.4 7.0 %shard_map.111 = (bf16[16,64,256]{2,1,0:T(8,128)(2,1)S(1)}, bf16[16,64,256]{2,1,0:T(8,128)(2,1)S(1)}, f32[2,16,64,256]{3,2,1,0:T(8,128)}) custom-call(s32[2]{0:T(128)S(1)} %pad_add_fusion.me_ref._, bf16[32,16,512]{2,1,0:T(8,128)(2,1)S(1)} %get-tuple-element.71.refs_0_, bf16[32,16,512]{2,1,0:T(8,128)(2,1)} %copy-done.9, bf16[32,16,512]{2,1,0:T(8,128)(2,1)} %copy-done.7, ...), custom_call_target="tpu_custom_call" | custom-call | flops 1 | bytes 1 | tf_op jit(solution)/shard_map/pallas_call | solution.py:100
  278.0 3.3 shard_map.114
  281.2 1.5 collective-permute-start.25
  282.7 3.2 shard_map.112
  286.5 9.5 %collective-permute-done.25.came_ref = bf16[16,64,256]{2,1,0:T(8,128)(2,1)S(1)} collective-permute-done((bf16[16,64,256]{2,1,0:T(8,128)(2,1)S(1)}, bf16[16,64,256]{2,1,0:T(8,128)(2,1)S(1)}, u32[]{:S(2)}, u32[]{:S(2)}) %collective-permute-start.25) | collective-permute-done | bytes 524320 | tf_op jit(solution)/shard_map/ppermute | solution.py:96
  297.3 1.6 shard_map.115.refs_0_
  298.8 7.5 %collective-permute-done.22.came_ref = bf16[16,64,256]{2,1,0:T(8,128)(2,1)S(1)} collective-permute-done((bf16[16,64,256]{2,1,0:T(8,128)(2,1)S(1)}, bf16[16,64,256]{2,1,0:T(8,128)(2,1)S(1)}, u32[]{:S(2)}, u32[]{:S(2)}) %collective-permute-start.22) | collective-permute-done | bytes 524320 | tf_op jit(solution)/shard_map/ppermute | solution.py:96
  306.4 1.6 shard_map.116
  308.0 93.3 %all-to-all-done.refs_0_ = bf16[4,48,32,512]{3,2,1,0:T(8,128)(2,1)} async-done(((bf16[4,48,32,512]{3,2,1,0:T(8,128)(2,1)}), bf16[4,48,32,512]{3,2,1,0:T(8,128)(2,1)}, u32[]{:S(2)}, u32[]{:S(2)}) %all-to-all-start) | async-done | bytes 6291488 | tf_op jit(solution)/shard_map/all_to_all | solution.py:627
  401.3 3.6 all-to-all-start.1
  404.9 13.6 %shard_map.117 = (bf16[512,8192]{1,0:T(8,128)(2,1)}, bf16[24,64,256]{2,1,0:T(8,128)(2,1)S(1)}, bf16[24,64,256]{2,1,0:T(8,128)(2,1)S(1)}, f32[2,24,64,256]{3,2,1,0:T(8,128)}) custom-call(s32[2]{0:T(128)S(1)} %pad_add_fusion.me_ref._, bf16[4,48,32,512]{3,2,1,0:T(8,128)(2,1)} %all-to-all-done.refs_0_, bf16[32,256,256]{2,1,0:T(8,128)(2,1)} %refs_1_.5, ...), custom_call_target="tpu_custom_call" | custom-call | flops 1 | bytes 1 | tf_op jit(solution)/shard_map/pallas_call | solution.py:100
  419.0 1.8 collective-permute-done.26.came_ref
  422.8 3.9 shard_map.118
  426.7 1.5 collective-permute-start.28
  428.2 18.1 %collective-permute-done.28.came_ref = bf16[24,64,256]{2,1,0:T(8,128)(2,1)S(1)} collective-permute-done((bf16[24,64,256]{2,1,0:T(8,128)(2,1)S(1)}, bf16[24,64,256]{2,1,0:T(8,128)(2,1)S(1)}, u32[]{:S(2)}, u32[]{:S(2)}) %collective-permute-start.28) | collective-permute-done | bytes 786464 | tf_op jit(solution)/shard_map/ppermute | solution.py:96
  446.3 3.2 shard_map.119.refs_0_
  449.5 4.0 all-to-all-done.1.refs_0_
  454.8 4.3 shard_map.120
  459.6 4.3 shard_map.121
  465.0 1.6 collective-permute-start.34
  467.8 3.6 collective-permute-done.34.came_ref
  (98 shorter events, 22.7 us)
Async XLA Ops:
  5.5 52.5 %collective-permute-start.1 = (bf16[32,16,512]{2,1,0:T(8,128)(2,1)S(1)}, bf16[32,16,512]{2,1,0:T(8,128)(2,1)S(1)}, u32[]{:S(2)}, u32[]{:S(2)}) collective-permute-start(bf16[32,16,512]{2,1,0:T(8,128)(2,1)S(1)} %get-tuple-element.78), channel_id=1, source_target_pairs={{0,8},{4,12},{8,0},{12,4},{1,9},{5,13},{9,1},{13,5},{2,10},{6,14},... | collective-permute-start | bytes 1572872 | tf_op jit(solution)/shard_map/ppermute | solution.py:96
  9.5 48.5 %collective-permute-start = (bf16[32,16,512]{2,1,0:T(8,128)(2,1)}, bf16[32,16,512]{2,1,0:T(8,128)(2,1)S(1)}, u32[]{:S(2)}, u32[]{:S(2)}) collective-permute-start(bf16[32,16,512]{2,1,0:T(8,128)(2,1)} %get-tuple-element.77), channel_id=1, source_target_pairs={{0,12},{4,8},{8,4},{12,0},{1,13},{5,9},{9,5},{13,1},{2,14},{6,10},... | collective-permute-start | bytes 1572872 | tf_op jit(solution)/shard_map/ppermute | solution.py:96
  10.9 47.2 %collective-permute-start.2 = (bf16[32,16,512]{2,1,0:T(8,128)(2,1)S(1)}, bf16[32,16,512]{2,1,0:T(8,128)(2,1)S(1)}, u32[]{:S(2)}, u32[]{:S(2)}) collective-permute-start(bf16[32,16,512]{2,1,0:T(8,128)(2,1)S(1)} %get-tuple-element.79), channel_id=1, source_target_pairs={{0,4},{4,0},{8,12},{12,8},{1,5},{5,1},{9,13},{13,9},{2,6},{6,2},{1... | collective-permute-start | bytes 1572872 | tf_op jit(solution)/shard_map/ppermute | solution.py:96
  11.1 9.1 %copy-start.17 = (bf16[8192]{0:T(1024)(128)(2,1)S(1)}, bf16[8192]{0:T(1024)(128)(2,1)}, u32[]{:S(2)}) copy-start(bf16[8192]{0:T(1024)(128)(2,1)} %param.10) | copy-start | bytes 49156
  58.0 1.9 copy-start.7
  58.0 4.4 copy-start.8
  58.1 4.4 copy-start.9
  58.1 36.7 %collective-permute-start.3 = (bf16[2,512,768]{2,1,0:T(8,128)(2,1)S(1)}, bf16[2,512,768]{2,1,0:T(8,128)(2,1)}, u32[]{:S(2)}, u32[]{:S(2)}) collective-permute-start(bf16[2,512,768]{2,1,0:T(8,128)(2,1)S(1)} %get-tuple-element.80), channel_id=1, source_target_pairs={{0,4},{4,0},{8,12},{12,8},{1,5},{5,1},{9,13},{13,9},{2,6},{6,2},{1... | collective-permute-start | bytes 4718600 | tf_op jit(solution)/shard_map/ppermute | solution.py:96
  59.9 60.5 %collective-permute-start.5 = (bf16[32,32,512]{2,1,0:T(8,128)(2,1)}, bf16[32,32,512]{2,1,0:T(8,128)(2,1)}, u32[]{:S(2)}, u32[]{:S(2)}) collective-permute-start(bf16[32,32,512]{2,1,0:T(8,128)(2,1)} %get-tuple-element.88), channel_id=1, source_target_pairs={{0,12},{4,8},{8,4},{12,0},{1,13},{5,9},{9,5},{13,1},{2,14},{6,10},... | collective-permute-start | bytes 3145736 | tf_op jit(solution)/shard_map/ppermute | solution.py:96
  74.2 77.8 %copy-start.19 = (bf16[32,32,512]{2,1,0:T(8,128)(2,1)S(1)}, bf16[32,32,512]{2,1,0:T(8,128)(2,1)}, u32[]{:S(2)}) copy-start(bf16[32,32,512]{2,1,0:T(8,128)(2,1)} %get-tuple-element.96) | copy-start | bytes 3145732
  74.2 77.8 %copy-start.18 = (bf16[32,32,512]{2,1,0:T(8,128)(2,1)S(1)}, bf16[32,32,512]{2,1,0:T(8,128)(2,1)}, u32[]{:S(2)}) copy-start(bf16[32,32,512]{2,1,0:T(8,128)(2,1)} %get-tuple-element.98) | copy-start | bytes 3145732
  94.8 129.5 %copy-start.20 = (bf16[32,16,512]{2,1,0:T(8,128)(2,1)S(1)}, bf16[32,16,512]{2,1,0:T(8,128)(2,1)}, u32[]{:S(2)}) copy-start(bf16[32,16,512]{2,1,0:T(8,128)(2,1)} %get-tuple-element.106) | copy-start | bytes 1572868
  99.0 52.9 %collective-permute-start.4 = (bf16[512,768]{1,0:T(8,128)(2,1)S(1)}, bf16[512,768]{1,0:T(8,128)(2,1)S(1)}, u32[]{:S(2)}, u32[]{:S(2)}) collective-permute-start(bf16[512,768]{1,0:T(8,128)(2,1)S(1)} %get-tuple-element.86), channel_id=1, source_target_pairs={{0,8},{4,12},{8,0},{12,4},{1,9},{5,13},{9,1},{13,5},{2,10},{6,14},... | collective-permute-start | bytes 2359304 | tf_op jit(solution)/shard_map/ppermute | solution.py:96
  102.6 51.3 %collective-permute-start.6 = (bf16[32,16,512]{2,1,0:T(8,128)(2,1)S(1)}, bf16[32,16,512]{2,1,0:T(8,128)(2,1)S(1)}, u32[]{:S(2)}, u32[]{:S(2)}) collective-permute-start(bf16[32,16,512]{2,1,0:T(8,128)(2,1)S(1)} %get-tuple-element.90), channel_id=1, source_target_pairs={{0,4},{4,0},{8,12},{12,8},{1,5},{5,1},{9,13},{13,9},{2,6},{6,2},{1... | collective-permute-start | bytes 1572872 | tf_op jit(solution)/shard_map/ppermute | solution.py:96
  151.9 58.9 %collective-permute-start.15 = (bf16[32,32,512]{2,1,0:T(8,128)(2,1)S(1)}, bf16[32,32,512]{2,1,0:T(8,128)(2,1)S(1)}, u32[]{:S(2)}, u32[]{:S(2)}) collective-permute-start(bf16[32,32,512]{2,1,0:T(8,128)(2,1)S(1)} %copy-done.19), channel_id=1, source_target_pairs={{0,8},{4,12},{8,0},{12,4},{1,9},{5,13},{9,1},{13,5},{2,10},{6,14},... | collective-permute-start | bytes 3145736 | tf_op jit(solution)/shard_map/ppermute | solution.py:96
  151.9 58.9 %collective-permute-start.16 = (bf16[32,32,512]{2,1,0:T(8,128)(2,1)S(1)}, bf16[32,32,512]{2,1,0:T(8,128)(2,1)S(1)}, u32[]{:S(2)}, u32[]{:S(2)}) collective-permute-start(bf16[32,32,512]{2,1,0:T(8,128)(2,1)S(1)} %copy-done.18), channel_id=1, source_target_pairs={{0,4},{4,0},{8,12},{12,8},{1,5},{5,1},{9,13},{13,9},{2,6},{6,2},{1... | collective-permute-start | bytes 3145736 | tf_op jit(solution)/shard_map/ppermute | solution.py:96
  153.8 96.3 %copy-start.10 = (bf16[32,16,512]{2,1,0:T(8,128)(2,1)}, bf16[32,16,512]{2,1,0:T(8,128)(2,1)S(1)}, u32[]{:S(2)}) copy-start(bf16[32,16,512]{2,1,0:T(8,128)(2,1)S(1)} %collective-permute-done.6.refs_9_) | copy-start | bytes 1572868
  157.0 9.3 %collective-permute-start.8 = (bf16[512,256]{1,0:T(8,128)(2,1)S(1)}, bf16[512,256]{1,0:T(8,128)(2,1)S(1)}, u32[]{:S(2)}, u32[]{:S(2)}) collective-permute-start(bf16[512,256]{1,0:T(8,128)(2,1)S(1)} %get-tuple-element.93.refs_0_), channel_id=1, source_target_pairs={{0,2},{1,3},{2,0},{3,1},{4,6},{5,7},{6,4},{7,5},{8,10},{9,11},{10,... | collective-permute-start | bytes 786440 | tf_op jit(solution)/shard_map/ppermute | solution.py:96
  158.6 7.8 %collective-permute-start.7 = (bf16[512,256]{1,0:T(8,128)(2,1)S(1)}, bf16[512,256]{1,0:T(8,128)(2,1)S(1)}, u32[]{:S(2)}, u32[]{:S(2)}) collective-permute-start(bf16[512,256]{1,0:T(8,128)(2,1)S(1)} %get-tuple-element.93.refs_0_), channel_id=1, source_target_pairs={{0,1},{1,0},{2,3},{3,2},{4,5},{5,4},{6,7},{7,6},{8,9},{9,8},{10,11... | collective-permute-start | bytes 786440 | tf_op jit(solution)/shard_map/ppermute | solution.py:96
  158.6 11.8 %collective-permute-start.11 = (bf16[512,256]{1,0:T(8,128)(2,1)S(1)}, bf16[512,256]{1,0:T(8,128)(2,1)S(1)}, u32[]{:S(2)}, u32[]{:S(2)}) collective-permute-start(bf16[512,256]{1,0:T(8,128)(2,1)S(1)} %get-tuple-element.94.refs_4_), channel_id=1, source_target_pairs={{0,2},{1,3},{2,0},{3,1},{4,6},{5,7},{6,4},{7,5},{8,10},{9,11},{10,... | collective-permute-start | bytes 786440 | tf_op jit(solution)/shard_map/ppermute | solution.py:96
  166.3 4.1 collective-permute-start.10
  166.3 4.1 collective-permute-start.9
  170.4 1.5 collective-permute-start.12
  179.9 30.6 %collective-permute-start.14 = (bf16[512,256]{1,0:T(8,128)(2,1)S(1)}, bf16[512,256]{1,0:T(8,128)(2,1)S(1)}, u32[]{:S(2)}, u32[]{:S(2)}) collective-permute-start(bf16[512,256]{1,0:T(8,128)(2,1)S(1)} %shard_map.109.own), channel_id=1, source_target_pairs={{0,8},{4,12},{8,0},{12,4},{1,9},{5,13},{9,1},{13,5},{2,10},{6,14},... | collective-permute-start | bytes 786440 | tf_op jit(solution)/shard_map/ppermute | solution.py:96
  181.2 29.5 %collective-permute-start.13 = (bf16[512,256]{1,0:T(8,128)(2,1)S(1)}, bf16[512,256]{1,0:T(8,128)(2,1)S(1)}, u32[]{:S(2)}, u32[]{:S(2)}) collective-permute-start(bf16[512,256]{1,0:T(8,128)(2,1)S(1)} %shard_map.109.own), channel_id=1, source_target_pairs={{0,4},{4,0},{8,12},{12,8},{1,5},{5,1},{9,13},{13,9},{2,6},{6,2},{1... | collective-permute-start | bytes 786440 | tf_op jit(solution)/shard_map/ppermute | solution.py:96
  210.8 39.3 %copy-start.5 = (bf16[32,32,512]{2,1,0:T(8,128)(2,1)}, bf16[32,32,512]{2,1,0:T(8,128)(2,1)S(1)}, u32[]{:S(2)}) copy-start(bf16[32,32,512]{2,1,0:T(8,128)(2,1)S(1)} %collective-permute-done.15.refs_6_) | copy-start | bytes 3145732
  210.8 39.3 %copy-start.6 = (bf16[32,32,512]{2,1,0:T(8,128)(2,1)}, bf16[32,32,512]{2,1,0:T(8,128)(2,1)S(1)}, u32[]{:S(2)}) copy-start(bf16[32,32,512]{2,1,0:T(8,128)(2,1)S(1)} %collective-permute-done.16.refs_5_) | copy-start | bytes 3145732
  210.8 13.5 %collective-permute-start.17 = (bf16[512,256]{1,0:T(8,128)(2,1)S(1)}, bf16[512,256]{1,0:T(8,128)(2,1)S(1)}, u32[]{:S(2)}, u32[]{:S(2)}) collective-permute-start(bf16[512,256]{1,0:T(8,128)(2,1)S(1)} %collective-permute-done.14.far), channel_id=1, source_target_pairs={{0,4},{4,0},{8,12},{12,8},{1,5},{5,1},{9,13},{13,9},{2,6},{6,2},{1... | collective-permute-start | bytes 786440 | tf_op jit(solution)/shard_map/ppermute | solution.py:96
  211.1 39.0 %collective-permute-start.18 = (bf16[32,16,512]{2,1,0:T(8,128)(2,1)S(1)}, bf16[32,16,512]{2,1,0:T(8,128)(2,1)S(1)}, u32[]{:S(2)}, u32[]{:S(2)}) collective-permute-start(bf16[32,16,512]{2,1,0:T(8,128)(2,1)S(1)} %get-tuple-element.104), channel_id=1, source_target_pairs={{0,8},{4,12},{8,0},{12,4},{1,9},{5,13},{9,1},{13,5},{2,10},{6,14},... | collective-permute-start | bytes 1572872 | tf_op jit(solution)/shard_map/ppermute | solution.py:96
  224.3 25.9 %collective-permute-start.19 = (bf16[32,16,512]{2,1,0:T(8,128)(2,1)S(1)}, bf16[32,16,512]{2,1,0:T(8,128)(2,1)S(1)}, u32[]{:S(2)}, u32[]{:S(2)}) collective-permute-start(bf16[32,16,512]{2,1,0:T(8,128)(2,1)S(1)} %copy-done.20), channel_id=1, source_target_pairs={{0,12},{4,8},{8,4},{12,0},{1,13},{5,9},{9,5},{13,1},{2,14},{6,10},... | collective-permute-start | bytes 1572872 | tf_op jit(solution)/shard_map/ppermute | solution.py:96
  251.1 150.2 %all-to-all-start = ((bf16[4,48,32,512]{3,2,1,0:T(8,128)(2,1)}), bf16[4,48,32,512]{3,2,1,0:T(8,128)(2,1)}, u32[]{:S(2)}, u32[]{:S(2)}) async-start(bf16[4,48,32,512]{3,2,1,0:T(8,128)(2,1)} %get-tuple-element.107), calls=%async_computation | async-start | bytes 12582912 | tf_op jit(solution)/shard_map/all_to_all | solution.py:627
  269.8 8.1 %collective-permute-start.23 = (bf16[16,64,256]{2,1,0:T(8,128)(2,1)S(1)}, bf16[16,64,256]{2,1,0:T(8,128)(2,1)S(1)}, u32[]{:S(2)}, u32[]{:S(2)}) collective-permute-start(bf16[16,64,256]{2,1,0:T(8,128)(2,1)S(1)} %get-tuple-element.115), channel_id=1, source_target_pairs={{0,1},{1,0},{2,3},{3,2},{4,5},{5,4},{6,7},{7,6},{8,9},{9,8},{10,11... | collective-permute-start | bytes 1572872 | tf_op jit(solution)/shard_map/ppermute | solution.py:96
  269.9 8.1 %collective-permute-start.24 = (bf16[16,64,256]{2,1,0:T(8,128)(2,1)S(1)}, bf16[16,64,256]{2,1,0:T(8,128)(2,1)S(1)}, u32[]{:S(2)}, u32[]{:S(2)}) collective-permute-start(bf16[16,64,256]{2,1,0:T(8,128)(2,1)S(1)} %get-tuple-element.116), channel_id=1, source_target_pairs={{0,1},{1,0},{2,3},{3,2},{4,5},{5,4},{6,7},{7,6},{8,9},{9,8},{10,11... | collective-permute-start | bytes 1572872 | tf_op jit(solution)/shard_map/ppermute | solution.py:96
  277.4 5.3 %collective-permute-start.20 = (bf16[16,64,256]{2,1,0:T(8,128)(2,1)S(1)}, bf16[16,64,256]{2,1,0:T(8,128)(2,1)S(1)}, u32[]{:S(2)}, u32[]{:S(2)}) collective-permute-start(bf16[16,64,256]{2,1,0:T(8,128)(2,1)S(1)} %get-tuple-element.110), channel_id=1, source_target_pairs={{0,1},{1,0},{2,3},{3,2},{4,5},{5,4},{6,7},{7,6},{8,9},{9,8},{10,11... | collective-permute-start | bytes 1572872 | tf_op jit(solution)/shard_map/ppermute | solution.py:96
  277.6 5.2 %collective-permute-start.21 = (bf16[16,64,256]{2,1,0:T(8,128)(2,1)S(1)}, bf16[16,64,256]{2,1,0:T(8,128)(2,1)S(1)}, u32[]{:S(2)}, u32[]{:S(2)}) collective-permute-start(bf16[16,64,256]{2,1,0:T(8,128)(2,1)S(1)} %get-tuple-element.111), channel_id=1, source_target_pairs={{0,1},{1,0},{2,3},{3,2},{4,5},{5,4},{6,7},{7,6},{8,9},{9,8},{10,11... | collective-permute-start | bytes 1572872 | tf_op jit(solution)/shard_map/ppermute | solution.py:96
  281.2 14.8 %collective-permute-start.25 = (bf16[16,64,256]{2,1,0:T(8,128)(2,1)S(1)}, bf16[16,64,256]{2,1,0:T(8,128)(2,1)S(1)}, u32[]{:S(2)}, u32[]{:S(2)}) collective-permute-start(bf16[16,64,256]{2,1,0:T(8,128)(2,1)S(1)} %get-tuple-element.118), channel_id=1, source_target_pairs={{0,2},{1,3},{2,0},{3,1},{4,6},{5,7},{6,4},{7,5},{8,10},{9,11},{10,... | collective-permute-start | bytes 1572872 | tf_op jit(solution)/shard_map/ppermute | solution.py:96
  286.0 20.4 %collective-permute-start.22 = (bf16[16,64,256]{2,1,0:T(8,128)(2,1)S(1)}, bf16[16,64,256]{2,1,0:T(8,128)(2,1)S(1)}, u32[]{:S(2)}, u32[]{:S(2)}) collective-permute-start(bf16[16,64,256]{2,1,0:T(8,128)(2,1)S(1)} %get-tuple-element.113), channel_id=1, source_target_pairs={{0,2},{1,3},{2,0},{3,1},{4,6},{5,7},{6,4},{7,5},{8,10},{9,11},{10,... | collective-permute-start | bytes 1572872 | tf_op jit(solution)/shard_map/ppermute | solution.py:96
  297.3 9.1 %copy-start.3 = (f32[16,64,256]{2,1,0:T(8,128)S(1)}, f32[16,64,256]{2,1,0:T(8,128)}, u32[]{:S(2)}) copy-start(f32[16,64,256]{2,1,0:T(8,128)} %get-tuple-element.112.mine_ref) | copy-start | bytes 3145732
  401.3 52.2 %all-to-all-start.1 = ((bf16[4,16,32,512]{3,2,1,0:T(8,128)(2,1)}), bf16[4,16,32,512]{3,2,1,0:T(8,128)(2,1)S(1)}, u32[]{:S(2)}, u32[]{:S(2)}) async-start(bf16[4,16,32,512]{3,2,1,0:T(8,128)(2,1)} %get-tuple-element.119), calls=%async_computation.1 | async-start | bytes 4194304 | tf_op jit(solution)/shard_map/all_to_all | solution.py:627
  418.5 2.3 collective-permute-start.26
  418.5 3.4 collective-permute-start.27
  426.7 19.6 %collective-permute-start.28 = (bf16[24,64,256]{2,1,0:T(8,128)(2,1)S(1)}, bf16[24,64,256]{2,1,0:T(8,128)(2,1)S(1)}, u32[]{:S(2)}, u32[]{:S(2)}) collective-permute-start(bf16[24,64,256]{2,1,0:T(8,128)(2,1)S(1)} %get-tuple-element.124), channel_id=1, source_target_pairs={{0,2},{1,3},{2,0},{3,1},{4,6},{5,7},{6,4},{7,5},{8,10},{9,11},{10,... | collective-permute-start | bytes 2359304 | tf_op jit(solution)/shard_map/ppermute | solution.py:96
  459.1 5.3 %collective-permute-start.32 = (bf16[4,64,256]{2,1,0:T(8,128)(2,1)S(1)}, bf16[4,64,256]{2,1,0:T(8,128)(2,1)S(1)}, u32[]{:S(2)}, u32[]{:S(2)}) collective-permute-start(bf16[4,64,256]{2,1,0:T(8,128)(2,1)S(1)} %get-tuple-element.135), channel_id=1, source_target_pairs={{0,1},{1,0},{2,3},{3,2},{4,5},{5,4},{6,7},{7,6},{8,9},{9,8},{10,11... | collective-permute-start | bytes 393224 | tf_op jit(solution)/shard_map/ppermute | solution.py:96
  459.1 5.3 %collective-permute-start.33 = (bf16[4,64,256]{2,1,0:T(8,128)(2,1)S(1)}, bf16[4,64,256]{2,1,0:T(8,128)(2,1)S(1)}, u32[]{:S(2)}, u32[]{:S(2)}) collective-permute-start(bf16[4,64,256]{2,1,0:T(8,128)(2,1)S(1)} %get-tuple-element.136), channel_id=1, source_target_pairs={{0,1},{1,0},{2,3},{3,2},{4,5},{5,4},{6,7},{7,6},{8,9},{9,8},{10,11... | collective-permute-start | bytes 393224 | tf_op jit(solution)/shard_map/ppermute | solution.py:96
  463.9 2.7 collective-permute-start.29
  463.9 2.7 collective-permute-start.30
  465.0 6.4 %collective-permute-start.34 = (bf16[4,64,256]{2,1,0:T(8,128)(2,1)S(1)}, bf16[4,64,256]{2,1,0:T(8,128)(2,1)S(1)}, u32[]{:S(2)}, u32[]{:S(2)}) collective-permute-start(bf16[4,64,256]{2,1,0:T(8,128)(2,1)S(1)} %get-tuple-element.138), channel_id=1, source_target_pairs={{0,2},{1,3},{2,0},{3,1},{4,6},{5,7},{6,4},{7,5},{8,10},{9,11},{10,... | collective-permute-start | bytes 393224 | tf_op jit(solution)/shard_map/ppermute | solution.py:96
  467.2 6.1 %collective-permute-start.31 = (bf16[4,64,256]{2,1,0:T(8,128)(2,1)S(1)}, bf16[4,64,256]{2,1,0:T(8,128)(2,1)S(1)}, u32[]{:S(2)}, u32[]{:S(2)}) collective-permute-start(bf16[4,64,256]{2,1,0:T(8,128)(2,1)S(1)} %get-tuple-element.133), channel_id=1, source_target_pairs={{0,2},{1,3},{2,0},{3,1},{4,6},{5,7},{6,4},{7,5},{8,10},{9,11},{10,... | collective-permute-start | bytes 393224 | tf_op jit(solution)/shard_map/ppermute | solution.py:96
  (10 other events, 10.8 us)

commit v12 on v10

--- a/solution.py
+++ b/solution.py
@@ -96,7 +96,9 @@
     return lax.ppermute(value, axis, pairs)
 
 
-def call(body, me, args, in_specs, outs, out_specs, grid=(1,), scratch=(), aliases=None):
+def call(
+    body, me, args, in_specs, outs, out_specs, grid=(1,), scratch=(), aliases=None, flops=1
+):
     return pl.pallas_call(
         body,
         out_shape=outs,
@@ -109,7 +111,7 @@
         ),
         input_output_aliases=aliases or {},
         compiler_params=pltpu.CompilerParams(vmem_limit_bytes=52 * 2**20),
-        cost_estimate=pl.CostEstimate(flops=1, bytes_accessed=1, transcendentals=0),
+        cost_estimate=pl.CostEstimate(flops=flops, bytes_accessed=1, transcendentals=0),
     )(me, *args)
 
 
@@ -569,6 +571,7 @@
             pltpu.VMEM((group, 4, size // 4, rows), BF16),
             pltpu.VMEM((group, size, size), F32),
         ],
+        flops=200 * 2 * count * size * size * rows,
     )
 
 
@@ -629,7 +632,7 @@
         else:
             got.append([pieces[0]] + [flip(pieces[bits], "gene", bits) for bits in (1, 2, 3)])
 
-    launch(0, *back[2][1:])
+    launch(0)
     denoised, shares = None, [None, None]
     back = sum(back, [])
 

time: 475 us -> 467 us (0.983)
  waiting for transfers between devices: 264 us -> 259 us
  transfers between devices with their start and end apart: 37 -> 37, of which waited for: 18 -> 17; matrix products, arithmetic and copies ran while one was open for 1% -> 1% of each run, Pallas kernels for 31% -> 31%
where the time goes in v12:
time: 467 us; the launch traced here: 466 us
  waiting for transfers between devices  259 us (55%)
  Pallas kernels  151 us (32%)
  starting transfers between devices  43.5 us (9%)
  local copies, waits for them, and re-layouts  11.1 us (2%)
    pallas_call x23, Pallas kernels, call(): pl.pallas_call(body, out_shape=outs, grid_spec=pltpu.PrefetchScalarGridSp...  151 us
    ppermute x35, waiting for transfers between devices, flip(): return lax.ppermute(value, axis, pairs)  142 us
    all_to_all x2, waiting for transfers between devices, launch(): lax.all_to_all(pieces[0], 'gene', split_axis=0, concat_axis=0, tiled=True)  117 us
    ppermute x35, starting transfers between devices, flip(): return lax.ppermute(value, axis, pairs)  33.8 us
    all_to_all x2, starting transfers between devices, launch(): lax.all_to_all(pieces[0], 'gene', split_axis=0, concat_axis=0, tiled=True)  9.69 us
  transfers between devices with their start and end apart: 37, of which 17 were waited for; matrix products, arithmetic and copies ran while one was open for 1% of the time, Pallas kernels for 31%

profile of v12, /device:TPU:0, one launch (start us, length us, event | category | flops | bytes accessed | tf_op | source)
XLA Modules:
  0.0 466.0 jit_solution(2336055540019046998)
XLA Ops:
  1.0 4.4 shard_map.103
  5.5 4.0 collective-permute-start.1
  11.1 8.1 %shard_map.104 = (bf16[32,32,512]{2,1,0:T(8,128)(2,1)S(1)}, bf16[32,32,512]{2,1,0:T(8,128)(2,1)}, bf16[32,32,512]{2,1,0:T(8,128)(2,1)}, bf16[32,32,512]{2,1,0:T(8,128)(2,1)}) custom-call(s32[2]{0:T(128)S(1)} %pad_add_fusion.me_ref._, bf16[256,256]{1,0:T(8,128)(2,1)S(1)} %fusion.turn_ref, bf16[32,256,256]{2,1,0:T(8,128)(2,1)} %refs_1_.5, ...), custom_call_target="tpu_custom_call" | custom-call | flops 1 | bytes 1 | tf_op jit(solution)/shard_map/pallas_call | solution.py:102
  20.2 37.8 %shard_map.105 = (bf16[512,8192]{1,0:T(8,128)(2,1)}, bf16[2,512,768]{2,1,0:T(8,128)(2,1)S(1)}, f32[2,512,768]{2,1,0:T(8,128)}) custom-call(s32[2]{0:T(128)S(1)} %pad_add_fusion.me_ref._, bf16[512,8192]{1,0:T(8,128)(2,1)} %value_ref, s32[512,8192]{1,0:T(8,128)} %mask_ref.1, bf16[1,8192]{1,0:T(2,128)(2,1)S(1)} %reshape.9.fill_ref, bf16[8192,3072]{1,0:T(8,128)(2,1)} %weight_ref.1), custom_call_target="tpu_custom_call" | custom-call | flops 1 | bytes 1 | tf_op jit(solution)/shard_map/pallas_call | solution.py:102
  58.0 1.9 collective-permute-start.3
  59.9 2.5 collective-permute-start.5
  62.4 4.5 shard_map.106
  67.7 6.4 %copy.16 = bf16[32,256,256]{1,2,0:T(8,128)(2,1)} copy(bf16[32,256,256]{2,1,0:T(8,128)(2,1)} %param.13) | data formatting | bytes 8388608 | tf_op jit(solution)/shard_map/optimization_barrier | solution.py:91
  74.1 20.6 %collective-permute-done.3.came_ref = bf16[2,512,768]{2,1,0:T(8,128)(2,1)} collective-permute-done((bf16[2,512,768]{2,1,0:T(8,128)(2,1)S(1)}, bf16[2,512,768]{2,1,0:T(8,128)(2,1)}, u32[]{:S(2)}, u32[]{:S(2)}) %collective-permute-start.3) | collective-permute-done | bytes 1572896 | tf_op jit(solution)/shard_map/ppermute | solution.py:96
  94.8 4.2 shard_map.107
  98.9 3.6 collective-permute-start.4
  102.5 17.8 %collective-permute-done.5.refs_7_ = bf16[32,32,512]{2,1,0:T(8,128)(2,1)} collective-permute-done((bf16[32,32,512]{2,1,0:T(8,128)(2,1)}, bf16[32,32,512]{2,1,0:T(8,128)(2,1)}, u32[]{:S(2)}, u32[]{:S(2)}) %collective-permute-start.5) | collective-permute-done | bytes 1048608 | tf_op jit(solution)/shard_map/ppermute | solution.py:96
  120.4 31.5 %collective-permute-done.4.came_ref = bf16[512,768]{1,0:T(8,128)(2,1)S(1)} collective-permute-done((bf16[512,768]{1,0:T(8,128)(2,1)S(1)}, bf16[512,768]{1,0:T(8,128)(2,1)S(1)}, u32[]{:S(2)}, u32[]{:S(2)}) %collective-permute-start.4) | collective-permute-done | bytes 786464 | tf_op jit(solution)/shard_map/ppermute | solution.py:96
  151.8 1.9 collective-permute-start.15
  153.7 3.2 shard_map.108
  156.9 1.6 collective-permute-start.7
  159.0 7.2 %collective-permute-done.7.refs_2_ = bf16[512,256]{1,0:T(8,128)(2,1)S(1)} collective-permute-done((bf16[512,256]{1,0:T(8,128)(2,1)S(1)}, bf16[512,256]{1,0:T(8,128)(2,1)S(1)}, u32[]{:S(2)}, u32[]{:S(2)}) %collective-permute-start.7) | collective-permute-done | bytes 262176 | tf_op jit(solution)/shard_map/ppermute | solution.py:96
  166.8 3.5 collective-permute-done.10.refs_6_
  170.3 1.5 collective-permute-done.11.refs_7_
  172.6 7.2 %shard_map.109.own = bf16[512,256]{1,0:T(8,128)(2,1)S(1)} custom-call(s32[2]{0:T(128)S(1)} %pad_add_fusion.me_ref._, bf16[512,256]{1,0:T(8,128)(2,1)S(1)} %get-tuple-element.88.query_ref, bf16[512,256]{1,0:T(8,128)(2,1)S(1)} %get-tuple-element.89.refs_0_, bf16[512,256]{1,0:T(8,128)(2,1)S(1)} %collective-permute-done.6.refs_1_, ...), custom_call_target="tpu_custom_call" | custom-call | flops 1 | bytes 1 | tf_op jit(solution)/shard_map/pallas_call | solution.py:102
  179.8 1.4 collective-permute-start.13
  181.2 1.7 collective-permute-start.12
  182.9 27.5 %collective-permute-done.13.far = bf16[512,256]{1,0:T(8,128)(2,1)S(1)} collective-permute-done((bf16[512,256]{1,0:T(8,128)(2,1)S(1)}, bf16[512,256]{1,0:T(8,128)(2,1)S(1)}, u32[]{:S(2)}, u32[]{:S(2)}) %collective-permute-start.13) | collective-permute-done | bytes 262176 | tf_op jit(solution)/shard_map/ppermute | solution.py:96
  211.1 2.5 collective-permute-start.18
  213.6 10.6 %collective-permute-done.16.rest = bf16[512,256]{1,0:T(8,128)(2,1)S(1)} collective-permute-done((bf16[512,256]{1,0:T(8,128)(2,1)S(1)}, bf16[512,256]{1,0:T(8,128)(2,1)S(1)}, u32[]{:S(2)}, u32[]{:S(2)}) %collective-permute-start.16) | collective-permute-done | bytes 262176 | tf_op jit(solution)/shard_map/ppermute | solution.py:96
  224.2 1.4 collective-permute-start.19
  225.6 24.5 %shard_map.110 = (bf16[512,8192]{1,0:T(8,128)(2,1)}, bf16[4,48,32,512]{3,2,1,0:T(8,128)(2,1)}, bf16[4,16,32,512]{3,2,1,0:T(8,128)(2,1)}) custom-call(s32[2]{0:T(128)S(1)} %pad_add_fusion.me_ref._, bf16[256,256]{1,0:T(8,128)(2,1)S(1)} %fusion.turn_ref, bf16[512,256]{1,0:T(8,128)(2,1)S(1)} %shard_map.109.own, ...), custom_call_target="tpu_custom_call" | custom-call | flops 1 | bytes 1 | tf_op jit(solution)/shard_map/pallas_call | solution.py:102
  250.1 5.2 %all-to-all-start = ((bf16[4,48,32,512]{3,2,1,0:T(8,128)(2,1)}), bf16[4,48,32,512]{3,2,1,0:T(8,128)(2,1)}, u32[]{:S(2)}, u32[]{:S(2)}) async-start(bf16[4,48,32,512]{3,2,1,0:T(8,128)(2,1)} %get-tuple-element.98), calls=%async_computation | async-start | bytes 12582912 | tf_op jit(solution)/shard_map/all_to_all | solution.py:631
  255.4 7.3 %shard_map.113 = (bf16[16,64,256]{2,1,0:T(8,128)(2,1)}, bf16[16,64,256]{2,1,0:T(8,128)(2,1)}, f32[2,16,64,256]{3,2,1,0:T(8,128)}) custom-call(s32[2]{0:T(128)S(1)} %pad_add_fusion.me_ref._, bf16[32,16,512]{2,1,0:T(8,128)(2,1)S(1)} %get-tuple-element.69.refs_0_, bf16[32,16,512]{2,1,0:T(8,128)(2,1)} %copy-done.15, bf16[32,16,512]{2,1,0:T(8,128)(2,1)} %copy-done.13, ...), custom_call_target="tpu_custom_call" | custom-call | flops 214748364800 | bytes 1 | tf_op jit(solution)/shard_map/pallas_call | solution.py:102
  263.2 7.0 %shard_map.111 = (bf16[16,64,256]{2,1,0:T(8,128)(2,1)S(1)}, bf16[16,64,256]{2,1,0:T(8,128)(2,1)S(1)}, f32[2,16,64,256]{3,2,1,0:T(8,128)}) custom-call(s32[2]{0:T(128)S(1)} %pad_add_fusion.me_ref._, bf16[32,16,512]{2,1,0:T(8,128)(2,1)S(1)} %get-tuple-element.69.refs_0_, bf16[32,16,512]{2,1,0:T(8,128)(2,1)} %copy-done.15, bf16[32,16,512]{2,1,0:T(8,128)(2,1)} %copy-done.13, ...), custom_call_target="tpu_custom_call" | custom-call | flops 214748364800 | bytes 1 | tf_op jit(solution)/shard_map/pallas_call | solution.py:102
  270.8 3.5 shard_map.114
  274.3 1.5 collective-permute-start.25
  275.7 3.2 shard_map.112
  279.5 9.5 %collective-permute-done.25.came_ref = bf16[16,64,256]{2,1,0:T(8,128)(2,1)S(1)} collective-permute-done((bf16[16,64,256]{2,1,0:T(8,128)(2,1)S(1)}, bf16[16,64,256]{2,1,0:T(8,128)(2,1)S(1)}, u32[]{:S(2)}, u32[]{:S(2)}) %collective-permute-start.25) | collective-permute-done | bytes 524320 | tf_op jit(solution)/shard_map/ppermute | solution.py:96
  290.3 1.6 shard_map.115.refs_0_
  291.9 7.5 %collective-permute-done.22.came_ref = bf16[16,64,256]{2,1,0:T(8,128)(2,1)S(1)} collective-permute-done((bf16[16,64,256]{2,1,0:T(8,128)(2,1)S(1)}, bf16[16,64,256]{2,1,0:T(8,128)(2,1)S(1)}, u32[]{:S(2)}, u32[]{:S(2)}) %collective-permute-start.22) | collective-permute-done | bytes 524320 | tf_op jit(solution)/shard_map/ppermute | solution.py:96
  299.4 1.6 shard_map.116
  301.0 93.2 %all-to-all-done.refs_0_ = bf16[4,48,32,512]{3,2,1,0:T(8,128)(2,1)} async-done(((bf16[4,48,32,512]{3,2,1,0:T(8,128)(2,1)}), bf16[4,48,32,512]{3,2,1,0:T(8,128)(2,1)}, u32[]{:S(2)}, u32[]{:S(2)}) %all-to-all-start) | async-done | bytes 6291488 | tf_op jit(solution)/shard_map/all_to_all | solution.py:631
  394.2 4.4 all-to-all-start.1
  398.6 13.6 %shard_map.117 = (bf16[512,8192]{1,0:T(8,128)(2,1)}, bf16[24,64,256]{2,1,0:T(8,128)(2,1)S(1)}, bf16[24,64,256]{2,1,0:T(8,128)(2,1)S(1)}, f32[2,24,64,256]{3,2,1,0:T(8,128)}) custom-call(s32[2]{0:T(128)S(1)} %pad_add_fusion.me_ref._, bf16[4,48,32,512]{3,2,1,0:T(8,128)(2,1)} %all-to-all-done.refs_0_, bf16[32,256,256]{2,1,0:T(8,128)(2,1)} %refs_1_.5, ...), custom_call_target="tpu_custom_call" | custom-call | flops 1 | bytes 1 | tf_op jit(solution)/shard_map/pallas_call | solution.py:102
  412.7 1.8 collective-permute-done.32.came_ref
  416.5 3.9 shard_map.122
  420.4 1.5 collective-permute-start.34
  421.9 24.3 %all-to-all-done.1.refs_0_ = bf16[4,16,32,512]{3,2,1,0:T(8,128)(2,1)} async-done(((bf16[4,16,32,512]{3,2,1,0:T(8,128)(2,1)}), bf16[4,16,32,512]{3,2,1,0:T(8,128)(2,1)}, u32[]{:S(2)}, u32[]{:S(2)}) %all-to-all-start.1) | async-done | bytes 2097184 | tf_op jit(solution)/shard_map/all_to_all | solution.py:631
  446.2 4.3 shard_map.118
  451.0 4.3 shard_map.119
  456.4 1.6 collective-permute-start.31
  459.2 3.2 shard_map.123.refs_0_
  (90 shorter events, 18.0 us)
Async XLA Ops:
  5.5 52.5 %collective-permute-start.1 = (bf16[32,16,512]{2,1,0:T(8,128)(2,1)S(1)}, bf16[32,16,512]{2,1,0:T(8,128)(2,1)S(1)}, u32[]{:S(2)}, u32[]{:S(2)}) collective-permute-start(bf16[32,16,512]{2,1,0:T(8,128)(2,1)S(1)} %get-tuple-element.76), channel_id=1, source_target_pairs={{0,8},{4,12},{8,0},{12,4},{1,9},{5,13},{9,1},{13,5},{2,10},{6,14},... | collective-permute-start | bytes 1572872 | tf_op jit(solution)/shard_map/ppermute | solution.py:96
  9.5 48.5 %collective-permute-start = (bf16[32,16,512]{2,1,0:T(8,128)(2,1)}, bf16[32,16,512]{2,1,0:T(8,128)(2,1)S(1)}, u32[]{:S(2)}, u32[]{:S(2)}) collective-permute-start(bf16[32,16,512]{2,1,0:T(8,128)(2,1)} %get-tuple-element.75), channel_id=1, source_target_pairs={{0,12},{4,8},{8,4},{12,0},{1,13},{5,9},{9,5},{13,1},{2,14},{6,10},... | collective-permute-start | bytes 1572872 | tf_op jit(solution)/shard_map/ppermute | solution.py:96
  10.9 47.2 %collective-permute-start.2 = (bf16[32,16,512]{2,1,0:T(8,128)(2,1)S(1)}, bf16[32,16,512]{2,1,0:T(8,128)(2,1)S(1)}, u32[]{:S(2)}, u32[]{:S(2)}) collective-permute-start(bf16[32,16,512]{2,1,0:T(8,128)(2,1)S(1)} %get-tuple-element.77), channel_id=1, source_target_pairs={{0,4},{4,0},{8,12},{12,8},{1,5},{5,1},{9,13},{13,9},{2,6},{6,2},{1... | collective-permute-start | bytes 1572872 | tf_op jit(solution)/shard_map/ppermute | solution.py:96
  11.1 9.1 %copy-start.8 = (bf16[8192]{0:T(1024)(128)(2,1)S(1)}, bf16[8192]{0:T(1024)(128)(2,1)}, u32[]{:S(2)}) copy-start(bf16[8192]{0:T(1024)(128)(2,1)} %param.10) | copy-start | bytes 49156
  58.0 1.9 copy-start.13
  58.0 4.4 copy-start.14
  58.0 4.4 copy-start.15
  58.0 36.7 %collective-permute-start.3 = (bf16[2,512,768]{2,1,0:T(8,128)(2,1)S(1)}, bf16[2,512,768]{2,1,0:T(8,128)(2,1)}, u32[]{:S(2)}, u32[]{:S(2)}) collective-permute-start(bf16[2,512,768]{2,1,0:T(8,128)(2,1)S(1)} %get-tuple-element.78), channel_id=1, source_target_pairs={{0,4},{4,0},{8,12},{12,8},{1,5},{5,1},{9,13},{13,9},{2,6},{6,2},{1... | collective-permute-start | bytes 4718600 | tf_op jit(solution)/shard_map/ppermute | solution.py:96
  59.9 60.4 %collective-permute-start.5 = (bf16[32,32,512]{2,1,0:T(8,128)(2,1)}, bf16[32,32,512]{2,1,0:T(8,128)(2,1)}, u32[]{:S(2)}, u32[]{:S(2)}) collective-permute-start(bf16[32,32,512]{2,1,0:T(8,128)(2,1)} %get-tuple-element.86), channel_id=1, source_target_pairs={{0,12},{4,8},{8,4},{12,0},{1,13},{5,9},{9,5},{13,1},{2,14},{6,10},... | collective-permute-start | bytes 3145736 | tf_op jit(solution)/shard_map/ppermute | solution.py:96
  74.1 77.7 %copy-start.12 = (bf16[32,32,512]{2,1,0:T(8,128)(2,1)S(1)}, bf16[32,32,512]{2,1,0:T(8,128)(2,1)}, u32[]{:S(2)}) copy-start(bf16[32,32,512]{2,1,0:T(8,128)(2,1)} %get-tuple-element.92) | copy-start | bytes 3145732
  74.1 77.7 %copy-start.11 = (bf16[32,32,512]{2,1,0:T(8,128)(2,1)S(1)}, bf16[32,32,512]{2,1,0:T(8,128)(2,1)}, u32[]{:S(2)}) copy-start(bf16[32,32,512]{2,1,0:T(8,128)(2,1)} %get-tuple-element.94) | copy-start | bytes 3145732
  94.8 129.4 %copy-start.16 = (bf16[32,16,512]{2,1,0:T(8,128)(2,1)S(1)}, bf16[32,16,512]{2,1,0:T(8,128)(2,1)}, u32[]{:S(2)}) copy-start(bf16[32,16,512]{2,1,0:T(8,128)(2,1)} %get-tuple-element.104) | copy-start | bytes 1572868
  98.9 52.9 %collective-permute-start.4 = (bf16[512,768]{1,0:T(8,128)(2,1)S(1)}, bf16[512,768]{1,0:T(8,128)(2,1)S(1)}, u32[]{:S(2)}, u32[]{:S(2)}) collective-permute-start(bf16[512,768]{1,0:T(8,128)(2,1)S(1)} %get-tuple-element.84), channel_id=1, source_target_pairs={{0,8},{4,12},{8,0},{12,4},{1,9},{5,13},{9,1},{13,5},{2,10},{6,14},... | collective-permute-start | bytes 2359304 | tf_op jit(solution)/shard_map/ppermute | solution.py:96
  151.8 58.9 %collective-permute-start.14 = (bf16[32,32,512]{2,1,0:T(8,128)(2,1)S(1)}, bf16[32,32,512]{2,1,0:T(8,128)(2,1)S(1)}, u32[]{:S(2)}, u32[]{:S(2)}) collective-permute-start(bf16[32,32,512]{2,1,0:T(8,128)(2,1)S(1)} %copy-done.12), channel_id=1, source_target_pairs={{0,8},{4,12},{8,0},{12,4},{1,9},{5,13},{9,1},{13,5},{2,10},{6,14},... | collective-permute-start | bytes 3145736 | tf_op jit(solution)/shard_map/ppermute | solution.py:96
  151.8 58.9 %collective-permute-start.15 = (bf16[32,32,512]{2,1,0:T(8,128)(2,1)S(1)}, bf16[32,32,512]{2,1,0:T(8,128)(2,1)S(1)}, u32[]{:S(2)}, u32[]{:S(2)}) collective-permute-start(bf16[32,32,512]{2,1,0:T(8,128)(2,1)S(1)} %copy-done.11), channel_id=1, source_target_pairs={{0,4},{4,0},{8,12},{12,8},{1,5},{5,1},{9,13},{13,9},{2,6},{6,2},{1... | collective-permute-start | bytes 3145736 | tf_op jit(solution)/shard_map/ppermute | solution.py:96
  156.9 9.3 %collective-permute-start.7 = (bf16[512,256]{1,0:T(8,128)(2,1)S(1)}, bf16[512,256]{1,0:T(8,128)(2,1)S(1)}, u32[]{:S(2)}, u32[]{:S(2)}) collective-permute-start(bf16[512,256]{1,0:T(8,128)(2,1)S(1)} %get-tuple-element.89.refs_0_), channel_id=1, source_target_pairs={{0,2},{1,3},{2,0},{3,1},{4,6},{5,7},{6,4},{7,5},{8,10},{9,11},{10,... | collective-permute-start | bytes 786440 | tf_op jit(solution)/shard_map/ppermute | solution.py:96
  158.5 7.8 %collective-permute-start.6 = (bf16[512,256]{1,0:T(8,128)(2,1)S(1)}, bf16[512,256]{1,0:T(8,128)(2,1)S(1)}, u32[]{:S(2)}, u32[]{:S(2)}) collective-permute-start(bf16[512,256]{1,0:T(8,128)(2,1)S(1)} %get-tuple-element.89.refs_0_), channel_id=1, source_target_pairs={{0,1},{1,0},{2,3},{3,2},{4,5},{5,4},{6,7},{7,6},{8,9},{9,8},{10,11... | collective-permute-start | bytes 786440 | tf_op jit(solution)/shard_map/ppermute | solution.py:96
  158.5 11.8 %collective-permute-start.10 = (bf16[512,256]{1,0:T(8,128)(2,1)S(1)}, bf16[512,256]{1,0:T(8,128)(2,1)S(1)}, u32[]{:S(2)}, u32[]{:S(2)}) collective-permute-start(bf16[512,256]{1,0:T(8,128)(2,1)S(1)} %get-tuple-element.90.refs_4_), channel_id=1, source_target_pairs={{0,2},{1,3},{2,0},{3,1},{4,6},{5,7},{6,4},{7,5},{8,10},{9,11},{10,... | collective-permute-start | bytes 786440 | tf_op jit(solution)/shard_map/ppermute | solution.py:96
  166.2 4.1 collective-permute-start.9
  166.3 4.1 collective-permute-start.8
  170.3 1.5 copy-start.5
  170.3 1.5 collective-permute-start.11
  179.8 30.6 %collective-permute-start.13 = (bf16[512,256]{1,0:T(8,128)(2,1)S(1)}, bf16[512,256]{1,0:T(8,128)(2,1)S(1)}, u32[]{:S(2)}, u32[]{:S(2)}) collective-permute-start(bf16[512,256]{1,0:T(8,128)(2,1)S(1)} %shard_map.109.own), channel_id=1, source_target_pairs={{0,8},{4,12},{8,0},{12,4},{1,9},{5,13},{9,1},{13,5},{2,10},{6,14},... | collective-permute-start | bytes 786440 | tf_op jit(solution)/shard_map/ppermute | solution.py:96
  181.2 29.5 %collective-permute-start.12 = (bf16[512,256]{1,0:T(8,128)(2,1)S(1)}, bf16[512,256]{1,0:T(8,128)(2,1)S(1)}, u32[]{:S(2)}, u32[]{:S(2)}) collective-permute-start(bf16[512,256]{1,0:T(8,128)(2,1)S(1)} %shard_map.109.own), channel_id=1, source_target_pairs={{0,4},{4,0},{8,12},{12,8},{1,5},{5,1},{9,13},{13,9},{2,6},{6,2},{1... | collective-permute-start | bytes 786440 | tf_op jit(solution)/shard_map/ppermute | solution.py:96
  210.7 39.4 %copy-start.9 = (bf16[32,32,512]{2,1,0:T(8,128)(2,1)}, bf16[32,32,512]{2,1,0:T(8,128)(2,1)S(1)}, u32[]{:S(2)}) copy-start(bf16[32,32,512]{2,1,0:T(8,128)(2,1)S(1)} %collective-permute-done.14.refs_6_) | copy-start | bytes 3145732
  210.7 39.4 %copy-start.10 = (bf16[32,32,512]{2,1,0:T(8,128)(2,1)}, bf16[32,32,512]{2,1,0:T(8,128)(2,1)S(1)}, u32[]{:S(2)}) copy-start(bf16[32,32,512]{2,1,0:T(8,128)(2,1)S(1)} %collective-permute-done.15.refs_5_) | copy-start | bytes 3145732
  210.7 13.5 %collective-permute-start.16 = (bf16[512,256]{1,0:T(8,128)(2,1)S(1)}, bf16[512,256]{1,0:T(8,128)(2,1)S(1)}, u32[]{:S(2)}, u32[]{:S(2)}) collective-permute-start(bf16[512,256]{1,0:T(8,128)(2,1)S(1)} %collective-permute-done.13.far), channel_id=1, source_target_pairs={{0,4},{4,0},{8,12},{12,8},{1,5},{5,1},{9,13},{13,9},{2,6},{6,2},{1... | collective-permute-start | bytes 786440 | tf_op jit(solution)/shard_map/ppermute | solution.py:96
  211.1 44.3 %collective-permute-start.18 = (bf16[32,16,512]{2,1,0:T(8,128)(2,1)S(1)}, bf16[32,16,512]{2,1,0:T(8,128)(2,1)}, u32[]{:S(2)}, u32[]{:S(2)}) collective-permute-start(bf16[32,16,512]{2,1,0:T(8,128)(2,1)S(1)} %get-tuple-element.102), channel_id=1, source_target_pairs={{0,8},{4,12},{8,0},{12,4},{1,9},{5,13},{9,1},{13,5},{2,10},{6,14},... | collective-permute-start | bytes 1572872 | tf_op jit(solution)/shard_map/ppermute | solution.py:96
  224.2 31.2 %collective-permute-start.17 = (bf16[32,16,512]{2,1,0:T(8,128)(2,1)S(1)}, bf16[32,16,512]{2,1,0:T(8,128)(2,1)}, u32[]{:S(2)}, u32[]{:S(2)}) collective-permute-start(bf16[32,16,512]{2,1,0:T(8,128)(2,1)S(1)} %get-tuple-element.100), channel_id=1, source_target_pairs={{0,4},{4,0},{8,12},{12,8},{1,5},{5,1},{9,13},{13,9},{2,6},{6,2},{1... | collective-permute-start | bytes 1572872 | tf_op jit(solution)/shard_map/ppermute | solution.py:96
  224.2 31.2 %collective-permute-start.19 = (bf16[32,16,512]{2,1,0:T(8,128)(2,1)S(1)}, bf16[32,16,512]{2,1,0:T(8,128)(2,1)}, u32[]{:S(2)}, u32[]{:S(2)}) collective-permute-start(bf16[32,16,512]{2,1,0:T(8,128)(2,1)S(1)} %copy-done.16), channel_id=1, source_target_pairs={{0,12},{4,8},{8,4},{12,0},{1,13},{5,9},{9,5},{13,1},{2,14},{6,10},... | collective-permute-start | bytes 1572872 | tf_op jit(solution)/shard_map/ppermute | solution.py:96
  250.1 144.1 %all-to-all-start = ((bf16[4,48,32,512]{3,2,1,0:T(8,128)(2,1)}), bf16[4,48,32,512]{3,2,1,0:T(8,128)(2,1)}, u32[]{:S(2)}, u32[]{:S(2)}) async-start(bf16[4,48,32,512]{3,2,1,0:T(8,128)(2,1)} %get-tuple-element.98), calls=%async_computation | async-start | bytes 12582912 | tf_op jit(solution)/shard_map/all_to_all | solution.py:631
  262.7 8.1 %collective-permute-start.23 = (bf16[16,64,256]{2,1,0:T(8,128)(2,1)}, bf16[16,64,256]{2,1,0:T(8,128)(2,1)}, u32[]{:S(2)}, u32[]{:S(2)}) collective-permute-start(bf16[16,64,256]{2,1,0:T(8,128)(2,1)} %get-tuple-element.112), channel_id=1, source_target_pairs={{0,1},{1,0},{2,3},{3,2},{4,5},{5,4},{6,7},{7,6},{8,9},{9,8},{10,11... | collective-permute-start | bytes 1572872 | tf_op jit(solution)/shard_map/ppermute | solution.py:96
  262.7 8.1 %collective-permute-start.24 = (bf16[16,64,256]{2,1,0:T(8,128)(2,1)}, bf16[16,64,256]{2,1,0:T(8,128)(2,1)}, u32[]{:S(2)}, u32[]{:S(2)}) collective-permute-start(bf16[16,64,256]{2,1,0:T(8,128)(2,1)} %get-tuple-element.113), channel_id=1, source_target_pairs={{0,1},{1,0},{2,3},{3,2},{4,5},{5,4},{6,7},{7,6},{8,9},{9,8},{10,11... | collective-permute-start | bytes 1572872 | tf_op jit(solution)/shard_map/ppermute | solution.py:96
  270.2 5.5 %collective-permute-start.20 = (bf16[16,64,256]{2,1,0:T(8,128)(2,1)S(1)}, bf16[16,64,256]{2,1,0:T(8,128)(2,1)S(1)}, u32[]{:S(2)}, u32[]{:S(2)}) collective-permute-start(bf16[16,64,256]{2,1,0:T(8,128)(2,1)S(1)} %get-tuple-element.107), channel_id=1, source_target_pairs={{0,1},{1,0},{2,3},{3,2},{4,5},{5,4},{6,7},{7,6},{8,9},{9,8},{10,11... | collective-permute-start | bytes 1572872 | tf_op jit(solution)/shard_map/ppermute | solution.py:96
  270.4 5.4 %collective-permute-start.21 = (bf16[16,64,256]{2,1,0:T(8,128)(2,1)S(1)}, bf16[16,64,256]{2,1,0:T(8,128)(2,1)S(1)}, u32[]{:S(2)}, u32[]{:S(2)}) collective-permute-start(bf16[16,64,256]{2,1,0:T(8,128)(2,1)S(1)} %get-tuple-element.108), channel_id=1, source_target_pairs={{0,1},{1,0},{2,3},{3,2},{4,5},{5,4},{6,7},{7,6},{8,9},{9,8},{10,11... | collective-permute-start | bytes 1572872 | tf_op jit(solution)/shard_map/ppermute | solution.py:96
  274.3 14.8 %collective-permute-start.25 = (bf16[16,64,256]{2,1,0:T(8,128)(2,1)S(1)}, bf16[16,64,256]{2,1,0:T(8,128)(2,1)S(1)}, u32[]{:S(2)}, u32[]{:S(2)}) collective-permute-start(bf16[16,64,256]{2,1,0:T(8,128)(2,1)S(1)} %get-tuple-element.115), channel_id=1, source_target_pairs={{0,2},{1,3},{2,0},{3,1},{4,6},{5,7},{6,4},{7,5},{8,10},{9,11},{10,... | collective-permute-start | bytes 1572872 | tf_op jit(solution)/shard_map/ppermute | solution.py:96
  279.0 20.4 %collective-permute-start.22 = (bf16[16,64,256]{2,1,0:T(8,128)(2,1)S(1)}, bf16[16,64,256]{2,1,0:T(8,128)(2,1)S(1)}, u32[]{:S(2)}, u32[]{:S(2)}) collective-permute-start(bf16[16,64,256]{2,1,0:T(8,128)(2,1)S(1)} %get-tuple-element.110), channel_id=1, source_target_pairs={{0,2},{1,3},{2,0},{3,1},{4,6},{5,7},{6,4},{7,5},{8,10},{9,11},{10,... | collective-permute-start | bytes 1572872 | tf_op jit(solution)/shard_map/ppermute | solution.py:96
  290.3 9.1 %copy-start.1 = (f32[16,64,256]{2,1,0:T(8,128)S(1)}, f32[16,64,256]{2,1,0:T(8,128)}, u32[]{:S(2)}) copy-start(f32[16,64,256]{2,1,0:T(8,128)} %get-tuple-element.109.mine_ref) | copy-start | bytes 3145732
  394.2 52.1 %all-to-all-start.1 = ((bf16[4,16,32,512]{3,2,1,0:T(8,128)(2,1)}), bf16[4,16,32,512]{3,2,1,0:T(8,128)(2,1)}, u32[]{:S(2)}, u32[]{:S(2)}) async-start(bf16[4,16,32,512]{3,2,1,0:T(8,128)(2,1)} %get-tuple-element.116), calls=%async_computation.1 | async-start | bytes 4194304 | tf_op jit(solution)/shard_map/all_to_all | solution.py:631
  412.2 2.3 collective-permute-start.32
  412.2 3.4 collective-permute-start.33
  420.4 38.8 %collective-permute-start.34 = (bf16[24,64,256]{2,1,0:T(8,128)(2,1)S(1)}, bf16[24,64,256]{2,1,0:T(8,128)(2,1)S(1)}, u32[]{:S(2)}, u32[]{:S(2)}) collective-permute-start(bf16[24,64,256]{2,1,0:T(8,128)(2,1)S(1)} %get-tuple-element.134), channel_id=1, source_target_pairs={{0,2},{1,3},{2,0},{3,1},{4,6},{5,7},{6,4},{7,5},{8,10},{9,11},{10,... | collective-permute-start | bytes 2359304 | tf_op jit(solution)/shard_map/ppermute | solution.py:96
  450.5 5.3 %collective-permute-start.29 = (bf16[4,64,256]{2,1,0:T(8,128)(2,1)S(1)}, bf16[4,64,256]{2,1,0:T(8,128)(2,1)S(1)}, u32[]{:S(2)}, u32[]{:S(2)}) collective-permute-start(bf16[4,64,256]{2,1,0:T(8,128)(2,1)S(1)} %get-tuple-element.126), channel_id=1, source_target_pairs={{0,1},{1,0},{2,3},{3,2},{4,5},{5,4},{6,7},{7,6},{8,9},{9,8},{10,11... | collective-permute-start | bytes 393224 | tf_op jit(solution)/shard_map/ppermute | solution.py:96
  450.5 5.3 %collective-permute-start.30 = (bf16[4,64,256]{2,1,0:T(8,128)(2,1)S(1)}, bf16[4,64,256]{2,1,0:T(8,128)(2,1)S(1)}, u32[]{:S(2)}, u32[]{:S(2)}) collective-permute-start(bf16[4,64,256]{2,1,0:T(8,128)(2,1)S(1)} %get-tuple-element.127), channel_id=1, source_target_pairs={{0,1},{1,0},{2,3},{3,2},{4,5},{5,4},{6,7},{7,6},{8,9},{9,8},{10,11... | collective-permute-start | bytes 393224 | tf_op jit(solution)/shard_map/ppermute | solution.py:96
  455.3 2.7 collective-permute-start.26
  455.3 2.7 collective-permute-start.27
  456.4 6.4 %collective-permute-start.31 = (bf16[4,64,256]{2,1,0:T(8,128)(2,1)S(1)}, bf16[4,64,256]{2,1,0:T(8,128)(2,1)S(1)}, u32[]{:S(2)}, u32[]{:S(2)}) collective-permute-start(bf16[4,64,256]{2,1,0:T(8,128)(2,1)S(1)} %get-tuple-element.129), channel_id=1, source_target_pairs={{0,2},{1,3},{2,0},{3,1},{4,6},{5,7},{6,4},{7,5},{8,10},{9,11},{10,... | collective-permute-start | bytes 393224 | tf_op jit(solution)/shard_map/ppermute | solution.py:96
  458.6 6.1 %collective-permute-start.28 = (bf16[4,64,256]{2,1,0:T(8,128)(2,1)S(1)}, bf16[4,64,256]{2,1,0:T(8,128)(2,1)S(1)}, u32[]{:S(2)}, u32[]{:S(2)}) collective-permute-start(bf16[4,64,256]{2,1,0:T(8,128)(2,1)S(1)} %get-tuple-element.124), channel_id=1, source_target_pairs={{0,2},{1,3},{2,0},{3,1},{4,6},{5,7},{6,4},{7,5},{8,10},{9,11},{10,... | collective-permute-start | bytes 393224 | tf_op jit(solution)/shard_map/ppermute | solution.py:96
  (6 other events, 6.1 us)

commit v13 on v12

--- a/solution.py
+++ b/solution.py
@@ -580,7 +580,7 @@
     blocks, size, _ = w_first.shape
     deep = size // 4
     counts = [blocks // 4, blocks // 2, blocks // 4]
-    chunks = [(3 * deep // 4, True), (deep // 4, True)]
+    chunks = [(13 * deep // 16, True), (3 * deep // 16, True)]
     matrix = grid_turn()
     sends, back = [None] * 3, [[None] * 4 for _ in range(3)]
 
@@ -651,13 +651,14 @@
         if t + 1 < len(chunks):
             launch(t + 1, *got[t], pin)
         start, count = (n * blocks // deep for n in (sum(n for n, _ in chunks[:t]), chunks[t][0]))
-        calls = 2 if t == len(chunks) - 1 else 1
-        count //= calls
-        for low in range(0, calls * count, count):
+        rest = count % 4
+        low = 0
+        for part in (count - rest, rest) if rest else (count,):
             denoised, *send, keep = second_call(
-                me, got[t], w_second, cotangent, hidden, denoised, start + low, low, count
+                me, got[t], w_second, cotangent, hidden, denoised, start + low, low, part
             )
             sum_cells(1, start + low, send, keep)
+            low += part
         pin = shares[1]
     return (denoised, *shares)
 

time: 467 us -> 470 us (level)
  waiting for transfers between devices: 259 us -> 254 us
    pallas_call x23 -> x26, Pallas kernels: 151 us -> 154 us  [call(): pl.pallas_call(body, out_shape=outs, grid_spec=pltpu.PrefetchScalarGridSp...]
    ppermute x35 -> x38, starting transfers between devices: 33.8 us -> 35.9 us  [flip(): return lax.ppermute(value, axis, pairs)]
    ppermute x35 -> x38, waiting for transfers between devices: 142 us -> 141 us  [flip(): return lax.ppermute(value, axis, pairs)]
  transfers between devices with their start and end apart: 37 -> 40, of which waited for: 17 -> 15; matrix products, arithmetic and copies ran while one was open for 1% -> 1% of each run, Pallas kernels for 31% -> 32%
where the time goes in v13:
time: 470 us; the launch traced here: 469 us
  waiting for transfers between devices  254 us (54%)
  Pallas kernels  154 us (33%)
  starting transfers between devices  45 us (10%)
  local copies, waits for them, and re-layouts  13.8 us (3%)
    pallas_call x26, Pallas kernels, call(): pl.pallas_call(body, out_shape=outs, grid_spec=pltpu.PrefetchScalarGridSp...  154 us
    ppermute x38, waiting for transfers between devices, flip(): return lax.ppermute(value, axis, pairs)  141 us
    all_to_all x2, waiting for transfers between devices, launch(): lax.all_to_all(pieces[0], 'gene', split_axis=0, concat_axis=0, tiled=True)  114 us
    ppermute x38, starting transfers between devices, flip(): return lax.ppermute(value, axis, pairs)  35.9 us
  transfers between devices with their start and end apart: 40, of which 15 were waited for; matrix products, arithmetic and copies ran while one was open for 1% of the time, Pallas kernels for 32%

profile of v13, /device:TPU:0, one launch (start us, length us, event | category | flops | bytes accessed | tf_op | source)
XLA Modules:
  0.0 468.8 jit_solution(700943705594720725)
XLA Ops:
  1.0 4.4 shard_map.103
  5.5 4.0 collective-permute-start.1
  11.1 8.1 %shard_map.104 = (bf16[32,32,512]{2,1,0:T(8,128)(2,1)S(1)}, bf16[32,32,512]{2,1,0:T(8,128)(2,1)}, bf16[32,32,512]{2,1,0:T(8,128)(2,1)}, bf16[32,32,512]{2,1,0:T(8,128)(2,1)}) custom-call(s32[2]{0:T(128)S(1)} %pad_add_fusion.me_ref._, bf16[256,256]{1,0:T(8,128)(2,1)S(1)} %fusion.turn_ref, bf16[32,256,256]{2,1,0:T(8,128)(2,1)} %refs_1_.7, ...), custom_call_target="tpu_custom_call" | custom-call | flops 1 | bytes 1 | tf_op jit(solution)/shard_map/pallas_call | solution.py:102
  20.2 37.8 %shard_map.105 = (bf16[512,8192]{1,0:T(8,128)(2,1)}, bf16[2,512,768]{2,1,0:T(8,128)(2,1)S(1)}, f32[2,512,768]{2,1,0:T(8,128)}) custom-call(s32[2]{0:T(128)S(1)} %pad_add_fusion.me_ref._, bf16[512,8192]{1,0:T(8,128)(2,1)} %value_ref, s32[512,8192]{1,0:T(8,128)} %mask_ref.1, bf16[1,8192]{1,0:T(2,128)(2,1)S(1)} %reshape.9.fill_ref, bf16[8192,3072]{1,0:T(8,128)(2,1)} %weight_ref.1), custom_call_target="tpu_custom_call" | custom-call | flops 1 | bytes 1 | tf_op jit(solution)/shard_map/pallas_call | solution.py:102
  58.1 1.9 collective-permute-start.3
  60.0 2.5 collective-permute-start.5
  62.4 4.5 shard_map.106
  67.8 6.5 %copy.18 = bf16[32,256,256]{1,2,0:T(8,128)(2,1)} copy(bf16[32,256,256]{2,1,0:T(8,128)(2,1)} %param.13) | data formatting | bytes 8388608 | tf_op jit(solution)/shard_map/optimization_barrier | solution.py:91
  74.2 20.6 %collective-permute-done.3.came_ref = bf16[2,512,768]{2,1,0:T(8,128)(2,1)} collective-permute-done((bf16[2,512,768]{2,1,0:T(8,128)(2,1)S(1)}, bf16[2,512,768]{2,1,0:T(8,128)(2,1)}, u32[]{:S(2)}, u32[]{:S(2)}) %collective-permute-start.3) | collective-permute-done | bytes 1572896 | tf_op jit(solution)/shard_map/ppermute | solution.py:96
  94.8 4.2 shard_map.107
  99.0 3.6 collective-permute-start.4
  102.6 17.8 %collective-permute-done.5.refs_7_ = bf16[32,32,512]{2,1,0:T(8,128)(2,1)} collective-permute-done((bf16[32,32,512]{2,1,0:T(8,128)(2,1)}, bf16[32,32,512]{2,1,0:T(8,128)(2,1)}, u32[]{:S(2)}, u32[]{:S(2)}) %collective-permute-start.5) | collective-permute-done | bytes 1048608 | tf_op jit(solution)/shard_map/ppermute | solution.py:96
  120.4 31.5 %collective-permute-done.4.came_ref = bf16[512,768]{1,0:T(8,128)(2,1)S(1)} collective-permute-done((bf16[512,768]{1,0:T(8,128)(2,1)S(1)}, bf16[512,768]{1,0:T(8,128)(2,1)S(1)}, u32[]{:S(2)}, u32[]{:S(2)}) %collective-permute-start.4) | collective-permute-done | bytes 786464 | tf_op jit(solution)/shard_map/ppermute | solution.py:96
  151.9 1.9 collective-permute-start.15
  153.8 3.2 shard_map.108
  157.0 1.6 collective-permute-start.7
  159.1 7.2 %collective-permute-done.7.refs_2_ = bf16[512,256]{1,0:T(8,128)(2,1)S(1)} collective-permute-done((bf16[512,256]{1,0:T(8,128)(2,1)S(1)}, bf16[512,256]{1,0:T(8,128)(2,1)S(1)}, u32[]{:S(2)}, u32[]{:S(2)}) %collective-permute-start.7) | collective-permute-done | bytes 262176 | tf_op jit(solution)/shard_map/ppermute | solution.py:96
  166.8 3.5 collective-permute-done.10.refs_6_
  170.4 1.5 collective-permute-done.11.refs_7_
  172.6 7.2 %shard_map.109.own = bf16[512,256]{1,0:T(8,128)(2,1)S(1)} custom-call(s32[2]{0:T(128)S(1)} %pad_add_fusion.me_ref._, bf16[512,256]{1,0:T(8,128)(2,1)S(1)} %get-tuple-element.94.query_ref, bf16[512,256]{1,0:T(8,128)(2,1)S(1)} %get-tuple-element.95.refs_0_, bf16[512,256]{1,0:T(8,128)(2,1)S(1)} %collective-permute-done.6.refs_1_, ...), custom_call_target="tpu_custom_call" | custom-call | flops 1 | bytes 1 | tf_op jit(solution)/shard_map/pallas_call | solution.py:102
  181.2 1.7 collective-permute-start.12
  182.9 27.5 %collective-permute-done.13.far = bf16[512,256]{1,0:T(8,128)(2,1)S(1)} collective-permute-done((bf16[512,256]{1,0:T(8,128)(2,1)S(1)}, bf16[512,256]{1,0:T(8,128)(2,1)S(1)}, u32[]{:S(2)}, u32[]{:S(2)}) %collective-permute-start.13) | collective-permute-done | bytes 262176 | tf_op jit(solution)/shard_map/ppermute | solution.py:96
  211.1 2.5 collective-permute-start.18
  213.7 10.6 %collective-permute-done.16.rest = bf16[512,256]{1,0:T(8,128)(2,1)S(1)} collective-permute-done((bf16[512,256]{1,0:T(8,128)(2,1)S(1)}, bf16[512,256]{1,0:T(8,128)(2,1)S(1)}, u32[]{:S(2)}, u32[]{:S(2)}) %collective-permute-start.16) | collective-permute-done | bytes 262176 | tf_op jit(solution)/shard_map/ppermute | solution.py:96
  225.6 24.5 %shard_map.110 = (bf16[512,8192]{1,0:T(8,128)(2,1)}, bf16[4,52,32,512]{3,2,1,0:T(8,128)(2,1)}, bf16[4,12,32,512]{3,2,1,0:T(8,128)(2,1)}) custom-call(s32[2]{0:T(128)S(1)} %pad_add_fusion.me_ref._, bf16[256,256]{1,0:T(8,128)(2,1)S(1)} %fusion.turn_ref, bf16[512,256]{1,0:T(8,128)(2,1)S(1)} %shard_map.109.own, ...), custom_call_target="tpu_custom_call" | custom-call | flops 1 | bytes 1 | tf_op jit(solution)/shard_map/pallas_call | solution.py:102
  250.1 5.3 %all-to-all-start = ((bf16[4,52,32,512]{3,2,1,0:T(8,128)(2,1)}), bf16[4,52,32,512]{3,2,1,0:T(8,128)(2,1)}, u32[]{:S(2)}, u32[]{:S(2)}) async-start(bf16[4,52,32,512]{3,2,1,0:T(8,128)(2,1)} %get-tuple-element.104), calls=%async_computation | async-start | bytes 13631488 | tf_op jit(solution)/shard_map/all_to_all | solution.py:631
  255.5 7.3 %shard_map.113 = (bf16[16,64,256]{2,1,0:T(8,128)(2,1)}, bf16[16,64,256]{2,1,0:T(8,128)(2,1)}, f32[2,16,64,256]{3,2,1,0:T(8,128)}) custom-call(s32[2]{0:T(128)S(1)} %pad_add_fusion.me_ref._, bf16[32,16,512]{2,1,0:T(8,128)(2,1)S(1)} %get-tuple-element.75.refs_0_, bf16[32,16,512]{2,1,0:T(8,128)(2,1)} %copy-done.17, bf16[32,16,512]{2,1,0:T(8,128)(2,1)} %copy-done.15, ...), custom_call_target="tpu_custom_call" | custom-call | flops 214748364800 | bytes 1 | tf_op jit(solution)/shard_map/pallas_call | solution.py:102
  263.3 7.0 %shard_map.111 = (bf16[16,64,256]{2,1,0:T(8,128)(2,1)S(1)}, bf16[16,64,256]{2,1,0:T(8,128)(2,1)S(1)}, f32[2,16,64,256]{3,2,1,0:T(8,128)}) custom-call(s32[2]{0:T(128)S(1)} %pad_add_fusion.me_ref._, bf16[32,16,512]{2,1,0:T(8,128)(2,1)S(1)} %get-tuple-element.75.refs_0_, bf16[32,16,512]{2,1,0:T(8,128)(2,1)} %copy-done.17, bf16[32,16,512]{2,1,0:T(8,128)(2,1)} %copy-done.15, ...), custom_call_target="tpu_custom_call" | custom-call | flops 214748364800 | bytes 1 | tf_op jit(solution)/shard_map/pallas_call | solution.py:102
  270.9 3.5 shard_map.114
  274.4 1.5 collective-permute-start.25
  275.9 3.2 shard_map.112
  279.7 9.5 %collective-permute-done.25.came_ref = bf16[16,64,256]{2,1,0:T(8,128)(2,1)S(1)} collective-permute-done((bf16[16,64,256]{2,1,0:T(8,128)(2,1)S(1)}, bf16[16,64,256]{2,1,0:T(8,128)(2,1)S(1)}, u32[]{:S(2)}, u32[]{:S(2)}) %collective-permute-start.25) | collective-permute-done | bytes 524320 | tf_op jit(solution)/shard_map/ppermute | solution.py:96
  290.4 1.6 shard_map.115.refs_0_
  292.0 7.5 %collective-permute-done.22.came_ref = bf16[16,64,256]{2,1,0:T(8,128)(2,1)S(1)} collective-permute-done((bf16[16,64,256]{2,1,0:T(8,128)(2,1)S(1)}, bf16[16,64,256]{2,1,0:T(8,128)(2,1)S(1)}, u32[]{:S(2)}, u32[]{:S(2)}) %collective-permute-start.22) | collective-permute-done | bytes 524320 | tf_op jit(solution)/shard_map/ppermute | solution.py:96
  299.6 1.6 shard_map.116
  301.2 104.3 %all-to-all-done.refs_0_ = bf16[4,52,32,512]{3,2,1,0:T(8,128)(2,1)} async-done(((bf16[4,52,32,512]{3,2,1,0:T(8,128)(2,1)}), bf16[4,52,32,512]{3,2,1,0:T(8,128)(2,1)}, u32[]{:S(2)}, u32[]{:S(2)}) %all-to-all-start) | async-done | bytes 6815776 | tf_op jit(solution)/shard_map/all_to_all | solution.py:631
  405.4 3.8 all-to-all-start.1
  409.2 13.6 %shard_map.117 = (bf16[512,8192]{1,0:T(8,128)(2,1)}, bf16[24,64,256]{2,1,0:T(8,128)(2,1)S(1)}, bf16[24,64,256]{2,1,0:T(8,128)(2,1)S(1)}, f32[2,24,64,256]{3,2,1,0:T(8,128)}) custom-call(s32[2]{0:T(128)S(1)} %pad_add_fusion.me_ref._, bf16[4,52,32,512]{3,2,1,0:T(8,128)(2,1)} %all-to-all-done.refs_0_, bf16[32,256,256]{2,1,0:T(8,128)(2,1)} %refs_1_.7, ...), custom_call_target="tpu_custom_call" | custom-call | flops 1 | bytes 1 | tf_op jit(solution)/shard_map/pallas_call | solution.py:102
  423.4 1.8 collective-permute-done.35.came_ref
  427.2 3.9 shard_map.124
  431.1 1.5 collective-permute-start.37
  432.6 3.2 shard_map.118
  435.8 9.6 %all-to-all-done.1.refs_0_ = bf16[4,12,32,512]{3,2,1,0:T(8,128)(2,1)S(1)} async-done(((bf16[4,12,32,512]{3,2,1,0:T(8,128)(2,1)}), bf16[4,12,32,512]{3,2,1,0:T(8,128)(2,1)S(1)}, u32[]{:S(2)}, u32[]{:S(2)}) %all-to-all-start.1) | async-done | bytes 1572896 | tf_op jit(solution)/shard_map/all_to_all | solution.py:631
  446.6 3.8 shard_map.119
  452.8 3.1 shard_map.120
  457.0 1.6 collective-permute-start.31
  460.4 1.6 collective-permute-start.28
  461.9 3.2 shard_map.125.refs_0_
  (103 shorter events, 24.6 us)
Async XLA Ops:
  5.5 52.6 %collective-permute-start.1 = (bf16[32,16,512]{2,1,0:T(8,128)(2,1)S(1)}, bf16[32,16,512]{2,1,0:T(8,128)(2,1)S(1)}, u32[]{:S(2)}, u32[]{:S(2)}) collective-permute-start(bf16[32,16,512]{2,1,0:T(8,128)(2,1)S(1)} %get-tuple-element.82), channel_id=1, source_target_pairs={{0,8},{4,12},{8,0},{12,4},{1,9},{5,13},{9,1},{13,5},{2,10},{6,14},... | collective-permute-start | bytes 1572872 | tf_op jit(solution)/shard_map/ppermute | solution.py:96
  9.5 48.5 %collective-permute-start = (bf16[32,16,512]{2,1,0:T(8,128)(2,1)}, bf16[32,16,512]{2,1,0:T(8,128)(2,1)S(1)}, u32[]{:S(2)}, u32[]{:S(2)}) collective-permute-start(bf16[32,16,512]{2,1,0:T(8,128)(2,1)} %get-tuple-element.81), channel_id=1, source_target_pairs={{0,12},{4,8},{8,4},{12,0},{1,13},{5,9},{9,5},{13,1},{2,14},{6,10},... | collective-permute-start | bytes 1572872 | tf_op jit(solution)/shard_map/ppermute | solution.py:96
  10.9 47.2 %collective-permute-start.2 = (bf16[32,16,512]{2,1,0:T(8,128)(2,1)S(1)}, bf16[32,16,512]{2,1,0:T(8,128)(2,1)S(1)}, u32[]{:S(2)}, u32[]{:S(2)}) collective-permute-start(bf16[32,16,512]{2,1,0:T(8,128)(2,1)S(1)} %get-tuple-element.83), channel_id=1, source_target_pairs={{0,4},{4,0},{8,12},{12,8},{1,5},{5,1},{9,13},{13,9},{2,6},{6,2},{1... | collective-permute-start | bytes 1572872 | tf_op jit(solution)/shard_map/ppermute | solution.py:96
  11.1 9.1 %copy-start.10 = (bf16[8192]{0:T(1024)(128)(2,1)S(1)}, bf16[8192]{0:T(1024)(128)(2,1)}, u32[]{:S(2)}) copy-start(bf16[8192]{0:T(1024)(128)(2,1)} %param.10) | copy-start | bytes 49156
  58.1 4.4 copy-start.16
  58.1 36.7 %collective-permute-start.3 = (bf16[2,512,768]{2,1,0:T(8,128)(2,1)S(1)}, bf16[2,512,768]{2,1,0:T(8,128)(2,1)}, u32[]{:S(2)}, u32[]{:S(2)}) collective-permute-start(bf16[2,512,768]{2,1,0:T(8,128)(2,1)S(1)} %get-tuple-element.84), channel_id=1, source_target_pairs={{0,4},{4,0},{8,12},{12,8},{1,5},{5,1},{9,13},{13,9},{2,6},{6,2},{1... | collective-permute-start | bytes 4718600 | tf_op jit(solution)/shard_map/ppermute | solution.py:96
  60.0 60.4 %collective-permute-start.5 = (bf16[32,32,512]{2,1,0:T(8,128)(2,1)}, bf16[32,32,512]{2,1,0:T(8,128)(2,1)}, u32[]{:S(2)}, u32[]{:S(2)}) collective-permute-start(bf16[32,32,512]{2,1,0:T(8,128)(2,1)} %get-tuple-element.92), channel_id=1, source_target_pairs={{0,12},{4,8},{8,4},{12,0},{1,13},{5,9},{9,5},{13,1},{2,14},{6,10},... | collective-permute-start | bytes 3145736 | tf_op jit(solution)/shard_map/ppermute | solution.py:96
  74.2 77.6 %copy-start.14 = (bf16[32,32,512]{2,1,0:T(8,128)(2,1)S(1)}, bf16[32,32,512]{2,1,0:T(8,128)(2,1)}, u32[]{:S(2)}) copy-start(bf16[32,32,512]{2,1,0:T(8,128)(2,1)} %get-tuple-element.98) | copy-start | bytes 3145732
  74.2 77.6 %copy-start.13 = (bf16[32,32,512]{2,1,0:T(8,128)(2,1)S(1)}, bf16[32,32,512]{2,1,0:T(8,128)(2,1)}, u32[]{:S(2)}) copy-start(bf16[32,32,512]{2,1,0:T(8,128)(2,1)} %get-tuple-element.100) | copy-start | bytes 3145732
  94.8 129.4 %copy-start.18 = (bf16[32,16,512]{2,1,0:T(8,128)(2,1)S(1)}, bf16[32,16,512]{2,1,0:T(8,128)(2,1)}, u32[]{:S(2)}) copy-start(bf16[32,16,512]{2,1,0:T(8,128)(2,1)} %get-tuple-element.110) | copy-start | bytes 1572868
  99.0 52.9 %collective-permute-start.4 = (bf16[512,768]{1,0:T(8,128)(2,1)S(1)}, bf16[512,768]{1,0:T(8,128)(2,1)S(1)}, u32[]{:S(2)}, u32[]{:S(2)}) collective-permute-start(bf16[512,768]{1,0:T(8,128)(2,1)S(1)} %get-tuple-element.90), channel_id=1, source_target_pairs={{0,8},{4,12},{8,0},{12,4},{1,9},{5,13},{9,1},{13,5},{2,10},{6,14},... | collective-permute-start | bytes 2359304 | tf_op jit(solution)/shard_map/ppermute | solution.py:96
  151.9 58.9 %collective-permute-start.14 = (bf16[32,32,512]{2,1,0:T(8,128)(2,1)S(1)}, bf16[32,32,512]{2,1,0:T(8,128)(2,1)S(1)}, u32[]{:S(2)}, u32[]{:S(2)}) collective-permute-start(bf16[32,32,512]{2,1,0:T(8,128)(2,1)S(1)} %copy-done.14), channel_id=1, source_target_pairs={{0,8},{4,12},{8,0},{12,4},{1,9},{5,13},{9,1},{13,5},{2,10},{6,14},... | collective-permute-start | bytes 3145736 | tf_op jit(solution)/shard_map/ppermute | solution.py:96
  151.9 58.9 %collective-permute-start.15 = (bf16[32,32,512]{2,1,0:T(8,128)(2,1)S(1)}, bf16[32,32,512]{2,1,0:T(8,128)(2,1)S(1)}, u32[]{:S(2)}, u32[]{:S(2)}) collective-permute-start(bf16[32,32,512]{2,1,0:T(8,128)(2,1)S(1)} %copy-done.13), channel_id=1, source_target_pairs={{0,4},{4,0},{8,12},{12,8},{1,5},{5,1},{9,13},{13,9},{2,6},{6,2},{1... | collective-permute-start | bytes 3145736 | tf_op jit(solution)/shard_map/ppermute | solution.py:96
  157.0 9.3 %collective-permute-start.7 = (bf16[512,256]{1,0:T(8,128)(2,1)S(1)}, bf16[512,256]{1,0:T(8,128)(2,1)S(1)}, u32[]{:S(2)}, u32[]{:S(2)}) collective-permute-start(bf16[512,256]{1,0:T(8,128)(2,1)S(1)} %get-tuple-element.95.refs_0_), channel_id=1, source_target_pairs={{0,2},{1,3},{2,0},{3,1},{4,6},{5,7},{6,4},{7,5},{8,10},{9,11},{10,... | collective-permute-start | bytes 786440 | tf_op jit(solution)/shard_map/ppermute | solution.py:96
  158.5 7.8 %collective-permute-start.6 = (bf16[512,256]{1,0:T(8,128)(2,1)S(1)}, bf16[512,256]{1,0:T(8,128)(2,1)S(1)}, u32[]{:S(2)}, u32[]{:S(2)}) collective-permute-start(bf16[512,256]{1,0:T(8,128)(2,1)S(1)} %get-tuple-element.95.refs_0_), channel_id=1, source_target_pairs={{0,1},{1,0},{2,3},{3,2},{4,5},{5,4},{6,7},{7,6},{8,9},{9,8},{10,11... | collective-permute-start | bytes 786440 | tf_op jit(solution)/shard_map/ppermute | solution.py:96
  158.5 11.8 %collective-permute-start.10 = (bf16[512,256]{1,0:T(8,128)(2,1)S(1)}, bf16[512,256]{1,0:T(8,128)(2,1)S(1)}, u32[]{:S(2)}, u32[]{:S(2)}) collective-permute-start(bf16[512,256]{1,0:T(8,128)(2,1)S(1)} %get-tuple-element.96.refs_4_), channel_id=1, source_target_pairs={{0,2},{1,3},{2,0},{3,1},{4,6},{5,7},{6,4},{7,5},{8,10},{9,11},{10,... | collective-permute-start | bytes 786440 | tf_op jit(solution)/shard_map/ppermute | solution.py:96
  166.3 4.1 collective-permute-start.9
  166.3 4.1 collective-permute-start.8
  170.3 1.5 collective-permute-start.11
  179.8 30.6 %collective-permute-start.13 = (bf16[512,256]{1,0:T(8,128)(2,1)S(1)}, bf16[512,256]{1,0:T(8,128)(2,1)S(1)}, u32[]{:S(2)}, u32[]{:S(2)}) collective-permute-start(bf16[512,256]{1,0:T(8,128)(2,1)S(1)} %shard_map.109.own), channel_id=1, source_target_pairs={{0,8},{4,12},{8,0},{12,4},{1,9},{5,13},{9,1},{13,5},{2,10},{6,14},... | collective-permute-start | bytes 786440 | tf_op jit(solution)/shard_map/ppermute | solution.py:96
  181.2 29.5 %collective-permute-start.12 = (bf16[512,256]{1,0:T(8,128)(2,1)S(1)}, bf16[512,256]{1,0:T(8,128)(2,1)S(1)}, u32[]{:S(2)}, u32[]{:S(2)}) collective-permute-start(bf16[512,256]{1,0:T(8,128)(2,1)S(1)} %shard_map.109.own), channel_id=1, source_target_pairs={{0,4},{4,0},{8,12},{12,8},{1,5},{5,1},{9,13},{13,9},{2,6},{6,2},{1... | collective-permute-start | bytes 786440 | tf_op jit(solution)/shard_map/ppermute | solution.py:96
  210.7 39.4 %copy-start.11 = (bf16[32,32,512]{2,1,0:T(8,128)(2,1)}, bf16[32,32,512]{2,1,0:T(8,128)(2,1)S(1)}, u32[]{:S(2)}) copy-start(bf16[32,32,512]{2,1,0:T(8,128)(2,1)S(1)} %collective-permute-done.14.refs_6_) | copy-start | bytes 3145732
  210.8 39.3 %copy-start.12 = (bf16[32,32,512]{2,1,0:T(8,128)(2,1)}, bf16[32,32,512]{2,1,0:T(8,128)(2,1)S(1)}, u32[]{:S(2)}) copy-start(bf16[32,32,512]{2,1,0:T(8,128)(2,1)S(1)} %collective-permute-done.15.refs_5_) | copy-start | bytes 3145732
  210.8 13.5 %collective-permute-start.16 = (bf16[512,256]{1,0:T(8,128)(2,1)S(1)}, bf16[512,256]{1,0:T(8,128)(2,1)S(1)}, u32[]{:S(2)}, u32[]{:S(2)}) collective-permute-start(bf16[512,256]{1,0:T(8,128)(2,1)S(1)} %collective-permute-done.13.far), channel_id=1, source_target_pairs={{0,4},{4,0},{8,12},{12,8},{1,5},{5,1},{9,13},{13,9},{2,6},{6,2},{1... | collective-permute-start | bytes 786440 | tf_op jit(solution)/shard_map/ppermute | solution.py:96
  211.1 44.3 %collective-permute-start.18 = (bf16[32,16,512]{2,1,0:T(8,128)(2,1)S(1)}, bf16[32,16,512]{2,1,0:T(8,128)(2,1)}, u32[]{:S(2)}, u32[]{:S(2)}) collective-permute-start(bf16[32,16,512]{2,1,0:T(8,128)(2,1)S(1)} %get-tuple-element.108), channel_id=1, source_target_pairs={{0,8},{4,12},{8,0},{12,4},{1,9},{5,13},{9,1},{13,5},{2,10},{6,14},... | collective-permute-start | bytes 1572872 | tf_op jit(solution)/shard_map/ppermute | solution.py:96
  224.2 31.2 %collective-permute-start.17 = (bf16[32,16,512]{2,1,0:T(8,128)(2,1)S(1)}, bf16[32,16,512]{2,1,0:T(8,128)(2,1)}, u32[]{:S(2)}, u32[]{:S(2)}) collective-permute-start(bf16[32,16,512]{2,1,0:T(8,128)(2,1)S(1)} %get-tuple-element.106), channel_id=1, source_target_pairs={{0,4},{4,0},{8,12},{12,8},{1,5},{5,1},{9,13},{13,9},{2,6},{6,2},{1... | collective-permute-start | bytes 1572872 | tf_op jit(solution)/shard_map/ppermute | solution.py:96
  224.2 31.2 %collective-permute-start.19 = (bf16[32,16,512]{2,1,0:T(8,128)(2,1)S(1)}, bf16[32,16,512]{2,1,0:T(8,128)(2,1)}, u32[]{:S(2)}, u32[]{:S(2)}) collective-permute-start(bf16[32,16,512]{2,1,0:T(8,128)(2,1)S(1)} %copy-done.18), channel_id=1, source_target_pairs={{0,12},{4,8},{8,4},{12,0},{1,13},{5,9},{9,5},{13,1},{2,14},{6,10},... | collective-permute-start | bytes 1572872 | tf_op jit(solution)/shard_map/ppermute | solution.py:96
  250.1 155.3 %all-to-all-start = ((bf16[4,52,32,512]{3,2,1,0:T(8,128)(2,1)}), bf16[4,52,32,512]{3,2,1,0:T(8,128)(2,1)}, u32[]{:S(2)}, u32[]{:S(2)}) async-start(bf16[4,52,32,512]{3,2,1,0:T(8,128)(2,1)} %get-tuple-element.104), calls=%async_computation | async-start | bytes 13631488 | tf_op jit(solution)/shard_map/all_to_all | solution.py:631
  262.8 8.1 %collective-permute-start.23 = (bf16[16,64,256]{2,1,0:T(8,128)(2,1)}, bf16[16,64,256]{2,1,0:T(8,128)(2,1)}, u32[]{:S(2)}, u32[]{:S(2)}) collective-permute-start(bf16[16,64,256]{2,1,0:T(8,128)(2,1)} %get-tuple-element.118), channel_id=1, source_target_pairs={{0,1},{1,0},{2,3},{3,2},{4,5},{5,4},{6,7},{7,6},{8,9},{9,8},{10,11... | collective-permute-start | bytes 1572872 | tf_op jit(solution)/shard_map/ppermute | solution.py:96
  262.9 8.1 %collective-permute-start.24 = (bf16[16,64,256]{2,1,0:T(8,128)(2,1)}, bf16[16,64,256]{2,1,0:T(8,128)(2,1)}, u32[]{:S(2)}, u32[]{:S(2)}) collective-permute-start(bf16[16,64,256]{2,1,0:T(8,128)(2,1)} %get-tuple-element.119), channel_id=1, source_target_pairs={{0,1},{1,0},{2,3},{3,2},{4,5},{5,4},{6,7},{7,6},{8,9},{9,8},{10,11... | collective-permute-start | bytes 1572872 | tf_op jit(solution)/shard_map/ppermute | solution.py:96
  270.3 5.6 %collective-permute-start.20 = (bf16[16,64,256]{2,1,0:T(8,128)(2,1)S(1)}, bf16[16,64,256]{2,1,0:T(8,128)(2,1)S(1)}, u32[]{:S(2)}, u32[]{:S(2)}) collective-permute-start(bf16[16,64,256]{2,1,0:T(8,128)(2,1)S(1)} %get-tuple-element.113), channel_id=1, source_target_pairs={{0,1},{1,0},{2,3},{3,2},{4,5},{5,4},{6,7},{7,6},{8,9},{9,8},{10,11... | collective-permute-start | bytes 1572872 | tf_op jit(solution)/shard_map/ppermute | solution.py:96
  270.5 5.4 %collective-permute-start.21 = (bf16[16,64,256]{2,1,0:T(8,128)(2,1)S(1)}, bf16[16,64,256]{2,1,0:T(8,128)(2,1)S(1)}, u32[]{:S(2)}, u32[]{:S(2)}) collective-permute-start(bf16[16,64,256]{2,1,0:T(8,128)(2,1)S(1)} %get-tuple-element.114), channel_id=1, source_target_pairs={{0,1},{1,0},{2,3},{3,2},{4,5},{5,4},{6,7},{7,6},{8,9},{9,8},{10,11... | collective-permute-start | bytes 1572872 | tf_op jit(solution)/shard_map/ppermute | solution.py:96
  274.4 14.8 %collective-permute-start.25 = (bf16[16,64,256]{2,1,0:T(8,128)(2,1)S(1)}, bf16[16,64,256]{2,1,0:T(8,128)(2,1)S(1)}, u32[]{:S(2)}, u32[]{:S(2)}) collective-permute-start(bf16[16,64,256]{2,1,0:T(8,128)(2,1)S(1)} %get-tuple-element.121), channel_id=1, source_target_pairs={{0,2},{1,3},{2,0},{3,1},{4,6},{5,7},{6,4},{7,5},{8,10},{9,11},{10,... | collective-permute-start | bytes 1572872 | tf_op jit(solution)/shard_map/ppermute | solution.py:96
  279.1 20.4 %collective-permute-start.22 = (bf16[16,64,256]{2,1,0:T(8,128)(2,1)S(1)}, bf16[16,64,256]{2,1,0:T(8,128)(2,1)S(1)}, u32[]{:S(2)}, u32[]{:S(2)}) collective-permute-start(bf16[16,64,256]{2,1,0:T(8,128)(2,1)S(1)} %get-tuple-element.116), channel_id=1, source_target_pairs={{0,2},{1,3},{2,0},{3,1},{4,6},{5,7},{6,4},{7,5},{8,10},{9,11},{10,... | collective-permute-start | bytes 1572872 | tf_op jit(solution)/shard_map/ppermute | solution.py:96
  290.4 9.1 %copy-start.3 = (f32[16,64,256]{2,1,0:T(8,128)S(1)}, f32[16,64,256]{2,1,0:T(8,128)}, u32[]{:S(2)}) copy-start(f32[16,64,256]{2,1,0:T(8,128)} %get-tuple-element.115.mine_ref) | copy-start | bytes 3145732
  405.4 40.0 %all-to-all-start.1 = ((bf16[4,12,32,512]{3,2,1,0:T(8,128)(2,1)}), bf16[4,12,32,512]{3,2,1,0:T(8,128)(2,1)S(1)}, u32[]{:S(2)}, u32[]{:S(2)}) async-start(bf16[4,12,32,512]{3,2,1,0:T(8,128)(2,1)} %get-tuple-element.122), calls=%async_computation.1 | async-start | bytes 3145728 | tf_op jit(solution)/shard_map/all_to_all | solution.py:631
  422.9 2.3 collective-permute-start.35
  422.9 3.4 collective-permute-start.36
  431.1 30.8 %collective-permute-start.37 = (bf16[24,64,256]{2,1,0:T(8,128)(2,1)S(1)}, bf16[24,64,256]{2,1,0:T(8,128)(2,1)S(1)}, u32[]{:S(2)}, u32[]{:S(2)}) collective-permute-start(bf16[24,64,256]{2,1,0:T(8,128)(2,1)S(1)} %get-tuple-element.146), channel_id=1, source_target_pairs={{0,2},{1,3},{2,0},{3,1},{4,6},{5,7},{6,4},{7,5},{8,10},{9,11},{10,... | collective-permute-start | bytes 2359304 | tf_op jit(solution)/shard_map/ppermute | solution.py:96
  450.4 5.5 %collective-permute-start.29 = (bf16[4,64,256]{2,1,0:T(8,128)(2,1)S(1)}, bf16[4,64,256]{2,1,0:T(8,128)(2,1)S(1)}, u32[]{:S(2)}, u32[]{:S(2)}) collective-permute-start(bf16[4,64,256]{2,1,0:T(8,128)(2,1)S(1)} %get-tuple-element.133), channel_id=1, source_target_pairs={{0,1},{1,0},{2,3},{3,2},{4,5},{5,4},{6,7},{7,6},{8,9},{9,8},{10,11... | collective-permute-start | bytes 393224 | tf_op jit(solution)/shard_map/ppermute | solution.py:96
  450.4 5.5 %collective-permute-start.30 = (bf16[4,64,256]{2,1,0:T(8,128)(2,1)S(1)}, bf16[4,64,256]{2,1,0:T(8,128)(2,1)S(1)}, u32[]{:S(2)}, u32[]{:S(2)}) collective-permute-start(bf16[4,64,256]{2,1,0:T(8,128)(2,1)S(1)} %get-tuple-element.134), channel_id=1, source_target_pairs={{0,1},{1,0},{2,3},{3,2},{4,5},{5,4},{6,7},{7,6},{8,9},{9,8},{10,11... | collective-permute-start | bytes 393224 | tf_op jit(solution)/shard_map/ppermute | solution.py:96
  450.9 6.1 %collective-permute-start.32 = (bf16[2,64,256]{2,1,0:T(8,128)(2,1)S(1)}, bf16[2,64,256]{2,1,0:T(8,128)(2,1)S(1)}, u32[]{:S(2)}, u32[]{:S(2)}) collective-permute-start(bf16[2,64,256]{2,1,0:T(8,128)(2,1)S(1)} %get-tuple-element.138), channel_id=1, source_target_pairs={{0,1},{1,0},{2,3},{3,2},{4,5},{5,4},{6,7},{7,6},{8,9},{9,8},{10,11... | collective-permute-start | bytes 196616 | tf_op jit(solution)/shard_map/ppermute | solution.py:96
  450.9 7.7 %collective-permute-start.33 = (bf16[2,64,256]{2,1,0:T(8,128)(2,1)S(1)}, bf16[2,64,256]{2,1,0:T(8,128)(2,1)S(1)}, u32[]{:S(2)}, u32[]{:S(2)}) collective-permute-start(bf16[2,64,256]{2,1,0:T(8,128)(2,1)S(1)} %get-tuple-element.139), channel_id=1, source_target_pairs={{0,1},{1,0},{2,3},{3,2},{4,5},{5,4},{6,7},{7,6},{8,9},{9,8},{10,11... | collective-permute-start | bytes 196616 | tf_op jit(solution)/shard_map/ppermute | solution.py:96
  455.9 3.9 collective-permute-start.26
  455.9 3.8 collective-permute-start.27
  457.0 9.3 %collective-permute-start.31 = (bf16[4,64,256]{2,1,0:T(8,128)(2,1)S(1)}, bf16[4,64,256]{2,1,0:T(8,128)(2,1)S(1)}, u32[]{:S(2)}, u32[]{:S(2)}) collective-permute-start(bf16[4,64,256]{2,1,0:T(8,128)(2,1)S(1)} %get-tuple-element.136), channel_id=1, source_target_pairs={{0,2},{1,3},{2,0},{3,1},{4,6},{5,7},{6,4},{7,5},{8,10},{9,11},{10,... | collective-permute-start | bytes 393224 | tf_op jit(solution)/shard_map/ppermute | solution.py:96
  459.2 6.0 %collective-permute-start.34 = (bf16[2,64,256]{2,1,0:T(8,128)(2,1)S(1)}, bf16[2,64,256]{2,1,0:T(8,128)(2,1)S(1)}, u32[]{:S(2)}, u32[]{:S(2)}) collective-permute-start(bf16[2,64,256]{2,1,0:T(8,128)(2,1)S(1)} %get-tuple-element.141), channel_id=1, source_target_pairs={{0,2},{1,3},{2,0},{3,1},{4,6},{5,7},{6,4},{7,5},{8,10},{9,11},{10,... | collective-permute-start | bytes 196616 | tf_op jit(solution)/shard_map/ppermute | solution.py:96
  460.4 7.3 %collective-permute-start.28 = (bf16[2,64,256]{2,1,0:T(8,128)(2,1)S(1)}, bf16[2,64,256]{2,1,0:T(8,128)(2,1)S(1)}, u32[]{:S(2)}, u32[]{:S(2)}) collective-permute-start(bf16[2,64,256]{2,1,0:T(8,128)(2,1)S(1)} %get-tuple-element.131), channel_id=1, source_target_pairs={{0,2},{1,3},{2,0},{3,1},{4,6},{5,7},{6,4},{7,5},{8,10},{9,11},{10,... | collective-permute-start | bytes 196616 | tf_op jit(solution)/shard_map/ppermute | solution.py:96
  (11 other events, 16.6 us)
